TPU v7x, 32 devices: a whole 2x2x4 slice. The times are simulated.
32 devices in a mesh: dp: 4 (over z), ctx: 8 (over y, x, core).
Axes of the slice: x: 2, y: 2, z: 4, core: 2. Of those that a mesh axis runs over, the one named last changes fastest.
Arguments:
- tokens: bfloat16 [8, 1536, 1152], P('dp', 'ctx'), may hold values from -6 to 6
- cotangent: bfloat16 [8, 1536, 1152], P('dp', 'ctx'), may hold values from -12 to 12
- segment_ids: int32 [8, 1536], P('dp', 'ctx'), may hold values from 0 to 4, as said below
- query_weight: bfloat16 [1152, 1024], P('ctx'), may hold values from -0.1875 to 0.1875
- key_weight: bfloat16 [1152, 256], P('ctx'), may hold values from -0.1875 to 0.1875
- value_weight: bfloat16 [1152, 256], P('ctx'), may hold values from -0.1875 to 0.1875
- out_weight: bfloat16 [1024, 1152], P('ctx'), may hold values from -0.1875 to 0.1875
- gate_weight: bfloat16 [1152, 6912], P('ctx'), may hold values from -0.1875 to 0.1875
- up_weight: bfloat16 [1152, 6912], P('ctx'), may hold values from -0.1875 to 0.1875
- down_weight: bfloat16 [6912, 1152], P('ctx'), may hold values from -0.078125 to 0.078125
- gain_input: bfloat16 [1152], replicated, may hold values from 0.25 to 1.75
- gain_query: bfloat16 [256], replicated, may hold values from 0.25 to 1.75
- gain_key: bfloat16 [256], replicated, may hold values from 0.25 to 1.75
- gain_attended: bfloat16 [1152], replicated, may hold values from 0.25 to 1.75
- gain_feed: bfloat16 [1152], replicated, may hold values from 0.25 to 1.75
- gain_result: bfloat16 [1152], replicated, may hold values from 0.25 to 1.75
Outputs:
- result: bfloat16 [8, 1536, 1152], P('dp', 'ctx')
- tokens_grad: bfloat16 [8, 1536, 1152], P('dp', 'ctx')
- query_weight_grad: float32 [1152, 1024], P('ctx')
- key_weight_grad: float32 [1152, 256], P('ctx')
- value_weight_grad: float32 [1152, 256], P('ctx')
- out_weight_grad: float32 [1024, 1152], P('ctx')
- gate_weight_grad: float32 [1152, 6912], P('ctx')
- up_weight_grad: float32 [1152, 6912], P('ctx')
- down_weight_grad: float32 [6912, 1152], P('ctx')
- gain_input_grad: float32 [1152], replicated
- gain_query_grad: float32 [256], replicated
- gain_key_grad: float32 [256], replicated
- gain_attended_grad: float32 [1152], replicated
- gain_feed_grad: float32 [1152], replicated
- gain_result_grad: float32 [1152], replicated
Inputs may be any that keep to these rules, and one draw needn't show every extreme that they name: `segment_ids`: taken in position order, ids never fall along a row; every row holds documents 0 to 4, each of one token or more; document 2 begins within the first 96 positions and ends within the last 96 positions.
All inputs are finite; a program needn't handle non-finite values.
Results may differ from a plain program's by a relative error of at most 0.024.
Values may be sent and summed in bfloat16 or wider, within the bound.
No kernel may reach another device: no remote copies, remote signals or barrier semaphores. Data moves between devices by JAX's collectives and lax.ppermute only.
A program may use at most 320 MiB of HBM per device.

v0:
```python
import jax
import jax.numpy as jnp
from jax import lax
from jax.sharding import PartitionSpec as P

EPSILON = 1e-06
ROPE_BASE = 1000000.0
SCORE_SCALE = 0.0625
NEGATIVE = -1e30
GELU_COEFF = 0.044715
ROOT_TWO_PI = 0.7978845608028654


def for_sending(x):
    return jax.tree.map(lambda a: a.astype(jnp.bfloat16) if a.dtype == jnp.float32 else a, x)


def rms_norm(values, gain_values):
    return (
        values
        * lax.rsqrt(jnp.mean(values * values, axis=-1, keepdims=True) + EPSILON)
        * gain_values
    )


def angles_for(positions, width):
    half_width = width // 2
    frequencies = jnp.power(ROPE_BASE, -jnp.arange(half_width, dtype=jnp.float32) / half_width)
    return positions[:, None] * frequencies[None, :]


def rotary(values, angles):
    half_width = values.shape[-1] // 2
    cosine = jnp.cos(angles)
    sine_part = jnp.sin(angles)
    first_half = values[..., :half_width]
    second_half = values[..., half_width:]
    return jnp.concatenate(
        [
            first_half * cosine - second_half * sine_part,
            second_half * cosine + first_half * sine_part,
        ],
        axis=-1,
    )


def geglu(gate_proj, up_proj):
    cubic = gate_proj + GELU_COEFF * gate_proj * gate_proj * gate_proj
    return 0.5 * gate_proj * (1.0 + jnp.tanh(ROOT_TWO_PI * cubic)) * up_proj


def stored_places(slot_count, span, pair_count):
    slots = jnp.arange(slot_count, dtype=jnp.int32)
    block = slots // span
    device = block // 2
    span_index = jnp.where(block % 2 == 1, 2 * pair_count - 1 - device, device)
    return span_index * span + slots % span


def reduce_grads(gradients):
    summed = jax.tree.map(
        lambda part: part.astype(jnp.float32),
        lax.psum_scatter(for_sending(gradients), "ctx", scatter_dimension=0, tiled=True),
    )
    return jax.tree.map(lambda part: part.astype(jnp.float32), lax.psum(for_sending(summed), "dp"))


def per_device(
    tokens,
    cotangent,
    segment_ids,
    query_weight,
    key_weight,
    value_weight,
    out_weight,
    gate_weight,
    up_weight,
    down_weight,
    gain_input,
    gain_query,
    gain_key,
    gain_attended,
    gain_feed,
    gain_result,
):
    bf16 = jnp.bfloat16
    wide = jnp.float32
    query_full, key_full, value_full, out_full, gate_full, up_full, down_full = (
        lax.all_gather(query_weight, "ctx", axis=0, tiled=True),
        lax.all_gather(key_weight, "ctx", axis=0, tiled=True),
        lax.all_gather(value_weight, "ctx", axis=0, tiled=True),
        lax.all_gather(out_weight, "ctx", axis=0, tiled=True),
        lax.all_gather(gate_weight, "ctx", axis=0, tiled=True),
        lax.all_gather(up_weight, "ctx", axis=0, tiled=True),
        lax.all_gather(down_weight, "ctx", axis=0, tiled=True),
    )
    row_segments = lax.all_gather(segment_ids, "ctx", axis=1, tiled=True)
    row_count = tokens.shape[0]
    count_local = tokens.shape[1]
    width = tokens.shape[2]
    total = row_count * count_local
    head_width = gain_query.shape[0]
    head_count = query_full.shape[1] // head_width
    pair_count = lax.axis_size("ctx")
    span = count_local // 2
    device_index = lax.axis_index("ctx")
    offsets = jnp.arange(span, dtype=jnp.int32)
    local_places = jnp.concatenate(
        [device_index * span + offsets, (2 * pair_count - 1 - device_index) * span + offsets]
    )
    places_all = stored_places(row_segments.shape[1], span, pair_count)
    starts = jnp.sum((row_segments[:, None, :] < segment_ids[:, :, None]).astype(jnp.int32), axis=2)
    positions = (local_places[None, :] - starts).reshape(total)
    angles = angles_for(positions.astype(wide), head_width)
    allowed = (segment_ids[:, :, None] == row_segments[:, None, :]) & (
        local_places[None, :, None] >= places_all[None, None, :]
    )
    scale_input = gain_input.astype(wide)
    scale_query = gain_query.astype(wide)
    scale_key = gain_key.astype(wide)
    scale_attended = gain_attended.astype(wide)
    scale_feed = gain_feed.astype(wide)
    scale_result = gain_result.astype(wide)

    def query_shape(raw_rows, gain_values):
        return rotary(
            rms_norm(raw_rows.reshape(total, head_count, head_width), gain_values),
            angles[:, None, :],
        )

    def key_shape(raw_rows, gain_values):
        return rotary(rms_norm(raw_rows, gain_values), angles)

    row_tokens = tokens.reshape(total, width).astype(wide)
    normed_wide, normed_pull = jax.vjp(rms_norm, row_tokens, scale_input)
    normed = normed_wide.astype(bf16)
    query_proj = jnp.dot(normed, query_full, preferred_element_type=wide)
    key_proj = jnp.dot(normed, key_full, preferred_element_type=wide)
    value_local = jnp.dot(normed, value_full, preferred_element_type=wide).astype(bf16)
    query_wide, query_pull = jax.vjp(query_shape, query_proj, scale_query)
    key_wide, key_pull = jax.vjp(key_shape, key_proj, scale_key)
    query_rot = query_wide.astype(bf16)
    key_local = key_wide.astype(bf16)
    key_rows = key_local.reshape(row_count, count_local, head_width)
    value_rows = value_local.reshape(row_count, count_local, head_width)
    keys_all, values_all = (
        lax.all_gather(key_rows, "ctx", axis=1, tiled=True),
        lax.all_gather(value_rows, "ctx", axis=1, tiled=True),
    )
    query_rows = query_rot.reshape(row_count, count_local, head_count, head_width)
    attended_rows = []
    log_rows = []
    for row in range(row_count):
        scores = (
            jnp.einsum("qhd,kd->hqk", query_rows[row], keys_all[row], preferred_element_type=wide)
            * SCORE_SCALE
        )
        scores = jnp.where(allowed[row][None, :, :], scores, NEGATIVE)
        maxima = jnp.max(scores, axis=-1, keepdims=True)
        exponents = jnp.exp(scores - maxima)
        totals = jnp.sum(exponents, axis=-1, keepdims=True)
        probabilities = exponents / totals
        log_rows.append(maxima + jnp.log(totals))
        attended_rows.append(
            jnp.einsum(
                "hqk,kd->qhd",
                probabilities.astype(bf16),
                values_all[row],
                preferred_element_type=wide,
            )
        )
    attended = (
        jnp.concatenate(attended_rows, axis=0).reshape(total, head_count * head_width).astype(bf16)
    )
    projected = jnp.dot(attended, out_full, preferred_element_type=wide)
    attn_normed, attn_pull = jax.vjp(rms_norm, projected, scale_attended)
    hidden = row_tokens + attn_normed
    inner_wide, inner_pull = jax.vjp(rms_norm, hidden, scale_feed)
    inner_rows = inner_wide.astype(bf16)
    gate_proj = jnp.dot(inner_rows, gate_full, preferred_element_type=wide)
    upward = jnp.dot(inner_rows, up_full, preferred_element_type=wide)
    active_wide, active_pull = jax.vjp(geglu, gate_proj, upward)
    active = active_wide.astype(bf16)
    lowered = jnp.dot(active, down_full, preferred_element_type=wide)
    out_normed, out_pull = jax.vjp(rms_norm, lowered, scale_result)
    result = hidden + out_normed
    upstream = cotangent.reshape(total, width).astype(wide)
    d_lowered, grad_result_gain = out_pull(upstream)
    d_lowered = d_lowered.astype(bf16)
    grad_down = jnp.einsum("tf,td->fd", active, d_lowered, preferred_element_type=wide)
    d_active = jnp.einsum("td,fd->tf", d_lowered, down_full, preferred_element_type=wide)
    d_gate, d_upward = active_pull(d_active)
    d_gate = d_gate.astype(bf16)
    d_upward = d_upward.astype(bf16)
    grad_gate = jnp.einsum("td,tf->df", inner_rows, d_gate, preferred_element_type=wide)
    grad_up = jnp.einsum("td,tf->df", inner_rows, d_upward, preferred_element_type=wide)
    d_inner = jnp.einsum("tf,df->td", d_gate, gate_full, preferred_element_type=wide) + jnp.einsum(
        "tf,df->td", d_upward, up_full, preferred_element_type=wide
    )
    d_hidden_part, grad_feed_gain = inner_pull(d_inner)
    d_hidden = upstream + d_hidden_part
    summed_gate, summed_up, summed_down = reduce_grads((grad_gate, grad_up, grad_down))
    d_projected, grad_attended_gain = attn_pull(d_hidden)
    d_projected = d_projected.astype(bf16)
    grad_out = jnp.einsum("tq,td->qd", attended, d_projected, preferred_element_type=wide)
    d_attended = jnp.einsum("td,qd->tq", d_projected, out_full, preferred_element_type=wide).astype(
        bf16
    )
    d_attended = d_attended.reshape(row_count, count_local, head_count, head_width)
    keys_back, values_back = (
        lax.all_gather(key_rows, "ctx", axis=1, tiled=True),
        lax.all_gather(value_rows, "ctx", axis=1, tiled=True),
    )
    key_parts = []
    value_parts = []
    query_grads = []
    for row in range(row_count):
        scores_back = (
            jnp.einsum("qhd,kd->hqk", query_rows[row], keys_back[row], preferred_element_type=wide)
            * SCORE_SCALE
        )
        scores_back = jnp.where(allowed[row][None, :, :], scores_back, NEGATIVE)
        probs_back = jnp.exp(scores_back - log_rows[row])
        d_probs = jnp.einsum(
            "qhd,kd->hqk", d_attended[row], values_back[row], preferred_element_type=wide
        )
        inner_sum = jnp.sum(probs_back * d_probs, axis=-1, keepdims=True)
        d_scores = (probs_back * (d_probs - inner_sum)).astype(bf16) * SCORE_SCALE
        value_parts.append(
            jnp.einsum(
                "hqk,qhd->kd", probs_back.astype(bf16), d_attended[row], preferred_element_type=wide
            )
        )
        key_parts.append(
            jnp.einsum("hqk,qhd->kd", d_scores, query_rows[row], preferred_element_type=wide)
        )
        query_grads.append(
            jnp.einsum("hqk,kd->qhd", d_scores, keys_back[row], preferred_element_type=wide)
        )
    d_key_rows, d_value_rows = (
        lax.psum_scatter(
            jnp.stack(key_parts).astype(jnp.bfloat16), "ctx", scatter_dimension=1, tiled=True
        ).astype(jnp.float32),
        lax.psum_scatter(
            jnp.stack(value_parts).astype(jnp.bfloat16), "ctx", scatter_dimension=1, tiled=True
        ).astype(jnp.float32),
    )
    d_query_rot = jnp.concatenate(query_grads, axis=0)
    d_query_raw, grad_query_gain = query_pull(d_query_rot)
    d_key_raw, grad_key_gain = key_pull(d_key_rows.reshape(total, head_width))
    d_query_raw = d_query_raw.astype(bf16)
    d_key_raw = d_key_raw.astype(bf16)
    d_value_raw = d_value_rows.reshape(total, head_width).astype(bf16)
    grad_query = jnp.einsum("td,tq->dq", normed, d_query_raw, preferred_element_type=wide)
    grad_key = jnp.einsum("td,tq->dq", normed, d_key_raw, preferred_element_type=wide)
    grad_value = jnp.einsum("td,tq->dq", normed, d_value_raw, preferred_element_type=wide)
    d_normed = (
        jnp.einsum("tq,dq->td", d_query_raw, query_full, preferred_element_type=wide)
        + jnp.einsum("tq,dq->td", d_key_raw, key_full, preferred_element_type=wide)
        + jnp.einsum("tq,dq->td", d_value_raw, value_full, preferred_element_type=wide)
    )
    d_tokens_part, grad_input_gain = normed_pull(d_normed)
    tokens_grad = (d_hidden + d_tokens_part).astype(bf16)
    summed_query, summed_key, summed_value, summed_out = reduce_grads(
        (grad_query, grad_key, grad_value, grad_out)
    )
    gain_sums = lax.psum(
        (
            grad_input_gain,
            grad_query_gain,
            grad_key_gain,
            grad_attended_gain,
            grad_feed_gain,
            grad_result_gain,
        ),
        ("dp", "ctx"),
    )
    return (
        result.reshape(row_count, count_local, width).astype(bf16),
        tokens_grad.reshape(row_count, count_local, width),
        summed_query,
        summed_key,
        summed_value,
        summed_out,
        summed_gate,
        summed_up,
        summed_down,
        gain_sums[0],
        gain_sums[1],
        gain_sums[2],
        gain_sums[3],
        gain_sums[4],
        gain_sums[5],
    )


def solution(mesh):
    return jax.shard_map(
        per_device,
        mesh=mesh,
        in_specs=(
            P("dp", "ctx", None),
            P("dp", "ctx", None),
            P("dp", "ctx"),
            P("ctx", None),
            P("ctx", None),
            P("ctx", None),
            P("ctx", None),
            P("ctx", None),
            P("ctx", None),
            P("ctx", None),
            P(),
            P(),
            P(),
            P(),
            P(),
            P(),
        ),
        out_specs=(
            P("dp", "ctx", None),
            P("dp", "ctx", None),
            P("ctx", None),
            P("ctx", None),
            P("ctx", None),
            P("ctx", None),
            P("ctx", None),
            P("ctx", None),
            P("ctx", None),
            P(),
            P(),
            P(),
            P(),
            P(),
            P(),
        ),
        check_vma=False,
    )
```

profile of v0, /device:TPU:0, one launch (start us, length us, event | category | flops | bytes accessed | tf_op | source)
XLA Modules:
  0.0 1335.4 jit_solution(17685818089556924929)
XLA Ops:
  8.6 1.4 fusion.50
  10.9 10.5 all-gather
  22.7 9.9 all_gather.35
  35.9 9.7 all_gather.32
  52.7 1.2 fusion.52
  53.9 3.0 copy.60
  56.9 2.6 multiply_reduce_fusion.9
  61.4 8.7 all-gather.11.cloned.1.call-done
  70.0 2.4 fusion.125
  73.3 1.4 copy-done.13
  76.5 2.2 copy-done.14
  79.5 18.7 %all-gather.9.cloned.1.call-done = bf16[2,1536,256]{2,1,0:T(8,128)(2,1)} async-done(((bf16[2,192,256]{2,1,0:T(8,128)(2,1)}), bf16[2,1536,256]{2,1,0:T(8,128)(2,1)}) %all-gather.9.cloned.1.call-update) | async-done | bytes 1572880 | tf_op jit(solution)/shard_map/all_gather | solution.py:148
  98.2 3.6 fusion.62
  104.0 25.0 %all-gather.15.cloned.1.call-done = bf16[1024,1152]{1,0:T(8,128)(2,1)} async-done(((bf16[128,1152]{1,0:T(8,128)(2,1)}), bf16[1024,1152]{1,0:T(8,128)(2,1)}) %all-gather.15.cloned.1.call-update) | async-done | bytes 2359312 | tf_op jit(solution)/shard_map/all_gather | solution.py:92
  129.0 3.0 multiply_reduce_fusion.6
  134.1 82.9 %all-gather.17.cloned.1.call-done = bf16[1152,6912]{1,0:T(8,128)(2,1)} async-done(((bf16[144,6912]{1,0:T(8,128)(2,1)}), bf16[1152,6912]{1,0:T(8,128)(2,1)}) %all-gather.17.cloned.1.call-update) | async-done | bytes 15925264 | tf_op jit(solution)/shard_map/all_gather | solution.py:93
  217.0 15.3 %fusion.127 = f32[384,6912]{1,0:T(8,128)} fusion(bf16[384,1152]{1,0:T(8,128)(2,1)S(1)} %multiply_convert_fusion.2, bf16[1152,6912]{1,0:T(8,128)(2,1)} %all-gather.17.cloned.1.call-done), kind=kOutput, calls=%fused_computation.247 | convolution fusion | flops 6115295232 | bytes 27426816 | tf_op jit(solution)/shard_map/dot_general | solution.py:180
  232.3 72.7 %all-gather.19.cloned.1.call-done = bf16[1152,6912]{1,0:T(8,128)(2,1)} async-done(((bf16[144,6912]{1,0:T(8,128)(2,1)}), bf16[1152,6912]{1,0:T(8,128)(2,1)}) %all-gather.19.cloned.1.call-update) | async-done | bytes 15925264 | tf_op jit(solution)/shard_map/all_gather | solution.py:94
  305.1 17.6 %multiply_convert_fusion.1 = (bf16[384,6912]{1,0:T(8,128)(2,1)}, f32[384,6912]{1,0:T(8,128)}) fusion(f32[384,6912]{1,0:T(8,128)} %fusion.127, bf16[384,1152]{1,0:T(8,128)(2,1)S(1)} %multiply_convert_fusion.2, bf16[1152,6912]{1,0:T(8,128)(2,1)} %all-gather.19.cloned.1.call-done), kind=kOutput, calls=%fused_computation.17 | convolution fusion | flops 6141837312 | bytes 43352064 | tf_op jit(solution)/shard_map/dot_general | solution.py:181
  322.7 70.5 %all-gather.21.cloned.1.call-done = bf16[6912,1152]{1,0:T(8,128)(2,1)} async-done(((bf16[864,1152]{1,0:T(8,128)(2,1)}), bf16[6912,1152]{1,0:T(8,128)(2,1)}) %all-gather.21.cloned.1.call-update) | async-done | bytes 15925264 | tf_op jit(solution)/shard_map/all_gather | solution.py:95
  393.3 13.1 multiply_reduce_fusion.4
  407.9 1.6 fusion.41
  409.5 21.0 %multiply_convert_fusion = (bf16[384,6912]{1,0:T(8,128)(2,1)}, bf16[384,6912]{1,0:T(8,128)(2,1)S(1)}) fusion(f32[384,6912]{1,0:T(8,128)} %fusion.127, f32[384,6912]{1,0:T(8,128)} %get-tuple-element.76, bf16[384,1152]{1,0:T(8,128)(2,1)S(1)} %get-tuple-element.49, bf16[6912,1152]{1,0:T(8,128)(2,1)} %all-gather.21.cloned.1.call-done), kind=kOutput, calls=%fused_computation.15 | convolution fusion | flops 6189613056 | bytes 48660480 | tf_op jit(solution)/shard_map/td,fd->tf/dot_general | solution.py:191
  430.5 13.5 %fusion.128 = f32[384,1152]{1,0:T(8,128)} fusion(bf16[384,6912]{1,0:T(8,128)(2,1)S(1)} %get-tuple-element.44, bf16[1152,6912]{1,0:T(8,128)(2,1)} %all-gather.17.cloned.1.call-done), kind=kOutput, calls=%fused_computation.248 | convolution fusion | flops 6115295232 | bytes 23003136 | tf_op jit(solution)/shard_map/tf,df->td/dot_general | solution.py:197
  444.1 17.0 %multiply_reduce_fusion = (f32[1152]{0:T(1024)}, f32[384]{0:T(512)}, f32[384,1152]{1,0:T(8,128)}) fusion(f32[384,1152]{1,0:T(8,128)} %copy-done.2, f32[384]{0:T(512)} %copy-done.76, f32[1152]{0:T(1024)S(1)} %copy-done.55, f32[384,1152]{1,0:T(8,128)} %fusion.128, bf16[384,6912]{1,0:T(8,128)(2,1)} %get-tuple-element.43, ...), kind=kOutput, calls=%fused_computation.100 | convolution fusion | flops 6118390272 | bytes 26554368 | tf_op jit(solution)/shard_map/tf,df->td/dot_general | solution.py:197
  461.8 3.7 multiply_reduce_fusion.1
  466.9 1.3 copy-done.23
  468.2 1.2 convolution_convert_fusion.6
  470.7 1.2 fusion.27
  471.9 1.3 pad_maximum_fusion.1
  473.9 3.0 fusion.68
  476.9 13.5 %fusion.29 = bf16[1,1536,256]{2,1,0:T(8,128)(2,1)} fusion(f32[1536,192,4]{0,1,2:T(8,128)} %fusion.68, f32[4,192,1536]{2,1,0:T(8,128)} %copy-done.14, f32[4,192]{1,0:T(4,128)S(1)} %copy-done.86, bf16[384,4,128]{0,2,1:T(8,128)(2,1)} %copy-done.43, bf16[384,4,128]{0,2,1:T(8,128)(2,1)} %copy-done.45), kind=kOutput, calls=%fused_computation.68 | convolution fusion | flops 616958208 | bytes 20455424 | tf_op jit(solution)/shard_map/hqk,qhd->kd/dot_general | solution.py:235
  490.4 3.0 fusion.69
  493.4 13.6 %fusion.28 = bf16[1,1536,256]{2,1,0:T(8,128)(2,1)} fusion(f32[1536,192,4]{0,1,2:T(8,128)} %fusion.69, f32[4,192,1536]{2,1,0:T(8,128)} %copy-done.13, f32[4,192]{1,0:T(4,128)S(1)} %copy-done.85, bf16[384,4,128]{0,2,1:T(8,128)(2,1)} %copy-done.45, bf16[384,4,128]{0,2,1:T(8,128)(2,1)S(1)} %copy-done.44), kind=kOutput, calls=%fused_computation.67 | convolution fusion | flops 616958208 | bytes 11013120 | tf_op jit(solution)/shard_map/hqk,qhd->kd/dot_general | solution.py:235
  507.0 2.5 pad_maximum_fusion
  509.6 2.3 reduce-scatter.12.cloned.1.call-done
  511.9 2.2 fusion.25
  514.2 40.0 %reduce-scatter.10.cloned.1.call-done = bf16[2,192,256]{2,1,0:T(8,128)(2,1)} async-done(((bf16[2,1536,256]{2,1,0:T(8,128)(2,1)}), bf16[2,192,256]{2,1,0:T(8,128)(2,1)}) %reduce-scatter.10.cloned.1.call-update) | async-done | bytes 196624 | tf_op jit(solution)/shard_map/reduce_scatter | solution.py:241
  556.5 1.3 convolution_convert_fusion.5
  558.1 4.0 convolution_convert_fusion.3
  562.2 11.4 fusion.57
  573.6 11.2 fusion.58
  587.9 2.9 convolution_convert_fusion.4
  590.9 13.8 %convolution_convert_fusion.1 = bf16[1152,6912]{1,0:T(8,128)(2,1)} fusion(bf16[384,1152]{1,0:T(8,128)(2,1)S(1)} %multiply_convert_fusion.2, bf16[384,6912]{1,0:T(8,128)(2,1)} %get-tuple-element.43), kind=kOutput, calls=%fused_computation.3 | convolution fusion | flops 6123257856 | bytes 22118400 | tf_op jit(solution)/shard_map/td,tf->df/dot_general | solution.py:196
  604.9 13.8 %convolution_convert_fusion.2 = bf16[1152,6912]{1,0:T(8,128)(2,1)} fusion(bf16[384,1152]{1,0:T(8,128)(2,1)S(1)} %multiply_convert_fusion.2, bf16[384,6912]{1,0:T(8,128)(2,1)} %copy-done.91), kind=kOutput, calls=%fused_computation.4 | convolution fusion | flops 6123257856 | bytes 22118400 | tf_op jit(solution)/shard_map/td,tf->df/dot_general | solution.py:195
  620.0 15.3 %convolution_convert_fusion = bf16[6912,1152]{1,0:T(8,128)(2,1)} fusion(bf16[384,6912]{1,0:T(8,128)(2,1)} %get-tuple-element.75, bf16[384,1152]{1,0:T(8,128)(2,1)S(1)} %copy-done.37), kind=kOutput, calls=%fused_computation.2 | convolution fusion | flops 6123257856 | bytes 22118400 | tf_op jit(solution)/shard_map/tf,td->fd/dot_general | solution.py:190
  635.4 40.1 %reduce-scatter.20.cloned.1.call-done = bf16[128,1152]{1,0:T(8,128)(2,1)} async-done(((bf16[1024,1152]{1,0:T(8,128)(2,1)}), bf16[128,1152]{1,0:T(8,128)(2,1)}) %reduce-scatter.20.cloned.1.call-update) | async-done | bytes 294928 | tf_op jit(solution)/shard_map/reduce_scatter | solution.py:63
  675.5 46.8 %reduce-scatter.14.cloned.1.call-done = bf16[144,1024]{1,0:T(8,128)(2,1)} async-done(((bf16[1152,1024]{1,0:T(8,128)(2,1)}), bf16[144,1024]{1,0:T(8,128)(2,1)}) %reduce-scatter.14.cloned.1.call-update) | async-done | bytes 294928 | tf_op jit(solution)/shard_map/reduce_scatter | solution.py:63
  722.3 116.4 %reduce-scatter.24.cloned.1.call-done = bf16[144,6912]{1,0:T(8,128)(2,1)} async-done(((bf16[1152,6912]{1,0:T(8,128)(2,1)}), bf16[144,6912]{1,0:T(8,128)(2,1)}) %reduce-scatter.24.cloned.1.call-update) | async-done | bytes 1990672 | tf_op jit(solution)/shard_map/reduce_scatter | solution.py:63
  838.7 116.8 %reduce-scatter.22.cloned.1.call-done = bf16[144,6912]{1,0:T(8,128)(2,1)} async-done(((bf16[1152,6912]{1,0:T(8,128)(2,1)}), bf16[144,6912]{1,0:T(8,128)(2,1)}) %reduce-scatter.22.cloned.1.call-update) | async-done | bytes 1990672 | tf_op jit(solution)/shard_map/reduce_scatter | solution.py:63
  955.5 116.4 %reduce-scatter.26.cloned.1.call-done = bf16[864,1152]{1,0:T(8,128)(2,1)} async-done(((bf16[6912,1152]{1,0:T(8,128)(2,1)}), bf16[864,1152]{1,0:T(8,128)(2,1)}) %reduce-scatter.26.cloned.1.call-update) | async-done | bytes 1990672 | tf_op jit(solution)/shard_map/reduce_scatter | solution.py:63
  1072.0 1.6 copy-done.22
  1073.8 1.2 fusion.129
  1076.5 1.9 fusion.49
  1078.4 45.4 %all-reduce.4 = (f32[1152]{0:T(1024)}, f32[256]{0:T(256)}, f32[256]{0:T(256)}, f32[1152]{0:T(1024)}, f32[1152]{0:T(1024)}, /*index=5*/f32[1152]{0:T(1024)}) all-reduce(f32[1152]{0:T(1024)S(1)} %get-tuple-element.23, f32[256]{0:T(256)S(1)} %get-tuple-element.19, ...), channel_id=1, replica_groups=mesh['dp'=4,'ctx'=8] {'dp','ctx'}, use_global_device_ids=true, to_apply=%region_36.37 | all-reduce | flops 5120 | bytes 40960 | tf_op jit(solution)/shard_map/psum | solution.py:267
  1123.8 2.9 fusion.44
  1126.7 187.9 %all-reduce.8.cloned.1.call-done = (bf16[144,1024]{1,0:T(8,128)(2,1)}, bf16[144,256]{1,0:T(8,128)(2,1)}, bf16[144,256]{1,0:T(8,128)(2,1)}, bf16[128,1152]{1,0:T(...) async-done(((bf16[144,1024]{1,0:T(8,128)(2,1)}, bf16[144,256]{1,0:T(8,128)(2,1)}, bf16[144,256]{1,0:T(8,128)(2,1)}, ...) | async-done | bytes 6709264 | tf_op jit(solution)/shard_map/psum | solution.py:65
  1314.6 1.7 convert_element_type.234
  1316.3 1.6 convert_element_type.236
  1317.9 1.8 convert_element_type.232
  1319.7 1.8 convert_element_type.238
  1321.5 2.2 convert_element_type.240
  1323.9 2.2 convert_element_type.242
  1326.2 2.2 convert_element_type.244
  (291 shorter events, 37.6 us)
Async XLA Ops:
  7.2 25.4 %copy-start = (bf16[2,192,1152]{2,1,0:T(8,128)(2,1)S(1)}, bf16[2,192,1152]{2,1,0:T(8,128)(2,1)}, u32[]{:S(2)}) copy-start(bf16[2,192,1152]{2,1,0:T(8,128)(2,1)} %param.16) | copy-start | bytes 2654212
  7.2 46.7 %all-gather.13.cloned.1.call-start = ((), (), s32[]{:S(2)}) async-start(), calls=%async_computation.11 | async-start | bytes 2654208 | tf_op jit(solution)/shard_map/all_gather | solution.py:89
  7.9 62.1 %all-gather.11.cloned.1.call-start = ((), (), s32[]{:S(2)}) async-start(), calls=%async_computation.10 | async-start | bytes 1769472 | tf_op jit(solution)/shard_map/all_gather | solution.py:147
  8.6 24.8 %copy-start.79 = (f32[256]{0:T(256)}, f32[256]{0:T(256)S(1)}, u32[]{:S(2)}) copy-start(f32[256]{0:T(256)S(1)} %convert_element_type.198) | copy-start | bytes 3076
  10.2 23.2 %copy-start.61 = (f32[384]{0:T(512)}, f32[384]{0:T(512)S(1)}, u32[]{:S(2)}) copy-start(f32[384]{0:T(512)S(1)} %rsqrt.63) | copy-start | bytes 4612
  10.9 41.9 %copy-start.48 = (f32[1152]{0:T(1024)}, f32[1152]{0:T(1024)S(1)}, u32[]{:S(2)}) copy-start(f32[1152]{0:T(1024)S(1)} %convert_element_type.195) | copy-start | bytes 13828
  22.7 11.6 copy-start.67
  22.7 11.6 copy-start.87
  32.6 2.5 copy-start.11
  32.8 12.7 copy-start.16
  32.8 3.0 copy-start.53
  35.8 62.4 %all-gather.9.cloned.1.call-start = ((), (), s32[]{:S(2)}) async-start(), calls=%async_computation.9 | async-start | bytes 1769472 | tf_op jit(solution)/shard_map/all_gather | solution.py:148
  46.7 82.3 %all-gather.15.cloned.1.call-start = ((), (), s32[]{:S(2)}) async-start(), calls=%async_computation.12 | async-start | bytes 2654208 | tf_op jit(solution)/shard_map/all_gather | solution.py:92
  47.3 169.7 %all-gather.17.cloned.1.call-start = ((), (), s32[]{:S(2)}) async-start(), calls=%async_computation.13 | async-start | bytes 17915904 | tf_op jit(solution)/shard_map/all_gather | solution.py:93
  47.9 3.4 copy-start.71
  48.0 257.1 %all-gather.19.cloned.1.call-start = ((), (), s32[]{:S(2)}) async-start(), calls=%async_computation.14 | async-start | bytes 17915904 | tf_op jit(solution)/shard_map/all_gather | solution.py:94
  48.5 344.7 %all-gather.21.cloned.1.call-start = ((), (), s32[]{:S(2)}) async-start(), calls=%async_computation.15 | async-start | bytes 17915904 | tf_op jit(solution)/shard_map/all_gather | solution.py:95
  49.3 462.6 %reduce-scatter.12.cloned.1.call-start = ((), (), s32[]{:S(2)}) async-start(), calls=%async_computation.17 | async-start | bytes 1769472 | tf_op jit(solution)/shard_map/reduce_scatter | solution.py:244
  49.5 10.1 copy-start.77
  50.3 10.8 copy-start.27
  60.8 9.2 copy-start.47
  61.3 13.4 copy-start.43
  61.4 13.3 copy-start.45
  72.5 2.9 copy-start.89
  98.2 4.0 copy-start.15
  98.2 4.5 copy-start.31
  104.0 27.9 %copy-start.18 = (bf16[384,4,256]{0,2,1:T(8,128)(2,1)}, bf16[384,4,256]{0,2,1:T(8,128)(2,1)S(1)}, u32[]{:S(2)}) copy-start(bf16[384,4,256]{0,2,1:T(8,128)(2,1)S(1)} %copy.65) | copy-start | bytes 2359300
  393.3 13.2 copy-start.8
  409.5 21.0 %copy-start.36 = (bf16[384,1152]{1,0:T(8,128)(2,1)}, bf16[384,1152]{1,0:T(8,128)(2,1)S(1)}, u32[]{:S(2)}) copy-start(bf16[384,1152]{1,0:T(8,128)(2,1)S(1)} %get-tuple-element.49) | copy-start | bytes 2654212
  430.5 13.6 %copy-start.91 = (bf16[384,6912]{1,0:T(8,128)(2,1)}, bf16[384,6912]{1,0:T(8,128)(2,1)S(1)}, u32[]{:S(2)}) copy-start(bf16[384,6912]{1,0:T(8,128)(2,1)S(1)} %get-tuple-element.44) | copy-start | bytes 15925252
  430.5 13.6 %copy-start.55 = (f32[1152]{0:T(1024)S(1)}, f32[1152]{0:T(1024)}, u32[]{:S(2)}) copy-start(f32[1152]{0:T(1024)} %convert_element_type.209) | copy-start | bytes 13828
  461.8 3.8 copy-start.70
  461.8 3.8 copy-start.59
  461.8 7.7 slice-start
  465.6 3.9 copy-start.4
  465.6 2.6 copy-start.23
  465.6 3.9 slice-start.1
  468.2 2.4 slice-start.2
  473.2 81.0 %reduce-scatter.10.cloned.1.call-start = ((), (), s32[]{:S(2)}) async-start(), calls=%async_computation.16 | async-start | bytes 1769472 | tf_op jit(solution)/shard_map/reduce_scatter | solution.py:241
  490.4 3.0 copy-start.44
  493.4 13.6 %copy-start.42 = (bf16[1,1536,256]{2,1,0:T(8,128)(2,1)S(1)}, bf16[1,1536,256]{2,1,0:T(8,128)(2,1)}, u32[]{:S(2)}) copy-start(bf16[1,1536,256]{2,1,0:T(8,128)(2,1)} %fusion.29) | copy-start | bytes 2359300
  507.0 4.9 copy-start.34
  509.5 45.7 %copy-start.68 = (f32[384]{0:T(512)S(1)}, f32[384]{0:T(512)}, u32[]{:S(2)}) copy-start(f32[384]{0:T(512)} %copy-done.67) | copy-start | bytes 4612
  509.5 45.7 %copy-start.88 = (f32[128]{0:T(128)S(1)}, f32[128]{0:T(128)}, u32[]{:S(2)}) copy-start(f32[128]{0:T(128)} %copy-done.87) | copy-start | bytes 1540
  509.5 46.5 %copy-start.10 = (f32[384,256]{1,0:T(8,128)S(1)}, f32[384,256]{1,0:T(8,128)}, u32[]{:S(2)}) copy-start(f32[384,256]{1,0:T(8,128)} %copy-done.9) | copy-start | bytes 1179652
  509.5 46.5 %copy-start.57 = (f32[384]{0:T(512)S(1)}, f32[384]{0:T(512)}, u32[]{:S(2)}) copy-start(f32[384]{0:T(512)} %copy-done.56) | copy-start | bytes 4612
  509.5 46.5 %copy-start.80 = (f32[256]{0:T(256)S(1)}, f32[256]{0:T(256)}, u32[]{:S(2)}) copy-start(f32[256]{0:T(256)} %copy-done.79) | copy-start | bytes 3076
  509.5 46.7 %copy-start.75 = (f32[384]{0:T(512)S(1)}, f32[384]{0:T(512)}, u32[]{:S(2)}) copy-start(f32[384]{0:T(512)} %copy-done.74) | copy-start | bytes 4612
  509.5 125.8 %reduce-scatter.18.cloned.1.call-start = ((), (), s32[]{:S(2)}) async-start(), calls=%async_computation.20 | async-start | bytes 663552 | tf_op jit(solution)/shard_map/reduce_scatter | solution.py:63
  514.1 42.3 %copy-start.17 = (bf16[384,1152]{1,0:T(8,128)(2,1)S(1)}, bf16[384,1152]{1,0:T(8,128)(2,1)}, u32[]{:S(2)}) copy-start(bf16[384,1152]{1,0:T(8,128)(2,1)} %copy-done.16) | copy-start | bytes 2654212
  514.1 121.2 %reduce-scatter.16.cloned.1.call-start = ((), (), s32[]{:S(2)}) async-start(), calls=%async_computation.19 | async-start | bytes 663552 | tf_op jit(solution)/shard_map/reduce_scatter | solution.py:63
  555.2 2.9 copy-start.19
  556.5 5.7 copy-start.38
  557.8 117.7 %reduce-scatter.20.cloned.1.call-start = ((), (), s32[]{:S(2)}) async-start(), calls=%async_computation.21 | async-start | bytes 2654208 | tf_op jit(solution)/shard_map/reduce_scatter | solution.py:63
  562.2 160.2 %reduce-scatter.14.cloned.1.call-start = ((), (), s32[]{:S(2)}) async-start(), calls=%async_computation.18 | async-start | bytes 2654208 | tf_op jit(solution)/shard_map/reduce_scatter | solution.py:63
  573.6 11.2 copy-start.28
  573.6 11.2 copy-start.30
  590.8 247.9 %reduce-scatter.24.cloned.1.call-start = ((), (), s32[]{:S(2)}) async-start(), calls=%async_computation.23 | async-start | bytes 17915904 | tf_op jit(solution)/shard_map/reduce_scatter | solution.py:63
  604.6 350.9 %reduce-scatter.22.cloned.1.call-start = ((), (), s32[]{:S(2)}) async-start(), calls=%async_computation.22 | async-start | bytes 17915904 | tf_op jit(solution)/shard_map/reduce_scatter | solution.py:63
  618.8 453.1 %reduce-scatter.26.cloned.1.call-start = ((), (), s32[]{:S(2)}) async-start(), calls=%async_computation.24 | async-start | bytes 17915904 | tf_op jit(solution)/shard_map/reduce_scatter | solution.py:63
  635.3 679.3 %all-reduce.8.cloned.1.call-start = ((), (), s32[]{:S(2)}) async-start(), calls=%async_computation.25 | async-start | bytes 13418496 | tf_op jit(solution)/shard_map/psum | solution.py:65
  1076.4 47.3 %copy-start.73 = (f32[384]{0:T(512)S(1)}, f32[384]{0:T(512)}, u32[]{:S(2)}) copy-start(f32[384]{0:T(512)} %copy-done.72) | copy-start | bytes 4612
  1076.4 47.3 %copy-start.5 = (f32[384,1152]{1,0:T(8,128)S(1)}, f32[384,1152]{1,0:T(8,128)}, u32[]{:S(2)}) copy-start(f32[384,1152]{1,0:T(8,128)} %copy-done.4) | copy-start | bytes 5308420
  1314.6 6.9 copy-start.26
  (49 other events, 73.7 us)
Sparse Core Ops, SparseCore 0:
  9.9 31.7 all-gather.12
  44.1 25.8 all-gather.10
  72.5 25.6 all-gather.8
  100.0 29.0 all-gather.14
  130.8 86.2 all-gather.16
  218.8 86.2 all-gather.18
  307.0 86.2 all-gather.20
  473.3 38.4 reduce-scatter.11
  515.7 38.4 reduce-scatter.9
  557.1 34.4 reduce-scatter.17
  594.8 34.3 reduce-scatter.15
  633.0 42.4 reduce-scatter.19
  679.8 42.4 reduce-scatter.13
  725.8 112.8 reduce-scatter.23
  842.6 112.8 reduce-scatter.21
  959.0 112.8 reduce-scatter.25
  1075.0 239.5 all-reduce.7
where the time goes:
time: 1340 us
  waiting for transfers between devices  949 us (71%)
  matrix products  229 us (17%)
  blocking collectives  75.4 us (6%)
  other arithmetic  43.7 us (3%)
  local copies, waits for them, and re-layouts  21.8 us (2%)
  between operations  15.6 us (1%)
    reduce_scatter x7, waiting for transfers between devices, reduce_grads(): lax.psum_scatter(for_sending(gradients), 'ctx', scatter_dimension=0, tile...  437 us
    psum x1, waiting for transfers between devices, reduce_grads(): lax.psum(for_sending(summed), 'dp')  188 us
    all_gather x1, waiting for transfers between devices, per_device(): lax.all_gather(gate_weight, 'ctx', axis=0, tiled=True)  82.9 us
    all_gather x1, waiting for transfers between devices, per_device(): lax.all_gather(up_weight, 'ctx', axis=0, tiled=True)  72.7 us
    all_gather x1, waiting for transfers between devices, per_device(): lax.all_gather(down_weight, 'ctx', axis=0, tiled=True)  70.5 us
    psum x1, blocking collectives, per_device(): lax.psum((grad_input_gain, grad_query_gain, grad_key_gain, grad_attended_...  45.4 us
    reduce_scatter x1, waiting for transfers between devices, per_device(): lax.psum_scatter(jnp.stack(key_parts).astype(jnp.bfloat16), 'ctx', scatte...  40 us
    dot_general x2, matrix products, per_device(): jnp.einsum('hqk,qhd->kd', d_scores, query_rows[row], preferred_element_ty...  27.1 us
  transfers between devices with their start and end apart: 17, of which 14 were waited for; matrix products, arithmetic and copies ran while one was open for 14% of the time, Pallas kernels for 0%

commit v1 on v0

v1 whole, which is shorter than its diff:
```python
import jax
import jax.numpy as jnp
from jax import lax
from jax.experimental import pallas as pl
from jax.experimental.pallas import tpu as pltpu
from jax.sharding import PartitionSpec as P

EPSILON = 1e-06
ROPE_BASE = 1000000.0
SCORE_SCALE = 0.0625
NEGATIVE = -1e30
GELU_COEFF = 0.044715
ROOT_TWO_PI = 0.7978845608028654
BF16 = jnp.bfloat16
WIDE = jnp.float32


def rms_norm(values, gain_values):
    return (
        values
        * lax.rsqrt(jnp.mean(values * values, axis=-1, keepdims=True) + EPSILON)
        * gain_values
    )


def angles_for(positions, width):
    half_width = width // 2
    frequencies = jnp.power(ROPE_BASE, -jnp.arange(half_width, dtype=jnp.float32) / half_width)
    return positions[:, None] * frequencies[None, :]


def gelu_parts(gate):
    square = gate * gate
    bent = jnp.tanh(ROOT_TWO_PI * (gate + GELU_COEFF * gate * square))
    rise = 0.5 * (1.0 + bent)
    slope = rise + 0.5 * gate * (1.0 - bent * bent) * ROOT_TWO_PI * (
        1.0 + 3.0 * GELU_COEFF * square
    )
    return gate * rise, slope


def dot(left, right):
    return jnp.dot(left, right, preferred_element_type=WIDE)


def dot_t(left, right):
    return lax.dot_general(left, right, (((1,), (1,)), ((), ())), preferred_element_type=WIDE)


def t_dot(left, right):
    return lax.dot_general(left, right, (((0,), (0,)), ((), ())), preferred_element_type=WIDE)


def after(x, *earlier):
    return lax.optimization_barrier((x,) + earlier)[0] if earlier else x


def xor_permute(x, axis_size, code):
    return lax.ppermute(x, "ctx", [(i, i ^ code) for i in range(axis_size)])


def xor_layout(n):
    far_y, far_x = n // 2, n // 4
    near = [1 << b for b in range((n // 4).bit_length() - 1)]
    codes = [0, far_x, far_y, far_x ^ far_y]
    for bit in near:
        codes = codes + [c ^ bit for c in codes]
    return far_x, far_y, near, codes


class Gather:
    def __init__(self, x, n):
        self.n = n
        self.far_x, self.far_y, self.near_bits, _ = xor_layout(n)
        self.x = x
        self.a = xor_permute(x, n, self.far_x)
        self.b = xor_permute(x, n, self.far_y)

    def mid(self, *earlier):
        half = self.x.shape[0] // 2
        a = after(self.a, *earlier)
        self.d1 = xor_permute(a[:half], self.n, self.far_y)
        self.d2 = xor_permute(self.b[half:], self.n, self.far_x)
        return self

    def near(self, *earlier):
        d1 = after(self.d1, *earlier)
        self.blocks = [stack_blocks(self.x, self.a, self.b, d1, self.d2)]
        for bit in self.near_bits:
            self.blocks = self.blocks + [xor_permute(b, self.n, bit) for b in self.blocks]
        return self

    def flat(self):
        return [b.reshape((4 * self.x.shape[0],) + self.x.shape[1:]) for b in self.blocks]


class Scatter:
    def __init__(self, blocks, n):
        self.n = n
        self.far_x, self.far_y, self.near_bits, _ = xor_layout(n)
        self.blocks = list(blocks)
        self.bits = list(reversed(self.near_bits))
        self.send_near()

    def send_near(self):
        if self.bits:
            count = len(self.blocks) // 2
            self.arrived = [xor_permute(b, self.n, self.bits[0]) for b in self.blocks[count:]]

    def mid(self, *earlier):
        while self.bits:
            count = len(self.blocks) // 2
            self.arrived[0] = after(self.arrived[0], *earlier)
            self.blocks = [
                (mine.astype(WIDE) + theirs.astype(WIDE)).astype(BF16)
                for mine, theirs in zip(self.blocks[:count], self.arrived)
            ]
            self.bits = self.bits[1:]
            self.send_near()
        self.sums = self.blocks[0]
        half = self.sums.shape[1] // 2
        self.d_x = xor_permute(self.sums[3, :half], self.n, self.far_x)
        self.d_y = xor_permute(self.sums[3, half:], self.n, self.far_y)
        return self

    def far(self, *earlier):
        half = self.sums.shape[1] // 2
        d_x = after(self.d_x, *earlier).astype(WIDE)
        d_y = self.d_y.astype(WIDE)
        x, y = self.sums[1].astype(WIDE), self.sums[2].astype(WIDE)
        to_x = jnp.concatenate([x[:half], x[half:] + d_y], axis=0).astype(BF16)
        to_y = jnp.concatenate([y[:half] + d_x, y[half:]], axis=0).astype(BF16)
        self.from_x = xor_permute(to_x, self.n, self.far_x)
        self.from_y = xor_permute(to_y, self.n, self.far_y)
        self.sent = (to_x, to_y)
        return self

    def finish(self, *earlier):
        return self.sums, after(self.from_x, *earlier), self.from_y


class Line:
    def __init__(self, part, n):
        self.n = n
        self.total = part
        mid = n // 2
        self.steps = []
        for s in range(mid - 1):
            self.steps.append(("in", [(s, s + 1), (n - 1 - s, n - 2 - s)], None))
        self.steps.append(("in", [(mid - 1, mid), (mid, mid - 1)], None))
        for s in range(mid - 2, -1, -1):
            self.steps.append(("out", [(s + 1, s), (n - 2 - s, n - 1 - s)], (s, n - 1 - s)))
        self.at = 0
        self.send()

    def send(self):
        if self.at < len(self.steps):
            self.moved = lax.ppermute(self.total, "dp", self.steps[self.at][1])

    def step(self, *earlier):
        kind, _, ends = self.steps[self.at]
        moved = after(self.moved, *earlier)
        if kind == "in":
            total = self.total.astype(WIDE) + moved.astype(WIDE)
            self.total = total.astype(self.total.dtype)
        else:
            me = lax.axis_index("dp")
            self.total = jnp.where((me == ends[0]) | (me == ends[1]), moved, self.total)
        self.at += 1
        self.send()
        return self.total

    def finish(self):
        while self.at < len(self.steps):
            self.step()
        return self.total


NT = (((1,), (1,)), ((), ()))
TN = (((0,), (0,)), ((), ()))
VMEM_LIMIT = 48 * 1024 * 1024


def vmem_call(kernel, out_shape, **kwargs):
    return pl.pallas_call(
        kernel,
        out_shape=out_shape,
        compiler_params=pltpu.CompilerParams(vmem_limit_bytes=VMEM_LIMIT),
        cost_estimate=pl.CostEstimate(flops=0, bytes_accessed=0, transcendentals=0),
        **kwargs,
    )


def whole_spec():
    return pl.BlockSpec(memory_space=pltpu.VMEM)


def smem_spec():
    return pl.BlockSpec(memory_space=pltpu.SMEM)


def full_spec(shape):
    return pl.BlockSpec(shape, lambda i: (0,) * len(shape))


def row_spec(shape, row):
    return pl.BlockSpec((1,) + shape, lambda i: (row,) + (0,) * len(shape))


def unit(values, gain_values):
    r = lax.rsqrt(jnp.mean(values * values, axis=-1, keepdims=True) + EPSILON)
    return values * r * gain_values, r


def unit_back(values, r, gain_values, e):
    ge = gain_values * e
    d_values = r * ge - values * (r * r * r * jnp.mean(ge * values, axis=-1, keepdims=True))
    return d_values, jnp.sum(e * values * r, axis=0, keepdims=True)


def stack_blocks(x, a, b, d1, d2):
    half = d1.shape[0]

    def kernel(x_ref, a_ref, b_ref, d1_ref, d2_ref, out_ref):
        out_ref[0] = x_ref[...]
        out_ref[1] = a_ref[...]
        out_ref[2] = b_ref[...]
        out_ref[3, :half] = d1_ref[...]
        out_ref[3, half:] = d2_ref[...]

    return vmem_call(
        kernel,
        jax.ShapeDtypeStruct((4,) + x.shape, x.dtype),
        in_specs=[whole_spec()] * 5,
        out_specs=whole_spec(),
    )(x, a, b, d1, d2)


def spread_pieces(flag, first, second, n):
    rows, columns = first.shape
    share = columns // n

    def kernel(flag_ref, first_ref, second_ref, out_ref):
        def fill(source):
            for k in range(n):
                out_ref[k] = source[:, k * share : (k + 1) * share]

        @pl.when(flag_ref[0] == 1)
        def _():
            fill(first_ref)

        @pl.when(flag_ref[0] != 1)
        def _():
            fill(second_ref)

    return vmem_call(
        kernel,
        jax.ShapeDtypeStruct((n, rows, share), first.dtype),
        in_specs=[smem_spec(), whole_spec(), whole_spec()],
        out_specs=whole_spec(),
    )(flag, first, second)


def in_order(flag, first, second):
    def kernel(flag_ref, first_ref, second_ref, a_ref, b_ref):
        @pl.when(flag_ref[0] == 1)
        def _():
            a_ref[...] = first_ref[...]
            b_ref[...] = second_ref[...]

        @pl.when(flag_ref[0] != 1)
        def _():
            a_ref[...] = second_ref[...]
            b_ref[...] = first_ref[...]

    parts, rows, columns = first.shape
    step = pl.BlockSpec((1, rows, columns), lambda i: (i, 0, 0))
    return vmem_call(
        kernel,
        (jax.ShapeDtypeStruct(first.shape, first.dtype),) * 2,
        grid=(parts,),
        in_specs=[smem_spec(), step, step],
        out_specs=(step, step),
    )(flag, first, second)


def assemble(flag, totals, moveds, rows, columns):
    count = len(totals)
    share = totals[0].shape[2]

    def kernel(flag_ref, *refs):
        out_ref = refs[-1]

        def fill(parts):
            at = 0
            for part in parts:
                for k in range(part.shape[0]):
                    out_ref[:, at * share : (at + 1) * share] = part[k].astype(WIDE)
                    at += 1

        @pl.when(flag_ref[0] == 1)
        def _():
            fill(refs[count : 2 * count])

        @pl.when(flag_ref[0] != 1)
        def _():
            fill(refs[:count])

    return vmem_call(
        kernel,
        jax.ShapeDtypeStruct((rows, columns), WIDE),
        in_specs=[smem_spec()] + [whole_spec()] * (2 * count),
        out_specs=whole_spec(),
    )(flag, *totals, *moveds)


def allowed_mask(start_ref, place_ref, key_place_ref):
    key_place = key_place_ref[...]
    return (start_ref[...] <= key_place) & (place_ref[...] >= key_place)


def lay_out(kv_refs, k_held, v_held, size):
    at = 0
    for ref in kv_refs:
        for slot in range(ref.shape[0]):
            tokens = ref.shape[2]
            k_held[at : at + tokens] = ref[slot, 0, :, :size]
            v_held[at : at + tokens] = ref[slot, 0, :, size:]
            at += tokens


def attend_forward(
    row, queries, kv_blocks, start, place, key_place, out_weight, tokens, gain_out, gain_feed, heads
):
    count = start.shape[0]
    width = tokens.shape[2]
    slots = kv_blocks[0].shape[0]
    size = kv_blocks[0].shape[3] // 2
    keys = slots * len(kv_blocks) * count
    lanes_all = heads * size

    def kernel(*refs):
        q_ref, start_ref, place_ref, key_place_ref, w_ref, x_ref, g1_ref, g2_ref = refs[:8]
        kv_refs = refs[8 : 8 + len(kv_blocks)]
        out_ref, log_ref, projected_ref, hidden_ref, inner_ref, k_held, v_held = refs[
            8 + len(kv_blocks) :
        ]
        lay_out(kv_refs, k_held, v_held, size)
        allowed = allowed_mask(start_ref, place_ref, key_place_ref)
        for h in range(heads):
            q = q_ref[:, h * size : (h + 1) * size]
            scores = lax.dot_general(q, k_held[...], NT, preferred_element_type=WIDE) * SCORE_SCALE
            scores = jnp.where(allowed, scores, NEGATIVE)
            peak = jnp.max(scores, axis=-1, keepdims=True)
            raised = jnp.exp(scores - peak)
            weight = jnp.sum(raised, axis=-1, keepdims=True)
            probabilities = (raised * (1.0 / weight)).astype(BF16)
            out = jnp.dot(probabilities, v_held[...], preferred_element_type=WIDE)
            out_ref[:, h * size : (h + 1) * size] = out.astype(BF16)
            log_ref[:, h : h + 1] = peak + jnp.log(weight)
        projected = jnp.dot(out_ref[...], w_ref[...], preferred_element_type=WIDE)
        projected_ref[...] = projected
        hidden = x_ref[0].astype(WIDE) + unit(projected, g1_ref[...].astype(WIDE))[0]
        hidden_ref[...] = hidden
        inner_ref[...] = unit(hidden, g2_ref[...].astype(WIDE))[0].astype(BF16)

    return vmem_call(
        kernel,
        (
            jax.ShapeDtypeStruct((count, lanes_all), BF16),
            jax.ShapeDtypeStruct((count, heads), WIDE),
            jax.ShapeDtypeStruct((count, width), WIDE),
            jax.ShapeDtypeStruct((count, width), WIDE),
            jax.ShapeDtypeStruct((count, width), BF16),
        ),
        grid=(1,),
        in_specs=[
            pl.BlockSpec((count, lanes_all), lambda i: (row, 0)),
            full_spec((count, 1)),
            full_spec((count, 1)),
            full_spec((1, keys)),
            full_spec((lanes_all, width)),
            row_spec((count, width), row),
            full_spec((1, width)),
            full_spec((1, width)),
        ]
        + [
            pl.BlockSpec((slots, 1, count, 2 * size), lambda i: (0, row, 0, 0)) for _ in kv_blocks
        ],
        out_specs=(
            full_spec((count, lanes_all)),
            full_spec((count, heads)),
            full_spec((count, width)),
            full_spec((count, width)),
            full_spec((count, width)),
        ),
        scratch_shapes=[pltpu.VMEM((keys, size), BF16), pltpu.VMEM((keys, size), BF16)],
    )(queries, start, place, key_place, out_weight, tokens, gain_out, gain_feed, *kv_blocks)


def close_row(row, parts, hidden, cotangent, gain):
    count, width = hidden.shape

    def kernel(a_ref, b_ref, c_ref, hidden_ref, e_ref, gain_ref, result_ref, d_ref, dg_ref):
        v = a_ref[0].astype(WIDE) + b_ref[...].astype(WIDE) + c_ref[...].astype(WIDE)
        g = gain_ref[...].astype(WIDE)
        z, r = unit(v, g)
        result_ref[...] = (hidden_ref[...] + z).astype(BF16)
        d_values, dg_ref[...] = unit_back(v, r, g, e_ref[0].astype(WIDE))
        d_ref[...] = d_values.astype(BF16)

    return vmem_call(
        kernel,
        (
            jax.ShapeDtypeStruct((count, width), BF16),
            jax.ShapeDtypeStruct((count, width), BF16),
            jax.ShapeDtypeStruct((1, width), WIDE),
        ),
        grid=(1,),
        in_specs=[
            row_spec((count, width), 0),
            full_spec((count, width)),
            full_spec((count, width)),
            full_spec((count, width)),
            row_spec((count, width), row),
            full_spec((1, width)),
        ],
        out_specs=(full_spec((count, width)), full_spec((count, width)), full_spec((1, width))),
    )(*parts, hidden, cotangent, gain)


def attend_backward(
    row,
    parts,
    kept,
    cotangent,
    out_weight,
    gain_out,
    gain_feed,
    queries,
    kv_blocks,
    place,
    key_place,
    raw,
    cosine,
    sine,
    gain,
    heads,
):
    count, width = kept["hidden"].shape
    slots = kv_blocks[0].shape[0]
    size = kv_blocks[0].shape[3] // 2
    half = size // 2
    keys = slots * len(kv_blocks) * count
    lanes_all = heads * size
    block_count = len(kv_blocks)

    def kernel(*refs):
        (
            a_ref,
            b_ref,
            c_ref,
            hidden_ref,
            projected_ref,
            e_ref,
            w_ref,
            g1_ref,
            g2_ref,
            q_ref,
            start_ref,
            place_ref,
            key_place_ref,
            log_ref,
            raw_ref,
            cos_ref,
            sin_ref,
            gain_ref,
        ) = refs[:18]
        kv_refs = refs[18 : 18 + block_count]
        outs = refs[18 + block_count :]
        d_hidden_ref, d_projected_ref, dg1_ref, dg2_ref, dq_ref, dgain_ref = outs[:6]
        dkv_refs = outs[6 : 6 + block_count]
        k_held, v_held, dk_acc, dv_acc, d_held = outs[6 + block_count :]
        g1 = g1_ref[...].astype(WIDE)
        g2 = g2_ref[...].astype(WIDE)
        e = a_ref[0].astype(WIDE) + b_ref[...].astype(WIDE) + c_ref[...].astype(WIDE)
        hidden = hidden_ref[...]
        d_values, dg2_ref[...] = unit_back(hidden, unit(hidden, g2)[1], g2, e)
        d_hidden = e_ref[0].astype(WIDE) + d_values
        d_hidden_ref[...] = d_hidden
        projected = projected_ref[...]
        d_values, dg1_ref[...] = unit_back(projected, unit(projected, g1)[1], g1, d_hidden)
        d_projected_ref[...] = d_values.astype(BF16)
        d_held[...] = lax.dot_general(
            d_projected_ref[...], w_ref[...], NT, preferred_element_type=WIDE
        ).astype(BF16)
        lay_out(kv_refs, k_held, v_held, size)
        allowed = allowed_mask(start_ref, place_ref, key_place_ref)
        gain_values = gain_ref[...].astype(WIDE)
        cos = cos_ref[...]
        sin = sin_ref[...]
        d_gain = jnp.zeros((1, size), WIDE)
        for h in range(heads):
            lanes = slice(h * size, (h + 1) * size)
            q = q_ref[:, lanes]
            d = d_held[:, lanes]
            k = k_held[...]
            scores = lax.dot_general(q, k, NT, preferred_element_type=WIDE) * SCORE_SCALE
            p = jnp.where(allowed, jnp.exp(scores - log_ref[:, h : h + 1]), 0.0)
            d_p = lax.dot_general(d, v_held[...], NT, preferred_element_type=WIDE)
            inner = jnp.sum(p * d_p, axis=-1, keepdims=True)
            d_s = (p * (d_p - inner)).astype(BF16)
            d_v = lax.dot_general(p.astype(BF16), d, TN, preferred_element_type=WIDE)
            d_k = lax.dot_general(d_s, q, TN, preferred_element_type=WIDE)
            if h == 0:
                dk_acc[...] = d_k
                dv_acc[...] = d_v
            else:
                dk_acc[...] += d_k
                dv_acc[...] += d_v
            d_q = jnp.dot(d_s, k, preferred_element_type=WIDE) * SCORE_SCALE
            d_a, d_b = d_q[:, :half], d_q[:, half:]
            turned = jnp.concatenate([d_a * cos + d_b * sin, d_b * cos - d_a * sin], axis=-1)
            u = raw_ref[:, lanes]
            d_u, d_part = unit_back(u, unit(u, gain_values)[1], gain_values, turned)
            dq_ref[:, lanes] = d_u.astype(BF16)
            d_gain += d_part
        dgain_ref[...] = d_gain
        at = 0
        for ref in dkv_refs:
            for slot in range(slots):
                ref[slot, :, :size] = (dk_acc[at : at + count] * SCORE_SCALE).astype(BF16)
                ref[slot, :, size:] = dv_acc[at : at + count].astype(BF16)
                at += count

    wide_rows = jax.ShapeDtypeStruct((count, width), WIDE)
    mine = pl.BlockSpec((count, lanes_all), lambda i: (row, 0))
    turn = pl.BlockSpec((count, half), lambda i: (row, 0))
    outs = vmem_call(
        kernel,
        (
            wide_rows,
            jax.ShapeDtypeStruct((count, width), BF16),
            jax.ShapeDtypeStruct((1, width), WIDE),
            jax.ShapeDtypeStruct((1, width), WIDE),
            jax.ShapeDtypeStruct((count, lanes_all), BF16),
            jax.ShapeDtypeStruct((1, size), WIDE),
        )
        + (jax.ShapeDtypeStruct((slots, count, 2 * size), BF16),) * block_count,
        grid=(1,),
        in_specs=[
            row_spec((count, width), 0),
            full_spec((count, width)),
            full_spec((count, width)),
            full_spec((count, width)),
            full_spec((count, width)),
            row_spec((count, width), row),
            full_spec((lanes_all, width)),
            full_spec((1, width)),
            full_spec((1, width)),
            mine,
            full_spec((count, 1)),
            full_spec((count, 1)),
            full_spec((1, keys)),
            full_spec((count, heads)),
            mine,
            turn,
            turn,
            full_spec((1, size)),
        ]
        + [
            pl.BlockSpec((slots, 1, count, 2 * size), lambda i: (0, row, 0, 0)) for _ in kv_blocks
        ],
        out_specs=(
            full_spec((count, width)),
            full_spec((count, width)),
            full_spec((1, width)),
            full_spec((1, width)),
            full_spec((count, lanes_all)),
            full_spec((1, size)),
        )
        + (full_spec((slots, count, 2 * size)),) * block_count,
        scratch_shapes=[
            pltpu.VMEM((keys, size), BF16),
            pltpu.VMEM((keys, size), BF16),
            pltpu.VMEM((keys, size), WIDE),
            pltpu.VMEM((keys, size), WIDE),
            pltpu.VMEM((count, lanes_all), BF16),
        ],
    )(
        *parts,
        kept["hidden"],
        kept["projected"],
        cotangent,
        out_weight,
        gain_out,
        gain_feed,
        queries,
        kept["start"],
        place,
        key_place,
        kept["log"],
        raw,
        cosine,
        sine,
        gain,
        *kv_blocks,
    )
    names = ("d_hidden", "d_projected", "grad_out_gain", "grad_feed_gain", "d_query_raw", "d_gain")
    kept.update(zip(names, outs[:6]))
    kept["d_kv"] = outs[6:]


def project_kv(order, normed, blocks, cosine, sine, gain, rows):
    tokens, width = normed.shape
    per_block, part, both = blocks[0].shape
    n = per_block * len(blocks)
    size = both // 2
    half = size // 2

    def kernel(order_ref, x_ref, cos_ref, sin_ref, gain_ref, *refs):
        block_refs = refs[: len(blocks)]
        kv_ref, raw_ref, held = refs[len(blocks) :]
        for d in range(n):
            slot = order_ref[d]
            for k, block in enumerate(block_refs):

                @pl.when((slot >= k * per_block) & (slot < (k + 1) * per_block))
                def _(d=d, k=k, block=block, slot=slot):
                    held[d * part : (d + 1) * part] = block[slot - k * per_block]

        both_raw = jnp.dot(x_ref[...], held[...], preferred_element_type=WIDE)
        u = both_raw[:, :size]
        raw_ref[...] = u
        k = unit(u, gain_ref[...].astype(WIDE))[0]
        cos, sin = cos_ref[...], sin_ref[...]
        a, b = k[:, :half], k[:, half:]
        kv = jnp.concatenate([a * cos - b * sin, b * cos + a * sin, both_raw[:, size:]], axis=-1)
        kv_ref[...] = kv.astype(BF16).reshape(rows, tokens // rows, both)

    return vmem_call(
        kernel,
        (
            jax.ShapeDtypeStruct((rows, tokens // rows, both), BF16),
            jax.ShapeDtypeStruct((tokens, size), WIDE),
            jax.ShapeDtypeStruct((width, both), BF16),
        ),
        in_specs=[smem_spec()] + [whole_spec()] * (4 + len(blocks)),
        out_specs=(whole_spec(), whole_spec(), whole_spec()),
    )(order, normed, cosine, sine, gain, *blocks)


def project_q(normed, weight, cosine, sine, gain, heads):
    tokens, width = normed.shape
    size = weight.shape[1] // heads
    half = size // 2

    def kernel(x_ref, w_ref, cos_ref, sin_ref, gain_ref, q_ref, raw_ref):
        cos, sin = cos_ref[...], sin_ref[...]
        raw_ref[...] = jnp.dot(x_ref[...], w_ref[...], preferred_element_type=WIDE)
        for h in range(heads):
            lanes = slice(h * size, (h + 1) * size)
            q = unit(raw_ref[:, lanes], gain_ref[...].astype(WIDE))[0]
            a, b = q[:, :half], q[:, half:]
            turned = jnp.concatenate([a * cos - b * sin, b * cos + a * sin], axis=-1)
            q_ref[:, lanes] = turned.astype(BF16)

    return vmem_call(
        kernel,
        (
            jax.ShapeDtypeStruct((tokens, heads * size), BF16),
            jax.ShapeDtypeStruct((tokens, heads * size), WIDE),
        ),
        in_specs=[whole_spec()] * 5,
        out_specs=(whole_spec(), whole_spec()),
    )(normed, weight, cosine, sine, gain)


def feed_steps(blocks):
    tokens, width = blocks[0].shape
    step = 256 if tokens % 256 == 0 else tokens
    per_block = tokens // step

    def spec(k):
        return pl.BlockSpec(
            (step, width), lambda i: (jnp.clip(i - k * per_block, 0, per_block - 1), 0)
        )

    return step, per_block, spec


def in_block(k, per_block):
    i = pl.program_id(0)
    return (i >= k * per_block) & (i < (k + 1) * per_block)


def feed_forward(blocks, gate_w, up_w, down_w):
    width = blocks[0].shape[1]
    share = gate_w.shape[1]
    step, per_block, spec = feed_steps(blocks)
    count = len(blocks)
    total = count * per_block * step

    def kernel(gate_ref, up_ref, down_ref, *refs):
        x_ref, slope_ref, value_ref, a_ref = refs[count : count + 4]
        low_refs = refs[count + 4 :]
        for k in range(count):

            @pl.when(in_block(k, per_block))
            def _(k=k):
                x_ref[...] = refs[k][...]

        x = x_ref[...]
        g = jnp.dot(x, gate_ref[...], preferred_element_type=WIDE)
        u = jnp.dot(x, up_ref[...], preferred_element_type=WIDE)
        value, slope = gelu_parts(g)
        active = (value * u).astype(BF16)
        slope_ref[...] = (slope * u).astype(BF16)
        value_ref[...] = value.astype(BF16)
        a_ref[...] = active
        low = jnp.dot(active, down_ref[...], preferred_element_type=WIDE).astype(BF16)
        for k in range(count):

            @pl.when(in_block(k, per_block))
            def _(k=k):
                low_refs[k][...] = low

    each = lambda columns: pl.BlockSpec((step, columns), lambda i: (i, 0))
    whole = lambda shape: pl.BlockSpec(shape, lambda i: (0, 0))
    hidden = jax.ShapeDtypeStruct((total, share), BF16)
    return vmem_call(
        kernel,
        (jax.ShapeDtypeStruct((total, width), BF16), hidden, hidden, hidden)
        + tuple(jax.ShapeDtypeStruct(b.shape, BF16) for b in blocks),
        grid=(total // step,),
        in_specs=[whole((width, share)), whole((width, share)), whole((share, width))]
        + [spec(k) for k in range(count)],
        out_specs=(each(width), each(share), each(share), each(share))
        + tuple(spec(k) for k in range(count)),
    )(gate_w, up_w, down_w, *blocks)


def feed_backward(blocks, slope, value, gate_w, up_w, down_w):
    width = blocks[0].shape[1]
    share = gate_w.shape[1]
    step, per_block, spec = feed_steps(blocks)
    count = len(blocks)
    total = count * per_block * step

    def kernel(gate_ref, up_ref, down_ref, slope_ref, value_ref, *refs):
        d_ref, dg_ref, du_ref = refs[count : count + 3]
        dx_refs = refs[count + 3 :]
        for k in range(count):

            @pl.when(in_block(k, per_block))
            def _(k=k):
                d_ref[...] = refs[k][...]

        d_active = lax.dot_general(d_ref[...], down_ref[...], NT, preferred_element_type=WIDE)
        d_gate = (d_active * slope_ref[...].astype(WIDE)).astype(BF16)
        d_up = (d_active * value_ref[...].astype(WIDE)).astype(BF16)
        dg_ref[...] = d_gate
        du_ref[...] = d_up
        d_x = lax.dot_general(d_gate, gate_ref[...], NT, preferred_element_type=WIDE)
        d_x += lax.dot_general(d_up, up_ref[...], NT, preferred_element_type=WIDE)
        d_x = d_x.astype(BF16)
        for k in range(count):

            @pl.when(in_block(k, per_block))
            def _(k=k):
                dx_refs[k][...] = d_x

    each = lambda columns: pl.BlockSpec((step, columns), lambda i: (i, 0))
    whole = lambda shape: pl.BlockSpec(shape, lambda i: (0, 0))
    hidden = jax.ShapeDtypeStruct((total, share), BF16)
    return vmem_call(
        kernel,
        (jax.ShapeDtypeStruct((total, width), BF16), hidden, hidden)
        + tuple(jax.ShapeDtypeStruct(b.shape, BF16) for b in blocks),
        grid=(total // step,),
        in_specs=[
            whole((width, share)),
            whole((width, share)),
            whole((share, width)),
            each(share),
            each(share),
        ]
        + [spec(k) for k in range(count)],
        out_specs=(each(width), each(share), each(share))
        + tuple(spec(k) for k in range(count)),
    )(gate_w, up_w, down_w, slope, value, *blocks)


def weight_grad(lefts, rights, parts):
    tokens, rows = lefts[0].shape
    columns = rights[0].shape[1]
    step = tokens // 2 if tokens % 32 == 0 else tokens
    per_pair = tokens // step
    count = len(lefts)
    last = count * per_pair - 1

    def kernel(*refs):
        out_ref, acc = refs[2 * count :]
        i = pl.program_id(0)
        for k in range(count):

            @pl.when(in_block(k, per_pair))
            def _(k=k):
                term = lax.dot_general(
                    refs[k][...], refs[count + k][...], TN, preferred_element_type=WIDE
                )
                if k == 0:

                    @pl.when(i == 0)
                    def _():
                        acc[...] = term

                    @pl.when(i != 0)
                    def _():
                        acc[...] += term

                else:
                    acc[...] += term

        @pl.when(i == last)
        def _():
            size = rows // parts
            for p in range(parts):
                out_ref[p] = acc[p * size : (p + 1) * size].astype(BF16)

    def spec(k, width):
        return pl.BlockSpec(
            (step, width), lambda i: (jnp.clip(i - k * per_pair, 0, per_pair - 1), 0)
        )

    return vmem_call(
        kernel,
        jax.ShapeDtypeStruct((parts, rows // parts, columns), BF16),
        grid=(last + 1,),
        in_specs=[spec(k, rows) for k in range(count)] + [spec(k, columns) for k in range(count)],
        out_specs=full_spec((parts, rows // parts, columns)),
        scratch_shapes=[pltpu.VMEM((rows, columns), WIDE)],
    )(*lefts, *rights)


def per_device(
    tokens,
    cotangent,
    segment_ids,
    query_weight,
    key_weight,
    value_weight,
    out_weight,
    gate_weight,
    up_weight,
    down_weight,
    gain_input,
    gain_query,
    gain_key,
    gain_attended,
    gain_feed,
    gain_result,
):
    n = lax.axis_size("ctx")
    n_dp = lax.axis_size("dp")
    me = lax.axis_index("ctx")
    my_dp = lax.axis_index("dp")
    row_count, count_local, width = tokens.shape
    total = row_count * count_local
    head_width = gain_query.shape[0]
    half_width = head_width // 2
    head_count = query_weight.shape[1] // head_width
    qw = head_count * head_width
    share = gate_weight.shape[1] // n
    span = count_local // 2
    codes = xor_layout(n)[3]
    gain_row = {
        "query": gain_query.reshape(1, -1),
        "key": gain_key.reshape(1, -1),
        "out": gain_attended.reshape(1, -1),
        "feed": gain_feed.reshape(1, -1),
        "result": gain_result.reshape(1, -1),
    }
    scale_input = gain_input.astype(WIDE)
    scale_key = gain_key.astype(WIDE)

    kv_weights = Gather(jnp.concatenate([key_weight, value_weight], axis=1), n)
    query_full = lax.all_gather(query_weight, "ctx", axis=0, tiled=True)
    even_flag = ((my_dp % 2) == 0).astype(jnp.int32).reshape(1)
    pieces = spread_pieces(even_flag, gate_weight, up_weight, n)
    spread = lax.all_to_all(pieces, "ctx", 0, 0)

    below = jnp.stack(
        [jnp.sum((segment_ids < s).astype(jnp.int32), axis=1) for s in range(5)], axis=1
    )
    code = 1
    while code < n:
        below = below + xor_permute(below, n, code)
        code *= 2
    starts = sum(jnp.where(segment_ids == s, below[:, s : s + 1], 0) for s in range(5))

    offsets = jnp.arange(span, dtype=jnp.int32)

    def places_of(device):
        return jnp.concatenate([device * span + offsets, (2 * n - 1 - device) * span + offsets])

    local_places = places_of(me)
    key_places = jnp.concatenate([places_of(me ^ code) for code in codes]).reshape(1, -1)
    place_column = local_places.reshape(-1, 1)
    angles = angles_for(local_places.astype(WIDE), head_width)
    cosine = jnp.concatenate([jnp.cos(angles)] * row_count, axis=0)
    sine = jnp.concatenate([jnp.sin(angles)] * row_count, axis=0)

    row_tokens = tokens.reshape(total, width).astype(WIDE)
    normed_wide, normed_pull = jax.vjp(rms_norm, row_tokens, scale_input)
    normed = normed_wide.astype(BF16)
    order_codes = me ^ jnp.arange(n, dtype=jnp.int32)
    order = sum(jnp.where(order_codes == c, k, 0) for k, c in enumerate(codes)).astype(jnp.int32)
    kv_weights.mid(pieces, normed).near()
    kv_local, key_raw, kv_full = project_kv(
        order, normed, kv_weights.blocks, cosine, sine, gain_row["key"], row_count
    )
    kv_gather = Gather(kv_local, n)
    out_full = lax.all_gather(after(out_weight, kv_local), "ctx", axis=0, tiled=True)
    queries, query_raw = project_q(
        after(normed, kv_local), query_full, cosine, sine, gain_row["query"], head_count
    )
    kv_gather.mid(queries)
    swapped = lax.ppermute(
        after(spread, kv_gather.a, kv_gather.b), "dp", [(i, i ^ 1) for i in range(n_dp)]
    )
    kv_gather.near()
    kv_blocks = kv_gather.blocks

    def before_feed(row, *earlier):
        r = {"start": starts[row].reshape(-1, 1)}
        names = ("attended", "log", "projected", "hidden", "inner_local")
        outs = attend_forward(
            row,
            after(queries, *earlier),
            kv_blocks,
            r["start"],
            place_column,
            key_places,
            out_full,
            tokens,
            gain_row["out"],
            gain_row["feed"],
            head_count,
        )
        r.update(zip(names, outs))
        return r

    def feed_piece(r, blocks, *earlier):
        blocks = [after(blocks[0], *earlier)] + blocks[1:]
        outs = feed_forward(blocks, gate_mine, up_mine, down_weight)
        r["inner"], r["slope"], r["value"], r["active"] = outs[:4]
        return [x.reshape(4, count_local, width) for x in outs[4:]]

    def back_piece(r, blocks, *earlier):
        blocks = [after(blocks[0], *earlier)] + blocks[1:]
        outs = feed_backward(blocks, r["slope"], r["value"], gate_mine, up_mine, down_weight)
        r["d_lowered"], r["d_gate"], r["d_up"] = outs[:3]
        return [x.reshape(4, count_local, width) for x in outs[3:]]

    def result_piece(row, r, parts):
        r["result"], d_lowered, r["grad_result_gain"] = close_row(
            row, parts, r["hidden"], cotangent, gain_row["result"]
        )
        return d_lowered

    def attend_back(row, r, parts):
        attend_backward(
            row,
            parts,
            r,
            cotangent,
            out_full,
            gain_row["out"],
            gain_row["feed"],
            queries,
            kv_blocks,
            place_column,
            key_places,
            query_raw,
            cosine,
            sine,
            gain_row["query"],
            head_count,
        )

    r0 = before_feed(0)
    g0 = Gather(r0["inner_local"], n)
    r1 = before_feed(1, r0["inner_local"])
    g0.mid(r1["inner_local"])
    g1 = Gather(after(r1["inner_local"], g0.a, g0.b), n)
    gate_mine, up_mine = in_order(even_flag, spread, swapped)
    gate_mine = gate_mine.reshape(width, share)
    up_mine = up_mine.reshape(width, share)
    g0.near(gate_mine)
    g1.mid(g0.blocks[0])
    low_0 = feed_piece(r0, g0.flat(), g1.a)
    s0 = Scatter(low_0, n)
    g1.near(low_0[0])
    s0.mid(g1.blocks[0])
    low_1 = feed_piece(r1, g1.flat(), s0.sums)
    s1 = Scatter(low_1, n)
    s0.far(low_1[0])
    s1.mid(*s0.sent)
    d_low_0 = result_piece(0, r0, s0.finish(s1.sums))
    h0 = Gather(d_low_0, n)
    s1.far(d_low_0)
    h0.mid(*s1.sent)
    d_low_1 = result_piece(1, r1, s1.finish(h0.a))
    h1 = Gather(d_low_1, n)
    h0.near(d_low_1)
    h1.mid(h0.blocks[0])
    d_in_0 = back_piece(r0, h0.flat(), h1.a)
    s0 = Scatter(d_in_0, n)
    h1.near(d_in_0[0])
    s0.mid(h1.blocks[0])
    d_in_1 = back_piece(r1, h1.flat(), s0.sums)
    s1 = Scatter(d_in_1, n)
    s0.far(d_in_1[0])
    rows = (r0, r1)

    def over_rows(left, right, parts, *earlier):
        return weight_grad(
            [after(r0[left], *earlier), r1[left]], [r0[right], r1[right]], parts
        )

    def exchange(grad):
        return lax.all_to_all(grad, "ctx", 0, 0)

    down_pieces = over_rows("active", "d_lowered", 2, *s0.sent)
    d0, d1 = [Line(x, n_dp) for x in (down_pieces[0], down_pieces[1])]
    s1.mid(d0.total, d1.total)
    grad_gate = over_rows("inner", "d_gate", n, s1.sums)
    s1.far(grad_gate)
    gate_pieces = exchange(after(grad_gate, *s1.sent))
    attend_back(0, r0, s0.finish(*s1.sent))
    d0.step(r0["d_kv"][0])
    grad_up = over_rows("inner", "d_up", n, d0.total)
    d1.step(grad_up)
    attend_back(1, r1, s1.finish(d1.total))
    kv_scatter = Scatter(
        [jnp.stack([a, b], axis=1) for a, b in zip(r0["d_kv"], r1["d_kv"])], n
    )
    d0.step(kv_scatter.blocks[-1])
    up_pieces = exchange(after(grad_up, gate_pieces, d0.total))
    half = n // 2
    g_lines = [Line(after(gate_pieces[:half], d0.total), n_dp)]
    grad_out = (
        t_dot(after(r0["attended"], g_lines[0].total), r0["d_projected"])
        + t_dot(r1["attended"], r1["d_projected"])
    ).astype(BF16)
    part_out = lax.psum_scatter(grad_out, "ctx", scatter_dimension=0, tiled=True)
    kv_scatter.mid(grad_out)
    d1.step(kv_scatter.sums)
    g_lines.append(Line(after(gate_pieces[half:], d1.total), n_dp))
    d_query_raw = jnp.concatenate([r["d_query_raw"] for r in rows], axis=0)
    grad_q = t_dot(after(normed, g_lines[1].total), d_query_raw).astype(BF16)
    kv_scatter.far(grad_q)
    d_normed_q = dot_t(after(d_query_raw, *kv_scatter.sent), query_full)
    g_lines[0].step(d_normed_q)
    d_kv_parts = kv_scatter.finish(g_lines[0].total)
    d_kv = (
        d_kv_parts[0][0].astype(WIDE) + d_kv_parts[1].astype(WIDE) + d_kv_parts[2].astype(WIDE)
    ).reshape(total, 2 * head_width)

    def key_shape(raw_rows, gain_values):
        unturned = rms_norm(raw_rows, gain_values)
        a, b = unturned[:, :half_width], unturned[:, half_width:]
        return jnp.concatenate([a * cosine - b * sine, b * cosine + a * sine], axis=1)

    key_pull = jax.vjp(key_shape, key_raw, scale_key)[1]
    d_key_raw, grad_key_gain = key_pull(d_kv[:, :head_width])
    d_kv_raw = jnp.concatenate([d_key_raw, d_kv[:, head_width:]], axis=1).astype(BF16)
    grad_kv = t_dot(normed, d_kv_raw).astype(BF16)
    grad_qkv = jnp.concatenate([grad_q, grad_kv], axis=1)
    part_qkv = lax.psum_scatter(grad_qkv, "ctx", scatter_dimension=0, tiled=True)
    g_lines[1].step(grad_qkv)
    quarter = max(n // 4, 1)
    cuts = [(0, half), (half, half + quarter), (half + quarter, n)]
    u_lines = [Line(after(up_pieces[:half], g_lines[1].total), n_dp)]
    d_normed = d_normed_q + dot_t(after(d_kv_raw, g_lines[1].total), kv_full)
    d_tokens_part, grad_input_gain = normed_pull(d_normed)
    d_hidden = jnp.concatenate([r["d_hidden"] for r in rows], axis=0)
    tokens_grad = (d_hidden + d_tokens_part).astype(BF16)
    gains = jnp.concatenate(
        [
            grad_input_gain,
            sum(r["d_gain"] for r in rows).reshape(-1),
            grad_key_gain,
            sum(r["grad_out_gain"] for r in rows).reshape(-1),
            sum(r["grad_feed_gain"] for r in rows).reshape(-1),
            sum(r["grad_result_gain"] for r in rows).reshape(-1),
        ]
    ).reshape(-1, 128)
    code = 1
    while code < n:
        gains = gains + xor_permute(gains, n, code)
        code *= 2
    clock = [tokens_grad]

    def step(line):
        if line.at < len(line.steps) - 1:
            line.step(*clock)
            clock[:] = [line.total]

    def begin(part):
        line = Line(after(part, *clock), n_dp)
        clock[:] = [line.total]
        return line

    step(g_lines[0])
    step(u_lines[0])
    u_lines.append(begin(up_pieces[cuts[1][0] : cuts[1][1]]))
    step(g_lines[1])
    u_lines.append(begin(up_pieces[cuts[2][0] : cuts[2][1]]))
    step(u_lines[0])
    step(u_lines[1])
    out_line = begin(part_out)
    step(u_lines[1])
    step(u_lines[2])
    qkv_line = begin(part_qkv)
    gain_line = begin(gains)
    step(u_lines[2])
    tail = [out_line, qkv_line, gain_line]
    for _ in range(n_dp):
        for line in [d0, d1] + g_lines + u_lines + tail:
            step(line)

    def side_by_side(lines):
        ends = lines[0].steps[-1][2]
        mine = (my_dp == ends[0]) | (my_dp == ends[1]) if ends else my_dp < 0
        return assemble(
            mine.astype(jnp.int32).reshape(1),
            [line.total for line in lines],
            [line.moved for line in lines],
            width // n,
            n * share,
        )

    summed_down = jnp.concatenate([d0.finish(), d1.finish()], axis=0).astype(WIDE)
    summed_gate = side_by_side(g_lines)
    summed_up = side_by_side(u_lines)
    summed_out = out_line.finish().astype(WIDE)
    summed_qkv = qkv_line.finish().astype(WIDE)
    gains = gain_line.finish().reshape(-1)
    sizes = [width, head_width, head_width, width, width, width]
    gain_grads = []
    start = 0
    for size in sizes:
        gain_grads.append(gains[start : start + size])
        start += size
    return (
        jnp.stack([r["result"] for r in rows]),
        tokens_grad.reshape(row_count, count_local, width),
        summed_qkv[:, :qw],
        summed_qkv[:, qw : qw + head_width],
        summed_qkv[:, qw + head_width :],
        summed_out,
        summed_gate,
        summed_up,
        summed_down,
        *gain_grads,
    )


def solution(mesh):
    return jax.shard_map(
        per_device,
        mesh=mesh,
        in_specs=(
            P("dp", "ctx", None),
            P("dp", "ctx", None),
            P("dp", "ctx"),
            P("ctx", None),
            P("ctx", None),
            P("ctx", None),
            P("ctx", None),
            P("ctx", None),
            P("ctx", None),
            P("ctx", None),
            P(),
            P(),
            P(),
            P(),
            P(),
            P(),
        ),
        out_specs=(
            P("dp", "ctx", None),
            P("dp", "ctx", None),
            P("ctx", None),
            P("ctx", None),
            P("ctx", None),
            P("ctx", None),
            P("ctx", None),
            P("ctx", None),
            P("ctx", None),
            P(),
            P(),
            P(),
            P(),
            P(),
            P(),
        ),
        check_vma=False,
    )
```

time: 1340 us -> 721 us (0.54)
  waiting for transfers between devices: 949 us -> 239 us
  matrix products: 229 us -> 14.6 us
  Pallas kernels: 0 us -> 170 us
  starting transfers between devices: 1.5 us -> 139 us
  blocking collectives: 75.4 us -> 0 us
  local copies, waits for them, and re-layouts: 21.8 us -> 71.7 us
  other arithmetic: 43.7 us -> 64.5 us
    reduce_scatter x9 -> x1, waiting for transfers between devices: 479 us -> 0.02 us  [per_device(): lax.psum_scatter(grad_out, 'ctx', scatter_dimension=0, tiled=True)]
    all_gather x7 -> x2, waiting for transfers between devices: 279 us -> 0.01 us  [the longest x1 0.01 us: per_device(): query_full = lax.all_gather(query_weight, 'ctx', axis=0, tiled=True)]
    ppermute x0 -> x92, waiting for transfers between devices: none -> 238 us  [the longest x61 162 us: xor_permute(): return lax.ppermute(x, 'ctx', [(i, i ^ code) for i in range(axis_size)])]
    dot_general x33 -> x6, matrix products: 229 us -> 14.6 us  [the longest x4 10 us: t_dot(): lax.dot_general(left, right, (((0,), (0,)), ((), ())), preferred_element_...]
    psum x1 -> x0, waiting for transfers between devices: 188 us -> none  [reduce_grads(): lax.psum(for_sending(summed), 'dp')]
    pallas_call x0 -> x25, Pallas kernels: none -> 170 us  [the longest x2 39.1 us: feed_backward(): vmem_call(kernel, (jax.ShapeDtypeStruct((total, width), BF16), hidden, hi...]
    ppermute x0 -> x92, starting transfers between devices: none -> 125 us  [the longest x30 75.7 us: send(): self.moved = lax.ppermute(self.total, 'dp', self.steps[self.at][1])]
    psum x1 -> x0, blocking collectives: 45.4 us -> none  [per_device(): lax.psum((grad_input_gain, grad_query_gain, grad_key_gain, grad_attended_...]
  transfers between devices with their start and end apart: 17 -> 99, of which waited for: 14 -> 43; matrix products, arithmetic and copies ran while one was open for 14% -> 16% of each run, Pallas kernels for 0% -> 16%
where the time goes in v1:
time: 721 us; the launch traced here: 715 us
  waiting for transfers between devices  239 us (33%)
  Pallas kernels  170 us (24%)
  starting transfers between devices  139 us (19%)
  local copies, waits for them, and re-layouts  71.7 us (10%)
  other arithmetic  64.5 us (9%)
  between operations  16.2 us (2%)
  matrix products  14.6 us (2%)
    ppermute x61, waiting for transfers between devices, xor_permute(): return lax.ppermute(x, 'ctx', [(i, i ^ code) for i in range(axis_size)])  162 us
    ppermute x30, starting transfers between devices, send(): self.moved = lax.ppermute(self.total, 'dp', self.steps[self.at][1])  75.7 us
    ppermute x30, waiting for transfers between devices, send(): self.moved = lax.ppermute(self.total, 'dp', self.steps[self.at][1])  73.4 us
    ppermute x61, starting transfers between devices, xor_permute(): return lax.ppermute(x, 'ctx', [(i, i ^ code) for i in range(axis_size)])  48.2 us
    unnamed x225, local copies, waits for them, and re-layouts  43.8 us
    pallas_call x2, Pallas kernels, feed_backward(): vmem_call(kernel, (jax.ShapeDtypeStruct((total, width), BF16), hidden, hi...  39.1 us
    pallas_call x2, Pallas kernels, feed_forward(): vmem_call(kernel, (jax.ShapeDtypeStruct((total, width), BF16), hidden, hi...  37 us
    pallas_call x3, Pallas kernels, weight_grad(): vmem_call(kernel, jax.ShapeDtypeStruct((parts, rows // parts, columns), B...  36.1 us
  transfers between devices with their start and end apart: 99, of which 43 were waited for; matrix products, arithmetic and copies ran while one was open for 16% of the time, Pallas kernels for 16%

profile of v1, /device:TPU:0, one launch (start us, length us, event | category | flops | bytes accessed | tf_op | source)
XLA Modules:
  0.0 714.8 jit_solution(17146359626713273678)
XLA Ops:
  9.8 2.9 collective-permute-start
  23.4 4.3 collective-permute-done.2.d1_ref
  33.8 4.6 all-to-all-start
  41.9 33.4 %collective-permute-done.6.b_ref = bf16[2,192,512]{2,1,0:T(8,128)(2,1)S(1)} collective-permute-done((bf16[2,192,512]{2,1,0:T(8,128)(2,1)}, bf16[2,192,512]{2,1,0:T(8,128)(2,1)S(1)}, u32[]{:S(2)}, u32[]{:S(2)}) %collective-permute-start.6) | collective-permute-done | bytes 393248 | tf_op jit(solution)/shard_map/ppermute | solution.py:59
  83.9 4.5 collective-permute-done.12.d2_ref
  98.7 3.3 collective-permute-done.9
  102.6 3.0 collective-permute-done.10
  110.1 7.2 %shard_map.277 = (bf16[192,1024]{1,0:T(8,128)(2,1)S(1)}, f32[192,4]{1,0:T(8,128)S(1)}, f32[192,1152]{1,0:T(8,128)S(1)}, f32[192,1152]{1,0:T(8,128)S(1)}, bf16[192,1152]{1,0:T(8,128)(2,1)}) custom-call(bf16[384,1024]{1,0:T(8,128)(2,1)S(1)} %get-tuple-element.157.refs_0_.refs_9_, s32[192,1]{1,0:T(8,128)S(1)} %copy-done.34, ...), custom_call_target="tpu_custom_call" | custom-call | tf_op jit(solution)/shard_map/pallas_call | solution.py:367
  124.6 6.4 shard_map.278
  138.6 2.5 collective-permute-done.7.second_ref
  141.1 4.9 shard_map.274
  150.5 12.2 %collective-permute-done.18.a_ref = bf16[192,1152]{1,0:T(8,128)(2,1)S(1)} collective-permute-done((bf16[192,1152]{1,0:T(8,128)(2,1)S(1)}, bf16[192,1152]{1,0:T(8,128)(2,1)S(1)}, u32[]{:S(2)}, u32[]{:S(2)}) %collective-permute-start.18) | collective-permute-done | bytes 442400 | tf_op jit(solution)/shard_map/ppermute | solution.py:59
  164.0 18.7 %shard_map.280 = (bf16[1536,1152]{1,0:T(8,128)(2,1)}, bf16[1536,864]{1,0:T(8,128)(2,1)}, bf16[1536,864]{1,0:T(8,128)(2,1)}, bf16[1536,864]{1,0:T(8,128)(2,1)}, b...) custom-call(bf16[1152,864]{1,0:T(8,128)(2,1)} %bitcast.198, bf16[1152,864]{1,0:T(8,128)(2,1)} %bitcast.202, ...), custom_call_target="tpu_custom_call" | custom-call | tf_op jit(solution)/shard_map/pallas_call | solution.py:731
  184.9 10.9 %collective-permute-done.21.b_ref = bf16[192,1152]{1,0:T(8,128)(2,1)S(1)} collective-permute-done((bf16[192,1152]{1,0:T(8,128)(2,1)S(1)}, bf16[192,1152]{1,0:T(8,128)(2,1)S(1)}, u32[]{:S(2)}, u32[]{:S(2)}) %collective-permute-start.21) | collective-permute-done | bytes 442400 | tf_op jit(solution)/shard_map/ppermute | solution.py:59
  196.1 3.9 collective-permute-done.22.d1_ref
  203.0 3.2 collective-permute-done.26
  207.5 18.3 %shard_map.282 = (bf16[1536,1152]{1,0:T(8,128)(2,1)}, bf16[1536,864]{1,0:T(8,128)(2,1)}, bf16[1536,864]{1,0:T(8,128)(2,1)}, bf16[1536,864]{1,0:T(8,128)(2,1)}, b...) custom-call(bf16[1152,864]{1,0:T(8,128)(2,1)} %bitcast.199, bf16[1152,864]{1,0:T(8,128)(2,1)} %bitcast.203, ...), custom_call_target="tpu_custom_call" | custom-call | tf_op jit(solution)/shard_map/pallas_call | solution.py:731
  227.0 6.8 collective-permute-done.28
  238.9 8.3 %collective-permute-done.25.b_ref = bf16[192,1152]{1,0:T(8,128)(2,1)S(1)} collective-permute-done((bf16[192,1152]{1,0:T(8,128)(2,1)S(1)}, bf16[192,1152]{1,0:T(8,128)(2,1)S(1)}, u32[]{:S(2)}, u32[]{:S(2)}) %collective-permute-start.25) | collective-permute-done | bytes 442400 | tf_op jit(solution)/shard_map/ppermute | solution.py:59
  255.0 7.9 %collective-permute-done.32.a_ref = bf16[192,1152]{1,0:T(8,128)(2,1)S(1)} collective-permute-done((bf16[192,1152]{1,0:T(8,128)(2,1)S(1)}, bf16[192,1152]{1,0:T(8,128)(2,1)S(1)}, u32[]{:S(2)}, u32[]{:S(2)}) %collective-permute-start.32) | collective-permute-done | bytes 442400 | tf_op jit(solution)/shard_map/ppermute | solution.py:59
  265.0 6.7 collective-permute-done.31.b_ref
  276.2 11.9 %collective-permute-done.38.a_ref = bf16[192,1152]{1,0:T(8,128)(2,1)S(1)} collective-permute-done((bf16[192,1152]{1,0:T(8,128)(2,1)S(1)}, bf16[192,1152]{1,0:T(8,128)(2,1)S(1)}, u32[]{:S(2)}, u32[]{:S(2)}) %collective-permute-start.38) | collective-permute-done | bytes 442400 | tf_op jit(solution)/shard_map/ppermute | solution.py:59
  289.4 19.7 %shard_map.286 = (bf16[1536,1152]{1,0:T(8,128)(2,1)}, bf16[1536,864]{1,0:T(8,128)(2,1)}, bf16[1536,864]{1,0:T(8,128)(2,1)}, bf16[768,1152]{1,0:T(8,128)(2,1)S(1)}, bf16[768,1152]{1,0:T(8,128)(2,1)}) custom-call(bf16[1152,864]{1,0:T(8,128)(2,1)} %bitcast.200, bf16[1152,864]{1,0:T(8,128)(2,1)} %bitcast.204, bf16[864,1152]{1,0:T(8,128)(2,1)} %down_ref.7, ...), custom_call_target="tpu_custom_call" | custom-call | tf_op jit(solution)/shard_map/pallas_call | solution.py:776
  311.4 10.8 %collective-permute-done.41.b_ref = bf16[192,1152]{1,0:T(8,128)(2,1)S(1)} collective-permute-done((bf16[192,1152]{1,0:T(8,128)(2,1)S(1)}, bf16[192,1152]{1,0:T(8,128)(2,1)S(1)}, u32[]{:S(2)}, u32[]{:S(2)}) %collective-permute-start.41) | collective-permute-done | bytes 442400 | tf_op jit(solution)/shard_map/ppermute | solution.py:59
  322.9 3.6 collective-permute-done.42.d1_ref
  333.1 19.3 %shard_map.288 = (bf16[1536,1152]{1,0:T(8,128)(2,1)}, bf16[1536,864]{1,0:T(8,128)(2,1)}, bf16[1536,864]{1,0:T(8,128)(2,1)}, bf16[768,1152]{1,0:T(8,128)(2,1)S(1)}, bf16[768,1152]{1,0:T(8,128)(2,1)S(1)}) custom-call(bf16[1152,864]{1,0:T(8,128)(2,1)} %bitcast.201, bf16[1152,864]{1,0:T(8,128)(2,1)} %bitcast.205, bf16[864,1152]{1,0:T(8,128)(2,1)} %down_ref.7, ...), custom_call_target="tpu_custom_call" | custom-call | tf_op jit(solution)/shard_map/pallas_call | solution.py:776
  354.4 11.2 %shard_map.289 = bf16[2,432,1152]{2,1,0:T(8,128)(2,1)S(1)} custom-call(bf16[1536,864]{1,0:T(8,128)(2,1)S(1)} %copy-done.22, bf16[1536,864]{1,0:T(8,128)(2,1)} %get-tuple-element.200.refs_1_, bf16[1536,1152]{1,0:T(8,128)(2,1)} %get-tuple-element.201.refs_2_, bf16[1536,1152]{1,0:T(8,128)(2,1)} %get-tuple-element.202.refs_3_), custom_call_target="tpu_custom_call" | custom-call | tf_op jit(solution)/shard_map/pallas_call | solution.py:836
  370.2 3.4 collective-permute-start.54
  374.9 12.0 %shard_map.290 = bf16[8,144,864]{2,1,0:T(8,128)(2,1)S(1)} custom-call(bf16[1536,1152]{1,0:T(8,128)(2,1)} %get-tuple-element.217.refs_0_, bf16[1536,1152]{1,0:T(8,128)(2,1)} %get-tuple-element.206.refs_1_, bf16[1536,864]{1,0:T(8,128)(2,1)S(1)} %copy-done.21, bf16[1536,864]{1,0:T(8,128)(2,1)} %get-tuple-element.208.refs_3_), custom_call_target="tpu_custom_call" | custom-call | tf_op jit(solution)/shard_map/pallas_call | solution.py:836
  395.2 10.7 %shard_map.291 = (f32[192,1152]{1,0:T(8,128)S(1)}, bf16[192,1152]{1,0:T(8,128)(2,1)S(1)}, f32[1,1152]{1,0:T(1,128)S(1)}, f32[1,1152]{1,0:T(1,128)S(1)}, bf16[192...) custom-call(bf16[4,192,1152]{2,1,0:T(8,128)(2,1)} %copy-done.70, ...), custom_call_target="tpu_custom_call" | custom-call | tf_op jit(solution)/shard_map/pallas_call | solution.py:539
  413.2 12.9 %shard_map.292 = bf16[8,144,864]{2,1,0:T(8,128)(2,1)} custom-call(bf16[1536,1152]{1,0:T(8,128)(2,1)} %get-tuple-element.217.refs_0_, bf16[1536,1152]{1,0:T(8,128)(2,1)} %get-tuple-element.206.refs_1_, bf16[1536,864]{1,0:T(8,128)(2,1)S(1)} %copy-done.20, bf16[1536,864]{1,0:T(8,128)(2,1)} %get-tuple-element.219.refs_3_), custom_call_target="tpu_custom_call" | custom-call | tf_op jit(solution)/shard_map/pallas_call | solution.py:836
  426.1 4.3 all-to-all-start.1
  430.5 2.5 add_convert_fusion.13
  434.7 11.0 %shard_map.293 = (f32[192,1152]{1,0:T(8,128)S(1)}, bf16[192,1152]{1,0:T(8,128)(2,1)S(1)}, f32[1,1152]{1,0:T(1,128)S(1)}, f32[1,1152]{1,0:T(1,128)S(1)}, bf16[192...) custom-call(bf16[4,192,1152]{2,1,0:T(8,128)(2,1)} %copy-done.69, ...), custom_call_target="tpu_custom_call" | custom-call | tf_op jit(solution)/shard_map/pallas_call | solution.py:539
  449.7 2.7 add_convert_fusion.12
  453.7 3.0 fusion.41
  456.8 3.0 fusion.39
  459.8 6.4 collective-permute-start.62
  466.2 4.5 all-to-all-start.2
  470.7 4.6 fusion
  475.5 3.2 collective-permute-done.88
  482.9 3.0 add_convert_fusion.11
  493.8 7.5 %collective-permute-done.59 = bf16[1,192,512]{2,1,0:T(8,128)(2,1)S(1)} collective-permute-done((bf16[1,192,512]{2,1,0:T(8,128)(2,1)S(1)}, bf16[1,192,512]{2,1,0:T(8,128)(2,1)S(1)}, u32[]{:S(2)}, u32[]{:S(2)}) %collective-permute-start.59) | collective-permute-done | bytes 196640 | tf_op jit(solution)/shard_map/ppermute | solution.py:59
  506.3 2.8 add_convert_fusion.10
  510.9 4.0 collective-permute-done.61
  520.7 5.8 copy.113
  533.3 3.4 collective-permute-start.66
  536.8 3.0 fusion.2
  541.7 16.0 %collective-permute-done.66 = bf16[4,144,864]{2,1,0:T(8,128)(2,1)S(1)} collective-permute-done((bf16[4,144,864]{2,1,0:T(8,128)(2,1)S(1)}, bf16[4,144,864]{2,1,0:T(8,128)(2,1)S(1)}, u32[]{:S(2)}, u32[]{:S(2)}) %collective-permute-start.66) | collective-permute-done | bytes 995360 | tf_op jit(solution)/shard_map/ppermute | solution.py:158
  560.9 6.2 collective-permute-start.69
  567.1 2.8 add_convert_fusion.6.refs_1_
  572.3 6.9 collective-permute-done.69
  594.8 13.1 %collective-permute-start.73 = (bf16[128,1152]{1,0:T(8,128)(2,1)}, bf16[128,1152]{1,0:T(8,128)(2,1)}, u32[]{:S(2)}, u32[]{:S(2)}) collective-permute-start(bf16[128,1152]{1,0:T(8,128)(2,1)} %reduce-scatter.5.cloned.1.call-done), channel_id=1, source_target_pairs={{0,8},{24,16},{1,9},{25,17},{2,10},{26,18},{3,11},{27,19},{4,12},{... | collective-permute-start | bytes 884744 | tf_op jit(solution)/shard_map/ppermute | solution.py:158
  607.9 3.4 maximum_convert_fusion
  612.6 4.1 collective-permute-done.83.refs_2_
  616.7 22.1 %collective-permute-done.84.refs_3_ = bf16[4,144,864]{2,1,0:T(8,128)(2,1)} collective-permute-done((bf16[4,144,864]{2,1,0:T(8,128)(2,1)}, bf16[4,144,864]{2,1,0:T(8,128)(2,1)}, u32[]{:S(2)}, u32[]{:S(2)}) %collective-permute-start.84) | collective-permute-done | bytes 995360 | tf_op jit(solution)/shard_map/ppermute | solution.py:158
  638.8 4.3 shard_map.294
  647.0 4.6 collective-permute-start.80
  654.2 5.4 collective-permute-start.72
  660.7 4.2 collective-permute-done.72
  678.2 3.3 collective-permute-done.87.refs_5_
  681.5 3.7 shard_map.295
  689.1 4.2 collective-permute-done.82
  697.4 7.2 %collective-permute-done.81 = bf16[144,1536]{1,0:T(8,128)(2,1)S(1)} collective-permute-done((bf16[144,1536]{1,0:T(8,128)(2,1)S(1)}, bf16[144,1536]{1,0:T(8,128)(2,1)S(1)}, u32[]{:S(2)}, u32[]{:S(2)}) %collective-permute-start.81) | collective-permute-done | bytes 442400 | tf_op jit(solution)/shard_map/ppermute | solution.py:158
  (541 shorter events, 222.8 us)
Async XLA Ops:
  7.2 71.0 %all-gather.3.cloned.1.call-start = ((), (), s32[]{:S(2)}) async-start(), calls=%async_computation.5 | async-start | bytes 2654208 | tf_op jit(solution)/shard_map/all_gather | solution.py:888
  7.9 100.6 %all-gather.5.cloned.1.call-start = ((), (), s32[]{:S(2)}) async-start(), calls=%async_computation.6 | async-start | bytes 2654208 | tf_op jit(solution)/shard_map/all_gather | solution.py:924
  9.8 12.9 %collective-permute-start = (bf16[144,512]{1,0:T(8,128)(2,1)S(1)}, bf16[144,512]{1,0:T(8,128)(2,1)S(1)}, u32[]{:S(2)}, u32[]{:S(2)}) collective-permute-start(bf16[144,512]{1,0:T(8,128)(2,1)S(1)} %constant_dynamic-update-slice_fusion.x_ref), channel_id=1, source_target_pairs={{0,2},{1,3},{2,0},{3,1},{4,6},{5,7},{6,4},{7,5},{8,10},{9,11},{10,... | collective-permute-start | bytes 442376 | tf_op jit(solution)/shard_map/ppermute | solution.py:59
  33.8 60.2 %all-to-all-start = ((bf16[8,144,864]{2,1,0:T(8,128)(2,1)}), bf16[8,144,864]{2,1,0:T(8,128)(2,1)}, u32[]{:S(2)}, u32[]{:S(2)}) async-start(bf16[8,144,864]{2,1,0:T(8,128)(2,1)} %shard_map.271), calls=%async_computation | async-start | bytes 4128768 | tf_op jit(solution)/shard_map/all_to_all | solution.py:891
  38.3 36.9 %collective-permute-start.6 = (bf16[2,192,512]{2,1,0:T(8,128)(2,1)}, bf16[2,192,512]{2,1,0:T(8,128)(2,1)S(1)}, u32[]{:S(2)}, u32[]{:S(2)}) collective-permute-start(bf16[2,192,512]{2,1,0:T(8,128)(2,1)} %get-tuple-element.148.x_ref), channel_id=1, source_target_pairs={{0,4},{1,5},{2,6},{3,7},{4,0},{5,1},{6,2},{7,3},{8,12},{9,13},{10,... | collective-permute-start | bytes 1179656 | tf_op jit(solution)/shard_map/ppermute | solution.py:59
  40.4 42.2 %collective-permute-start.5 = (bf16[2,192,512]{2,1,0:T(8,128)(2,1)}, bf16[2,192,512]{2,1,0:T(8,128)(2,1)S(1)}, u32[]{:S(2)}, u32[]{:S(2)}) collective-permute-start(bf16[2,192,512]{2,1,0:T(8,128)(2,1)} %get-tuple-element.148.x_ref), channel_id=1, source_target_pairs={{0,2},{1,3},{2,0},{3,1},{4,6},{5,7},{6,4},{7,5},{8,10},{9,11},{10,... | collective-permute-start | bytes 1179656 | tf_op jit(solution)/shard_map/ppermute | solution.py:59
  92.1 16.5 %collective-permute-start.13 = (bf16[4,2,192,512]{3,2,1,0:T(8,128)(2,1)S(1)}, bf16[4,2,192,512]{3,2,1,0:T(8,128)(2,1)}, u32[]{:S(2)}, u32[]{:S(2)}) collective-permute-start(bf16[4,2,192,512]{3,2,1,0:T(8,128)(2,1)S(1)} %shard_map.276.refs_8_.refs_18_), channel_id=1, source_target_pairs={{0,1},{1,0},{2,3},{3,2},{4,5},{5,4},{6,7},{7,6},{8,9},{9,8},{10,11... | collective-permute-start | bytes 4718600 | tf_op jit(solution)/shard_map/ppermute | solution.py:59
  93.9 47.2 %collective-permute-start.7 = (bf16[8,144,864]{2,1,0:T(8,128)(2,1)}, bf16[8,144,864]{2,1,0:T(8,128)(2,1)}, u32[]{:S(2)}, u32[]{:S(2)}) collective-permute-start(bf16[8,144,864]{2,1,0:T(8,128)(2,1)} %all-to-all-done.first_ref), channel_id=1, source_target_pairs={{0,8},{8,0},{16,24},{24,16},{1,9},{9,1},{17,25},{25,17},{2,10},{10... | collective-permute-start | bytes 5971976 | tf_op jit(solution)/shard_map/ppermute | solution.py:929
  120.8 15.0 %collective-permute-start.15 = (bf16[192,1152]{1,0:T(8,128)(2,1)}, bf16[192,1152]{1,0:T(8,128)(2,1)}, u32[]{:S(2)}, u32[]{:S(2)}) collective-permute-start(bf16[192,1152]{1,0:T(8,128)(2,1)} %get-tuple-element.156.x_ref), channel_id=1, source_target_pairs={{0,4},{1,5},{2,6},{3,7},{4,0},{5,1},{6,2},{7,3},{8,12},{9,13},{10,... | collective-permute-start | bytes 1327112 | tf_op jit(solution)/shard_map/ppermute | solution.py:59
  134.5 14.2 %collective-permute-start.16 = (bf16[96,1152]{1,0:T(8,128)(2,1)S(1)}, bf16[96,1152]{1,0:T(8,128)(2,1)S(1)}, u32[]{:S(2)}, u32[]{:S(2)}) collective-permute-start(bf16[96,1152]{1,0:T(8,128)(2,1)S(1)} %slice.364), channel_id=1, source_target_pairs={{0,4},{1,5},{2,6},{3,7},{4,0},{5,1},{6,2},{7,3},{8,12},{9,13},{10,... | collective-permute-start | bytes 663560 | tf_op jit(solution)/shard_map/ppermute | solution.py:59
  182.7 19.9 %collective-permute-start.20 = (bf16[4,192,1152]{2,1,0:T(8,128)(2,1)S(1)}, bf16[4,192,1152]{2,1,0:T(8,128)(2,1)S(1)}, u32[]{:S(2)}, u32[]{:S(2)}) collective-permute-start(bf16[4,192,1152]{2,1,0:T(8,128)(2,1)S(1)} %bitcast.221), channel_id=1, source_target_pairs={{0,1},{1,0},{2,3},{3,2},{4,5},{5,4},{6,7},{7,6},{8,9},{9,8},{10,11... | collective-permute-start | bytes 5308424 | tf_op jit(solution)/shard_map/ppermute | solution.py:59
  182.7 13.0 %collective-permute-start.21 = (bf16[192,1152]{1,0:T(8,128)(2,1)S(1)}, bf16[192,1152]{1,0:T(8,128)(2,1)S(1)}, u32[]{:S(2)}, u32[]{:S(2)}) collective-permute-start(bf16[192,1152]{1,0:T(8,128)(2,1)S(1)} %get-tuple-element.161.x_ref), channel_id=1, source_target_pairs={{0,4},{1,5},{2,6},{3,7},{4,0},{5,1},{6,2},{7,3},{8,12},{9,13},{10,... | collective-permute-start | bytes 1327112 | tf_op jit(solution)/shard_map/ppermute | solution.py:59
  183.4 16.6 %collective-permute-start.22 = (bf16[96,1152]{1,0:T(8,128)(2,1)S(1)}, bf16[96,1152]{1,0:T(8,128)(2,1)S(1)}, u32[]{:S(2)}, u32[]{:S(2)}) collective-permute-start(bf16[96,1152]{1,0:T(8,128)(2,1)S(1)} %slice.366), channel_id=1, source_target_pairs={{0,4},{1,5},{2,6},{3,7},{4,0},{5,1},{6,2},{7,3},{8,12},{9,13},{10,... | collective-permute-start | bytes 663560 | tf_op jit(solution)/shard_map/ppermute | solution.py:59
  234.0 13.2 %collective-permute-start.25 = (bf16[192,1152]{1,0:T(8,128)(2,1)S(1)}, bf16[192,1152]{1,0:T(8,128)(2,1)S(1)}, u32[]{:S(2)}, u32[]{:S(2)}) collective-permute-start(bf16[192,1152]{1,0:T(8,128)(2,1)S(1)} %pad_maximum_fusion.3), channel_id=1, source_target_pairs={{0,2},{1,3},{2,0},{3,1},{4,6},{5,7},{6,4},{7,5},{8,10},{9,11},{10,... | collective-permute-start | bytes 1327112 | tf_op jit(solution)/shard_map/ppermute | solution.py:59
  235.8 13.2 %collective-permute-start.29 = (bf16[192,1152]{1,0:T(8,128)(2,1)S(1)}, bf16[192,1152]{1,0:T(8,128)(2,1)S(1)}, u32[]{:S(2)}, u32[]{:S(2)}) collective-permute-start(bf16[192,1152]{1,0:T(8,128)(2,1)S(1)} %pad_maximum_fusion.4), channel_id=1, source_target_pairs={{0,4},{1,5},{2,6},{3,7},{4,0},{5,1},{6,2},{7,3},{8,12},{9,13},{10,... | collective-permute-start | bytes 1327112 | tf_op jit(solution)/shard_map/ppermute | solution.py:59
  237.0 14.9 %collective-permute-start.33 = (bf16[96,1152]{1,0:T(8,128)(2,1)S(1)}, bf16[96,1152]{1,0:T(8,128)(2,1)S(1)}, u32[]{:S(2)}, u32[]{:S(2)}) collective-permute-start(bf16[96,1152]{1,0:T(8,128)(2,1)S(1)} %get-tuple-element.373), channel_id=1, source_target_pairs={{0,2},{1,3},{2,0},{3,1},{4,6},{5,7},{6,4},{7,5},{8,10},{9,11},{10,... | collective-permute-start | bytes 663560 | tf_op jit(solution)/shard_map/ppermute | solution.py:59
  237.4 16.3 %collective-permute-start.30 = (bf16[96,1152]{1,0:T(8,128)(2,1)S(1)}, bf16[96,1152]{1,0:T(8,128)(2,1)S(1)}, u32[]{:S(2)}, u32[]{:S(2)}) collective-permute-start(bf16[96,1152]{1,0:T(8,128)(2,1)S(1)} %get-tuple-element.375), channel_id=1, source_target_pairs={{0,4},{1,5},{2,6},{3,7},{4,0},{5,1},{6,2},{7,3},{8,12},{9,13},{10,... | collective-permute-start | bytes 663560 | tf_op jit(solution)/shard_map/ppermute | solution.py:59
  249.7 13.2 %collective-permute-start.32 = (bf16[192,1152]{1,0:T(8,128)(2,1)S(1)}, bf16[192,1152]{1,0:T(8,128)(2,1)S(1)}, u32[]{:S(2)}, u32[]{:S(2)}) collective-permute-start(bf16[192,1152]{1,0:T(8,128)(2,1)S(1)} %get-tuple-element.176.x_ref), channel_id=1, source_target_pairs={{0,2},{1,3},{2,0},{3,1},{4,6},{5,7},{6,4},{7,5},{8,10},{9,11},{10,... | collective-permute-start | bytes 1327112 | tf_op jit(solution)/shard_map/ppermute | solution.py:59
  250.1 13.5 %collective-permute-start.35 = (bf16[192,1152]{1,0:T(8,128)(2,1)S(1)}, bf16[192,1152]{1,0:T(8,128)(2,1)S(1)}, u32[]{:S(2)}, u32[]{:S(2)}) collective-permute-start(bf16[192,1152]{1,0:T(8,128)(2,1)S(1)} %get-tuple-element.176.x_ref), channel_id=1, source_target_pairs={{0,4},{1,5},{2,6},{3,7},{4,0},{5,1},{6,2},{7,3},{8,12},{9,13},{10,... | collective-permute-start | bytes 1327112 | tf_op jit(solution)/shard_map/ppermute | solution.py:59
  253.9 17.8 %collective-permute-start.31 = (bf16[192,1152]{1,0:T(8,128)(2,1)S(1)}, bf16[192,1152]{1,0:T(8,128)(2,1)S(1)}, u32[]{:S(2)}, u32[]{:S(2)}) collective-permute-start(bf16[192,1152]{1,0:T(8,128)(2,1)S(1)} %pad_maximum_fusion.5), channel_id=1, source_target_pairs={{0,2},{1,3},{2,0},{3,1},{4,6},{5,7},{6,4},{7,5},{8,10},{9,11},{10,... | collective-permute-start | bytes 1327112 | tf_op jit(solution)/shard_map/ppermute | solution.py:59
  254.3 18.4 %collective-permute-start.34 = (bf16[192,1152]{1,0:T(8,128)(2,1)S(1)}, bf16[192,1152]{1,0:T(8,128)(2,1)S(1)}, u32[]{:S(2)}, u32[]{:S(2)}) collective-permute-start(bf16[192,1152]{1,0:T(8,128)(2,1)S(1)} %pad_maximum_fusion.6), channel_id=1, source_target_pairs={{0,4},{1,5},{2,6},{3,7},{4,0},{5,1},{6,2},{7,3},{8,12},{9,13},{10,... | collective-permute-start | bytes 1327112 | tf_op jit(solution)/shard_map/ppermute | solution.py:59
  309.1 20.2 %collective-permute-start.40 = (bf16[4,192,1152]{2,1,0:T(8,128)(2,1)}, bf16[4,192,1152]{2,1,0:T(8,128)(2,1)}, u32[]{:S(2)}, u32[]{:S(2)}) collective-permute-start(bf16[4,192,1152]{2,1,0:T(8,128)(2,1)} %bitcast.37), channel_id=1, source_target_pairs={{0,1},{1,0},{2,3},{3,2},{4,5},{5,4},{6,7},{7,6},{8,9},{9,8},{10,11... | collective-permute-start | bytes 5308424 | tf_op jit(solution)/shard_map/ppermute | solution.py:59
  309.2 13.0 %collective-permute-start.41 = (bf16[192,1152]{1,0:T(8,128)(2,1)S(1)}, bf16[192,1152]{1,0:T(8,128)(2,1)S(1)}, u32[]{:S(2)}, u32[]{:S(2)}) collective-permute-start(bf16[192,1152]{1,0:T(8,128)(2,1)S(1)} %get-tuple-element.184.x_ref), channel_id=1, source_target_pairs={{0,4},{1,5},{2,6},{3,7},{4,0},{5,1},{6,2},{7,3},{8,12},{9,13},{10,... | collective-permute-start | bytes 1327112 | tf_op jit(solution)/shard_map/ppermute | solution.py:59
  309.9 16.6 %collective-permute-start.42 = (bf16[96,1152]{1,0:T(8,128)(2,1)S(1)}, bf16[96,1152]{1,0:T(8,128)(2,1)S(1)}, u32[]{:S(2)}, u32[]{:S(2)}) collective-permute-start(bf16[96,1152]{1,0:T(8,128)(2,1)S(1)} %slice.394), channel_id=1, source_target_pairs={{0,4},{1,5},{2,6},{3,7},{4,0},{5,1},{6,2},{7,3},{8,12},{9,13},{10,... | collective-permute-start | bytes 663560 | tf_op jit(solution)/shard_map/ppermute | solution.py:59
  331.8 20.7 %collective-permute-start.48 = (bf16[96,1152]{1,0:T(8,128)(2,1)S(1)}, bf16[96,1152]{1,0:T(8,128)(2,1)S(1)}, u32[]{:S(2)}, u32[]{:S(2)}) collective-permute-start(bf16[96,1152]{1,0:T(8,128)(2,1)S(1)} %get-tuple-element.367), channel_id=1, source_target_pairs={{0,2},{1,3},{2,0},{3,1},{4,6},{5,7},{6,4},{7,5},{8,10},{9,11},{10,... | collective-permute-start | bytes 663560 | tf_op jit(solution)/shard_map/ppermute | solution.py:59
  332.5 20.0 %collective-permute-start.44 = (bf16[96,1152]{1,0:T(8,128)(2,1)S(1)}, bf16[96,1152]{1,0:T(8,128)(2,1)S(1)}, u32[]{:S(2)}, u32[]{:S(2)}) collective-permute-start(bf16[96,1152]{1,0:T(8,128)(2,1)S(1)} %get-tuple-element.369), channel_id=1, source_target_pairs={{0,4},{1,5},{2,6},{3,7},{4,0},{5,1},{6,2},{7,3},{8,12},{9,13},{10,... | collective-permute-start | bytes 663560 | tf_op jit(solution)/shard_map/ppermute | solution.py:59
  352.4 13.3 %collective-permute-start.47 = (bf16[4,192,1152]{2,1,0:T(8,128)(2,1)S(1)}, bf16[4,192,1152]{2,1,0:T(8,128)(2,1)S(1)}, u32[]{:S(2)}, u32[]{:S(2)}) collective-permute-start(bf16[4,192,1152]{2,1,0:T(8,128)(2,1)S(1)} %bitcast.222), channel_id=1, source_target_pairs={{0,1},{1,0},{2,3},{3,2},{4,5},{5,4},{6,7},{7,6},{8,9},{9,8},{10,11... | collective-permute-start | bytes 5308424 | tf_op jit(solution)/shard_map/ppermute | solution.py:59
  366.3 21.9 %collective-permute-start.50 = (bf16[96,1152]{1,0:T(8,128)(2,1)S(1)}, bf16[96,1152]{1,0:T(8,128)(2,1)S(1)}, u32[]{:S(2)}, u32[]{:S(2)}) collective-permute-start(bf16[96,1152]{1,0:T(8,128)(2,1)S(1)} %get-tuple-element.361), channel_id=1, source_target_pairs={{0,2},{1,3},{2,0},{3,1},{4,6},{5,7},{6,4},{7,5},{8,10},{9,11},{10,... | collective-permute-start | bytes 663560 | tf_op jit(solution)/shard_map/ppermute | solution.py:59
  367.8 22.8 %collective-permute-start.49 = (bf16[96,1152]{1,0:T(8,128)(2,1)S(1)}, bf16[96,1152]{1,0:T(8,128)(2,1)S(1)}, u32[]{:S(2)}, u32[]{:S(2)}) collective-permute-start(bf16[96,1152]{1,0:T(8,128)(2,1)S(1)} %get-tuple-element.363), channel_id=1, source_target_pairs={{0,4},{1,5},{2,6},{3,7},{4,0},{5,1},{6,2},{7,3},{8,12},{9,13},{10,... | collective-permute-start | bytes 663560 | tf_op jit(solution)/shard_map/ppermute | solution.py:59
  370.2 40.0 %collective-permute-start.54 = (bf16[432,1152]{1,0:T(8,128)(2,1)S(1)}, bf16[432,1152]{1,0:T(8,128)(2,1)S(1)}, u32[]{:S(2)}, u32[]{:S(2)}) collective-permute-start(bf16[432,1152]{1,0:T(8,128)(2,1)S(1)} %get-tuple-element.358), channel_id=1, source_target_pairs={{0,8},{24,16},{1,9},{25,17},{2,10},{26,18},{3,11},{27,19},{4,12},{... | collective-permute-start | bytes 2985992 | tf_op jit(solution)/shard_map/ppermute | solution.py:158
  373.6 20.1 %collective-permute-start.45 = (bf16[192,1152]{1,0:T(8,128)(2,1)}, bf16[192,1152]{1,0:T(8,128)(2,1)S(1)}, u32[]{:S(2)}, u32[]{:S(2)}) collective-permute-start(bf16[192,1152]{1,0:T(8,128)(2,1)} %pad_maximum_fusion.7), channel_id=1, source_target_pairs={{0,2},{1,3},{2,0},{3,1},{4,6},{5,7},{6,4},{7,5},{8,10},{9,11},{10,... | collective-permute-start | bytes 1327112 | tf_op jit(solution)/shard_map/ppermute | solution.py:59
  374.3 20.9 %collective-permute-start.51 = (bf16[192,1152]{1,0:T(8,128)(2,1)S(1)}, bf16[192,1152]{1,0:T(8,128)(2,1)S(1)}, u32[]{:S(2)}, u32[]{:S(2)}) collective-permute-start(bf16[192,1152]{1,0:T(8,128)(2,1)S(1)} %copy-done.82), channel_id=1, source_target_pairs={{0,4},{1,5},{2,6},{3,7},{4,0},{5,1},{6,2},{7,3},{8,12},{9,13},{10,... | collective-permute-start | bytes 1327112 | tf_op jit(solution)/shard_map/ppermute | solution.py:59
  388.2 37.9 %collective-permute-start.53 = (bf16[432,1152]{1,0:T(8,128)(2,1)S(1)}, bf16[432,1152]{1,0:T(8,128)(2,1)}, u32[]{:S(2)}, u32[]{:S(2)}) collective-permute-start(bf16[432,1152]{1,0:T(8,128)(2,1)S(1)} %get-tuple-element.357), channel_id=1, source_target_pairs={{0,8},{24,16},{1,9},{25,17},{2,10},{26,18},{3,11},{27,19},{4,12},{... | collective-permute-start | bytes 2985992 | tf_op jit(solution)/shard_map/ppermute | solution.py:158
  391.5 43.2 %collective-permute-start.52 = (bf16[192,1152]{1,0:T(8,128)(2,1)}, bf16[192,1152]{1,0:T(8,128)(2,1)}, u32[]{:S(2)}, u32[]{:S(2)}) collective-permute-start(bf16[192,1152]{1,0:T(8,128)(2,1)} %pad_maximum_fusion.9), channel_id=1, source_target_pairs={{0,2},{1,3},{2,0},{3,1},{4,6},{5,7},{6,4},{7,5},{8,10},{9,11},{10,... | collective-permute-start | bytes 1327112 | tf_op jit(solution)/shard_map/ppermute | solution.py:59
  393.7 41.0 %collective-permute-start.55 = (bf16[192,1152]{1,0:T(8,128)(2,1)}, bf16[192,1152]{1,0:T(8,128)(2,1)}, u32[]{:S(2)}, u32[]{:S(2)}) collective-permute-start(bf16[192,1152]{1,0:T(8,128)(2,1)} %pad_maximum_fusion.10), channel_id=1, source_target_pairs={{0,4},{1,5},{2,6},{3,7},{4,0},{5,1},{6,2},{7,3},{8,12},{9,13},{10,... | collective-permute-start | bytes 1327112 | tf_op jit(solution)/shard_map/ppermute | solution.py:59
  411.4 37.4 %collective-permute-start.57 = (bf16[432,1152]{1,0:T(8,128)(2,1)}, bf16[432,1152]{1,0:T(8,128)(2,1)}, u32[]{:S(2)}, u32[]{:S(2)}) collective-permute-start(bf16[432,1152]{1,0:T(8,128)(2,1)} %add_convert_fusion.14), channel_id=1, source_target_pairs={{8,16},{16,8},{9,17},{17,9},{10,18},{18,10},{11,19},{19,11},{12,20... | collective-permute-start | bytes 2985992 | tf_op jit(solution)/shard_map/ppermute | solution.py:158
  426.1 30.7 %all-to-all-start.1 = ((bf16[8,144,864]{2,1,0:T(8,128)(2,1)}), bf16[8,144,864]{2,1,0:T(8,128)(2,1)}, u32[]{:S(2)}, u32[]{:S(2)}) async-start(bf16[8,144,864]{2,1,0:T(8,128)(2,1)} %copy-done.8), calls=%async_computation.1 | async-start | bytes 4128768 | tf_op jit(solution)/shard_map/all_to_all | solution.py:1033
  433.0 49.9 %collective-permute-start.60 = (bf16[432,1152]{1,0:T(8,128)(2,1)}, bf16[432,1152]{1,0:T(8,128)(2,1)}, u32[]{:S(2)}, u32[]{:S(2)}) collective-permute-start(bf16[432,1152]{1,0:T(8,128)(2,1)} %add_convert_fusion.13), channel_id=1, source_target_pairs={{8,16},{16,8},{9,17},{17,9},{10,18},{18,10},{11,19},{19,11},{12,20... | collective-permute-start | bytes 2985992 | tf_op jit(solution)/shard_map/ppermute | solution.py:158
  447.2 33.8 %collective-permute-start.56 = (bf16[4,2,192,512]{3,2,0,1:T(8,128)(2,1)}, bf16[4,2,192,512]{3,2,0,1:T(8,128)(2,1)}, u32[]{:S(2)}, u32[]{:S(2)}) collective-permute-start(bf16[4,2,192,512]{3,2,0,1:T(8,128)(2,1)} %pad_maximum_fusion.1), channel_id=1, source_target_pairs={{0,1},{1,0},{2,3},{3,2},{4,5},{5,4},{6,7},{7,6},{8,9},{9,8},{10,11... | collective-permute-start | bytes 4718600 | tf_op jit(solution)/shard_map/ppermute | solution.py:59
  452.4 26.3 %collective-permute-start.88 = (bf16[432,1152]{1,0:T(8,128)(2,1)}, bf16[432,1152]{1,0:T(8,128)(2,1)}, u32[]{:S(2)}, u32[]{:S(2)}) collective-permute-start(bf16[432,1152]{1,0:T(8,128)(2,1)} %add_convert_fusion.12), channel_id=1, source_target_pairs={{8,0},{16,24},{9,1},{17,25},{10,2},{18,26},{11,3},{19,27},{12,4},{... | collective-permute-start | bytes 2985992 | tf_op jit(solution)/shard_map/ppermute | solution.py:158
  459.8 46.5 %collective-permute-start.62 = (bf16[4,144,864]{2,1,0:T(8,128)(2,1)}, bf16[4,144,864]{2,1,0:T(8,128)(2,1)}, u32[]{:S(2)}, u32[]{:S(2)}) collective-permute-start(bf16[4,144,864]{2,1,0:T(8,128)(2,1)} %get-tuple-element.233), channel_id=1, source_target_pairs={{0,8},{24,16},{1,9},{25,17},{2,10},{26,18},{3,11},{27,19},{4,12},{... | collective-permute-start | bytes 2985992 | tf_op jit(solution)/shard_map/ppermute | solution.py:158
  466.2 65.5 %all-to-all-start.2 = ((bf16[8,144,864]{2,1,0:T(8,128)(2,1)}), bf16[8,144,864]{2,1,0:T(8,128)(2,1)}, u32[]{:S(2)}, u32[]{:S(2)}) async-start(bf16[8,144,864]{2,1,0:T(8,128)(2,1)} %shard_map.292), calls=%async_computation.2 | async-start | bytes 4128768 | tf_op jit(solution)/shard_map/all_to_all | solution.py:1033
  470.7 116.3 %reduce-scatter.5.cloned.1.call-start = ((), (), s32[]{:S(2)}) async-start(), calls=%async_computation.7 | async-start | bytes 2654208 | tf_op jit(solution)/shard_map/reduce_scatter | solution.py:1057
  475.4 169.2 %reduce-scatter.7.cloned.1.call-start = ((), (), s32[]{:S(2)}) async-start(), calls=%async_computation.8 | async-start | bytes 3981312
  486.0 40.5 %collective-permute-start.64 = (bf16[4,144,864]{2,1,0:T(8,128)(2,1)S(1)}, bf16[4,144,864]{2,1,0:T(8,128)(2,1)S(1)}, u32[]{:S(2)}, u32[]{:S(2)}) collective-permute-start(bf16[4,144,864]{2,1,0:T(8,128)(2,1)S(1)} %copy-done.72), channel_id=1, source_target_pairs={{0,8},{24,16},{1,9},{25,17},{2,10},{26,18},{3,11},{27,19},{4,12},{... | collective-permute-start | bytes 2985992 | tf_op jit(solution)/shard_map/ppermute | solution.py:158
  487.5 93.3 %collective-permute-start.89 = (bf16[432,1152]{1,0:T(8,128)(2,1)}, bf16[432,1152]{1,0:T(8,128)(2,1)}, u32[]{:S(2)}, u32[]{:S(2)}) collective-permute-start(bf16[432,1152]{1,0:T(8,128)(2,1)} %add_convert_fusion.11), channel_id=1, source_target_pairs={{8,0},{16,24},{9,1},{17,25},{10,2},{18,26},{11,3},{19,27},{12,4},{... | collective-permute-start | bytes 2985992 | tf_op jit(solution)/shard_map/ppermute | solution.py:158
  509.1 30.7 %collective-permute-start.67 = (bf16[4,144,864]{2,1,0:T(8,128)(2,1)}, bf16[4,144,864]{2,1,0:T(8,128)(2,1)}, u32[]{:S(2)}, u32[]{:S(2)}) collective-permute-start(bf16[4,144,864]{2,1,0:T(8,128)(2,1)} %add_convert_fusion.10), channel_id=1, source_target_pairs={{8,16},{16,8},{9,17},{17,9},{10,18},{18,10},{11,19},{19,11},{12,20... | collective-permute-start | bytes 2985992 | tf_op jit(solution)/shard_map/ppermute | solution.py:158
  527.8 39.4 %collective-permute-start.65 = (bf16[4,144,864]{2,1,0:T(8,128)(2,1)}, bf16[4,144,864]{2,1,0:T(8,128)(2,1)}, u32[]{:S(2)}, u32[]{:S(2)}) collective-permute-start(bf16[4,144,864]{2,1,0:T(8,128)(2,1)} %add_convert_fusion.9), channel_id=1, source_target_pairs={{8,16},{16,8},{9,17},{17,9},{10,18},{18,10},{11,19},{19,11},{12,20... | collective-permute-start | bytes 2985992 | tf_op jit(solution)/shard_map/ppermute | solution.py:158
  533.3 24.3 %collective-permute-start.66 = (bf16[4,144,864]{2,1,0:T(8,128)(2,1)S(1)}, bf16[4,144,864]{2,1,0:T(8,128)(2,1)S(1)}, u32[]{:S(2)}, u32[]{:S(2)}) collective-permute-start(bf16[4,144,864]{2,1,0:T(8,128)(2,1)S(1)} %slice.512), channel_id=1, source_target_pairs={{0,8},{24,16},{1,9},{25,17},{2,10},{26,18},{3,11},{27,19},{4,12},{... | collective-permute-start | bytes 2985992 | tf_op jit(solution)/shard_map/ppermute | solution.py:158
  557.9 14.1 %collective-permute-start.70 = (bf16[4,144,864]{2,1,0:T(8,128)(2,1)S(1)}, bf16[4,144,864]{2,1,0:T(8,128)(2,1)S(1)}, u32[]{:S(2)}, u32[]{:S(2)}) collective-permute-start(bf16[4,144,864]{2,1,0:T(8,128)(2,1)S(1)} %add_convert_fusion.7), channel_id=1, source_target_pairs={{8,16},{16,8},{9,17},{17,9},{10,18},{18,10},{11,19},{19,11},{12,20... | collective-permute-start | bytes 2985992 | tf_op jit(solution)/shard_map/ppermute | solution.py:158
  558.7 24.3 %collective-permute-start.75 = (f32[40,128]{1,0:T(8,128)S(1)}, f32[40,128]{1,0:T(8,128)S(1)}, u32[]{:S(2)}, u32[]{:S(2)}) collective-permute-start(f32[40,128]{1,0:T(8,128)S(1)} %bitcast.229), channel_id=1, source_target_pairs={{0,1},{1,0},{2,3},{3,2},{4,5},{5,4},{6,7},{7,6},{8,9},{9,8},{10,11... | collective-permute-start | bytes 61448 | tf_op jit(solution)/shard_map/ppermute | solution.py:59
  560.9 18.3 %collective-permute-start.69 = (bf16[2,144,864]{2,1,0:T(8,128)(2,1)S(1)}, bf16[2,144,864]{2,1,0:T(8,128)(2,1)S(1)}, u32[]{:S(2)}, u32[]{:S(2)}) collective-permute-start(bf16[2,144,864]{2,1,0:T(8,128)(2,1)S(1)} %get-tuple-element.254), channel_id=1, source_target_pairs={{0,8},{24,16},{1,9},{25,17},{2,10},{26,18},{3,11},{27,19},{4,12},{... | collective-permute-start | bytes 1493000 | tf_op jit(solution)/shard_map/ppermute | solution.py:158
  569.9 20.0 %collective-permute-start.68 = (bf16[2,144,864]{2,1,0:T(8,128)(2,1)}, bf16[2,144,864]{2,1,0:T(8,128)(2,1)}, u32[]{:S(2)}, u32[]{:S(2)}) collective-permute-start(bf16[2,144,864]{2,1,0:T(8,128)(2,1)} %get-tuple-element.256), channel_id=1, source_target_pairs={{0,8},{24,16},{1,9},{25,17},{2,10},{26,18},{3,11},{27,19},{4,12},{... | collective-permute-start | bytes 1493000 | tf_op jit(solution)/shard_map/ppermute | solution.py:158
  584.4 32.3 %collective-permute-start.83 = (bf16[4,144,864]{2,1,0:T(8,128)(2,1)S(1)}, bf16[4,144,864]{2,1,0:T(8,128)(2,1)}, u32[]{:S(2)}, u32[]{:S(2)}) collective-permute-start(bf16[4,144,864]{2,1,0:T(8,128)(2,1)S(1)} %add_convert_fusion.8.refs_0_), channel_id=1, source_target_pairs={{8,0},{16,24},{9,1},{17,25},{10,2},{18,26},{11,3},{19,27},{12,4},{... | collective-permute-start | bytes 2985992 | tf_op jit(solution)/shard_map/ppermute | solution.py:158
  585.7 53.1 %collective-permute-start.84 = (bf16[4,144,864]{2,1,0:T(8,128)(2,1)}, bf16[4,144,864]{2,1,0:T(8,128)(2,1)}, u32[]{:S(2)}, u32[]{:S(2)}) collective-permute-start(bf16[4,144,864]{2,1,0:T(8,128)(2,1)} %add_convert_fusion.6.refs_1_), channel_id=1, source_target_pairs={{8,0},{16,24},{9,1},{17,25},{10,2},{18,26},{11,3},{19,27},{12,4},{... | collective-permute-start | bytes 2985992 | tf_op jit(solution)/shard_map/ppermute | solution.py:158
  592.0 59.6 %collective-permute-start.74 = (bf16[2,144,864]{2,1,0:T(8,128)(2,1)}, bf16[2,144,864]{2,1,0:T(8,128)(2,1)}, u32[]{:S(2)}, u32[]{:S(2)}) collective-permute-start(bf16[2,144,864]{2,1,0:T(8,128)(2,1)} %add_convert_fusion.18), channel_id=1, source_target_pairs={{8,16},{16,8},{9,17},{17,9},{10,18},{18,10},{11,19},{19,11},{12,20... | collective-permute-start | bytes 1493000 | tf_op jit(solution)/shard_map/ppermute | solution.py:158
  593.4 17.8 %collective-permute-start.77 = (f32[40,128]{1,0:T(8,128)S(1)}, f32[40,128]{1,0:T(8,128)S(1)}, u32[]{:S(2)}, u32[]{:S(2)}) collective-permute-start(f32[40,128]{1,0:T(8,128)S(1)} %fusion.54), channel_id=1, source_target_pairs={{0,4},{1,5},{2,6},{3,7},{4,0},{5,1},{6,2},{7,3},{8,12},{9,13},{10,... | collective-permute-start | bytes 61448 | tf_op jit(solution)/shard_map/ppermute | solution.py:59
  594.8 59.4 %collective-permute-start.73 = (bf16[128,1152]{1,0:T(8,128)(2,1)}, bf16[128,1152]{1,0:T(8,128)(2,1)}, u32[]{:S(2)}, u32[]{:S(2)}) collective-permute-start(bf16[128,1152]{1,0:T(8,128)(2,1)} %reduce-scatter.5.cloned.1.call-done), channel_id=1, source_target_pairs={{0,8},{24,16},{1,9},{25,17},{2,10},{26,18},{3,11},{27,19},{4,12},{... | collective-permute-start | bytes 884744 | tf_op jit(solution)/shard_map/ppermute | solution.py:158
  611.3 66.9 %collective-permute-start.85 = (bf16[4,144,864]{2,1,0:T(8,128)(2,1)S(1)}, bf16[4,144,864]{2,1,0:T(8,128)(2,1)}, u32[]{:S(2)}, u32[]{:S(2)}) collective-permute-start(bf16[4,144,864]{2,1,0:T(8,128)(2,1)S(1)} %add_convert_fusion.5.refs_0_), channel_id=1, source_target_pairs={{8,0},{16,24},{9,1},{17,25},{10,2},{18,26},{11,3},{19,27},{12,4},{... | collective-permute-start | bytes 2985992 | tf_op jit(solution)/shard_map/ppermute | solution.py:158
  643.1 33.8 %collective-permute-start.86 = (bf16[2,144,864]{2,1,0:T(8,128)(2,1)S(1)}, bf16[2,144,864]{2,1,0:T(8,128)(2,1)S(1)}, u32[]{:S(2)}, u32[]{:S(2)}) collective-permute-start(bf16[2,144,864]{2,1,0:T(8,128)(2,1)S(1)} %add_convert_fusion.19.refs_1_), channel_id=1, source_target_pairs={{8,0},{16,24},{9,1},{17,25},{10,2},{18,26},{11,3},{19,27},{12,4},{... | collective-permute-start | bytes 1493000 | tf_op jit(solution)/shard_map/ppermute | solution.py:158
  647.0 26.1 %collective-permute-start.80 = (f32[40,128]{1,0:T(8,128)S(1)}, f32[40,128]{1,0:T(8,128)S(1)}, u32[]{:S(2)}, u32[]{:S(2)}) collective-permute-start(f32[40,128]{1,0:T(8,128)S(1)} %add.408), channel_id=1, source_target_pairs={{0,8},{24,16},{1,9},{25,17},{2,10},{26,18},{3,11},{27,19},{4,12},{... | collective-permute-start | bytes 61448 | tf_op jit(solution)/shard_map/ppermute | solution.py:158
  652.9 28.6 %collective-permute-start.87 = (bf16[2,144,864]{2,1,0:T(8,128)(2,1)S(1)}, bf16[2,144,864]{2,1,0:T(8,128)(2,1)S(1)}, u32[]{:S(2)}, u32[]{:S(2)}) collective-permute-start(bf16[2,144,864]{2,1,0:T(8,128)(2,1)S(1)} %add_convert_fusion.17.refs_2_), channel_id=1, source_target_pairs={{8,0},{16,24},{9,1},{17,25},{10,2},{18,26},{11,3},{19,27},{12,4},{... | collective-permute-start | bytes 1493000 | tf_op jit(solution)/shard_map/ppermute | solution.py:158
  673.0 14.8 %collective-permute-start.90 = (f32[40,128]{1,0:T(8,128)S(1)}, f32[40,128]{1,0:T(8,128)S(1)}, u32[]{:S(2)}, u32[]{:S(2)}) collective-permute-start(f32[40,128]{1,0:T(8,128)S(1)} %add.412), channel_id=1, source_target_pairs={{8,16},{16,8},{9,17},{17,9},{10,18},{18,10},{11,19},{19,11},{12,20... | collective-permute-start | bytes 61448 | tf_op jit(solution)/shard_map/ppermute | solution.py:158
  676.9 16.4 %collective-permute-start.82 = (bf16[128,1152]{1,0:T(8,128)(2,1)}, bf16[128,1152]{1,0:T(8,128)(2,1)S(1)}, u32[]{:S(2)}, u32[]{:S(2)}) collective-permute-start(bf16[128,1152]{1,0:T(8,128)(2,1)} %add_convert_fusion.21), channel_id=1, source_target_pairs={{8,0},{16,24},{9,1},{17,25},{10,2},{18,26},{11,3},{19,27},{12,4},{... | collective-permute-start | bytes 884744 | tf_op jit(solution)/shard_map/ppermute | solution.py:158
  (142 other events, 1581.7 us)
Sparse Core Ops, SparseCore 0:
  9.9 33.3 all-gather.2
  45.2 44.6 all-gather.4
  475.5 47.3 reduce-scatter.4
  527.2 48.0 reduce-scatter.6

commit v2 on v1

--- a/solution.py
+++ b/solution.py
@@ -178,14 +178,14 @@
 
 NT = (((1,), (1,)), ((), ()))
 TN = (((0,), (0,)), ((), ()))
-VMEM_LIMIT = 48 * 1024 * 1024
-
-
-def vmem_call(kernel, out_shape, **kwargs):
+MIB = 1024 * 1024
+
+
+def vmem_call(kernel, out_shape, limit=32, **kwargs):
     return pl.pallas_call(
         kernel,
         out_shape=out_shape,
-        compiler_params=pltpu.CompilerParams(vmem_limit_bytes=VMEM_LIMIT),
+        compiler_params=pltpu.CompilerParams(vmem_limit_bytes=limit * MIB),
         cost_estimate=pl.CostEstimate(flops=0, bytes_accessed=0, transcendentals=0),
         **kwargs,
     )
@@ -287,6 +287,7 @@
 def assemble(flag, totals, moveds, rows, columns):
     count = len(totals)
     share = totals[0].shape[2]
+    moveds = moveds or []
 
     def kernel(flag_ref, *refs):
         out_ref = refs[-1]
@@ -298,6 +299,10 @@
                     out_ref[:, at * share : (at + 1) * share] = part[k].astype(WIDE)
                     at += 1
 
+        if not moveds:
+            fill(refs[:count])
+            return
+
         @pl.when(flag_ref[0] == 1)
         def _():
             fill(refs[count : 2 * count])
@@ -309,7 +314,7 @@
     return vmem_call(
         kernel,
         jax.ShapeDtypeStruct((rows, columns), WIDE),
-        in_specs=[smem_spec()] + [whole_spec()] * (2 * count),
+        in_specs=[smem_spec()] + [whole_spec()] * (count + len(moveds)),
         out_specs=whole_spec(),
     )(flag, *totals, *moveds)
 
@@ -676,40 +681,16 @@
     )(normed, weight, cosine, sine, gain)
 
 
-def feed_steps(blocks):
-    tokens, width = blocks[0].shape
-    step = 256 if tokens % 256 == 0 else tokens
-    per_block = tokens // step
-
-    def spec(k):
-        return pl.BlockSpec(
-            (step, width), lambda i: (jnp.clip(i - k * per_block, 0, per_block - 1), 0)
-        )
-
-    return step, per_block, spec
-
-
-def in_block(k, per_block):
-    i = pl.program_id(0)
-    return (i >= k * per_block) & (i < (k + 1) * per_block)
-
-
-def feed_forward(blocks, gate_w, up_w, down_w):
-    width = blocks[0].shape[1]
+def feed_step(tokens):
+    return 256 if tokens % 256 == 0 else tokens
+
+
+def feed_forward(inner, gate_w, up_w, down_w):
+    tokens, width = inner.shape
     share = gate_w.shape[1]
-    step, per_block, spec = feed_steps(blocks)
-    count = len(blocks)
-    total = count * per_block * step
-
-    def kernel(gate_ref, up_ref, down_ref, *refs):
-        x_ref, slope_ref, value_ref, a_ref = refs[count : count + 4]
-        low_refs = refs[count + 4 :]
-        for k in range(count):
-
-            @pl.when(in_block(k, per_block))
-            def _(k=k):
-                x_ref[...] = refs[k][...]
-
+    step = feed_step(tokens)
+
+    def kernel(x_ref, gate_ref, up_ref, down_ref, slope_ref, value_ref, a_ref, low_ref):
         x = x_ref[...]
         g = jnp.dot(x, gate_ref[...], preferred_element_type=WIDE)
         u = jnp.dot(x, up_ref[...], preferred_element_type=WIDE)
@@ -718,44 +699,26 @@
         slope_ref[...] = (slope * u).astype(BF16)
         value_ref[...] = value.astype(BF16)
         a_ref[...] = active
-        low = jnp.dot(active, down_ref[...], preferred_element_type=WIDE).astype(BF16)
-        for k in range(count):
-
-            @pl.when(in_block(k, per_block))
-            def _(k=k):
-                low_refs[k][...] = low
+        low_ref[...] = jnp.dot(active, down_ref[...], preferred_element_type=WIDE).astype(BF16)
 
     each = lambda columns: pl.BlockSpec((step, columns), lambda i: (i, 0))
-    whole = lambda shape: pl.BlockSpec(shape, lambda i: (0, 0))
-    hidden = jax.ShapeDtypeStruct((total, share), BF16)
-    return vmem_call(
-        kernel,
-        (jax.ShapeDtypeStruct((total, width), BF16), hidden, hidden, hidden)
-        + tuple(jax.ShapeDtypeStruct(b.shape, BF16) for b in blocks),
-        grid=(total // step,),
-        in_specs=[whole((width, share)), whole((width, share)), whole((share, width))]
-        + [spec(k) for k in range(count)],
-        out_specs=(each(width), each(share), each(share), each(share))
-        + tuple(spec(k) for k in range(count)),
-    )(gate_w, up_w, down_w, *blocks)
-
-
-def feed_backward(blocks, slope, value, gate_w, up_w, down_w):
-    width = blocks[0].shape[1]
+    hidden = jax.ShapeDtypeStruct((tokens, share), BF16)
+    return vmem_call(
+        kernel,
+        (hidden, hidden, hidden, jax.ShapeDtypeStruct((tokens, width), BF16)),
+        limit=24,
+        grid=(tokens // step,),
+        in_specs=[each(width), whole_spec(), whole_spec(), whole_spec()],
+        out_specs=(each(share), each(share), each(share), each(width)),
+    )(inner, gate_w, up_w, down_w)
+
+
+def feed_backward(d_lowered, slope, value, gate_w, up_w, down_w):
+    tokens, width = d_lowered.shape
     share = gate_w.shape[1]
-    step, per_block, spec = feed_steps(blocks)
-    count = len(blocks)
-    total = count * per_block * step
-
-    def kernel(gate_ref, up_ref, down_ref, slope_ref, value_ref, *refs):
-        d_ref, dg_ref, du_ref = refs[count : count + 3]
-        dx_refs = refs[count + 3 :]
-        for k in range(count):
-
-            @pl.when(in_block(k, per_block))
-            def _(k=k):
-                d_ref[...] = refs[k][...]
-
+    step = feed_step(tokens)
+
+    def kernel(d_ref, slope_ref, value_ref, gate_ref, up_ref, down_ref, dg_ref, du_ref, dx_ref):
         d_active = lax.dot_general(d_ref[...], down_ref[...], NT, preferred_element_type=WIDE)
         d_gate = (d_active * slope_ref[...].astype(WIDE)).astype(BF16)
         d_up = (d_active * value_ref[...].astype(WIDE)).astype(BF16)
@@ -763,84 +726,154 @@
         du_ref[...] = d_up
         d_x = lax.dot_general(d_gate, gate_ref[...], NT, preferred_element_type=WIDE)
         d_x += lax.dot_general(d_up, up_ref[...], NT, preferred_element_type=WIDE)
-        d_x = d_x.astype(BF16)
-        for k in range(count):
-
-            @pl.when(in_block(k, per_block))
-            def _(k=k):
-                dx_refs[k][...] = d_x
+        dx_ref[...] = d_x.astype(BF16)
 
     each = lambda columns: pl.BlockSpec((step, columns), lambda i: (i, 0))
-    whole = lambda shape: pl.BlockSpec(shape, lambda i: (0, 0))
-    hidden = jax.ShapeDtypeStruct((total, share), BF16)
-    return vmem_call(
-        kernel,
-        (jax.ShapeDtypeStruct((total, width), BF16), hidden, hidden)
-        + tuple(jax.ShapeDtypeStruct(b.shape, BF16) for b in blocks),
-        grid=(total // step,),
+    hidden = jax.ShapeDtypeStruct((tokens, share), BF16)
+    return vmem_call(
+        kernel,
+        (hidden, hidden, jax.ShapeDtypeStruct((tokens, width), BF16)),
+        limit=24,
+        grid=(tokens // step,),
+        in_specs=[each(width), each(share), each(share), whole_spec(), whole_spec(), whole_spec()],
+        out_specs=(each(share), each(share), each(width)),
+    )(d_lowered, slope, value, gate_w, up_w, down_w)
+
+
+def weight_grad(lefts, rights):
+    rows = lefts[0].shape[1]
+    columns = rights[0].shape[1]
+    count = len(lefts)
+    size = 384
+
+    def kernel(*refs):
+        out_ref = refs[2 * count]
+        for at in range(0, rows, size):
+            lanes = slice(at, min(at + size, rows))
+            term = None
+            for k in range(count):
+                part = lax.dot_general(
+                    refs[k][:, lanes], refs[count + k][...], TN, preferred_element_type=WIDE
+                )
+                term = part if term is None else term + part
+            out_ref[lanes, :] = term.astype(BF16)
+
+    return vmem_call(
+        kernel,
+        jax.ShapeDtypeStruct((rows, columns), BF16),
+        limit=24,
+        in_specs=[whole_spec()] * (2 * count),
+        out_specs=whole_spec(),
+    )(*lefts, *rights)
+
+
+def blocks_grad(order, left_sets, right_sets, n):
+    rows = left_sets[0].shape[1]
+    part = rows // n
+    widths = [r.shape[1] for r in right_sets[0]]
+    per_row = len(widths)
+    count = len(left_sets)
+    blocks = n // 4
+
+    def kernel(order_ref, *refs):
+        lefts = refs[:count]
+        rights = refs[count : count + count * per_row]
+        outs = refs[count + count * per_row : -1]
+        held = refs[-1]
+        for d in range(n):
+            lanes = slice(d * part, (d + 1) * part)
+            at = 0
+            for j, size in enumerate(widths):
+                term = None
+                for k in range(count):
+                    product = lax.dot_general(
+                        lefts[k][:, lanes],
+                        rights[k * per_row + j][...],
+                        TN,
+                        preferred_element_type=WIDE,
+                    )
+                    term = product if term is None else term + product
+                held[order_ref[d], :, at : at + size] = term.astype(BF16)
+                at += size
+        for b, out in enumerate(outs):
+            out[...] = held[4 * b : 4 * b + 4]
+
+    flat = [r for rights in right_sets for r in rights]
+    shape = jax.ShapeDtypeStruct((4, part, sum(widths)), BF16)
+    return vmem_call(
+        kernel,
+        (shape,) * blocks,
+        limit=24,
+        in_specs=[smem_spec()] + [whole_spec()] * (count + len(flat)),
+        out_specs=(whole_spec(),) * blocks,
+        scratch_shapes=[pltpu.VMEM((n, part, sum(widths)), BF16)],
+    )(order, *left_sets, *flat)
+
+
+def close_keys(parts, raw, cosine, sine, gain):
+    slots, rows, count, both = parts[0].shape
+    size = both // 2
+    half = size // 2
+
+    def kernel(a_ref, b_ref, c_ref, raw_ref, cos_ref, sin_ref, gain_ref, *outs):
+        gain_values = gain_ref[...].astype(WIDE)
+        d_gain = jnp.zeros((1, size), WIDE)
+        for row in range(rows):
+            span = slice(row * count, (row + 1) * count)
+            e = (
+                a_ref[0, row].astype(WIDE) + b_ref[row].astype(WIDE) + c_ref[row].astype(WIDE)
+            )
+            cos, sin = cos_ref[span], sin_ref[span]
+            d_a, d_b = e[:, :half], e[:, half:size]
+            turned = jnp.concatenate([d_a * cos + d_b * sin, d_b * cos - d_a * sin], axis=-1)
+            u = raw_ref[span]
+            d_u, d_part = unit_back(u, unit(u, gain_values)[1], gain_values, turned)
+            d_gain += d_part
+            outs[row][:, :size] = d_u.astype(BF16)
+            outs[row][:, size:] = e[:, size:].astype(BF16)
+        outs[rows][...] = d_gain
+
+    return vmem_call(
+        kernel,
+        (jax.ShapeDtypeStruct((count, both), BF16),) * rows
+        + (jax.ShapeDtypeStruct((1, size), WIDE),),
+        grid=(1,),
         in_specs=[
-            whole((width, share)),
-            whole((width, share)),
-            whole((share, width)),
-            each(share),
-            each(share),
-        ]
-        + [spec(k) for k in range(count)],
-        out_specs=(each(width), each(share), each(share))
-        + tuple(spec(k) for k in range(count)),
-    )(gate_w, up_w, down_w, slope, value, *blocks)
-
-
-def weight_grad(lefts, rights, parts):
-    tokens, rows = lefts[0].shape
-    columns = rights[0].shape[1]
-    step = tokens // 2 if tokens % 32 == 0 else tokens
-    per_pair = tokens // step
-    count = len(lefts)
-    last = count * per_pair - 1
-
-    def kernel(*refs):
-        out_ref, acc = refs[2 * count :]
-        i = pl.program_id(0)
-        for k in range(count):
-
-            @pl.when(in_block(k, per_pair))
-            def _(k=k):
-                term = lax.dot_general(
-                    refs[k][...], refs[count + k][...], TN, preferred_element_type=WIDE
-                )
-                if k == 0:
-
-                    @pl.when(i == 0)
-                    def _():
-                        acc[...] = term
-
-                    @pl.when(i != 0)
-                    def _():
-                        acc[...] += term
-
-                else:
-                    acc[...] += term
-
-        @pl.when(i == last)
-        def _():
-            size = rows // parts
-            for p in range(parts):
-                out_ref[p] = acc[p * size : (p + 1) * size].astype(BF16)
-
-    def spec(k, width):
-        return pl.BlockSpec(
-            (step, width), lambda i: (jnp.clip(i - k * per_pair, 0, per_pair - 1), 0)
-        )
-
-    return vmem_call(
-        kernel,
-        jax.ShapeDtypeStruct((parts, rows // parts, columns), BF16),
-        grid=(last + 1,),
-        in_specs=[spec(k, rows) for k in range(count)] + [spec(k, columns) for k in range(count)],
-        out_specs=full_spec((parts, rows // parts, columns)),
-        scratch_shapes=[pltpu.VMEM((rows, columns), WIDE)],
-    )(*lefts, *rights)
+            pl.BlockSpec((1, rows, count, both), lambda i: (0, 0, 0, 0)),
+            full_spec((rows, count, both)),
+            full_spec((rows, count, both)),
+            full_spec(raw.shape),
+            full_spec(cosine.shape),
+            full_spec(sine.shape),
+            full_spec((1, size)),
+        ],
+        out_specs=(full_spec((count, both)),) * rows + (full_spec((1, size)),),
+    )(*parts, raw, cosine, sine, gain)
+
+
+def close_tokens(tokens, d_queries, d_kvs, query_w, kv_w, d_hiddens, gain):
+    rows, count, width = tokens.shape
+
+    def kernel(x_ref, q_ref, kv_ref, gain_ref, *refs):
+        out_ref, dg_ref = refs[3 * rows :]
+        g = gain_ref[...].astype(WIDE)
+        d_gain = jnp.zeros((1, width), WIDE)
+        for row in range(rows):
+            d_q, d_kv, d_hidden = refs[row], refs[rows + row], refs[2 * rows + row]
+            e = lax.dot_general(d_q[...], q_ref[...], NT, preferred_element_type=WIDE)
+            e += lax.dot_general(d_kv[...], kv_ref[...], NT, preferred_element_type=WIDE)
+            x = x_ref[row].astype(WIDE)
+            d_x, d_part = unit_back(x, unit(x, g)[1], g, e)
+            d_gain += d_part
+            out_ref[row] = (d_hidden[...] + d_x).astype(BF16)
+        dg_ref[...] = d_gain
+
+    return vmem_call(
+        kernel,
+        (jax.ShapeDtypeStruct(tokens.shape, BF16), jax.ShapeDtypeStruct((1, width), WIDE)),
+        in_specs=[whole_spec()] * (4 + 3 * rows),
+        out_specs=(whole_spec(), whole_spec()),
+    )(tokens, query_w, kv_w, gain, *d_queries, *d_kvs, *d_hiddens)
 
 
 def per_device(
@@ -868,27 +901,24 @@
     row_count, count_local, width = tokens.shape
     total = row_count * count_local
     head_width = gain_query.shape[0]
-    half_width = head_width // 2
     head_count = query_weight.shape[1] // head_width
     qw = head_count * head_width
     share = gate_weight.shape[1] // n
     span = count_local // 2
     codes = xor_layout(n)[3]
-    gain_row = {
-        "query": gain_query.reshape(1, -1),
-        "key": gain_key.reshape(1, -1),
-        "out": gain_attended.reshape(1, -1),
-        "feed": gain_feed.reshape(1, -1),
-        "result": gain_result.reshape(1, -1),
-    }
-    scale_input = gain_input.astype(WIDE)
-    scale_key = gain_key.astype(WIDE)
-
     kv_weights = Gather(jnp.concatenate([key_weight, value_weight], axis=1), n)
     query_full = lax.all_gather(query_weight, "ctx", axis=0, tiled=True)
     even_flag = ((my_dp % 2) == 0).astype(jnp.int32).reshape(1)
     pieces = spread_pieces(even_flag, gate_weight, up_weight, n)
     spread = lax.all_to_all(pieces, "ctx", 0, 0)
+    gain_row = {
+        "input": after(gain_input, pieces).reshape(1, -1),
+        "query": after(gain_query, pieces).reshape(1, -1),
+        "key": after(gain_key, pieces).reshape(1, -1),
+        "out": after(gain_attended, pieces).reshape(1, -1),
+        "feed": after(gain_feed, pieces).reshape(1, -1),
+        "result": after(gain_result, pieces).reshape(1, -1),
+    }
 
     below = jnp.stack(
         [jnp.sum((segment_ids < s).astype(jnp.int32), axis=1) for s in range(5)], axis=1
@@ -911,29 +941,29 @@
     cosine = jnp.concatenate([jnp.cos(angles)] * row_count, axis=0)
     sine = jnp.concatenate([jnp.sin(angles)] * row_count, axis=0)
 
-    row_tokens = tokens.reshape(total, width).astype(WIDE)
-    normed_wide, normed_pull = jax.vjp(rms_norm, row_tokens, scale_input)
-    normed = normed_wide.astype(BF16)
+    normed_rows = rms_norm(tokens.astype(WIDE), gain_input.astype(WIDE)).astype(BF16)
+    normed = normed_rows.reshape(total, width)
     order_codes = me ^ jnp.arange(n, dtype=jnp.int32)
     order = sum(jnp.where(order_codes == c, k, 0) for k, c in enumerate(codes)).astype(jnp.int32)
-    kv_weights.mid(pieces, normed).near()
+    start_columns = [starts[row].reshape(-1, 1) for row in range(row_count)]
+    kv_weights.mid(pieces).near()
     kv_local, key_raw, kv_full = project_kv(
-        order, normed, kv_weights.blocks, cosine, sine, gain_row["key"], row_count
+        order, after(normed, spread), kv_weights.blocks, cosine, sine, gain_row["key"], row_count
     )
     kv_gather = Gather(kv_local, n)
     out_full = lax.all_gather(after(out_weight, kv_local), "ctx", axis=0, tiled=True)
     queries, query_raw = project_q(
         after(normed, kv_local), query_full, cosine, sine, gain_row["query"], head_count
     )
-    kv_gather.mid(queries)
+    kv_gather.mid(queries, *start_columns, *gain_row.values(), key_places, place_column)
     swapped = lax.ppermute(
-        after(spread, kv_gather.a, kv_gather.b), "dp", [(i, i ^ 1) for i in range(n_dp)]
+        after(spread, kv_local), "dp", [(i, i ^ 1) for i in range(n_dp)]
     )
     kv_gather.near()
     kv_blocks = kv_gather.blocks
 
     def before_feed(row, *earlier):
-        r = {"start": starts[row].reshape(-1, 1)}
+        r = {"start": start_columns[row]}
         names = ("attended", "log", "projected", "hidden", "inner_local")
         outs = attend_forward(
             row,
@@ -951,17 +981,26 @@
         r.update(zip(names, outs))
         return r
 
-    def feed_piece(r, blocks, *earlier):
-        blocks = [after(blocks[0], *earlier)] + blocks[1:]
-        outs = feed_forward(blocks, gate_mine, up_mine, down_weight)
-        r["inner"], r["slope"], r["value"], r["active"] = outs[:4]
-        return [x.reshape(4, count_local, width) for x in outs[4:]]
-
-    def back_piece(r, blocks, *earlier):
-        blocks = [after(blocks[0], *earlier)] + blocks[1:]
-        outs = feed_backward(blocks, r["slope"], r["value"], gate_mine, up_mine, down_weight)
-        r["d_lowered"], r["d_gate"], r["d_up"] = outs[:3]
-        return [x.reshape(4, count_local, width) for x in outs[3:]]
+    def feed_piece(r, block, *earlier):
+        outs = feed_forward(after(block, *earlier), gate_mine, up_mine, down_weight)
+        for name, out in zip(("inner", "slope", "value", "active"), (block,) + tuple(outs[:3])):
+            r.setdefault(name, []).append(out)
+        return outs[3].reshape(4, count_local, width)
+
+    def back_piece(r, block, *earlier):
+        k = len(r.setdefault("d_lowered", []))
+        outs = feed_backward(
+            after(block, *earlier), r["slope"][k], r["value"][k], gate_mine, up_mine, down_weight
+        )
+        for name, out in zip(("d_lowered", "d_gate", "d_up"), (block,) + tuple(outs[:2])):
+            r.setdefault(name, []).append(out)
+        return outs[2].reshape(4, count_local, width)
+
+    def pieces_of(piece, r, blocks, *earlier):
+        outs = []
+        for block in blocks:
+            outs.append(piece(r, block, *earlier, *outs[-1:]))
+        return outs
 
     def result_piece(row, r, parts):
         r["result"], d_lowered, r["grad_result_gain"] = close_row(
@@ -998,14 +1037,18 @@
     gate_mine = gate_mine.reshape(width, share)
     up_mine = up_mine.reshape(width, share)
     g0.near(gate_mine)
-    g1.mid(g0.blocks[0])
-    low_0 = feed_piece(r0, g0.flat(), g1.a)
+    blocks_0 = g0.flat()
+    low_0 = [feed_piece(r0, blocks_0[0])]
+    g1.mid(low_0[0])
+    low_0 += pieces_of(feed_piece, r0, blocks_0[1:], low_0[0], g1.a)
     s0 = Scatter(low_0, n)
-    g1.near(low_0[0])
-    s0.mid(g1.blocks[0])
-    low_1 = feed_piece(r1, g1.flat(), s0.sums)
+    g1.near(low_0[-1])
+    blocks_1 = g1.flat()
+    low_1 = [feed_piece(r1, blocks_1[0])]
+    s0.mid(low_1[0])
+    low_1 += pieces_of(feed_piece, r1, blocks_1[1:], low_1[0], s0.sums)
     s1 = Scatter(low_1, n)
-    s0.far(low_1[0])
+    s0.far(low_1[-1])
     s1.mid(*s0.sent)
     d_low_0 = result_piece(0, r0, s0.finish(s1.sums))
     h0 = Gather(d_low_0, n)
@@ -1014,140 +1057,175 @@
     d_low_1 = result_piece(1, r1, s1.finish(h0.a))
     h1 = Gather(d_low_1, n)
     h0.near(d_low_1)
-    h1.mid(h0.blocks[0])
-    d_in_0 = back_piece(r0, h0.flat(), h1.a)
+    blocks_0 = h0.flat()
+    d_in_0 = [back_piece(r0, blocks_0[0])]
+    h1.mid(d_in_0[0])
+    d_in_0 += pieces_of(back_piece, r0, blocks_0[1:], d_in_0[0], h1.a)
     s0 = Scatter(d_in_0, n)
-    h1.near(d_in_0[0])
-    s0.mid(h1.blocks[0])
-    d_in_1 = back_piece(r1, h1.flat(), s0.sums)
+    h1.near(d_in_0[-1])
+    blocks_1 = h1.flat()
+    d_in_1 = [back_piece(r1, blocks_1[0])]
+    s0.mid(d_in_1[0])
+    rows = (r0, r1)
+
+    def over_rows(left, right, *earlier):
+        lefts, rights = r0[left] + r1[left], r0[right] + r1[right]
+        return weight_grad([after(lefts[0], *earlier)] + lefts[1:], rights)
+
+    grad_down = weight_grad(
+        [after(r0["active"][0], s0.sums)] + r0["active"][1:] + r1["active"],
+        r0["d_lowered"] + blocks_1,
+    )
+    def begin(part, *earlier):
+        line = Line(after(part, *earlier), n_dp)
+        clock[:] = [line.total]
+        return line
+
+    def land(line):
+        line.moved = after(line.moved, *clock)
+        clock[:] = [line.moved]
+
+    def step(line, *earlier):
+        if line.at < len(line.steps) - 1:
+            line.step(*clock, *earlier)
+            clock[:] = [line.total]
+
+    def halves(x):
+        half = x.shape[0] // 2
+        return [x[:half], x[half:]]
+
+    def exchange(grad):
+        return lax.all_to_all(grad.reshape(n, width // n, share), "ctx", 0, 0)
+
+    clock = [grad_down]
+    summed_down = lax.psum(grad_down, "dp")
+    d_in_1 += pieces_of(back_piece, r1, blocks_1[1:], *clock)
     s1 = Scatter(d_in_1, n)
-    s0.far(d_in_1[0])
-    rows = (r0, r1)
-
-    def over_rows(left, right, parts, *earlier):
-        return weight_grad(
-            [after(r0[left], *earlier), r1[left]], [r0[right], r1[right]], parts
-        )
-
-    def exchange(grad):
-        return lax.all_to_all(grad, "ctx", 0, 0)
-
-    down_pieces = over_rows("active", "d_lowered", 2, *s0.sent)
-    d0, d1 = [Line(x, n_dp) for x in (down_pieces[0], down_pieces[1])]
-    s1.mid(d0.total, d1.total)
-    grad_gate = over_rows("inner", "d_gate", n, s1.sums)
-    s1.far(grad_gate)
-    gate_pieces = exchange(after(grad_gate, *s1.sent))
-    attend_back(0, r0, s0.finish(*s1.sent))
-    d0.step(r0["d_kv"][0])
-    grad_up = over_rows("inner", "d_up", n, d0.total)
-    d1.step(grad_up)
-    attend_back(1, r1, s1.finish(d1.total))
+    s0.far(d_in_1[-1])
+    grad_gate = over_rows("inner", "d_gate", *s0.sent)
+    gate_pieces = exchange(grad_gate)
+    grad_up = over_rows("inner", "d_up", grad_gate)
+    s1.mid(grad_up)
+    clock[:] = [s1.sums]
+    attend_back(0, r0, s0.finish(*clock))
+    s1.far(r0["d_kv"][0])
+    gate_halves = halves(gate_pieces)
+    gl0 = begin(gate_halves[0], *s1.sent)
+    gl1 = begin(gate_halves[1], *clock)
+    up_pieces = exchange(after(grad_up, *clock))
+    attend_back(1, r1, s1.finish(summed_down, *clock))
+    clock[:] = [r1["d_kv"][0]]
+    step(gl0)
     kv_scatter = Scatter(
         [jnp.stack([a, b], axis=1) for a, b in zip(r0["d_kv"], r1["d_kv"])], n
     )
-    d0.step(kv_scatter.blocks[-1])
-    up_pieces = exchange(after(grad_up, gate_pieces, d0.total))
-    half = n // 2
-    g_lines = [Line(after(gate_pieces[:half], d0.total), n_dp)]
+    clock[:] = [gl0.total, *kv_scatter.blocks[-1:]]
     grad_out = (
-        t_dot(after(r0["attended"], g_lines[0].total), r0["d_projected"])
+        t_dot(after(r0["attended"], *clock), r0["d_projected"])
         + t_dot(r1["attended"], r1["d_projected"])
     ).astype(BF16)
     part_out = lax.psum_scatter(grad_out, "ctx", scatter_dimension=0, tiled=True)
+    def total_of(parts):
+        return (
+            parts[0][0].astype(WIDE) + parts[1].astype(WIDE) + parts[2].astype(WIDE)
+        ).astype(BF16)
+
+    def last(line):
+        line.moved = after(line.moved, *clock)
+        total = line.finish().astype(WIDE)
+        clock[:] = [total]
+        return total
+
+    def side_by_side(lines):
+        ends = lines[0].steps[-1][2]
+        mine = (my_dp == ends[0]) | (my_dp == ends[1]) if ends else my_dp < 0
+        total = assemble(
+            mine.astype(jnp.int32).reshape(1),
+            [line.total for line in lines],
+            [after(line.moved, *clock) for line in lines],
+            width // n,
+            n * share,
+        )
+        clock[:] = [total]
+        return total
+
     kv_scatter.mid(grad_out)
-    d1.step(kv_scatter.sums)
-    g_lines.append(Line(after(gate_pieces[half:], d1.total), n_dp))
-    d_query_raw = jnp.concatenate([r["d_query_raw"] for r in rows], axis=0)
-    grad_q = t_dot(after(normed, g_lines[1].total), d_query_raw).astype(BF16)
-    kv_scatter.far(grad_q)
-    d_normed_q = dot_t(after(d_query_raw, *kv_scatter.sent), query_full)
-    g_lines[0].step(d_normed_q)
-    d_kv_parts = kv_scatter.finish(g_lines[0].total)
-    d_kv = (
-        d_kv_parts[0][0].astype(WIDE) + d_kv_parts[1].astype(WIDE) + d_kv_parts[2].astype(WIDE)
-    ).reshape(total, 2 * head_width)
-
-    def key_shape(raw_rows, gain_values):
-        unturned = rms_norm(raw_rows, gain_values)
-        a, b = unturned[:, :half_width], unturned[:, half_width:]
-        return jnp.concatenate([a * cosine - b * sine, b * cosine + a * sine], axis=1)
-
-    key_pull = jax.vjp(key_shape, key_raw, scale_key)[1]
-    d_key_raw, grad_key_gain = key_pull(d_kv[:, :head_width])
-    d_kv_raw = jnp.concatenate([d_key_raw, d_kv[:, head_width:]], axis=1).astype(BF16)
-    grad_kv = t_dot(normed, d_kv_raw).astype(BF16)
-    grad_qkv = jnp.concatenate([grad_q, grad_kv], axis=1)
-    part_qkv = lax.psum_scatter(grad_qkv, "ctx", scatter_dimension=0, tiled=True)
-    g_lines[1].step(grad_qkv)
-    quarter = max(n // 4, 1)
-    cuts = [(0, half), (half, half + quarter), (half + quarter, n)]
-    u_lines = [Line(after(up_pieces[:half], g_lines[1].total), n_dp)]
-    d_normed = d_normed_q + dot_t(after(d_kv_raw, g_lines[1].total), kv_full)
-    d_tokens_part, grad_input_gain = normed_pull(d_normed)
-    d_hidden = jnp.concatenate([r["d_hidden"] for r in rows], axis=0)
-    tokens_grad = (d_hidden + d_tokens_part).astype(BF16)
+    up_halves = halves(up_pieces)
+    u0 = begin(up_halves[0], kv_scatter.sums)
+    kv_scatter.far(*clock)
+    clock[:] = [*kv_scatter.sent]
+    step(gl1)
+    *d_kvs, grad_key_gain = close_keys(
+        kv_scatter.finish(*clock), key_raw, cosine, sine, gain_row["key"]
+    )
+    clock[:] = [d_kvs[0]]
+    step(gl0)
+    grad_qkv = blocks_grad(
+        order,
+        [
+            after(normed[row * count_local : (row + 1) * count_local], *clock)
+            for row in range(row_count)
+        ],
+        [[r["d_query_raw"], d_kv] for r, d_kv in zip(rows, d_kvs)],
+        n,
+    )
+    qkv_scatter = Scatter(grad_qkv, n)
+    clock[:] = [grad_qkv[0]]
+    step(u0)
+    u1 = begin(up_halves[1], *clock)
+    step(gl1)
+    qkv_scatter.mid(*clock)
+    clock[:] = [qkv_scatter.sums]
+    land(gl0)
+    tokens_grad, grad_input_gain = close_tokens(
+        tokens,
+        [after(r["d_query_raw"], *clock) for r in rows],
+        d_kvs,
+        query_full,
+        kv_full,
+        [r["d_hidden"] for r in rows],
+        gain_row["input"],
+    )
+    qkv_scatter.far(tokens_grad)
     gains = jnp.concatenate(
         [
             grad_input_gain,
-            sum(r["d_gain"] for r in rows).reshape(-1),
+            sum(r["d_gain"] for r in rows),
             grad_key_gain,
-            sum(r["grad_out_gain"] for r in rows).reshape(-1),
-            sum(r["grad_feed_gain"] for r in rows).reshape(-1),
-            sum(r["grad_result_gain"] for r in rows).reshape(-1),
-        ]
+            sum(r["grad_out_gain"] for r in rows),
+            sum(r["grad_feed_gain"] for r in rows),
+            sum(r["grad_result_gain"] for r in rows),
+        ],
+        axis=1,
     ).reshape(-1, 128)
+    clock[:] = [*qkv_scatter.sent]
+    step(u1)
+    step(u0)
+    part_qkv = total_of(qkv_scatter.finish(*clock))
+    clock[:] = [part_qkv]
+    qkv_line = begin(part_qkv, *clock)
+    land(gl1)
+    out_line = begin(part_out, *clock)
     code = 1
+    gains = after(gains, *clock)
     while code < n:
         gains = gains + xor_permute(gains, n, code)
         code *= 2
-    clock = [tokens_grad]
-
-    def step(line):
-        if line.at < len(line.steps) - 1:
-            line.step(*clock)
-            clock[:] = [line.total]
-
-    def begin(part):
-        line = Line(after(part, *clock), n_dp)
-        clock[:] = [line.total]
-        return line
-
-    step(g_lines[0])
-    step(u_lines[0])
-    u_lines.append(begin(up_pieces[cuts[1][0] : cuts[1][1]]))
-    step(g_lines[1])
-    u_lines.append(begin(up_pieces[cuts[2][0] : cuts[2][1]]))
-    step(u_lines[0])
-    step(u_lines[1])
-    out_line = begin(part_out)
-    step(u_lines[1])
-    step(u_lines[2])
-    qkv_line = begin(part_qkv)
-    gain_line = begin(gains)
-    step(u_lines[2])
-    tail = [out_line, qkv_line, gain_line]
+    clock[:] = [gains]
+    gain_line = begin(gains, *clock)
+    step(u1)
+    land(u0)
+    step(qkv_line)
+    step(out_line)
+    step(gain_line)
     for _ in range(n_dp):
-        for line in [d0, d1] + g_lines + u_lines + tail:
+        for line in (gl0, gl1, u0, u1, qkv_line, out_line, gain_line):
             step(line)
-
-    def side_by_side(lines):
-        ends = lines[0].steps[-1][2]
-        mine = (my_dp == ends[0]) | (my_dp == ends[1]) if ends else my_dp < 0
-        return assemble(
-            mine.astype(jnp.int32).reshape(1),
-            [line.total for line in lines],
-            [line.moved for line in lines],
-            width // n,
-            n * share,
-        )
-
-    summed_down = jnp.concatenate([d0.finish(), d1.finish()], axis=0).astype(WIDE)
-    summed_gate = side_by_side(g_lines)
-    summed_up = side_by_side(u_lines)
-    summed_out = out_line.finish().astype(WIDE)
-    summed_qkv = qkv_line.finish().astype(WIDE)
-    gains = gain_line.finish().reshape(-1)
+    summed_gate = side_by_side([gl0, gl1])
+    summed_up = side_by_side([u0, u1])
+    summed_out = last(out_line)
+    summed_qkv = last(qkv_line)
+    gains = last(gain_line).reshape(-1)
     sizes = [width, head_width, head_width, width, width, width]
     gain_grads = []
     start = 0
@@ -1156,14 +1234,14 @@
         start += size
     return (
         jnp.stack([r["result"] for r in rows]),
-        tokens_grad.reshape(row_count, count_local, width),
+        tokens_grad,
         summed_qkv[:, :qw],
         summed_qkv[:, qw : qw + head_width],
         summed_qkv[:, qw + head_width :],
         summed_out,
         summed_gate,
         summed_up,
-        summed_down,
+        summed_down.astype(WIDE),
         *gain_grads,
     )
 

time: 721 us -> 647 us (0.90)
  Pallas kernels: 170 us -> 137 us
  other arithmetic: 64.5 us -> 46.6 us
  local copies, waits for them, and re-layouts: 71.7 us -> 89.3 us
  starting transfers between devices: 139 us -> 123 us
  waiting for transfers between devices: 239 us -> 226 us
  matrix products: 14.6 us -> 3.21 us
    unnamed x225 -> x355, local copies, waits for them, and re-layouts: 43.8 us -> 74.4 us
    ppermute x30 -> x21, starting transfers between devices: 75.7 us -> 46 us  [send(): self.moved = lax.ppermute(self.total, 'dp', self.steps[self.at][1])]
    ppermute x30 -> x21, waiting for transfers between devices: 73.4 us -> 45.4 us  [send(): self.moved = lax.ppermute(self.total, 'dp', self.steps[self.at][1])]
    pallas_call x7 -> x14, Pallas kernels: 112 us -> 89.4 us  [the longest x4 28.9 us: feed_backward(): vmem_call(kernel, (hidden, hidden, jax.ShapeDtypeStruct((tokens, width),...]
    ppermute x61 -> x66, starting transfers between devices: 48.2 us -> 61.3 us  [xor_permute(): return lax.ppermute(x, 'ctx', [(i, i ^ code) for i in range(axis_size)])]
    ppermute x1, waiting for transfers between devices: 2.5 us -> 15.2 us  [per_device(): lax.ppermute(after(spread, kv_local), 'dp', [(i, i ^ 1) for i in range(n_...]
    convert_element_type x18 -> x12, other arithmetic: 30.1 us -> 18 us  [step(): self.total = total.astype(self.total.dtype)]
    all_to_all x2, waiting for transfers between devices: 0.07 us -> 9.07 us  [exchange(): return lax.all_to_all(grad.reshape(n, width // n, share), 'ctx', 0, 0)]
  transfers between devices with their start and end apart: 99 -> 95, of which waited for: 43 -> 51; matrix products, arithmetic and copies ran while one was open for 16% -> 9% of each run, Pallas kernels for 16% -> 14%
where the time goes in v2:
time: 647 us; the launch traced here: 641 us
  waiting for transfers between devices  226 us (35%)
  Pallas kernels  137 us (21%)
  starting transfers between devices  123 us (19%)
  local copies, waits for them, and re-layouts  89.3 us (14%)
  other arithmetic  46.6 us (7%)
  between operations  16.5 us (3%)
    ppermute x66, waiting for transfers between devices, xor_permute(): return lax.ppermute(x, 'ctx', [(i, i ^ code) for i in range(axis_size)])  154 us
    unnamed x355, local copies, waits for them, and re-layouts  74.4 us
    ppermute x66, starting transfers between devices, xor_permute(): return lax.ppermute(x, 'ctx', [(i, i ^ code) for i in range(axis_size)])  61.3 us
    ppermute x21, starting transfers between devices, send(): self.moved = lax.ppermute(self.total, 'dp', self.steps[self.at][1])  46 us
    ppermute x21, waiting for transfers between devices, send(): self.moved = lax.ppermute(self.total, 'dp', self.steps[self.at][1])  45.4 us
    pallas_call x4, Pallas kernels, feed_backward(): vmem_call(kernel, (hidden, hidden, jax.ShapeDtypeStruct((tokens, width),...  28.9 us
    pallas_call x4, Pallas kernels, feed_forward(): vmem_call(kernel, (hidden, hidden, hidden, jax.ShapeDtypeStruct((tokens,...  27 us
    pallas_call x3, Pallas kernels, weight_grad(): vmem_call(kernel, jax.ShapeDtypeStruct((rows, columns), BF16), limit=24,...  23.9 us
  transfers between devices with their start and end apart: 95, of which 51 were waited for; matrix products, arithmetic and copies ran while one was open for 9% of the time, Pallas kernels for 14%

profile of v2, /device:TPU:0, one launch (start us, length us, event | category | flops | bytes accessed | tf_op | source)
XLA Modules:
  0.0 641.1 jit_solution(14483780833920796473)
XLA Ops:
  9.7 2.9 collective-permute-start
  19.1 4.5 all-to-all-start
  28.1 28.7 %collective-permute-done.2.d1_ref = bf16[72,512]{1,0:T(8,128)(2,1)S(1)} collective-permute-done((bf16[72,512]{1,0:T(8,128)(2,1)S(1)}, bf16[72,512]{1,0:T(8,128)(2,1)S(1)}, u32[]{:S(2)}, u32[]{:S(2)}) %collective-permute-start.2) | collective-permute-done | bytes 73760 | tf_op jit(solution)/shard_map/ppermute | solution.py:59
  65.0 2.2 collective-permute-done.6
  73.1 10.6 %collective-permute-done.9.b_ref = bf16[2,192,512]{2,1,0:T(8,128)(2,1)S(1)} collective-permute-done((bf16[2,192,512]{2,1,0:T(8,128)(2,1)S(1)}, bf16[2,192,512]{2,1,0:T(8,128)(2,1)S(1)}, u32[]{:S(2)}, u32[]{:S(2)}) %collective-permute-start.9) | collective-permute-done | bytes 393248 | tf_op jit(solution)/shard_map/ppermute | solution.py:59
  89.1 5.9 collective-permute-done.11.d2_ref
  104.2 5.3 shard_map.276
  118.9 4.5 shard_map.277
  129.3 15.2 %collective-permute-done.16.second_ref = bf16[8,144,864]{2,1,0:T(8,128)(2,1)} collective-permute-done((bf16[8,144,864]{2,1,0:T(8,128)(2,1)}, bf16[8,144,864]{2,1,0:T(8,128)(2,1)}, u32[]{:S(2)}, u32[]{:S(2)}) %collective-permute-start.16) | collective-permute-done | bytes 1990688 | tf_op jit(solution)/shard_map/ppermute | solution.py:959
  144.5 5.1 shard_map.278
  149.7 2.2 shard_map.279
  153.5 6.7 %shard_map.280 = (bf16[768,864]{1,0:T(8,128)(2,1)S(1)}, bf16[768,864]{1,0:T(8,128)(2,1)S(1)}, bf16[768,864]{1,0:T(8,128)(2,1)S(1)}, bf16[768,1152]{1,0:T(8,128)(2,1)S(1)}) custom-call(bf16[768,1152]{1,0:T(8,128)(2,1)S(1)} %bitcast.189, bf16[1152,864]{1,0:T(8,128)(2,1)S(1)} %bitcast.173, bf16[1152,864]{1,0:T(8,128)(2,1)S(1)} %bitcast.181, ...), custom_call_target="tpu_custom_call" | custom-call | tf_op jit(solution)/shard_map/pallas_call | solution.py:706
  160.2 4.3 collective-permute-done.19.a_ref
  164.5 6.6 %shard_map.281 = (bf16[768,864]{1,0:T(8,128)(2,1)S(1)}, bf16[768,864]{1,0:T(8,128)(2,1)S(1)}, bf16[768,864]{1,0:T(8,128)(2,1)S(1)}, bf16[768,1152]{1,0:T(8,128)(2,1)S(1)}) custom-call(bf16[768,1152]{1,0:T(8,128)(2,1)S(1)} %bitcast.195, bf16[1152,864]{1,0:T(8,128)(2,1)S(1)} %bitcast.174, bf16[1152,864]{1,0:T(8,128)(2,1)S(1)} %bitcast.182, ...), custom_call_target="tpu_custom_call" | custom-call | tf_op jit(solution)/shard_map/pallas_call | solution.py:706
  173.4 10.9 %collective-permute-done.21.b_ref = bf16[192,1152]{1,0:T(8,128)(2,1)S(1)} collective-permute-done((bf16[192,1152]{1,0:T(8,128)(2,1)S(1)}, bf16[192,1152]{1,0:T(8,128)(2,1)S(1)}, u32[]{:S(2)}, u32[]{:S(2)}) %collective-permute-start.21) | collective-permute-done | bytes 442400 | tf_op jit(solution)/shard_map/ppermute | solution.py:59
  185.8 2.7 collective-permute-done.22.d1_ref
  188.6 2.3 collective-permute-done.23.d2_ref
  191.1 6.7 %shard_map.283 = (bf16[768,864]{1,0:T(8,128)(2,1)S(1)}, bf16[768,864]{1,0:T(8,128)(2,1)S(1)}, bf16[768,864]{1,0:T(8,128)(2,1)S(1)}, bf16[768,1152]{1,0:T(8,128)(2,1)S(1)}) custom-call(bf16[768,1152]{1,0:T(8,128)(2,1)S(1)} %bitcast.192, bf16[1152,864]{1,0:T(8,128)(2,1)S(1)} %bitcast.175, bf16[1152,864]{1,0:T(8,128)(2,1)S(1)} %bitcast.183, ...), custom_call_target="tpu_custom_call" | custom-call | tf_op jit(solution)/shard_map/pallas_call | solution.py:706
  198.4 7.0 %shard_map.284 = (bf16[768,864]{1,0:T(8,128)(2,1)S(1)}, bf16[768,864]{1,0:T(8,128)(2,1)S(1)}, bf16[768,864]{1,0:T(8,128)(2,1)S(1)}, bf16[768,1152]{1,0:T(8,128)(2,1)S(1)}) custom-call(bf16[768,1152]{1,0:T(8,128)(2,1)S(1)} %bitcast.198, bf16[1152,864]{1,0:T(8,128)(2,1)S(1)} %bitcast.176, bf16[1152,864]{1,0:T(8,128)(2,1)S(1)} %bitcast.184, ...), custom_call_target="tpu_custom_call" | custom-call | tf_op jit(solution)/shard_map/pallas_call | solution.py:706
  208.1 5.3 collective-permute-done.28
  219.7 8.3 %collective-permute-done.25.b_ref = bf16[192,1152]{1,0:T(8,128)(2,1)S(1)} collective-permute-done((bf16[192,1152]{1,0:T(8,128)(2,1)S(1)}, bf16[192,1152]{1,0:T(8,128)(2,1)S(1)}, u32[]{:S(2)}, u32[]{:S(2)}) %collective-permute-start.25) | collective-permute-done | bytes 442400 | tf_op jit(solution)/shard_map/ppermute | solution.py:59
  235.7 6.8 %collective-permute-done.32.a_ref = bf16[192,1152]{1,0:T(8,128)(2,1)S(1)} collective-permute-done((bf16[192,1152]{1,0:T(8,128)(2,1)S(1)}, bf16[192,1152]{1,0:T(8,128)(2,1)S(1)}, u32[]{:S(2)}, u32[]{:S(2)}) %collective-permute-start.32) | collective-permute-done | bytes 442400 | tf_op jit(solution)/shard_map/ppermute | solution.py:59
  244.8 7.1 %collective-permute-done.31.b_ref = bf16[192,1152]{1,0:T(8,128)(2,1)S(1)} collective-permute-done((bf16[192,1152]{1,0:T(8,128)(2,1)S(1)}, bf16[192,1152]{1,0:T(8,128)(2,1)S(1)}, u32[]{:S(2)}, u32[]{:S(2)}) %collective-permute-start.31) | collective-permute-done | bytes 442400 | tf_op jit(solution)/shard_map/ppermute | solution.py:59
  256.4 7.0 %shard_map.288 = (bf16[768,864]{1,0:T(8,128)(2,1)S(1)}, bf16[768,864]{1,0:T(8,128)(2,1)S(1)}, bf16[768,1152]{1,0:T(8,128)(2,1)S(1)}) custom-call(bf16[768,1152]{1,0:T(8,128)(2,1)S(1)} %bitcast.201, bf16[768,864]{1,0:T(8,128)(2,1)S(1)} %get-tuple-element.217.slope_ref, bf16[768,864]{1,0:T(8,128)(2,1)S(1)} %get-tuple-element.218.value_ref, ...), custom_call_target="tpu_custom_call" | custom-call | tf_op jit(solution)/shard_map/pallas_call | solution.py:733
  264.5 3.0 collective-permute-done.39.a_ref
  267.5 7.0 %shard_map.289 = (bf16[768,864]{1,0:T(8,128)(2,1)S(1)}, bf16[768,864]{1,0:T(8,128)(2,1)S(1)}, bf16[768,1152]{1,0:T(8,128)(2,1)S(1)}) custom-call(bf16[768,1152]{1,0:T(8,128)(2,1)S(1)} %bitcast.208, bf16[768,864]{1,0:T(8,128)(2,1)S(1)} %get-tuple-element.221.slope_ref, bf16[768,864]{1,0:T(8,128)(2,1)S(1)} %get-tuple-element.222.value_ref, ...), custom_call_target="tpu_custom_call" | custom-call | tf_op jit(solution)/shard_map/pallas_call | solution.py:733
  278.8 10.9 %collective-permute-done.41.b_ref = bf16[192,1152]{1,0:T(8,128)(2,1)S(1)} collective-permute-done((bf16[192,1152]{1,0:T(8,128)(2,1)S(1)}, bf16[192,1152]{1,0:T(8,128)(2,1)S(1)}, u32[]{:S(2)}, u32[]{:S(2)}) %collective-permute-start.41) | collective-permute-done | bytes 442400 | tf_op jit(solution)/shard_map/ppermute | solution.py:59
  291.2 2.8 collective-permute-done.42.d1_ref
  294.0 2.4 collective-permute-done.43.d2_ref
  296.7 7.2 %shard_map.291 = (bf16[768,864]{1,0:T(8,128)(2,1)S(1)}, bf16[768,864]{1,0:T(8,128)(2,1)S(1)}, bf16[768,1152]{1,0:T(8,128)(2,1)S(1)}) custom-call(bf16[768,1152]{1,0:T(8,128)(2,1)S(1)} %bitcast.203, bf16[768,864]{1,0:T(8,128)(2,1)S(1)} %get-tuple-element.226.slope_ref, bf16[768,864]{1,0:T(8,128)(2,1)S(1)} %get-tuple-element.227.value_ref, ...), custom_call_target="tpu_custom_call" | custom-call | tf_op jit(solution)/shard_map/pallas_call | solution.py:733
  306.5 7.6 %shard_map.292 = bf16[864,1152]{1,0:T(8,128)(2,1)S(1)} custom-call(bf16[768,864]{1,0:T(8,128)(2,1)S(1)} %get-tuple-element.231.refs_0_, bf16[768,864]{1,0:T(8,128)(2,1)S(1)} %get-tuple-element.232.refs_1_, bf16[768,864]{1,0:T(8,128)(2,1)S(1)} %get-tuple-element.233.refs_2_, bf16[768,864]{1,0:T(8,128)(2,1)S(1)} %get-tuple-element.234.refs_3_, ...), custom_call_target="tpu_custom_call" | custom-call | tf_op jit(solution)/shard_map/pallas_call | solution.py:761
  322.6 7.8 %shard_map.293 = (bf16[768,864]{1,0:T(8,128)(2,1)S(1)}, bf16[768,864]{1,0:T(8,128)(2,1)S(1)}, bf16[768,1152]{1,0:T(8,128)(2,1)}) custom-call(bf16[768,1152]{1,0:T(8,128)(2,1)S(1)} %bitcast.211, bf16[768,864]{1,0:T(8,128)(2,1)S(1)} %get-tuple-element.236.slope_ref, bf16[768,864]{1,0:T(8,128)(2,1)S(1)} %copy-done.73, bf16[1152,864]{1,0:T(8,128)(2,1)S(1)} %bitcast.180, ...), custom_call_target="tpu_custom_call" | custom-call | tf_op jit(solution)/shard_map/pallas_call | solution.py:733
  334.8 5.8 collective-permute-done.48
  356.4 7.5 %shard_map.294 = bf16[1152,864]{1,0:T(8,128)(2,1)S(1)} custom-call(bf16[768,1152]{1,0:T(8,128)(2,1)S(1)} %bitcast.190, bf16[768,1152]{1,0:T(8,128)(2,1)S(1)} %bitcast.196, bf16[768,1152]{1,0:T(8,128)(2,1)S(1)} %bitcast.193, bf16[768,1152]{1,0:T(8,128)(2,1)S(1)} %bitcast.199, bf16[768,864]{1,0:T(8,128)(2,1)S(1)} %copy-done.79, ...), custom_call_target="tpu_custom_call" | custom-call | tf_op jit(solution)/shard_map/pallas_call | solution.py:761
  365.2 4.7 all-to-all-start.1
  378.3 8.8 %shard_map.295 = bf16[1152,864]{1,0:T(8,128)(2,1)} custom-call(bf16[768,1152]{1,0:T(8,128)(2,1)S(1)} %bitcast.191, bf16[768,1152]{1,0:T(8,128)(2,1)S(1)} %bitcast.197, bf16[768,1152]{1,0:T(8,128)(2,1)S(1)} %bitcast.194, bf16[768,1152]{1,0:T(8,128)(2,1)S(1)} %bitcast.200, bf16[768,864]{1,0:T(8,128)(2,1)S(1)} %copy-done.75, bf16[768,864]{1,0:T(8,128)(2,1)S(1)} %copy-done.77, ...), custom_call_target="tpu_custom_call" | custom-call | tf_op jit(solution)/shard_map/pallas_call | solution.py:761
  393.0 9.0 %shard_map.296 = (f32[192,1152]{1,0:T(8,128)S(1)}, bf16[192,1152]{1,0:T(8,128)(2,1)S(1)}, f32[1,1152]{1,0:T(1,128)S(1)}, f32[1,1152]{1,0:T(1,128)S(1)}, bf16[192...) custom-call(bf16[4,192,1152]{2,1,0:T(8,128)(2,1)S(1)} %copy-done.32,, ...), custom_call_target="tpu_custom_call" | custom-call | tf_op jit(solution)/shard_map/pallas_call | solution.py:544
  409.3 3.0 fusion.35
  412.3 4.5 collective-permute-start.52
  433.2 8.9 %shard_map.297 = (f32[192,1152]{1,0:T(8,128)S(1)}, bf16[192,1152]{1,0:T(8,128)(2,1)S(1)}, f32[1,1152]{1,0:T(1,128)S(1)}, f32[1,1152]{1,0:T(1,128)S(1)}, bf16[192...) custom-call(bf16[4,192,1152]{2,1,0:T(8,128)(2,1)S(1)} %copy-done.34,, ...), custom_call_target="tpu_custom_call" | custom-call | tf_op jit(solution)/shard_map/pallas_call | solution.py:544
  444.7 4.5 all-to-all-start.2
  449.3 4.3 collective-permute-start.59
  454.5 2.8 add_convert_fusion.13
  459.3 2.3 fusion
  467.0 9.1 %all-to-all-done.2 = bf16[8,144,864]{2,1,0:T(8,128)(2,1)} async-done(((bf16[8,144,864]{2,1,0:T(8,128)(2,1)}), bf16[8,144,864]{2,1,0:T(8,128)(2,1)}, u32[]{:S(2)}, u32[]{:S(2)}) %all-to-all-start.2) | async-done | bytes 1990688 | tf_op jit(solution)/shard_map/all_to_all | solution.py:1098
  476.0 3.0 fusion.34
  481.2 2.8 add_convert_fusion.12
  484.0 5.7 collective-permute-done.58.b_ref
  493.7 5.5 shard_map.299
  500.4 3.5 collective-permute-start.65
  507.1 19.8 %collective-permute-done.65 = bf16[4,144,864]{2,1,0:T(8,128)(2,1)S(1)} collective-permute-done((bf16[4,144,864]{2,1,0:T(8,128)(2,1)}, bf16[4,144,864]{2,1,0:T(8,128)(2,1)S(1)}, u32[]{:S(2)}, u32[]{:S(2)}) %collective-permute-start.65) | collective-permute-done | bytes 995360 | tf_op jit(solution)/shard_map/ppermute | solution.py:158
  529.2 7.1 %collective-permute-start.69 = (bf16[4,144,864]{2,1,0:T(8,128)(2,1)S(1)}, bf16[4,144,864]{2,1,0:T(8,128)(2,1)S(1)}, u32[]{:S(2)}, u32[]{:S(2)}) collective-permute-start(bf16[4,144,864]{2,1,0:T(8,128)(2,1)S(1)} %copy-done.164), channel_id=1, source_target_pairs={{0,8},{24,16},{1,9},{25,17},{2,10},{26,18},{3,11},{27,19},{4,12},{... | collective-permute-start | bytes 2985992 | tf_op jit(solution)/shard_map/ppermute | solution.py:158
  539.5 2.3 add_convert_fusion
  544.5 3.6 shard_map.300
  548.2 2.4 collective-permute-done.70
  553.1 5.0 collective-permute-done.69
  563.5 6.5 %collective-permute-start.72 = (bf16[144,1536]{1,0:T(8,128)(2,1)S(1)}, bf16[144,1536]{1,0:T(8,128)(2,1)}, u32[]{:S(2)}, u32[]{:S(2)}) collective-permute-start(bf16[144,1536]{1,0:T(8,128)(2,1)S(1)} %fusion.5), channel_id=1, source_target_pairs={{0,8},{24,16},{1,9},{25,17},{2,10},{26,18},{3,11},{27,19},{4,12},{... | collective-permute-start | bytes 1327112 | tf_op jit(solution)/shard_map/ppermute | solution.py:158
  574.0 3.5 collective-permute-done.77
  582.7 2.8 add_convert_fusion.6.refs_1_
  596.3 3.9 convert_element_type.378
  602.8 2.4 shard_map.301
  605.3 7.8 %collective-permute-done.86.refs_3_ = bf16[4,144,864]{2,1,0:T(8,128)(2,1)} collective-permute-done((bf16[4,144,864]{2,1,0:T(8,128)(2,1)}, bf16[4,144,864]{2,1,0:T(8,128)(2,1)}, u32[]{:S(2)}, u32[]{:S(2)}) %collective-permute-start.86) | collective-permute-done | bytes 995360 | tf_op jit(solution)/shard_map/ppermute | solution.py:158
  613.1 4.3 shard_map.302
  620.7 10.6 %collective-permute-done.82 = bf16[144,1536]{1,0:T(8,128)(2,1)S(1)} collective-permute-done((bf16[144,1536]{1,0:T(8,128)(2,1)S(1)}, bf16[144,1536]{1,0:T(8,128)(2,1)S(1)}, u32[]{:S(2)}, u32[]{:S(2)}) %collective-permute-start.82) | collective-permute-done | bytes 442400 | tf_op jit(solution)/shard_map/ppermute | solution.py:158
  (639 shorter events, 229.5 us)
Async XLA Ops:
  7.2 77.9 %all-gather.3.cloned.1.call-start = ((), (), s32[]{:S(2)}) async-start(), calls=%async_computation.4 | async-start | bytes 2654208 | tf_op jit(solution)/shard_map/all_gather | solution.py:910
  9.7 14.9 %collective-permute-start = (bf16[144,512]{1,0:T(8,128)(2,1)S(1)}, bf16[144,512]{1,0:T(8,128)(2,1)S(1)}, u32[]{:S(2)}, u32[]{:S(2)}) collective-permute-start(bf16[144,512]{1,0:T(8,128)(2,1)S(1)} %constant_dynamic-update-slice_fusion.x_ref), channel_id=1, source_target_pairs={{0,2},{1,3},{2,0},{3,1},{4,6},{5,7},{6,4},{7,5},{8,10},{9,11},{10,... | collective-permute-start | bytes 442376 | tf_op jit(solution)/shard_map/ppermute | solution.py:59
  12.6 13.9 %collective-permute-start.1 = (bf16[144,512]{1,0:T(8,128)(2,1)S(1)}, bf16[144,512]{1,0:T(8,128)(2,1)S(1)}, u32[]{:S(2)}, u32[]{:S(2)}) collective-permute-start(bf16[144,512]{1,0:T(8,128)(2,1)S(1)} %constant_dynamic-update-slice_fusion.x_ref), channel_id=1, source_target_pairs={{0,4},{1,5},{2,6},{3,7},{4,0},{5,1},{6,2},{7,3},{8,12},{9,13},{10,... | collective-permute-start | bytes 442376 | tf_op jit(solution)/shard_map/ppermute | solution.py:59
  19.1 38.2 %all-to-all-start = ((bf16[8,144,864]{2,1,0:T(8,128)(2,1)}), bf16[8,144,864]{2,1,0:T(8,128)(2,1)}, u32[]{:S(2)}, u32[]{:S(2)}) async-start(bf16[8,144,864]{2,1,0:T(8,128)(2,1)} %copy-done.43), calls=%async_computation | async-start | bytes 4128768 | tf_op jit(solution)/shard_map/all_to_all | solution.py:913
  23.6 75.1 %all-gather.5.cloned.1.call-start = ((), (), s32[]{:S(2)}) async-start(), calls=%async_computation.5 | async-start | bytes 2654208 | tf_op jit(solution)/shard_map/all_gather | solution.py:954
  24.6 32.2 %collective-permute-start.2 = (bf16[72,512]{1,0:T(8,128)(2,1)S(1)}, bf16[72,512]{1,0:T(8,128)(2,1)S(1)}, u32[]{:S(2)}, u32[]{:S(2)}) collective-permute-start(bf16[72,512]{1,0:T(8,128)(2,1)S(1)} %slice.393), channel_id=1, source_target_pairs={{0,4},{1,5},{2,6},{3,7},{4,0},{5,1},{6,2},{7,3},{8,12},{9,13},{10,... | collective-permute-start | bytes 221192 | tf_op jit(solution)/shard_map/ppermute | solution.py:59
  26.5 30.3 %collective-permute-start.3 = (bf16[72,512]{1,0:T(8,128)(2,1)S(1)}, bf16[72,512]{1,0:T(8,128)(2,1)S(1)}, u32[]{:S(2)}, u32[]{:S(2)}) collective-permute-start(bf16[72,512]{1,0:T(8,128)(2,1)S(1)} %slice.520), channel_id=1, source_target_pairs={{0,2},{1,3},{2,0},{3,1},{4,6},{5,7},{6,4},{7,5},{8,10},{9,11},{10,... | collective-permute-start | bytes 221192 | tf_op jit(solution)/shard_map/ppermute | solution.py:59
  61.5 356.4 %all-reduce.2.cloned.1.call-start = ((), (), s32[]{:S(2)}) async-start(), calls=%async_computation.6 | async-start | bytes 3981312 | tf_op jit(solution)/shard_map/psum | solution.py:1101
  71.0 17.2 %collective-permute-start.8 = (bf16[2,192,512]{2,1,0:T(8,128)(2,1)S(1)}, bf16[2,192,512]{2,1,0:T(8,128)(2,1)S(1)}, u32[]{:S(2)}, u32[]{:S(2)}) collective-permute-start(bf16[2,192,512]{2,1,0:T(8,128)(2,1)S(1)} %get-tuple-element.175.x_ref), channel_id=1, source_target_pairs={{0,2},{1,3},{2,0},{3,1},{4,6},{5,7},{6,4},{7,5},{8,10},{9,11},{10,... | collective-permute-start | bytes 1179656 | tf_op jit(solution)/shard_map/ppermute | solution.py:59
  96.8 47.7 %collective-permute-start.16 = (bf16[8,144,864]{2,1,0:T(8,128)(2,1)}, bf16[8,144,864]{2,1,0:T(8,128)(2,1)}, u32[]{:S(2)}, u32[]{:S(2)}) collective-permute-start(bf16[8,144,864]{2,1,0:T(8,128)(2,1)} %all-to-all-done.first_ref), channel_id=1, source_target_pairs={{0,8},{8,0},{16,24},{24,16},{1,9},{9,1},{17,25},{25,17},{2,10},{10... | collective-permute-start | bytes 5971976 | tf_op jit(solution)/shard_map/ppermute | solution.py:959
  112.7 12.5 %collective-permute-start.13 = (bf16[192,1152]{1,0:T(8,128)(2,1)}, bf16[192,1152]{1,0:T(8,128)(2,1)}, u32[]{:S(2)}, u32[]{:S(2)}) collective-permute-start(bf16[192,1152]{1,0:T(8,128)(2,1)} %get-tuple-element.185.x_ref), channel_id=1, source_target_pairs={{0,2},{1,3},{2,0},{3,1},{4,6},{5,7},{6,4},{7,5},{8,10},{9,11},{10,... | collective-permute-start | bytes 1327112 | tf_op jit(solution)/shard_map/ppermute | solution.py:59
  114.2 13.0 %collective-permute-start.14 = (bf16[192,1152]{1,0:T(8,128)(2,1)}, bf16[192,1152]{1,0:T(8,128)(2,1)}, u32[]{:S(2)}, u32[]{:S(2)}) collective-permute-start(bf16[192,1152]{1,0:T(8,128)(2,1)} %get-tuple-element.185.x_ref), channel_id=1, source_target_pairs={{0,4},{1,5},{2,6},{3,7},{4,0},{5,1},{6,2},{7,3},{8,12},{9,13},{10,... | collective-permute-start | bytes 1327112 | tf_op jit(solution)/shard_map/ppermute | solution.py:59
  126.2 23.5 %collective-permute-start.15 = (bf16[96,1152]{1,0:T(8,128)(2,1)S(1)}, bf16[96,1152]{1,0:T(8,128)(2,1)S(1)}, u32[]{:S(2)}, u32[]{:S(2)}) collective-permute-start(bf16[96,1152]{1,0:T(8,128)(2,1)S(1)} %slice.404), channel_id=1, source_target_pairs={{0,4},{1,5},{2,6},{3,7},{4,0},{5,1},{6,2},{7,3},{8,12},{9,13},{10,... | collective-permute-start | bytes 663560 | tf_op jit(solution)/shard_map/ppermute | solution.py:59
  128.1 21.6 %collective-permute-start.17 = (bf16[96,1152]{1,0:T(8,128)(2,1)S(1)}, bf16[96,1152]{1,0:T(8,128)(2,1)S(1)}, u32[]{:S(2)}, u32[]{:S(2)}) collective-permute-start(bf16[96,1152]{1,0:T(8,128)(2,1)S(1)} %slice.524), channel_id=1, source_target_pairs={{0,2},{1,3},{2,0},{3,1},{4,6},{5,7},{6,4},{7,5},{8,10},{9,11},{10,... | collective-permute-start | bytes 663560 | tf_op jit(solution)/shard_map/ppermute | solution.py:59
  151.9 12.7 %collective-permute-start.18 = (bf16[4,192,1152]{2,1,0:T(8,128)(2,1)S(1)}, bf16[4,192,1152]{2,1,0:T(8,128)(2,1)S(1)}, u32[]{:S(2)}, u32[]{:S(2)}) collective-permute-start(bf16[4,192,1152]{2,1,0:T(8,128)(2,1)S(1)} %shard_map.279), channel_id=1, source_target_pairs={{0,1},{1,0},{2,3},{3,2},{4,5},{5,4},{6,7},{7,6},{8,9},{9,8},{10,11... | collective-permute-start | bytes 5308424 | tf_op jit(solution)/shard_map/ppermute | solution.py:59
  152.0 12.6 %collective-permute-start.19 = (bf16[192,1152]{1,0:T(8,128)(2,1)S(1)}, bf16[192,1152]{1,0:T(8,128)(2,1)S(1)}, u32[]{:S(2)}, u32[]{:S(2)}) collective-permute-start(bf16[192,1152]{1,0:T(8,128)(2,1)S(1)} %get-tuple-element.194.x_ref), channel_id=1, source_target_pairs={{0,2},{1,3},{2,0},{3,1},{4,6},{5,7},{6,4},{7,5},{8,10},{9,11},{10,... | collective-permute-start | bytes 1327112 | tf_op jit(solution)/shard_map/ppermute | solution.py:59
  171.2 26.7 %collective-permute-start.20 = (bf16[4,192,1152]{2,1,0:T(8,128)(2,1)S(1)}, bf16[4,192,1152]{2,1,0:T(8,128)(2,1)S(1)}, u32[]{:S(2)}, u32[]{:S(2)}) collective-permute-start(bf16[4,192,1152]{2,1,0:T(8,128)(2,1)S(1)} %bitcast.224), channel_id=1, source_target_pairs={{0,1},{1,0},{2,3},{3,2},{4,5},{5,4},{6,7},{7,6},{8,9},{9,8},{10,11... | collective-permute-start | bytes 5308424 | tf_op jit(solution)/shard_map/ppermute | solution.py:59
  171.2 13.0 %collective-permute-start.21 = (bf16[192,1152]{1,0:T(8,128)(2,1)S(1)}, bf16[192,1152]{1,0:T(8,128)(2,1)S(1)}, u32[]{:S(2)}, u32[]{:S(2)}) collective-permute-start(bf16[192,1152]{1,0:T(8,128)(2,1)S(1)} %get-tuple-element.194.x_ref), channel_id=1, source_target_pairs={{0,4},{1,5},{2,6},{3,7},{4,0},{5,1},{6,2},{7,3},{8,12},{9,13},{10,... | collective-permute-start | bytes 1327112 | tf_op jit(solution)/shard_map/ppermute | solution.py:59
  171.6 16.9 %collective-permute-start.22 = (bf16[96,1152]{1,0:T(8,128)(2,1)S(1)}, bf16[96,1152]{1,0:T(8,128)(2,1)S(1)}, u32[]{:S(2)}, u32[]{:S(2)}) collective-permute-start(bf16[96,1152]{1,0:T(8,128)(2,1)S(1)} %slice.406), channel_id=1, source_target_pairs={{0,4},{1,5},{2,6},{3,7},{4,0},{5,1},{6,2},{7,3},{8,12},{9,13},{10,... | collective-permute-start | bytes 663560 | tf_op jit(solution)/shard_map/ppermute | solution.py:59
  214.8 13.2 %collective-permute-start.25 = (bf16[192,1152]{1,0:T(8,128)(2,1)S(1)}, bf16[192,1152]{1,0:T(8,128)(2,1)S(1)}, u32[]{:S(2)}, u32[]{:S(2)}) collective-permute-start(bf16[192,1152]{1,0:T(8,128)(2,1)S(1)} %pad_maximum_fusion.2), channel_id=1, source_target_pairs={{0,2},{1,3},{2,0},{3,1},{4,6},{5,7},{6,4},{7,5},{8,10},{9,11},{10,... | collective-permute-start | bytes 1327112 | tf_op jit(solution)/shard_map/ppermute | solution.py:59
  215.5 13.2 %collective-permute-start.29 = (bf16[192,1152]{1,0:T(8,128)(2,1)S(1)}, bf16[192,1152]{1,0:T(8,128)(2,1)S(1)}, u32[]{:S(2)}, u32[]{:S(2)}) collective-permute-start(bf16[192,1152]{1,0:T(8,128)(2,1)S(1)} %pad_maximum_fusion.3), channel_id=1, source_target_pairs={{0,4},{1,5},{2,6},{3,7},{4,0},{5,1},{6,2},{7,3},{8,12},{9,13},{10,... | collective-permute-start | bytes 1327112 | tf_op jit(solution)/shard_map/ppermute | solution.py:59
  216.4 16.3 %collective-permute-start.33 = (bf16[96,1152]{1,0:T(8,128)(2,1)S(1)}, bf16[96,1152]{1,0:T(8,128)(2,1)S(1)}, u32[]{:S(2)}, u32[]{:S(2)}) collective-permute-start(bf16[96,1152]{1,0:T(8,128)(2,1)S(1)} %get-tuple-element.363), channel_id=1, source_target_pairs={{0,2},{1,3},{2,0},{3,1},{4,6},{5,7},{6,4},{7,5},{8,10},{9,11},{10,... | collective-permute-start | bytes 663560 | tf_op jit(solution)/shard_map/ppermute | solution.py:59
  218.2 15.2 %collective-permute-start.30 = (bf16[96,1152]{1,0:T(8,128)(2,1)S(1)}, bf16[96,1152]{1,0:T(8,128)(2,1)S(1)}, u32[]{:S(2)}, u32[]{:S(2)}) collective-permute-start(bf16[96,1152]{1,0:T(8,128)(2,1)S(1)} %get-tuple-element.365), channel_id=1, source_target_pairs={{0,4},{1,5},{2,6},{3,7},{4,0},{5,1},{6,2},{7,3},{8,12},{9,13},{10,... | collective-permute-start | bytes 663560 | tf_op jit(solution)/shard_map/ppermute | solution.py:59
  229.4 13.2 %collective-permute-start.32 = (bf16[192,1152]{1,0:T(8,128)(2,1)S(1)}, bf16[192,1152]{1,0:T(8,128)(2,1)S(1)}, u32[]{:S(2)}, u32[]{:S(2)}) collective-permute-start(bf16[192,1152]{1,0:T(8,128)(2,1)S(1)} %get-tuple-element.208.x_ref), channel_id=1, source_target_pairs={{0,2},{1,3},{2,0},{3,1},{4,6},{5,7},{6,4},{7,5},{8,10},{9,11},{10,... | collective-permute-start | bytes 1327112 | tf_op jit(solution)/shard_map/ppermute | solution.py:59
  230.9 13.1 %collective-permute-start.35 = (bf16[192,1152]{1,0:T(8,128)(2,1)S(1)}, bf16[192,1152]{1,0:T(8,128)(2,1)S(1)}, u32[]{:S(2)}, u32[]{:S(2)}) collective-permute-start(bf16[192,1152]{1,0:T(8,128)(2,1)S(1)} %get-tuple-element.208.x_ref), channel_id=1, source_target_pairs={{0,4},{1,5},{2,6},{3,7},{4,0},{5,1},{6,2},{7,3},{8,12},{9,13},{10,... | collective-permute-start | bytes 1327112 | tf_op jit(solution)/shard_map/ppermute | solution.py:59
  233.5 18.3 %collective-permute-start.31 = (bf16[192,1152]{1,0:T(8,128)(2,1)S(1)}, bf16[192,1152]{1,0:T(8,128)(2,1)S(1)}, u32[]{:S(2)}, u32[]{:S(2)}) collective-permute-start(bf16[192,1152]{1,0:T(8,128)(2,1)S(1)} %pad_maximum_fusion.4), channel_id=1, source_target_pairs={{0,2},{1,3},{2,0},{3,1},{4,6},{5,7},{6,4},{7,5},{8,10},{9,11},{10,... | collective-permute-start | bytes 1327112 | tf_op jit(solution)/shard_map/ppermute | solution.py:59
  235.1 17.2 %collective-permute-start.34 = (bf16[192,1152]{1,0:T(8,128)(2,1)S(1)}, bf16[192,1152]{1,0:T(8,128)(2,1)S(1)}, u32[]{:S(2)}, u32[]{:S(2)}) collective-permute-start(bf16[192,1152]{1,0:T(8,128)(2,1)S(1)} %pad_maximum_fusion.5), channel_id=1, source_target_pairs={{0,4},{1,5},{2,6},{3,7},{4,0},{5,1},{6,2},{7,3},{8,12},{9,13},{10,... | collective-permute-start | bytes 1327112 | tf_op jit(solution)/shard_map/ppermute | solution.py:59
  242.6 12.1 %collective-permute-start.36 = (bf16[96,1152]{1,0:T(8,128)(2,1)S(1)}, bf16[96,1152]{1,0:T(8,128)(2,1)S(1)}, u32[]{:S(2)}, u32[]{:S(2)}) collective-permute-start(bf16[96,1152]{1,0:T(8,128)(2,1)S(1)} %slice.432), channel_id=1, source_target_pairs={{0,4},{1,5},{2,6},{3,7},{4,0},{5,1},{6,2},{7,3},{8,12},{9,13},{10,... | collective-permute-start | bytes 663560 | tf_op jit(solution)/shard_map/ppermute | solution.py:59
  254.8 12.7 %collective-permute-start.38 = (bf16[4,192,1152]{2,1,0:T(8,128)(2,1)S(1)}, bf16[4,192,1152]{2,1,0:T(8,128)(2,1)S(1)}, u32[]{:S(2)}, u32[]{:S(2)}) collective-permute-start(bf16[4,192,1152]{2,1,0:T(8,128)(2,1)S(1)} %shard_map.287), channel_id=1, source_target_pairs={{0,1},{1,0},{2,3},{3,2},{4,5},{5,4},{6,7},{7,6},{8,9},{9,8},{10,11... | collective-permute-start | bytes 5308424 | tf_op jit(solution)/shard_map/ppermute | solution.py:59
  254.9 12.6 %collective-permute-start.39 = (bf16[192,1152]{1,0:T(8,128)(2,1)S(1)}, bf16[192,1152]{1,0:T(8,128)(2,1)S(1)}, u32[]{:S(2)}, u32[]{:S(2)}) collective-permute-start(bf16[192,1152]{1,0:T(8,128)(2,1)S(1)} %get-tuple-element.215.x_ref), channel_id=1, source_target_pairs={{0,2},{1,3},{2,0},{3,1},{4,6},{5,7},{6,4},{7,5},{8,10},{9,11},{10,... | collective-permute-start | bytes 1327112 | tf_op jit(solution)/shard_map/ppermute | solution.py:59
  276.7 27.2 %collective-permute-start.40 = (bf16[4,192,1152]{2,1,0:T(8,128)(2,1)S(1)}, bf16[4,192,1152]{2,1,0:T(8,128)(2,1)S(1)}, u32[]{:S(2)}, u32[]{:S(2)}) collective-permute-start(bf16[4,192,1152]{2,1,0:T(8,128)(2,1)S(1)} %bitcast.223), channel_id=1, source_target_pairs={{0,1},{1,0},{2,3},{3,2},{4,5},{5,4},{6,7},{7,6},{8,9},{9,8},{10,11... | collective-permute-start | bytes 5308424 | tf_op jit(solution)/shard_map/ppermute | solution.py:59
  276.7 13.0 %collective-permute-start.41 = (bf16[192,1152]{1,0:T(8,128)(2,1)S(1)}, bf16[192,1152]{1,0:T(8,128)(2,1)S(1)}, u32[]{:S(2)}, u32[]{:S(2)}) collective-permute-start(bf16[192,1152]{1,0:T(8,128)(2,1)S(1)} %get-tuple-element.215.x_ref), channel_id=1, source_target_pairs={{0,4},{1,5},{2,6},{3,7},{4,0},{5,1},{6,2},{7,3},{8,12},{9,13},{10,... | collective-permute-start | bytes 1327112 | tf_op jit(solution)/shard_map/ppermute | solution.py:59
  277.2 16.8 %collective-permute-start.42 = (bf16[96,1152]{1,0:T(8,128)(2,1)S(1)}, bf16[96,1152]{1,0:T(8,128)(2,1)S(1)}, u32[]{:S(2)}, u32[]{:S(2)}) collective-permute-start(bf16[96,1152]{1,0:T(8,128)(2,1)S(1)} %slice.434), channel_id=1, source_target_pairs={{0,4},{1,5},{2,6},{3,7},{4,0},{5,1},{6,2},{7,3},{8,12},{9,13},{10,... | collective-permute-start | bytes 663560 | tf_op jit(solution)/shard_map/ppermute | solution.py:59
  331.4 55.7 %collective-permute-start.47 = (bf16[4,192,1152]{2,1,0:T(8,128)(2,1)}, bf16[4,192,1152]{2,1,0:T(8,128)(2,1)}, u32[]{:S(2)}, u32[]{:S(2)}) collective-permute-start(bf16[4,192,1152]{2,1,0:T(8,128)(2,1)} %bitcast.44), channel_id=1, source_target_pairs={{0,1},{1,0},{2,3},{3,2},{4,5},{5,4},{6,7},{7,6},{8,9},{9,8},{10,11... | collective-permute-start | bytes 5308424 | tf_op jit(solution)/shard_map/ppermute | solution.py:59
  344.9 48.0 %collective-permute-start.45 = (bf16[192,1152]{1,0:T(8,128)(2,1)}, bf16[192,1152]{1,0:T(8,128)(2,1)}, u32[]{:S(2)}, u32[]{:S(2)}) collective-permute-start(bf16[192,1152]{1,0:T(8,128)(2,1)} %pad_maximum_fusion.6), channel_id=1, source_target_pairs={{0,2},{1,3},{2,0},{3,1},{4,6},{5,7},{6,4},{7,5},{8,10},{9,11},{10,... | collective-permute-start | bytes 1327112 | tf_op jit(solution)/shard_map/ppermute | solution.py:59
  347.3 45.6 %collective-permute-start.49 = (bf16[192,1152]{1,0:T(8,128)(2,1)}, bf16[192,1152]{1,0:T(8,128)(2,1)}, u32[]{:S(2)}, u32[]{:S(2)}) collective-permute-start(bf16[192,1152]{1,0:T(8,128)(2,1)} %pad_maximum_fusion.7), channel_id=1, source_target_pairs={{0,4},{1,5},{2,6},{3,7},{4,0},{5,1},{6,2},{7,3},{8,12},{9,13},{10,... | collective-permute-start | bytes 1327112 | tf_op jit(solution)/shard_map/ppermute | solution.py:59
  365.2 44.1 %all-to-all-start.1 = ((bf16[8,144,864]{2,1,0:T(8,128)(2,1)}), bf16[8,144,864]{2,1,0:T(8,128)(2,1)}, u32[]{:S(2)}, u32[]{:S(2)}) async-start(bf16[8,144,864]{2,1,0:T(8,128)(2,1)} %bitcast.207), calls=%async_computation.1 | async-start | bytes 4128768 | tf_op jit(solution)/shard_map/all_to_all | solution.py:1098
  389.4 15.3 %collective-permute-start.51 = (bf16[96,1152]{1,0:T(8,128)(2,1)S(1)}, bf16[96,1152]{1,0:T(8,128)(2,1)S(1)}, u32[]{:S(2)}, u32[]{:S(2)}) collective-permute-start(bf16[96,1152]{1,0:T(8,128)(2,1)S(1)} %get-tuple-element.351), channel_id=1, source_target_pairs={{0,2},{1,3},{2,0},{3,1},{4,6},{5,7},{6,4},{7,5},{8,10},{9,11},{10,... | collective-permute-start | bytes 663560 | tf_op jit(solution)/shard_map/ppermute | solution.py:59
  391.4 13.3 %collective-permute-start.50 = (bf16[96,1152]{1,0:T(8,128)(2,1)S(1)}, bf16[96,1152]{1,0:T(8,128)(2,1)S(1)}, u32[]{:S(2)}, u32[]{:S(2)}) collective-permute-start(bf16[96,1152]{1,0:T(8,128)(2,1)S(1)} %get-tuple-element.353), channel_id=1, source_target_pairs={{0,4},{1,5},{2,6},{3,7},{4,0},{5,1},{6,2},{7,3},{8,12},{9,13},{10,... | collective-permute-start | bytes 663560 | tf_op jit(solution)/shard_map/ppermute | solution.py:59
  406.5 11.9 %collective-permute-start.53 = (bf16[192,1152]{1,0:T(8,128)(2,1)}, bf16[192,1152]{1,0:T(8,128)(2,1)}, u32[]{:S(2)}, u32[]{:S(2)}) collective-permute-start(bf16[192,1152]{1,0:T(8,128)(2,1)} %pad_maximum_fusion.8), channel_id=1, source_target_pairs={{0,2},{1,3},{2,0},{3,1},{4,6},{5,7},{6,4},{7,5},{8,10},{9,11},{10,... | collective-permute-start | bytes 1327112 | tf_op jit(solution)/shard_map/ppermute | solution.py:59
  407.8 12.2 %collective-permute-start.54 = (bf16[192,1152]{1,0:T(8,128)(2,1)}, bf16[192,1152]{1,0:T(8,128)(2,1)}, u32[]{:S(2)}, u32[]{:S(2)}) collective-permute-start(bf16[192,1152]{1,0:T(8,128)(2,1)} %pad_maximum_fusion.9), channel_id=1, source_target_pairs={{0,4},{1,5},{2,6},{3,7},{4,0},{5,1},{6,2},{7,3},{8,12},{9,13},{10,... | collective-permute-start | bytes 1327112 | tf_op jit(solution)/shard_map/ppermute | solution.py:59
  412.3 42.3 %collective-permute-start.52 = (bf16[4,144,864]{2,1,0:T(8,128)(2,1)}, bf16[4,144,864]{2,1,0:T(8,128)(2,1)}, u32[]{:S(2)}, u32[]{:S(2)}) collective-permute-start(bf16[4,144,864]{2,1,0:T(8,128)(2,1)} %get-tuple-element.258), channel_id=1, source_target_pairs={{0,8},{24,16},{1,9},{25,17},{2,10},{26,18},{3,11},{27,19},{4,12},{... | collective-permute-start | bytes 2985992 | tf_op jit(solution)/shard_map/ppermute | solution.py:158
  444.3 17.3 %collective-permute-start.56 = (bf16[4,2,192,512]{3,2,1,0:T(8,128)(2,1)}, bf16[4,2,192,512]{3,2,1,0:T(8,128)(2,1)}, u32[]{:S(2)}, u32[]{:S(2)}) collective-permute-start(bf16[4,2,192,512]{3,2,1,0:T(8,128)(2,1)} %pad_maximum_fusion), channel_id=1, source_target_pairs={{0,1},{1,0},{2,3},{3,2},{4,5},{5,4},{6,7},{7,6},{8,9},{9,8},{10,11... | collective-permute-start | bytes 4718600 | tf_op jit(solution)/shard_map/ppermute | solution.py:59
  444.7 31.3 %all-to-all-start.2 = ((bf16[8,144,864]{2,1,0:T(8,128)(2,1)}), bf16[8,144,864]{2,1,0:T(8,128)(2,1)}, u32[]{:S(2)}, u32[]{:S(2)}) async-start(bf16[8,144,864]{2,1,0:T(8,128)(2,1)} %bitcast.64), calls=%async_computation.2 | async-start | bytes 4128768 | tf_op jit(solution)/shard_map/all_to_all | solution.py:1098
  449.2 122.4 %reduce-scatter.2.cloned.1.call-start = ((), (), s32[]{:S(2)}) async-start(), calls=%async_computation.7 | async-start | bytes 2654208 | tf_op jit(solution)/shard_map/reduce_scatter | solution.py:1127
  449.3 31.9 %collective-permute-start.59 = (bf16[4,144,864]{2,1,0:T(8,128)(2,1)}, bf16[4,144,864]{2,1,0:T(8,128)(2,1)}, u32[]{:S(2)}, u32[]{:S(2)}) collective-permute-start(bf16[4,144,864]{2,1,0:T(8,128)(2,1)} %get-tuple-element.259), channel_id=1, source_target_pairs={{0,8},{24,16},{1,9},{25,17},{2,10},{26,18},{3,11},{27,19},{4,12},{... | collective-permute-start | bytes 2985992 | tf_op jit(solution)/shard_map/ppermute | solution.py:158
  457.4 34.3 %collective-permute-start.55 = (bf16[4,144,864]{2,1,0:T(8,128)(2,1)}, bf16[4,144,864]{2,1,0:T(8,128)(2,1)}, u32[]{:S(2)}, u32[]{:S(2)}) collective-permute-start(bf16[4,144,864]{2,1,0:T(8,128)(2,1)} %add_convert_fusion.13), channel_id=1, source_target_pairs={{8,16},{16,8},{9,17},{17,9},{10,18},{18,10},{11,19},{19,11},{12,20... | collective-permute-start | bytes 2985992 | tf_op jit(solution)/shard_map/ppermute | solution.py:158
  463.6 15.5 %collective-permute-start.60 = (bf16[1,192,512]{2,1,0:T(8,128)(2,1)S(1)}, bf16[1,192,512]{2,1,0:T(8,128)(2,1)S(1)}, u32[]{:S(2)}, u32[]{:S(2)}) collective-permute-start(bf16[1,192,512]{2,1,0:T(8,128)(2,1)S(1)} %get-tuple-element.375), channel_id=1, source_target_pairs={{0,2},{1,3},{2,0},{3,1},{4,6},{5,7},{6,4},{7,5},{8,10},{9,11},{10,... | collective-permute-start | bytes 589832 | tf_op jit(solution)/shard_map/ppermute | solution.py:59
  465.5 13.6 %collective-permute-start.57 = (bf16[1,192,512]{2,1,0:T(8,128)(2,1)S(1)}, bf16[1,192,512]{2,1,0:T(8,128)(2,1)S(1)}, u32[]{:S(2)}, u32[]{:S(2)}) collective-permute-start(bf16[1,192,512]{2,1,0:T(8,128)(2,1)S(1)} %get-tuple-element.377), channel_id=1, source_target_pairs={{0,4},{1,5},{2,6},{3,7},{4,0},{5,1},{6,2},{7,3},{8,12},{9,13},{10,... | collective-permute-start | bytes 589832 | tf_op jit(solution)/shard_map/ppermute | solution.py:59
  500.4 39.0 %collective-permute-start.63 = (bf16[4,144,1536]{2,1,0:T(8,128)(2,1)}, bf16[4,144,1536]{2,1,0:T(8,128)(2,1)}, u32[]{:S(2)}, u32[]{:S(2)}) collective-permute-start(bf16[4,144,1536]{2,1,0:T(8,128)(2,1)} %get-tuple-element.286), channel_id=1, source_target_pairs={{0,1},{1,0},{2,3},{3,2},{4,5},{5,4},{6,7},{7,6},{8,9},{9,8},{10,11... | collective-permute-start | bytes 5308424 | tf_op jit(solution)/shard_map/ppermute | solution.py:59
  500.4 26.5 %collective-permute-start.65 = (bf16[4,144,864]{2,1,0:T(8,128)(2,1)}, bf16[4,144,864]{2,1,0:T(8,128)(2,1)S(1)}, u32[]{:S(2)}, u32[]{:S(2)}) collective-permute-start(bf16[4,144,864]{2,1,0:T(8,128)(2,1)} %get-tuple-element.274), channel_id=1, source_target_pairs={{0,8},{24,16},{1,9},{25,17},{2,10},{26,18},{3,11},{27,19},{4,12},{... | collective-permute-start | bytes 2985992 | tf_op jit(solution)/shard_map/ppermute | solution.py:158
  503.9 32.4 %collective-permute-start.64 = (bf16[4,144,864]{2,1,0:T(8,128)(2,1)}, bf16[4,144,864]{2,1,0:T(8,128)(2,1)}, u32[]{:S(2)}, u32[]{:S(2)}) collective-permute-start(bf16[4,144,864]{2,1,0:T(8,128)(2,1)} %add_convert_fusion.12), channel_id=1, source_target_pairs={{8,16},{16,8},{9,17},{17,9},{10,18},{18,10},{11,19},{19,11},{12,20... | collective-permute-start | bytes 2985992 | tf_op jit(solution)/shard_map/ppermute | solution.py:158
  505.6 36.2 %collective-permute-start.62 = (bf16[4,144,864]{2,1,0:T(8,128)(2,1)S(1)}, bf16[4,144,864]{2,1,0:T(8,128)(2,1)S(1)}, u32[]{:S(2)}, u32[]{:S(2)}) collective-permute-start(bf16[4,144,864]{2,1,0:T(8,128)(2,1)S(1)} %add_convert_fusion.11.refs_0_), channel_id=1, source_target_pairs={{8,0},{16,24},{9,1},{17,25},{10,2},{18,26},{11,3},{19,27},{12,4},{... | collective-permute-start | bytes 2985992 | tf_op jit(solution)/shard_map/ppermute | solution.py:158
  528.3 32.7 %collective-permute-start.68 = (bf16[4,144,864]{2,1,0:T(8,128)(2,1)S(1)}, bf16[4,144,864]{2,1,0:T(8,128)(2,1)S(1)}, u32[]{:S(2)}, u32[]{:S(2)}) collective-permute-start(bf16[4,144,864]{2,1,0:T(8,128)(2,1)S(1)} %add_convert_fusion.10), channel_id=1, source_target_pairs={{8,16},{16,8},{9,17},{17,9},{10,18},{18,10},{11,19},{19,11},{12,20... | collective-permute-start | bytes 2985992 | tf_op jit(solution)/shard_map/ppermute | solution.py:158
  529.2 28.8 %collective-permute-start.69 = (bf16[4,144,864]{2,1,0:T(8,128)(2,1)S(1)}, bf16[4,144,864]{2,1,0:T(8,128)(2,1)S(1)}, u32[]{:S(2)}, u32[]{:S(2)}) collective-permute-start(bf16[4,144,864]{2,1,0:T(8,128)(2,1)S(1)} %copy-done.164), channel_id=1, source_target_pairs={{0,8},{24,16},{1,9},{25,17},{2,10},{26,18},{3,11},{27,19},{4,12},{... | collective-permute-start | bytes 2985992 | tf_op jit(solution)/shard_map/ppermute | solution.py:158
  538.1 32.5 %collective-permute-start.75 = (bf16[4,144,864]{2,1,0:T(8,128)(2,1)S(1)}, bf16[4,144,864]{2,1,0:T(8,128)(2,1)S(1)}, u32[]{:S(2)}, u32[]{:S(2)}) collective-permute-start(bf16[4,144,864]{2,1,0:T(8,128)(2,1)S(1)} %add_convert_fusion.9.refs_1_), channel_id=1, source_target_pairs={{8,0},{16,24},{9,1},{17,25},{10,2},{18,26},{11,3},{19,27},{12,4},{... | collective-permute-start | bytes 2985992 | tf_op jit(solution)/shard_map/ppermute | solution.py:158
  550.9 11.7 %collective-permute-start.67 = (bf16[144,1536]{1,0:T(8,128)(2,1)S(1)}, bf16[144,1536]{1,0:T(8,128)(2,1)S(1)}, u32[]{:S(2)}, u32[]{:S(2)}) collective-permute-start(bf16[144,1536]{1,0:T(8,128)(2,1)S(1)} %pad_maximum_fusion.10), channel_id=1, source_target_pairs={{0,2},{1,3},{2,0},{3,1},{4,6},{5,7},{6,4},{7,5},{8,10},{9,11},{10,... | collective-permute-start | bytes 1327112 | tf_op jit(solution)/shard_map/ppermute | solution.py:59
  559.3 23.4 %collective-permute-start.74 = (bf16[4,144,864]{2,1,0:T(8,128)(2,1)}, bf16[4,144,864]{2,1,0:T(8,128)(2,1)}, u32[]{:S(2)}, u32[]{:S(2)}) collective-permute-start(bf16[4,144,864]{2,1,0:T(8,128)(2,1)} %add_convert_fusion.8), channel_id=1, source_target_pairs={{8,16},{16,8},{9,17},{17,9},{10,18},{18,10},{11,19},{19,11},{12,20... | collective-permute-start | bytes 2985992 | tf_op jit(solution)/shard_map/ppermute | solution.py:158
  561.3 26.0 %collective-permute-start.73 = (bf16[4,144,864]{2,1,0:T(8,128)(2,1)S(1)}, bf16[4,144,864]{2,1,0:T(8,128)(2,1)}, u32[]{:S(2)}, u32[]{:S(2)}) collective-permute-start(bf16[4,144,864]{2,1,0:T(8,128)(2,1)S(1)} %add_convert_fusion.7.refs_0_), channel_id=1, source_target_pairs={{8,0},{16,24},{9,1},{17,25},{10,2},{18,26},{11,3},{19,27},{12,4},{... | collective-permute-start | bytes 2985992 | tf_op jit(solution)/shard_map/ppermute | solution.py:158
  563.5 23.8 %collective-permute-start.72 = (bf16[144,1536]{1,0:T(8,128)(2,1)S(1)}, bf16[144,1536]{1,0:T(8,128)(2,1)}, u32[]{:S(2)}, u32[]{:S(2)}) collective-permute-start(bf16[144,1536]{1,0:T(8,128)(2,1)S(1)} %fusion.5), channel_id=1, source_target_pairs={{0,8},{24,16},{1,9},{25,17},{2,10},{26,18},{3,11},{27,19},{4,12},{... | collective-permute-start | bytes 1327112 | tf_op jit(solution)/shard_map/ppermute | solution.py:158
  585.5 27.6 %collective-permute-start.86 = (bf16[4,144,864]{2,1,0:T(8,128)(2,1)}, bf16[4,144,864]{2,1,0:T(8,128)(2,1)}, u32[]{:S(2)}, u32[]{:S(2)}) collective-permute-start(bf16[4,144,864]{2,1,0:T(8,128)(2,1)} %add_convert_fusion.6.refs_1_), channel_id=1, source_target_pairs={{8,0},{16,24},{9,1},{17,25},{10,2},{18,26},{11,3},{19,27},{12,4},{... | collective-permute-start | bytes 2985992 | tf_op jit(solution)/shard_map/ppermute | solution.py:158
  592.3 26.6 %collective-permute-start.84 = (bf16[128,1152]{1,0:T(8,128)(2,1)}, bf16[128,1152]{1,0:T(8,128)(2,1)}, u32[]{:S(2)}, u32[]{:S(2)}) collective-permute-start(bf16[128,1152]{1,0:T(8,128)(2,1)} %add_convert_fusion.16), channel_id=1, source_target_pairs={{8,0},{16,24},{9,1},{17,25},{10,2},{18,26},{11,3},{19,27},{12,4},{... | collective-permute-start | bytes 884744 | tf_op jit(solution)/shard_map/ppermute | solution.py:158
  600.2 31.1 %collective-permute-start.82 = (bf16[144,1536]{1,0:T(8,128)(2,1)S(1)}, bf16[144,1536]{1,0:T(8,128)(2,1)S(1)}, u32[]{:S(2)}, u32[]{:S(2)}) collective-permute-start(bf16[144,1536]{1,0:T(8,128)(2,1)S(1)} %copy-done.165), channel_id=1, source_target_pairs={{8,0},{16,24},{9,1},{17,25},{10,2},{18,26},{11,3},{19,27},{12,4},{... | collective-permute-start | bytes 1327112 | tf_op jit(solution)/shard_map/ppermute | solution.py:158
  601.5 30.0 %collective-permute-start.87 = (f32[40,128]{1,0:T(8,128)S(1)}, f32[40,128]{1,0:T(8,128)S(1)}, u32[]{:S(2)}, u32[]{:S(2)}) collective-permute-start(f32[40,128]{1,0:T(8,128)S(1)} %add.378), channel_id=1, source_target_pairs={{8,0},{16,24},{9,1},{17,25},{10,2},{18,26},{11,3},{19,27},{12,4},{... | collective-permute-start | bytes 61448 | tf_op jit(solution)/shard_map/ppermute | solution.py:158
  (207 other events, 1599.9 us)
Sparse Core Ops, SparseCore 0:
  9.9 49.0 all-gather.2
  61.6 35.5 all-gather.4
  335.0 82.9 all-reduce.1
  505.7 42.3 reduce-scatter.1

commit v3 on v2

--- a/solution.py
+++ b/solution.py
@@ -55,6 +55,10 @@
     return lax.optimization_barrier((x,) + earlier)[0] if earlier else x
 
 
+def together(xs, *earlier):
+    return lax.optimization_barrier(tuple(xs) + earlier)[: len(xs)]
+
+
 def xor_permute(x, axis_size, code):
     return lax.ppermute(x, "ctx", [(i, i ^ code) for i in range(axis_size)])
 
@@ -78,14 +82,14 @@
 
     def mid(self, *earlier):
         half = self.x.shape[0] // 2
-        a = after(self.a, *earlier)
+        a, b = together((self.a, self.b), *earlier)
         self.d1 = xor_permute(a[:half], self.n, self.far_y)
-        self.d2 = xor_permute(self.b[half:], self.n, self.far_x)
+        self.d2 = xor_permute(b[half:], self.n, self.far_x)
         return self
 
     def near(self, *earlier):
-        d1 = after(self.d1, *earlier)
-        self.blocks = [stack_blocks(self.x, self.a, self.b, d1, self.d2)]
+        d1, d2 = together((self.d1, self.d2), *earlier)
+        self.blocks = [stack_blocks(self.x, self.a, self.b, d1, d2)]
         for bit in self.near_bits:
             self.blocks = self.blocks + [xor_permute(b, self.n, bit) for b in self.blocks]
         return self
@@ -125,8 +129,8 @@
 
     def far(self, *earlier):
         half = self.sums.shape[1] // 2
-        d_x = after(self.d_x, *earlier).astype(WIDE)
-        d_y = self.d_y.astype(WIDE)
+        d_x, d_y = together((self.d_x, self.d_y), *earlier)
+        d_x, d_y = d_x.astype(WIDE), d_y.astype(WIDE)
         x, y = self.sums[1].astype(WIDE), self.sums[2].astype(WIDE)
         to_x = jnp.concatenate([x[:half], x[half:] + d_y], axis=0).astype(BF16)
         to_y = jnp.concatenate([y[:half] + d_x, y[half:]], axis=0).astype(BF16)
@@ -136,7 +140,7 @@
         return self
 
     def finish(self, *earlier):
-        return self.sums, after(self.from_x, *earlier), self.from_y
+        return self.sums, *together((self.from_x, self.from_y), *earlier)
 
 
 class Line:
@@ -378,6 +382,7 @@
             jax.ShapeDtypeStruct((count, width), WIDE),
             jax.ShapeDtypeStruct((count, width), BF16),
         ),
+        limit=48,
         grid=(1,),
         in_specs=[
             pl.BlockSpec((count, lanes_all), lambda i: (row, 0)),
@@ -552,6 +557,7 @@
             jax.ShapeDtypeStruct((1, size), WIDE),
         )
         + (jax.ShapeDtypeStruct((slots, count, 2 * size), BF16),) * block_count,
+        limit=48,
         grid=(1,),
         in_specs=[
             row_spec((count, width), 0),
@@ -909,8 +915,21 @@
     kv_weights = Gather(jnp.concatenate([key_weight, value_weight], axis=1), n)
     query_full = lax.all_gather(query_weight, "ctx", axis=0, tiled=True)
     even_flag = ((my_dp % 2) == 0).astype(jnp.int32).reshape(1)
-    pieces = spread_pieces(even_flag, gate_weight, up_weight, n)
+    below = jnp.stack(
+        [jnp.sum((segment_ids < s).astype(jnp.int32), axis=1) for s in range(5)], axis=1
+    )
+    code = 1
+    while code < n:
+        below = below + xor_permute(below, n, code)
+        code *= 2
+    starts = sum(jnp.where(segment_ids == s, below[:, s : s + 1], 0) for s in range(5))
+    start_columns = [starts[row].reshape(-1, 1) for row in range(row_count)]
+    kv_weights.mid()
+    pieces = spread_pieces(
+        even_flag, after(gate_weight, kv_weights.a, kv_weights.b, starts), up_weight, n
+    )
     spread = lax.all_to_all(pieces, "ctx", 0, 0)
+    kv_weights.near(pieces)
     gain_row = {
         "input": after(gain_input, pieces).reshape(1, -1),
         "query": after(gain_query, pieces).reshape(1, -1),
@@ -920,15 +939,6 @@
         "result": after(gain_result, pieces).reshape(1, -1),
     }
 
-    below = jnp.stack(
-        [jnp.sum((segment_ids < s).astype(jnp.int32), axis=1) for s in range(5)], axis=1
-    )
-    code = 1
-    while code < n:
-        below = below + xor_permute(below, n, code)
-        code *= 2
-    starts = sum(jnp.where(segment_ids == s, below[:, s : s + 1], 0) for s in range(5))
-
     offsets = jnp.arange(span, dtype=jnp.int32)
 
     def places_of(device):
@@ -945,21 +955,19 @@
     normed = normed_rows.reshape(total, width)
     order_codes = me ^ jnp.arange(n, dtype=jnp.int32)
     order = sum(jnp.where(order_codes == c, k, 0) for k, c in enumerate(codes)).astype(jnp.int32)
-    start_columns = [starts[row].reshape(-1, 1) for row in range(row_count)]
-    kv_weights.mid(pieces).near()
     kv_local, key_raw, kv_full = project_kv(
-        order, after(normed, spread), kv_weights.blocks, cosine, sine, gain_row["key"], row_count
+        order, normed, kv_weights.blocks, cosine, sine, gain_row["key"], row_count
     )
     kv_gather = Gather(kv_local, n)
     out_full = lax.all_gather(after(out_weight, kv_local), "ctx", axis=0, tiled=True)
     queries, query_raw = project_q(
         after(normed, kv_local), query_full, cosine, sine, gain_row["query"], head_count
     )
-    kv_gather.mid(queries, *start_columns, *gain_row.values(), key_places, place_column)
+    kv_gather.mid(spread, *start_columns, *gain_row.values(), key_places, place_column)
     swapped = lax.ppermute(
-        after(spread, kv_local), "dp", [(i, i ^ 1) for i in range(n_dp)]
-    )
-    kv_gather.near()
+        after(spread, kv_gather.a, kv_gather.b), "dp", [(i, i ^ 1) for i in range(n_dp)]
+    )
+    kv_gather.near(queries)
     kv_blocks = kv_gather.blocks
 
     def before_feed(row, *earlier):
@@ -1036,11 +1044,11 @@
     gate_mine, up_mine = in_order(even_flag, spread, swapped)
     gate_mine = gate_mine.reshape(width, share)
     up_mine = up_mine.reshape(width, share)
-    g0.near(gate_mine)
+    g0.near(gate_mine, g1.a, g1.b)
+    g1.mid(g0.blocks[0])
     blocks_0 = g0.flat()
     low_0 = [feed_piece(r0, blocks_0[0])]
-    g1.mid(low_0[0])
-    low_0 += pieces_of(feed_piece, r0, blocks_0[1:], low_0[0], g1.a)
+    low_0 += pieces_of(feed_piece, r0, blocks_0[1:], low_0[0])
     s0 = Scatter(low_0, n)
     g1.near(low_0[-1])
     blocks_1 = g1.flat()
@@ -1060,7 +1068,7 @@
     blocks_0 = h0.flat()
     d_in_0 = [back_piece(r0, blocks_0[0])]
     h1.mid(d_in_0[0])
-    d_in_0 += pieces_of(back_piece, r0, blocks_0[1:], d_in_0[0], h1.a)
+    d_in_0 += pieces_of(back_piece, r0, blocks_0[1:], d_in_0[0], h1.a, h1.b)
     s0 = Scatter(d_in_0, n)
     h1.near(d_in_0[-1])
     blocks_1 = h1.flat()
@@ -1104,17 +1112,15 @@
     s0.far(d_in_1[-1])
     grad_gate = over_rows("inner", "d_gate", *s0.sent)
     gate_pieces = exchange(grad_gate)
-    grad_up = over_rows("inner", "d_up", grad_gate)
-    s1.mid(grad_up)
-    clock[:] = [s1.sums]
-    attend_back(0, r0, s0.finish(*clock))
+    s1.mid(grad_gate)
+    attend_back(0, r0, s0.finish(s1.sums))
     s1.far(r0["d_kv"][0])
+    grad_up = over_rows("inner", "d_up", *s1.sent)
+    up_pieces = exchange(grad_up)
     gate_halves = halves(gate_pieces)
-    gl0 = begin(gate_halves[0], *s1.sent)
-    gl1 = begin(gate_halves[1], *clock)
-    up_pieces = exchange(after(grad_up, *clock))
+    gl0 = begin(gate_halves[0], grad_up)
     attend_back(1, r1, s1.finish(summed_down, *clock))
-    clock[:] = [r1["d_kv"][0]]
+    gl1 = begin(gate_halves[1], r1["d_kv"][0])
     step(gl0)
     kv_scatter = Scatter(
         [jnp.stack([a, b], axis=1) for a, b in zip(r0["d_kv"], r1["d_kv"])], n
@@ -1160,6 +1166,9 @@
     )
     clock[:] = [d_kvs[0]]
     step(gl0)
+    step(u0)
+    step(gl1)
+    u1 = begin(up_halves[1], *clock)
     grad_qkv = blocks_grad(
         order,
         [
@@ -1170,16 +1179,10 @@
         n,
     )
     qkv_scatter = Scatter(grad_qkv, n)
-    clock[:] = [grad_qkv[0]]
-    step(u0)
-    u1 = begin(up_halves[1], *clock)
-    step(gl1)
-    qkv_scatter.mid(*clock)
-    clock[:] = [qkv_scatter.sums]
-    land(gl0)
+    qkv_scatter.mid(grad_qkv[0])
     tokens_grad, grad_input_gain = close_tokens(
         tokens,
-        [after(r["d_query_raw"], *clock) for r in rows],
+        [after(r["d_query_raw"], qkv_scatter.sums) for r in rows],
         d_kvs,
         query_full,
         kv_full,
@@ -1199,25 +1202,30 @@
         axis=1,
     ).reshape(-1, 128)
     clock[:] = [*qkv_scatter.sent]
+    gains = after(gains, *clock)
+    land(gl0)
     step(u1)
     step(u0)
+    summed_down = after(summed_down, *clock).astype(WIDE)
+    result = after(jnp.stack([r["result"] for r in rows]), *clock)
+    clock[:] = [summed_down, result]
     part_qkv = total_of(qkv_scatter.finish(*clock))
     clock[:] = [part_qkv]
     qkv_line = begin(part_qkv, *clock)
     land(gl1)
     out_line = begin(part_out, *clock)
     code = 1
-    gains = after(gains, *clock)
     while code < n:
         gains = gains + xor_permute(gains, n, code)
         code *= 2
-    clock[:] = [gains]
-    gain_line = begin(gains, *clock)
+    step(qkv_line)
     step(u1)
     land(u0)
+    step(out_line)
+    gain_line = begin(gains, *clock)
     step(qkv_line)
+    step(gain_line)
     step(out_line)
-    step(gain_line)
     for _ in range(n_dp):
         for line in (gl0, gl1, u0, u1, qkv_line, out_line, gain_line):
             step(line)
@@ -1233,7 +1241,7 @@
         gain_grads.append(gains[start : start + size])
         start += size
     return (
-        jnp.stack([r["result"] for r in rows]),
+        result,
         tokens_grad,
         summed_qkv[:, :qw],
         summed_qkv[:, qw : qw + head_width],
@@ -1241,7 +1249,7 @@
         summed_out,
         summed_gate,
         summed_up,
-        summed_down.astype(WIDE),
+        summed_down,
         *gain_grads,
     )
 

time: 647 us -> 611 us (0.944)
  waiting for transfers between devices: 226 us -> 191 us
  local copies, waits for them, and re-layouts: 89.3 us -> 78.1 us
  Pallas kernels: 137 us -> 147 us
    ppermute x66, waiting for transfers between devices: 154 us -> 128 us  [xor_permute(): return lax.ppermute(x, 'ctx', [(i, i ^ code) for i in range(axis_size)])]
    unnamed x355 -> x313, local copies, waits for them, and re-layouts: 74.4 us -> 61.9 us
    ppermute x21, waiting for transfers between devices: 45.4 us -> 36 us  [send(): self.moved = lax.ppermute(self.total, 'dp', self.steps[self.at][1])]
  transfers between devices with their start and end apart: 95 -> 95, of which waited for: 51 -> 48; matrix products, arithmetic and copies ran while one was open for 9% -> 10% of each run, Pallas kernels for 14% -> 17%
where the time goes in v3:
time: 611 us; the launch traced here: 605 us
  waiting for transfers between devices  191 us (31%)
  Pallas kernels  147 us (24%)
  starting transfers between devices  126 us (21%)
  local copies, waits for them, and re-layouts  78.1 us (13%)
  other arithmetic  43.2 us (7%)
  between operations  16.3 us (3%)
    ppermute x66, waiting for transfers between devices, xor_permute(): return lax.ppermute(x, 'ctx', [(i, i ^ code) for i in range(axis_size)])  128 us
    ppermute x66, starting transfers between devices, xor_permute(): return lax.ppermute(x, 'ctx', [(i, i ^ code) for i in range(axis_size)])  62.5 us
    unnamed x313, local copies, waits for them, and re-layouts  61.9 us
    ppermute x21, starting transfers between devices, send(): self.moved = lax.ppermute(self.total, 'dp', self.steps[self.at][1])  47.7 us
    ppermute x21, waiting for transfers between devices, send(): self.moved = lax.ppermute(self.total, 'dp', self.steps[self.at][1])  36 us
    pallas_call x4, Pallas kernels, feed_backward(): vmem_call(kernel, (hidden, hidden, jax.ShapeDtypeStruct((tokens, width),...  29 us
    pallas_call x4, Pallas kernels, feed_forward(): vmem_call(kernel, (hidden, hidden, hidden, jax.ShapeDtypeStruct((tokens,...  27.7 us
    pallas_call x3, Pallas kernels, weight_grad(): vmem_call(kernel, jax.ShapeDtypeStruct((rows, columns), BF16), limit=24,...  24.1 us
  transfers between devices with their start and end apart: 95, of which 48 were waited for; matrix products, arithmetic and copies ran while one was open for 10% of the time, Pallas kernels for 17%

profile of v3, /device:TPU:0, one launch (start us, length us, event | category | flops | bytes accessed | tf_op | source)
XLA Modules:
  0.0 604.9 jit_solution(205808545317584389)
XLA Ops:
  9.8 2.9 collective-permute-start
  18.4 3.0 collective-permute-done.3
  22.0 3.1 collective-permute-done.4
  32.4 2.2 shard_map.273
  36.4 4.4 all-to-all-start
  45.4 36.6 %collective-permute-done.8.a_ref = bf16[2,192,512]{2,1,0:T(8,128)(2,1)S(1)} collective-permute-done((bf16[2,192,512]{2,1,0:T(8,128)(2,1)}, bf16[2,192,512]{2,1,0:T(8,128)(2,1)S(1)}, u32[]{:S(2)}, u32[]{:S(2)}) %collective-permute-start.8) | collective-permute-done | bytes 393248 | tf_op jit(solution)/shard_map/ppermute | solution.py:63
  97.1 7.2 %shard_map.276 = (bf16[192,1024]{1,0:T(8,128)(2,1)S(1)}, f32[192,4]{1,0:T(8,128)S(1)}, f32[192,1152]{1,0:T(8,128)S(1)}, f32[192,1152]{1,0:T(8,128)S(1)}, bf16[192,1152]{1,0:T(8,128)(2,1)}) custom-call(bf16[384,1024]{1,0:T(8,128)(2,1)S(1)} %get-tuple-element.220.refs_0_.refs_9_, s32[192,1]{1,0:T(8,128)S(1)} %copy.57.refs_1_.refs_10_, ...), custom_call_target="tpu_custom_call" | custom-call | tf_op jit(solution)/shard_map/pallas_call | solution.py:376
  110.0 6.5 %shard_map.277 = (bf16[192,1024]{1,0:T(8,128)(2,1)S(1)}, f32[192,4]{1,0:T(8,128)S(1)}, f32[192,1152]{1,0:T(8,128)S(1)}, f32[192,1152]{1,0:T(8,128)S(1)}, bf16[192,1152]{1,0:T(8,128)(2,1)S(1)}) custom-call(bf16[384,1024]{1,0:T(8,128)(2,1)S(1)} %get-tuple-element.220.refs_0_.refs_9_, s32[192,1]{1,0:T(8,128)S(1)} %copy.59.refs_1_.refs_10_, ...), custom_call_target="tpu_custom_call" | custom-call | tf_op jit(solution)/shard_map/pallas_call | solution.py:376
  126.6 14.7 %collective-permute-done.17.second_ref = bf16[8,144,864]{2,1,0:T(8,128)(2,1)} collective-permute-done((bf16[8,144,864]{2,1,0:T(8,128)(2,1)}, bf16[8,144,864]{2,1,0:T(8,128)(2,1)}, u32[]{:S(2)}, u32[]{:S(2)}) %collective-permute-start.17) | collective-permute-done | bytes 1990688 | tf_op jit(solution)/shard_map/ppermute | solution.py:967
  141.2 5.1 shard_map.278
  146.4 2.2 shard_map.279
  149.1 6.8 %shard_map.280 = (bf16[768,864]{1,0:T(8,128)(2,1)S(1)}, bf16[768,864]{1,0:T(8,128)(2,1)S(1)}, bf16[768,864]{1,0:T(8,128)(2,1)S(1)}, bf16[768,1152]{1,0:T(8,128)(2,1)S(1)}) custom-call(bf16[768,1152]{1,0:T(8,128)(2,1)S(1)} %bitcast.189, bf16[1152,864]{1,0:T(8,128)(2,1)S(1)} %bitcast.173, bf16[1152,864]{1,0:T(8,128)(2,1)S(1)} %bitcast.181, ...), custom_call_target="tpu_custom_call" | custom-call | tf_op jit(solution)/shard_map/pallas_call | solution.py:712
  156.0 6.8 %shard_map.281 = (bf16[768,864]{1,0:T(8,128)(2,1)S(1)}, bf16[768,864]{1,0:T(8,128)(2,1)S(1)}, bf16[768,864]{1,0:T(8,128)(2,1)S(1)}, bf16[768,1152]{1,0:T(8,128)(2,1)S(1)}) custom-call(bf16[768,1152]{1,0:T(8,128)(2,1)S(1)} %bitcast.195, bf16[1152,864]{1,0:T(8,128)(2,1)S(1)} %bitcast.174, bf16[1152,864]{1,0:T(8,128)(2,1)S(1)} %bitcast.182, ...), custom_call_target="tpu_custom_call" | custom-call | tf_op jit(solution)/shard_map/pallas_call | solution.py:712
  165.5 5.3 collective-permute-done.22.d1_ref
  171.5 6.8 %shard_map.283 = (bf16[768,864]{1,0:T(8,128)(2,1)S(1)}, bf16[768,864]{1,0:T(8,128)(2,1)S(1)}, bf16[768,864]{1,0:T(8,128)(2,1)S(1)}, bf16[768,1152]{1,0:T(8,128)(2,1)S(1)}) custom-call(bf16[768,1152]{1,0:T(8,128)(2,1)S(1)} %bitcast.192, bf16[1152,864]{1,0:T(8,128)(2,1)S(1)} %bitcast.175, bf16[1152,864]{1,0:T(8,128)(2,1)S(1)} %bitcast.183, ...), custom_call_target="tpu_custom_call" | custom-call | tf_op jit(solution)/shard_map/pallas_call | solution.py:712
  179.9 7.2 %shard_map.284 = (bf16[768,864]{1,0:T(8,128)(2,1)S(1)}, bf16[768,864]{1,0:T(8,128)(2,1)S(1)}, bf16[768,864]{1,0:T(8,128)(2,1)S(1)}, bf16[768,1152]{1,0:T(8,128)(2,1)S(1)}) custom-call(bf16[768,1152]{1,0:T(8,128)(2,1)S(1)} %bitcast.198, bf16[1152,864]{1,0:T(8,128)(2,1)S(1)} %bitcast.176, bf16[1152,864]{1,0:T(8,128)(2,1)S(1)} %bitcast.184, ...), custom_call_target="tpu_custom_call" | custom-call | tf_op jit(solution)/shard_map/pallas_call | solution.py:712
  189.9 5.2 collective-permute-done.24
  201.6 8.3 %collective-permute-done.28.c_ref = bf16[192,1152]{1,0:T(8,128)(2,1)S(1)} collective-permute-done((bf16[192,1152]{1,0:T(8,128)(2,1)S(1)}, bf16[192,1152]{1,0:T(8,128)(2,1)S(1)}, u32[]{:S(2)}, u32[]{:S(2)}) %collective-permute-start.28) | collective-permute-done | bytes 442400 | tf_op jit(solution)/shard_map/ppermute | solution.py:63
  217.5 7.2 %collective-permute-done.34.a_ref = bf16[192,1152]{1,0:T(8,128)(2,1)S(1)} collective-permute-done((bf16[192,1152]{1,0:T(8,128)(2,1)S(1)}, bf16[192,1152]{1,0:T(8,128)(2,1)S(1)}, u32[]{:S(2)}, u32[]{:S(2)}) %collective-permute-start.34) | collective-permute-done | bytes 442400 | tf_op jit(solution)/shard_map/ppermute | solution.py:63
  228.2 5.6 collective-permute-done.33.c_ref
  239.0 7.0 %shard_map.288 = (bf16[768,864]{1,0:T(8,128)(2,1)S(1)}, bf16[768,864]{1,0:T(8,128)(2,1)S(1)}, bf16[768,1152]{1,0:T(8,128)(2,1)S(1)}) custom-call(bf16[768,1152]{1,0:T(8,128)(2,1)S(1)} %bitcast.201, bf16[768,864]{1,0:T(8,128)(2,1)S(1)} %get-tuple-element.260.slope_ref, bf16[768,864]{1,0:T(8,128)(2,1)S(1)} %get-tuple-element.261.value_ref, ...), custom_call_target="tpu_custom_call" | custom-call | tf_op jit(solution)/shard_map/pallas_call | solution.py:739
  246.0 3.3 collective-permute-done.35.a_ref
  250.3 7.0 %shard_map.289 = (bf16[768,864]{1,0:T(8,128)(2,1)S(1)}, bf16[768,864]{1,0:T(8,128)(2,1)S(1)}, bf16[768,1152]{1,0:T(8,128)(2,1)S(1)}) custom-call(bf16[768,1152]{1,0:T(8,128)(2,1)S(1)} %bitcast.208, bf16[768,864]{1,0:T(8,128)(2,1)S(1)} %get-tuple-element.266.slope_ref, bf16[768,864]{1,0:T(8,128)(2,1)S(1)} %get-tuple-element.267.value_ref, ...), custom_call_target="tpu_custom_call" | custom-call | tf_op jit(solution)/shard_map/pallas_call | solution.py:739
  259.9 5.4 collective-permute-done.40.d1_ref
  266.3 7.2 %shard_map.291 = (bf16[768,864]{1,0:T(8,128)(2,1)S(1)}, bf16[768,864]{1,0:T(8,128)(2,1)S(1)}, bf16[768,1152]{1,0:T(8,128)(2,1)S(1)}) custom-call(bf16[768,1152]{1,0:T(8,128)(2,1)S(1)} %bitcast.203, bf16[768,864]{1,0:T(8,128)(2,1)S(1)} %get-tuple-element.271.slope_ref, bf16[768,864]{1,0:T(8,128)(2,1)S(1)} %get-tuple-element.272.value_ref, ...), custom_call_target="tpu_custom_call" | custom-call | tf_op jit(solution)/shard_map/pallas_call | solution.py:739
  277.9 7.6 %shard_map.292 = bf16[864,1152]{1,0:T(8,128)(2,1)S(1)} custom-call(bf16[768,864]{1,0:T(8,128)(2,1)S(1)} %copy-done.70, bf16[768,864]{1,0:T(8,128)(2,1)S(1)} %copy-done.72, bf16[768,864]{1,0:T(8,128)(2,1)S(1)} %copy-done.74, bf16[768,864]{1,0:T(8,128)(2,1)S(1)} %copy-done.76, bf16[768,1152]{1,0:T(8,128)(2,1)S(1)} %bitcast.202, ...), custom_call_target="tpu_custom_call" | custom-call | tf_op jit(solution)/shard_map/pallas_call | solution.py:767
  294.0 7.8 %shard_map.293 = (bf16[768,864]{1,0:T(8,128)(2,1)S(1)}, bf16[768,864]{1,0:T(8,128)(2,1)S(1)}, bf16[768,1152]{1,0:T(8,128)(2,1)}) custom-call(bf16[768,1152]{1,0:T(8,128)(2,1)S(1)} %bitcast.211, bf16[768,864]{1,0:T(8,128)(2,1)S(1)} %get-tuple-element.281.slope_ref, bf16[768,864]{1,0:T(8,128)(2,1)S(1)} %copy-done.52, bf16[1152,864]{1,0:T(8,128)(2,1)S(1)} %bitcast.180, ...), custom_call_target="tpu_custom_call" | custom-call | tf_op jit(solution)/shard_map/pallas_call | solution.py:739
  306.2 5.9 collective-permute-done.46
  328.5 7.5 %shard_map.294 = bf16[1152,864]{1,0:T(8,128)(2,1)S(1)} custom-call(bf16[768,1152]{1,0:T(8,128)(2,1)S(1)} %bitcast.190, bf16[768,1152]{1,0:T(8,128)(2,1)S(1)} %bitcast.196, bf16[768,1152]{1,0:T(8,128)(2,1)S(1)} %bitcast.193, bf16[768,1152]{1,0:T(8,128)(2,1)S(1)} %bitcast.199, bf16[768,864]{1,0:T(8,128)(2,1)S(1)} %copy-done.62, ...), custom_call_target="tpu_custom_call" | custom-call | tf_op jit(solution)/shard_map/pallas_call | solution.py:767
  337.3 4.8 all-to-all-start.2
  342.1 2.5 add_convert_fusion.1.refs_0_
  348.2 11.1 %shard_map.295 = (f32[192,1152]{1,0:T(8,128)S(1)}, bf16[192,1152]{1,0:T(8,128)(2,1)S(1)}, f32[1,1152]{1,0:T(1,128)S(1)}, f32[1,1152]{1,0:T(1,128)S(1)}, bf16[192...) custom-call(bf16[4,192,1152]{2,1,0:T(8,128)(2,1)} %add_convert_fusio, ...), custom_call_target="tpu_custom_call" | custom-call | tf_op jit(solution)/shard_map/pallas_call | solution.py:549
  365.2 6.5 %collective-permute-done.48 = bf16[96,1152]{1,0:T(8,128)(2,1)S(1)} collective-permute-done((bf16[96,1152]{1,0:T(8,128)(2,1)S(1)}, bf16[96,1152]{1,0:T(8,128)(2,1)S(1)}, u32[]{:S(2)}, u32[]{:S(2)}) %collective-permute-start.48) | collective-permute-done | bytes 221216 | tf_op jit(solution)/shard_map/ppermute | solution.py:63
  375.5 3.2 fusion.35
  384.0 9.0 %shard_map.296 = bf16[1152,864]{1,0:T(8,128)(2,1)} custom-call(bf16[768,1152]{1,0:T(8,128)(2,1)S(1)} %bitcast.191, bf16[768,1152]{1,0:T(8,128)(2,1)S(1)} %bitcast.197, bf16[768,1152]{1,0:T(8,128)(2,1)S(1)} %bitcast.194, bf16[768,1152]{1,0:T(8,128)(2,1)S(1)} %bitcast.200, bf16[768,864]{1,0:T(8,128)(2,1)S(1)} %copy-done.54, bf16[768,864]{1,0:T(8,128)(2,1)S(1)} %copy-done.56, ...), custom_call_target="tpu_custom_call" | custom-call | tf_op jit(solution)/shard_map/pallas_call | solution.py:767
  393.0 3.5 collective-permute-start.55
  403.6 11.1 %shard_map.297 = (f32[192,1152]{1,0:T(8,128)S(1)}, bf16[192,1152]{1,0:T(8,128)(2,1)S(1)}, f32[1,1152]{1,0:T(1,128)S(1)}, f32[1,1152]{1,0:T(1,128)S(1)}, bf16[192...) custom-call(bf16[4,192,1152]{2,1,0:T(8,128)(2,1)} %copy-done.142, ...), custom_call_target="tpu_custom_call" | custom-call | tf_op jit(solution)/shard_map/pallas_call | solution.py:549
  416.4 4.5 all-to-all-start.1
  421.0 2.3 collective-permute-start.62
  424.2 2.5 add_convert_fusion.13
  428.3 2.3 fusion
  430.6 2.1 add_convert_fusion.5.a_ref
  436.2 11.6 %all-to-all-done.1 = bf16[8,144,864]{2,1,0:T(8,128)(2,1)} async-done(((bf16[8,144,864]{2,1,0:T(8,128)(2,1)}), bf16[8,144,864]{2,1,0:T(8,128)(2,1)}, u32[]{:S(2)}, u32[]{:S(2)}) %all-to-all-start.1) | async-done | bytes 1990688 | tf_op jit(solution)/shard_map/all_to_all | solution.py:1106
  447.7 2.7 fusion.34
  456.1 5.2 collective-permute-done.61.c_ref
  464.9 5.7 collective-permute-done.56
  472.8 5.6 shard_map.299
  482.7 12.2 %collective-permute-start.65 = (bf16[4,144,864]{2,1,0:T(8,128)(2,1)}, bf16[4,144,864]{2,1,0:T(8,128)(2,1)S(1)}, u32[]{:S(2)}, u32[]{:S(2)}) collective-permute-start(bf16[4,144,864]{2,1,0:T(8,128)(2,1)} %get-tuple-element.332), channel_id=1, source_target_pairs={{0,8},{24,16},{1,9},{25,17},{2,10},{26,18},{3,11},{27,19},{4,12},{... | collective-permute-start | bytes 2985992 | tf_op jit(solution)/shard_map/ppermute | solution.py:162
  494.9 2.8 add_convert_fusion
  500.1 3.6 shard_map.300
  508.5 4.5 collective-permute-done.66.refs_2_
  514.3 3.3 collective-permute-done.65
  522.2 2.2 convert_element_type.358
  525.5 5.8 collective-permute-start.72
  533.9 2.5 collective-permute-done.76
  538.1 2.1 collective-permute-done.77
  545.1 2.8 add_convert_fusion.6.refs_1_
  549.2 8.1 %collective-permute-done.79.refs_2_ = bf16[4,144,864]{2,1,0:T(8,128)(2,1)} collective-permute-done((bf16[4,144,864]{2,1,0:T(8,128)(2,1)S(1)}, bf16[4,144,864]{2,1,0:T(8,128)(2,1)}, u32[]{:S(2)}, u32[]{:S(2)}) %collective-permute-start.79) | collective-permute-done | bytes 995360 | tf_op jit(solution)/shard_map/ppermute | solution.py:162
  558.1 4.5 collective-permute-start.83
  573.5 2.4 shard_map.301
  575.9 3.5 collective-permute-done.86.refs_3_
  579.4 4.3 shard_map.302
  583.7 2.0 collective-permute-done.84
  587.5 7.6 %collective-permute-done.81 = bf16[144,1536]{1,0:T(8,128)(2,1)S(1)} collective-permute-done((bf16[144,1536]{1,0:T(8,128)(2,1)S(1)}, bf16[144,1536]{1,0:T(8,128)(2,1)S(1)}, u32[]{:S(2)}, u32[]{:S(2)}) %collective-permute-start.81) | collective-permute-done | bytes 442400 | tf_op jit(solution)/shard_map/ppermute | solution.py:162
  (597 shorter events, 212.8 us)
Async XLA Ops:
  7.2 78.1 %all-gather.3.cloned.1.call-start = ((), (), s32[]{:S(2)}) async-start(), calls=%async_computation.4 | async-start | bytes 2654208 | tf_op jit(solution)/shard_map/all_gather | solution.py:916
  7.9 87.7 %all-gather.5.cloned.1.call-start = ((), (), s32[]{:S(2)}) async-start(), calls=%async_computation.5 | async-start | bytes 2654208 | tf_op jit(solution)/shard_map/all_gather | solution.py:962
  9.8 15.5 %collective-permute-start = (bf16[144,512]{1,0:T(8,128)(2,1)S(1)}, bf16[144,512]{1,0:T(8,128)(2,1)S(1)}, u32[]{:S(2)}, u32[]{:S(2)}) collective-permute-start(bf16[144,512]{1,0:T(8,128)(2,1)S(1)} %constant_dynamic-update-slice_fusion.x_ref), channel_id=1, source_target_pairs={{0,2},{1,3},{2,0},{3,1},{4,6},{5,7},{6,4},{7,5},{8,10},{9,11},{10,... | collective-permute-start | bytes 442376 | tf_op jit(solution)/shard_map/ppermute | solution.py:63
  12.7 12.6 %collective-permute-start.1 = (bf16[144,512]{1,0:T(8,128)(2,1)S(1)}, bf16[144,512]{1,0:T(8,128)(2,1)S(1)}, u32[]{:S(2)}, u32[]{:S(2)}) collective-permute-start(bf16[144,512]{1,0:T(8,128)(2,1)S(1)} %constant_dynamic-update-slice_fusion.x_ref), channel_id=1, source_target_pairs={{0,4},{1,5},{2,6},{3,7},{4,0},{5,1},{6,2},{7,3},{8,12},{9,13},{10,... | collective-permute-start | bytes 442376 | tf_op jit(solution)/shard_map/ppermute | solution.py:63
  36.4 45.5 %all-to-all-start = ((bf16[8,144,864]{2,1,0:T(8,128)(2,1)}), bf16[8,144,864]{2,1,0:T(8,128)(2,1)}, u32[]{:S(2)}, u32[]{:S(2)}) async-start(bf16[8,144,864]{2,1,0:T(8,128)(2,1)} %copy-done.25), calls=%async_computation | async-start | bytes 4128768 | tf_op jit(solution)/shard_map/all_to_all | solution.py:931
  40.8 355.7 %all-reduce.2.cloned.1.call-start = ((), (), s32[]{:S(2)}) async-start(), calls=%async_computation.6 | async-start | bytes 3981312 | tf_op jit(solution)/shard_map/psum | solution.py:1109
  41.1 40.8 %collective-permute-start.8 = (bf16[2,192,512]{2,1,0:T(8,128)(2,1)}, bf16[2,192,512]{2,1,0:T(8,128)(2,1)S(1)}, u32[]{:S(2)}, u32[]{:S(2)}) collective-permute-start(bf16[2,192,512]{2,1,0:T(8,128)(2,1)} %get-tuple-element.206.x_ref), channel_id=1, source_target_pairs={{0,2},{1,3},{2,0},{3,1},{4,6},{5,7},{6,4},{7,5},{8,10},{9,11},{10,... | collective-permute-start | bytes 1179656 | tf_op jit(solution)/shard_map/ppermute | solution.py:63
  43.1 38.9 %collective-permute-start.9 = (bf16[2,192,512]{2,1,0:T(8,128)(2,1)}, bf16[2,192,512]{2,1,0:T(8,128)(2,1)S(1)}, u32[]{:S(2)}, u32[]{:S(2)}) collective-permute-start(bf16[2,192,512]{2,1,0:T(8,128)(2,1)} %get-tuple-element.206.x_ref), channel_id=1, source_target_pairs={{0,4},{1,5},{2,6},{3,7},{4,0},{5,1},{6,2},{7,3},{8,12},{9,13},{10,... | collective-permute-start | bytes 1179656 | tf_op jit(solution)/shard_map/ppermute | solution.py:63
  93.6 47.7 %collective-permute-start.17 = (bf16[8,144,864]{2,1,0:T(8,128)(2,1)}, bf16[8,144,864]{2,1,0:T(8,128)(2,1)}, u32[]{:S(2)}, u32[]{:S(2)}) collective-permute-start(bf16[8,144,864]{2,1,0:T(8,128)(2,1)} %all-to-all-done.first_ref), channel_id=1, source_target_pairs={{0,8},{8,0},{16,24},{24,16},{1,9},{9,1},{17,25},{25,17},{2,10},{10... | collective-permute-start | bytes 5971976 | tf_op jit(solution)/shard_map/ppermute | solution.py:967
  107.5 12.5 %collective-permute-start.13 = (bf16[192,1152]{1,0:T(8,128)(2,1)}, bf16[192,1152]{1,0:T(8,128)(2,1)}, u32[]{:S(2)}, u32[]{:S(2)}) collective-permute-start(bf16[192,1152]{1,0:T(8,128)(2,1)} %get-tuple-element.219.x_ref), channel_id=1, source_target_pairs={{0,2},{1,3},{2,0},{3,1},{4,6},{5,7},{6,4},{7,5},{8,10},{9,11},{10,... | collective-permute-start | bytes 1327112 | tf_op jit(solution)/shard_map/ppermute | solution.py:63
  108.2 12.2 %collective-permute-start.14 = (bf16[192,1152]{1,0:T(8,128)(2,1)}, bf16[192,1152]{1,0:T(8,128)(2,1)}, u32[]{:S(2)}, u32[]{:S(2)}) collective-permute-start(bf16[192,1152]{1,0:T(8,128)(2,1)} %get-tuple-element.219.x_ref), channel_id=1, source_target_pairs={{0,4},{1,5},{2,6},{3,7},{4,0},{5,1},{6,2},{7,3},{8,12},{9,13},{10,... | collective-permute-start | bytes 1327112 | tf_op jit(solution)/shard_map/ppermute | solution.py:63
  120.5 25.9 %collective-permute-start.18 = (bf16[192,1152]{1,0:T(8,128)(2,1)S(1)}, bf16[192,1152]{1,0:T(8,128)(2,1)S(1)}, u32[]{:S(2)}, u32[]{:S(2)}) collective-permute-start(bf16[192,1152]{1,0:T(8,128)(2,1)S(1)} %get-tuple-element.226.x_ref), channel_id=1, source_target_pairs={{0,2},{1,3},{2,0},{3,1},{4,6},{5,7},{6,4},{7,5},{8,10},{9,11},{10,... | collective-permute-start | bytes 1327112 | tf_op jit(solution)/shard_map/ppermute | solution.py:63
  121.8 24.6 %collective-permute-start.19 = (bf16[192,1152]{1,0:T(8,128)(2,1)S(1)}, bf16[192,1152]{1,0:T(8,128)(2,1)S(1)}, u32[]{:S(2)}, u32[]{:S(2)}) collective-permute-start(bf16[192,1152]{1,0:T(8,128)(2,1)S(1)} %get-tuple-element.226.x_ref), channel_id=1, source_target_pairs={{0,4},{1,5},{2,6},{3,7},{4,0},{5,1},{6,2},{7,3},{8,12},{9,13},{10,... | collective-permute-start | bytes 1327112 | tf_op jit(solution)/shard_map/ppermute | solution.py:63
  123.3 23.1 %collective-permute-start.15 = (bf16[96,1152]{1,0:T(8,128)(2,1)S(1)}, bf16[96,1152]{1,0:T(8,128)(2,1)S(1)}, u32[]{:S(2)}, u32[]{:S(2)}) collective-permute-start(bf16[96,1152]{1,0:T(8,128)(2,1)S(1)} %slice.404), channel_id=1, source_target_pairs={{0,4},{1,5},{2,6},{3,7},{4,0},{5,1},{6,2},{7,3},{8,12},{9,13},{10,... | collective-permute-start | bytes 663560 | tf_op jit(solution)/shard_map/ppermute | solution.py:63
  125.8 20.6 %collective-permute-start.16 = (bf16[96,1152]{1,0:T(8,128)(2,1)S(1)}, bf16[96,1152]{1,0:T(8,128)(2,1)S(1)}, u32[]{:S(2)}, u32[]{:S(2)}) collective-permute-start(bf16[96,1152]{1,0:T(8,128)(2,1)S(1)} %slice.405), channel_id=1, source_target_pairs={{0,2},{1,3},{2,0},{3,1},{4,6},{5,7},{6,4},{7,5},{8,10},{9,11},{10,... | collective-permute-start | bytes 663560 | tf_op jit(solution)/shard_map/ppermute | solution.py:63
  162.8 16.6 %collective-permute-start.21 = (bf16[4,192,1152]{2,1,0:T(8,128)(2,1)S(1)}, bf16[4,192,1152]{2,1,0:T(8,128)(2,1)S(1)}, u32[]{:S(2)}, u32[]{:S(2)}) collective-permute-start(bf16[4,192,1152]{2,1,0:T(8,128)(2,1)S(1)} %bitcast.224), channel_id=1, source_target_pairs={{0,1},{1,0},{2,3},{3,2},{4,5},{5,4},{6,7},{7,6},{8,9},{9,8},{10,11... | collective-permute-start | bytes 5308424 | tf_op jit(solution)/shard_map/ppermute | solution.py:63
  187.1 11.6 %collective-permute-start.29 = (bf16[4,192,1152]{2,1,0:T(8,128)(2,1)S(1)}, bf16[4,192,1152]{2,1,0:T(8,128)(2,1)S(1)}, u32[]{:S(2)}, u32[]{:S(2)}) collective-permute-start(bf16[4,192,1152]{2,1,0:T(8,128)(2,1)S(1)} %bitcast.222), channel_id=1, source_target_pairs={{0,1},{1,0},{2,3},{3,2},{4,5},{5,4},{6,7},{7,6},{8,9},{9,8},{10,11... | collective-permute-start | bytes 5308424 | tf_op jit(solution)/shard_map/ppermute | solution.py:63
  196.8 13.2 %collective-permute-start.28 = (bf16[192,1152]{1,0:T(8,128)(2,1)S(1)}, bf16[192,1152]{1,0:T(8,128)(2,1)S(1)}, u32[]{:S(2)}, u32[]{:S(2)}) collective-permute-start(bf16[192,1152]{1,0:T(8,128)(2,1)S(1)} %pad_maximum_fusion.3), channel_id=1, source_target_pairs={{0,4},{1,5},{2,6},{3,7},{4,0},{5,1},{6,2},{7,3},{8,12},{9,13},{10,... | collective-permute-start | bytes 1327112 | tf_op jit(solution)/shard_map/ppermute | solution.py:63
  197.3 13.2 %collective-permute-start.27 = (bf16[192,1152]{1,0:T(8,128)(2,1)S(1)}, bf16[192,1152]{1,0:T(8,128)(2,1)S(1)}, u32[]{:S(2)}, u32[]{:S(2)}) collective-permute-start(bf16[192,1152]{1,0:T(8,128)(2,1)S(1)} %pad_maximum_fusion.2), channel_id=1, source_target_pairs={{0,2},{1,3},{2,0},{3,1},{4,6},{5,7},{6,4},{7,5},{8,10},{9,11},{10,... | collective-permute-start | bytes 1327112 | tf_op jit(solution)/shard_map/ppermute | solution.py:63
  199.2 16.0 %collective-permute-start.30 = (bf16[96,1152]{1,0:T(8,128)(2,1)S(1)}, bf16[96,1152]{1,0:T(8,128)(2,1)S(1)}, u32[]{:S(2)}, u32[]{:S(2)}) collective-permute-start(bf16[96,1152]{1,0:T(8,128)(2,1)S(1)} %get-tuple-element.421), channel_id=1, source_target_pairs={{0,2},{1,3},{2,0},{3,1},{4,6},{5,7},{6,4},{7,5},{8,10},{9,11},{10,... | collective-permute-start | bytes 663560 | tf_op jit(solution)/shard_map/ppermute | solution.py:63
  200.0 15.2 %collective-permute-start.31 = (bf16[96,1152]{1,0:T(8,128)(2,1)S(1)}, bf16[96,1152]{1,0:T(8,128)(2,1)S(1)}, u32[]{:S(2)}, u32[]{:S(2)}) collective-permute-start(bf16[96,1152]{1,0:T(8,128)(2,1)S(1)} %get-tuple-element.420), channel_id=1, source_target_pairs={{0,4},{1,5},{2,6},{3,7},{4,0},{5,1},{6,2},{7,3},{8,12},{9,13},{10,... | collective-permute-start | bytes 663560 | tf_op jit(solution)/shard_map/ppermute | solution.py:63
  211.2 13.5 %collective-permute-start.34 = (bf16[192,1152]{1,0:T(8,128)(2,1)S(1)}, bf16[192,1152]{1,0:T(8,128)(2,1)S(1)}, u32[]{:S(2)}, u32[]{:S(2)}) collective-permute-start(bf16[192,1152]{1,0:T(8,128)(2,1)S(1)} %get-tuple-element.248.x_ref), channel_id=1, source_target_pairs={{0,2},{1,3},{2,0},{3,1},{4,6},{5,7},{6,4},{7,5},{8,10},{9,11},{10,... | collective-permute-start | bytes 1327112 | tf_op jit(solution)/shard_map/ppermute | solution.py:63
  212.6 13.1 %collective-permute-start.37 = (bf16[192,1152]{1,0:T(8,128)(2,1)S(1)}, bf16[192,1152]{1,0:T(8,128)(2,1)S(1)}, u32[]{:S(2)}, u32[]{:S(2)}) collective-permute-start(bf16[192,1152]{1,0:T(8,128)(2,1)S(1)} %get-tuple-element.248.x_ref), channel_id=1, source_target_pairs={{0,4},{1,5},{2,6},{3,7},{4,0},{5,1},{6,2},{7,3},{8,12},{9,13},{10,... | collective-permute-start | bytes 1327112 | tf_op jit(solution)/shard_map/ppermute | solution.py:63
  215.4 18.5 %collective-permute-start.33 = (bf16[192,1152]{1,0:T(8,128)(2,1)S(1)}, bf16[192,1152]{1,0:T(8,128)(2,1)S(1)}, u32[]{:S(2)}, u32[]{:S(2)}) collective-permute-start(bf16[192,1152]{1,0:T(8,128)(2,1)S(1)} %pad_maximum_fusion.5), channel_id=1, source_target_pairs={{0,4},{1,5},{2,6},{3,7},{4,0},{5,1},{6,2},{7,3},{8,12},{9,13},{10,... | collective-permute-start | bytes 1327112 | tf_op jit(solution)/shard_map/ppermute | solution.py:63
  217.1 17.0 %collective-permute-start.32 = (bf16[192,1152]{1,0:T(8,128)(2,1)S(1)}, bf16[192,1152]{1,0:T(8,128)(2,1)S(1)}, u32[]{:S(2)}, u32[]{:S(2)}) collective-permute-start(bf16[192,1152]{1,0:T(8,128)(2,1)S(1)} %pad_maximum_fusion.4), channel_id=1, source_target_pairs={{0,2},{1,3},{2,0},{3,1},{4,6},{5,7},{6,4},{7,5},{8,10},{9,11},{10,... | collective-permute-start | bytes 1327112 | tf_op jit(solution)/shard_map/ppermute | solution.py:63
  225.7 10.5 %collective-permute-start.38 = (bf16[96,1152]{1,0:T(8,128)(2,1)S(1)}, bf16[96,1152]{1,0:T(8,128)(2,1)S(1)}, u32[]{:S(2)}, u32[]{:S(2)}) collective-permute-start(bf16[96,1152]{1,0:T(8,128)(2,1)S(1)} %slice.432), channel_id=1, source_target_pairs={{0,4},{1,5},{2,6},{3,7},{4,0},{5,1},{6,2},{7,3},{8,12},{9,13},{10,... | collective-permute-start | bytes 663560 | tf_op jit(solution)/shard_map/ppermute | solution.py:63
  236.6 13.7 %collective-permute-start.42 = (bf16[4,192,1152]{2,1,0:T(8,128)(2,1)S(1)}, bf16[4,192,1152]{2,1,0:T(8,128)(2,1)S(1)}, u32[]{:S(2)}, u32[]{:S(2)}) collective-permute-start(bf16[4,192,1152]{2,1,0:T(8,128)(2,1)S(1)} %shard_map.287), channel_id=1, source_target_pairs={{0,1},{1,0},{2,3},{3,2},{4,5},{5,4},{6,7},{7,6},{8,9},{9,8},{10,11... | collective-permute-start | bytes 5308424 | tf_op jit(solution)/shard_map/ppermute | solution.py:63
  236.7 12.6 %collective-permute-start.35 = (bf16[192,1152]{1,0:T(8,128)(2,1)S(1)}, bf16[192,1152]{1,0:T(8,128)(2,1)S(1)}, u32[]{:S(2)}, u32[]{:S(2)}) collective-permute-start(bf16[192,1152]{1,0:T(8,128)(2,1)S(1)} %get-tuple-element.255.x_ref), channel_id=1, source_target_pairs={{0,2},{1,3},{2,0},{3,1},{4,6},{5,7},{6,4},{7,5},{8,10},{9,11},{10,... | collective-permute-start | bytes 1327112 | tf_op jit(solution)/shard_map/ppermute | solution.py:63
  238.1 12.2 %collective-permute-start.36 = (bf16[192,1152]{1,0:T(8,128)(2,1)S(1)}, bf16[192,1152]{1,0:T(8,128)(2,1)S(1)}, u32[]{:S(2)}, u32[]{:S(2)}) collective-permute-start(bf16[192,1152]{1,0:T(8,128)(2,1)S(1)} %get-tuple-element.255.x_ref), channel_id=1, source_target_pairs={{0,4},{1,5},{2,6},{3,7},{4,0},{5,1},{6,2},{7,3},{8,12},{9,13},{10,... | collective-permute-start | bytes 1327112 | tf_op jit(solution)/shard_map/ppermute | solution.py:63
  257.3 16.2 %collective-permute-start.44 = (bf16[4,192,1152]{2,1,0:T(8,128)(2,1)S(1)}, bf16[4,192,1152]{2,1,0:T(8,128)(2,1)S(1)}, u32[]{:S(2)}, u32[]{:S(2)}) collective-permute-start(bf16[4,192,1152]{2,1,0:T(8,128)(2,1)S(1)} %bitcast.223), channel_id=1, source_target_pairs={{0,1},{1,0},{2,3},{3,2},{4,5},{5,4},{6,7},{7,6},{8,9},{9,8},{10,11... | collective-permute-start | bytes 5308424 | tf_op jit(solution)/shard_map/ppermute | solution.py:63
  302.9 39.1 %collective-permute-start.45 = (bf16[4,192,1152]{2,1,0:T(8,128)(2,1)}, bf16[4,192,1152]{2,1,0:T(8,128)(2,1)}, u32[]{:S(2)}, u32[]{:S(2)}) collective-permute-start(bf16[4,192,1152]{2,1,0:T(8,128)(2,1)} %bitcast.41), channel_id=1, source_target_pairs={{0,1},{1,0},{2,3},{3,2},{4,5},{5,4},{6,7},{7,6},{8,9},{9,8},{10,11... | collective-permute-start | bytes 5308424 | tf_op jit(solution)/shard_map/ppermute | solution.py:63
  316.3 31.8 %collective-permute-start.51 = (bf16[192,1152]{1,0:T(8,128)(2,1)}, bf16[192,1152]{1,0:T(8,128)(2,1)}, u32[]{:S(2)}, u32[]{:S(2)}) collective-permute-start(bf16[192,1152]{1,0:T(8,128)(2,1)} %pad_maximum_fusion.7), channel_id=1, source_target_pairs={{0,4},{1,5},{2,6},{3,7},{4,0},{5,1},{6,2},{7,3},{8,12},{9,13},{10,... | collective-permute-start | bytes 1327112 | tf_op jit(solution)/shard_map/ppermute | solution.py:63
  318.8 29.4 %collective-permute-start.50 = (bf16[192,1152]{1,0:T(8,128)(2,1)}, bf16[192,1152]{1,0:T(8,128)(2,1)}, u32[]{:S(2)}, u32[]{:S(2)}) collective-permute-start(bf16[192,1152]{1,0:T(8,128)(2,1)} %pad_maximum_fusion.6), channel_id=1, source_target_pairs={{0,2},{1,3},{2,0},{3,1},{4,6},{5,7},{6,4},{7,5},{8,10},{9,11},{10,... | collective-permute-start | bytes 1327112 | tf_op jit(solution)/shard_map/ppermute | solution.py:63
  337.3 38.2 %all-to-all-start.2 = ((bf16[8,144,864]{2,1,0:T(8,128)(2,1)}), bf16[8,144,864]{2,1,0:T(8,128)(2,1)}, u32[]{:S(2)}, u32[]{:S(2)}) async-start(bf16[8,144,864]{2,1,0:T(8,128)(2,1)} %bitcast.207), calls=%async_computation.2 | async-start | bytes 4128768 | tf_op jit(solution)/shard_map/all_to_all | solution.py:1106
  344.7 27.0 %collective-permute-start.48 = (bf16[96,1152]{1,0:T(8,128)(2,1)S(1)}, bf16[96,1152]{1,0:T(8,128)(2,1)S(1)}, u32[]{:S(2)}, u32[]{:S(2)}) collective-permute-start(bf16[96,1152]{1,0:T(8,128)(2,1)S(1)} %get-tuple-element.409), channel_id=1, source_target_pairs={{0,2},{1,3},{2,0},{3,1},{4,6},{5,7},{6,4},{7,5},{8,10},{9,11},{10,... | collective-permute-start | bytes 663560 | tf_op jit(solution)/shard_map/ppermute | solution.py:63
  346.7 25.0 %collective-permute-start.49 = (bf16[96,1152]{1,0:T(8,128)(2,1)S(1)}, bf16[96,1152]{1,0:T(8,128)(2,1)S(1)}, u32[]{:S(2)}, u32[]{:S(2)}) collective-permute-start(bf16[96,1152]{1,0:T(8,128)(2,1)S(1)} %get-tuple-element.408), channel_id=1, source_target_pairs={{0,4},{1,5},{2,6},{3,7},{4,0},{5,1},{6,2},{7,3},{8,12},{9,13},{10,... | collective-permute-start | bytes 663560 | tf_op jit(solution)/shard_map/ppermute | solution.py:63
  372.7 23.9 %collective-permute-start.53 = (bf16[192,1152]{1,0:T(8,128)(2,1)}, bf16[192,1152]{1,0:T(8,128)(2,1)}, u32[]{:S(2)}, u32[]{:S(2)}) collective-permute-start(bf16[192,1152]{1,0:T(8,128)(2,1)} %pad_maximum_fusion.9), channel_id=1, source_target_pairs={{0,4},{1,5},{2,6},{3,7},{4,0},{5,1},{6,2},{7,3},{8,12},{9,13},{10,... | collective-permute-start | bytes 1327112 | tf_op jit(solution)/shard_map/ppermute | solution.py:63
  374.9 21.6 %collective-permute-start.52 = (bf16[192,1152]{1,0:T(8,128)(2,1)}, bf16[192,1152]{1,0:T(8,128)(2,1)}, u32[]{:S(2)}, u32[]{:S(2)}) collective-permute-start(bf16[192,1152]{1,0:T(8,128)(2,1)} %pad_maximum_fusion.8), channel_id=1, source_target_pairs={{0,2},{1,3},{2,0},{3,1},{4,6},{5,7},{6,4},{7,5},{8,10},{9,11},{10,... | collective-permute-start | bytes 1327112 | tf_op jit(solution)/shard_map/ppermute | solution.py:63
  393.0 31.2 %collective-permute-start.55 = (bf16[4,144,864]{2,1,0:T(8,128)(2,1)}, bf16[4,144,864]{2,1,0:T(8,128)(2,1)S(1)}, u32[]{:S(2)}, u32[]{:S(2)}) collective-permute-start(bf16[4,144,864]{2,1,0:T(8,128)(2,1)} %get-tuple-element.305), channel_id=1, source_target_pairs={{0,8},{24,16},{1,9},{25,17},{2,10},{26,18},{3,11},{27,19},{4,12},{... | collective-permute-start | bytes 2985992 | tf_op jit(solution)/shard_map/ppermute | solution.py:162
  416.2 14.5 %collective-permute-start.54 = (bf16[4,2,192,512]{3,2,1,0:T(8,128)(2,1)}, bf16[4,2,192,512]{3,2,1,0:T(8,128)(2,1)}, u32[]{:S(2)}, u32[]{:S(2)}) collective-permute-start(bf16[4,2,192,512]{3,2,1,0:T(8,128)(2,1)} %pad_maximum_fusion), channel_id=1, source_target_pairs={{0,1},{1,0},{2,3},{3,2},{4,5},{5,4},{6,7},{7,6},{8,9},{9,8},{10,11... | collective-permute-start | bytes 4718600 | tf_op jit(solution)/shard_map/ppermute | solution.py:63
  416.4 31.3 %all-to-all-start.1 = ((bf16[8,144,864]{2,1,0:T(8,128)(2,1)}), bf16[8,144,864]{2,1,0:T(8,128)(2,1)}, u32[]{:S(2)}, u32[]{:S(2)}) async-start(bf16[8,144,864]{2,1,0:T(8,128)(2,1)} %bitcast.54), calls=%async_computation.1 | async-start | bytes 4128768 | tf_op jit(solution)/shard_map/all_to_all | solution.py:1106
  420.9 120.9 %reduce-scatter.2.cloned.1.call-start = ((), (), s32[]{:S(2)}) async-start(), calls=%async_computation.7 | async-start | bytes 2654208 | tf_op jit(solution)/shard_map/reduce_scatter | solution.py:1133
  421.0 32.6 %collective-permute-start.62 = (bf16[4,144,864]{2,1,0:T(8,128)(2,1)}, bf16[4,144,864]{2,1,0:T(8,128)(2,1)}, u32[]{:S(2)}, u32[]{:S(2)}) collective-permute-start(bf16[4,144,864]{2,1,0:T(8,128)(2,1)} %get-tuple-element.314), channel_id=1, source_target_pairs={{0,8},{24,16},{1,9},{25,17},{2,10},{26,18},{3,11},{27,19},{4,12},{... | collective-permute-start | bytes 2985992 | tf_op jit(solution)/shard_map/ppermute | solution.py:162
  426.7 36.4 %collective-permute-start.57 = (bf16[4,144,864]{2,1,0:T(8,128)(2,1)}, bf16[4,144,864]{2,1,0:T(8,128)(2,1)}, u32[]{:S(2)}, u32[]{:S(2)}) collective-permute-start(bf16[4,144,864]{2,1,0:T(8,128)(2,1)} %add_convert_fusion.13), channel_id=1, source_target_pairs={{8,16},{16,8},{9,17},{17,9},{10,18},{18,10},{11,19},{19,11},{12,20... | collective-permute-start | bytes 2985992 | tf_op jit(solution)/shard_map/ppermute | solution.py:162
  432.8 19.2 %collective-permute-start.58 = (bf16[1,192,512]{2,1,0:T(8,128)(2,1)S(1)}, bf16[1,192,512]{2,1,0:T(8,128)(2,1)S(1)}, u32[]{:S(2)}, u32[]{:S(2)}) collective-permute-start(bf16[1,192,512]{2,1,0:T(8,128)(2,1)S(1)} %get-tuple-element.433), channel_id=1, source_target_pairs={{0,2},{1,3},{2,0},{3,1},{4,6},{5,7},{6,4},{7,5},{8,10},{9,11},{10,... | collective-permute-start | bytes 589832 | tf_op jit(solution)/shard_map/ppermute | solution.py:63
  434.7 17.4 %collective-permute-start.59 = (bf16[1,192,512]{2,1,0:T(8,128)(2,1)S(1)}, bf16[1,192,512]{2,1,0:T(8,128)(2,1)S(1)}, u32[]{:S(2)}, u32[]{:S(2)}) collective-permute-start(bf16[1,192,512]{2,1,0:T(8,128)(2,1)S(1)} %get-tuple-element.432), channel_id=1, source_target_pairs={{0,4},{1,5},{2,6},{3,7},{4,0},{5,1},{6,2},{7,3},{8,12},{9,13},{10,... | collective-permute-start | bytes 589832 | tf_op jit(solution)/shard_map/ppermute | solution.py:63
  450.5 20.1 %collective-permute-start.56 = (bf16[4,144,864]{2,1,0:T(8,128)(2,1)S(1)}, bf16[4,144,864]{2,1,0:T(8,128)(2,1)S(1)}, u32[]{:S(2)}, u32[]{:S(2)}) collective-permute-start(bf16[4,144,864]{2,1,0:T(8,128)(2,1)S(1)} %get-tuple-element.321), channel_id=1, source_target_pairs={{0,8},{24,16},{1,9},{25,17},{2,10},{26,18},{3,11},{27,19},{4,12},{... | collective-permute-start | bytes 2985992 | tf_op jit(solution)/shard_map/ppermute | solution.py:162
  455.3 16.5 %collective-permute-start.64 = (bf16[4,144,864]{2,1,0:T(8,128)(2,1)S(1)}, bf16[4,144,864]{2,1,0:T(8,128)(2,1)S(1)}, u32[]{:S(2)}, u32[]{:S(2)}) collective-permute-start(bf16[4,144,864]{2,1,0:T(8,128)(2,1)S(1)} %add_convert_fusion.12), channel_id=1, source_target_pairs={{8,16},{16,8},{9,17},{17,9},{10,18},{18,10},{11,19},{19,11},{12,20... | collective-permute-start | bytes 2985992 | tf_op jit(solution)/shard_map/ppermute | solution.py:162
  479.6 15.3 %collective-permute-start.67 = (bf16[4,144,1536]{2,1,0:T(8,128)(2,1)}, bf16[4,144,1536]{2,1,0:T(8,128)(2,1)}, u32[]{:S(2)}, u32[]{:S(2)}) collective-permute-start(bf16[4,144,1536]{2,1,0:T(8,128)(2,1)} %get-tuple-element.339), channel_id=1, source_target_pairs={{0,1},{1,0},{2,3},{3,2},{4,5},{5,4},{6,7},{7,6},{8,9},{9,8},{10,11... | collective-permute-start | bytes 5308424 | tf_op jit(solution)/shard_map/ppermute | solution.py:63
  480.6 32.3 %collective-permute-start.66 = (bf16[4,144,864]{2,1,0:T(8,128)(2,1)S(1)}, bf16[4,144,864]{2,1,0:T(8,128)(2,1)S(1)}, u32[]{:S(2)}, u32[]{:S(2)}) collective-permute-start(bf16[4,144,864]{2,1,0:T(8,128)(2,1)S(1)} %add_convert_fusion.11.refs_0_), channel_id=1, source_target_pairs={{8,0},{16,24},{9,1},{17,25},{10,2},{18,26},{11,3},{19,27},{12,4},{... | collective-permute-start | bytes 2985992 | tf_op jit(solution)/shard_map/ppermute | solution.py:162
  481.9 38.7 %collective-permute-start.63 = (bf16[4,144,864]{2,1,0:T(8,128)(2,1)}, bf16[4,144,864]{2,1,0:T(8,128)(2,1)S(1)}, u32[]{:S(2)}, u32[]{:S(2)}) collective-permute-start(bf16[4,144,864]{2,1,0:T(8,128)(2,1)} %add_convert_fusion.10), channel_id=1, source_target_pairs={{8,16},{16,8},{9,17},{17,9},{10,18},{18,10},{11,19},{19,11},{12,20... | collective-permute-start | bytes 2985992 | tf_op jit(solution)/shard_map/ppermute | solution.py:162
  482.7 34.9 %collective-permute-start.65 = (bf16[4,144,864]{2,1,0:T(8,128)(2,1)}, bf16[4,144,864]{2,1,0:T(8,128)(2,1)S(1)}, u32[]{:S(2)}, u32[]{:S(2)}) collective-permute-start(bf16[4,144,864]{2,1,0:T(8,128)(2,1)} %get-tuple-element.332), channel_id=1, source_target_pairs={{0,8},{24,16},{1,9},{25,17},{2,10},{26,18},{3,11},{27,19},{4,12},{... | collective-permute-start | bytes 2985992 | tf_op jit(solution)/shard_map/ppermute | solution.py:162
  505.2 35.6 %collective-permute-start.73 = (bf16[4,144,864]{2,1,0:T(8,128)(2,1)S(1)}, bf16[4,144,864]{2,1,0:T(8,128)(2,1)S(1)}, u32[]{:S(2)}, u32[]{:S(2)}) collective-permute-start(bf16[4,144,864]{2,1,0:T(8,128)(2,1)S(1)} %add_convert_fusion.9.refs_1_), channel_id=1, source_target_pairs={{8,0},{16,24},{9,1},{17,25},{10,2},{18,26},{11,3},{19,27},{12,4},{... | collective-permute-start | bytes 2985992 | tf_op jit(solution)/shard_map/ppermute | solution.py:162
  506.7 17.8 %collective-permute-start.71 = (bf16[144,1536]{1,0:T(8,128)(2,1)S(1)}, bf16[144,1536]{1,0:T(8,128)(2,1)S(1)}, u32[]{:S(2)}, u32[]{:S(2)}) collective-permute-start(bf16[144,1536]{1,0:T(8,128)(2,1)S(1)} %pad_maximum_fusion.11), channel_id=1, source_target_pairs={{0,4},{1,5},{2,6},{3,7},{4,0},{5,1},{6,2},{7,3},{8,12},{9,13},{10,... | collective-permute-start | bytes 1327112 | tf_op jit(solution)/shard_map/ppermute | solution.py:63
  512.9 12.4 %collective-permute-start.70 = (bf16[144,1536]{1,0:T(8,128)(2,1)S(1)}, bf16[144,1536]{1,0:T(8,128)(2,1)S(1)}, u32[]{:S(2)}, u32[]{:S(2)}) collective-permute-start(bf16[144,1536]{1,0:T(8,128)(2,1)S(1)} %pad_maximum_fusion.10), channel_id=1, source_target_pairs={{0,2},{1,3},{2,0},{3,1},{4,6},{5,7},{6,4},{7,5},{8,10},{9,11},{10,... | collective-permute-start | bytes 1327112 | tf_op jit(solution)/shard_map/ppermute | solution.py:63
  518.9 26.2 %collective-permute-start.80 = (bf16[4,144,864]{2,1,0:T(8,128)(2,1)}, bf16[4,144,864]{2,1,0:T(8,128)(2,1)}, u32[]{:S(2)}, u32[]{:S(2)}) collective-permute-start(bf16[4,144,864]{2,1,0:T(8,128)(2,1)} %add_convert_fusion.8), channel_id=1, source_target_pairs={{8,16},{16,8},{9,17},{17,9},{10,18},{18,10},{11,19},{19,11},{12,20... | collective-permute-start | bytes 2985992 | tf_op jit(solution)/shard_map/ppermute | solution.py:162
  520.9 36.4 %collective-permute-start.79 = (bf16[4,144,864]{2,1,0:T(8,128)(2,1)S(1)}, bf16[4,144,864]{2,1,0:T(8,128)(2,1)}, u32[]{:S(2)}, u32[]{:S(2)}) collective-permute-start(bf16[4,144,864]{2,1,0:T(8,128)(2,1)S(1)} %add_convert_fusion.7.refs_0_), channel_id=1, source_target_pairs={{8,0},{16,24},{9,1},{17,25},{10,2},{18,26},{11,3},{19,27},{12,4},{... | collective-permute-start | bytes 2985992 | tf_op jit(solution)/shard_map/ppermute | solution.py:162
  525.5 17.6 %collective-permute-start.72 = (bf16[144,1536]{1,0:T(8,128)(2,1)S(1)}, bf16[144,1536]{1,0:T(8,128)(2,1)}, u32[]{:S(2)}, u32[]{:S(2)}) collective-permute-start(bf16[144,1536]{1,0:T(8,128)(2,1)S(1)} %fusion.5), channel_id=1, source_target_pairs={{0,8},{24,16},{1,9},{25,17},{2,10},{26,18},{3,11},{27,19},{4,12},{... | collective-permute-start | bytes 1327112 | tf_op jit(solution)/shard_map/ppermute | solution.py:162
  541.8 15.5 %collective-permute-start.78 = (bf16[128,1152]{1,0:T(8,128)(2,1)}, bf16[128,1152]{1,0:T(8,128)(2,1)S(1)}, u32[]{:S(2)}, u32[]{:S(2)}) collective-permute-start(bf16[128,1152]{1,0:T(8,128)(2,1)} %reduce-scatter.2.cloned.1.call-done), channel_id=1, source_target_pairs={{0,8},{24,16},{1,9},{25,17},{2,10},{26,18},{3,11},{27,19},{4,12},{... | collective-permute-start | bytes 884744 | tf_op jit(solution)/shard_map/ppermute | solution.py:162
  544.2 18.3 %collective-permute-start.74 = (bf16[144,1536]{1,0:T(8,128)(2,1)S(1)}, bf16[144,1536]{1,0:T(8,128)(2,1)S(1)}, u32[]{:S(2)}, u32[]{:S(2)}) collective-permute-start(bf16[144,1536]{1,0:T(8,128)(2,1)S(1)} %add_convert_fusion.15), channel_id=1, source_target_pairs={{8,16},{16,8},{9,17},{17,9},{10,18},{18,10},{11,19},{19,11},{12,20... | collective-permute-start | bytes 1327112 | tf_op jit(solution)/shard_map/ppermute | solution.py:162
  547.9 31.5 %collective-permute-start.86 = (bf16[4,144,864]{2,1,0:T(8,128)(2,1)}, bf16[4,144,864]{2,1,0:T(8,128)(2,1)}, u32[]{:S(2)}, u32[]{:S(2)}) collective-permute-start(bf16[4,144,864]{2,1,0:T(8,128)(2,1)} %add_convert_fusion.6.refs_1_), channel_id=1, source_target_pairs={{8,0},{16,24},{9,1},{17,25},{10,2},{18,26},{11,3},{19,27},{12,4},{... | collective-permute-start | bytes 2985992 | tf_op jit(solution)/shard_map/ppermute | solution.py:162
  565.1 20.6 %collective-permute-start.84 = (bf16[128,1152]{1,0:T(8,128)(2,1)}, bf16[128,1152]{1,0:T(8,128)(2,1)}, u32[]{:S(2)}, u32[]{:S(2)}) collective-permute-start(bf16[128,1152]{1,0:T(8,128)(2,1)} %add_convert_fusion.16), channel_id=1, source_target_pairs={{8,0},{16,24},{9,1},{17,25},{10,2},{18,26},{11,3},{19,27},{12,4},{... | collective-permute-start | bytes 884744 | tf_op jit(solution)/shard_map/ppermute | solution.py:162
  567.7 27.4 %collective-permute-start.81 = (bf16[144,1536]{1,0:T(8,128)(2,1)S(1)}, bf16[144,1536]{1,0:T(8,128)(2,1)S(1)}, u32[]{:S(2)}, u32[]{:S(2)}) collective-permute-start(bf16[144,1536]{1,0:T(8,128)(2,1)S(1)} %add_convert_fusion.14), channel_id=1, source_target_pairs={{8,0},{16,24},{9,1},{17,25},{10,2},{18,26},{11,3},{19,27},{12,4},{... | collective-permute-start | bytes 1327112 | tf_op jit(solution)/shard_map/ppermute | solution.py:162
  569.7 25.6 %collective-permute-start.87 = (f32[40,128]{1,0:T(8,128)S(1)}, f32[40,128]{1,0:T(8,128)S(1)}, u32[]{:S(2)}, u32[]{:S(2)}) collective-permute-start(f32[40,128]{1,0:T(8,128)S(1)} %add.378), channel_id=1, source_target_pairs={{8,0},{16,24},{9,1},{17,25},{10,2},{18,26},{11,3},{19,27},{12,4},{... | collective-permute-start | bytes 61448 | tf_op jit(solution)/shard_map/ppermute | solution.py:162
  (186 other events, 1485.2 us)
Sparse Core Ops, SparseCore 0:
  9.9 32.3 all-gather.2
  44.2 41.3 all-gather.4
  306.3 83.6 all-reduce.1
  480.8 53.3 reduce-scatter.1

commit v4 on v3

--- a/solution.py
+++ b/solution.py
@@ -1080,10 +1080,6 @@
         lefts, rights = r0[left] + r1[left], r0[right] + r1[right]
         return weight_grad([after(lefts[0], *earlier)] + lefts[1:], rights)
 
-    grad_down = weight_grad(
-        [after(r0["active"][0], s0.sums)] + r0["active"][1:] + r1["active"],
-        r0["d_lowered"] + blocks_1,
-    )
     def begin(part, *earlier):
         line = Line(after(part, *earlier), n_dp)
         clock[:] = [line.total]
@@ -1105,22 +1101,30 @@
     def exchange(grad):
         return lax.all_to_all(grad.reshape(n, width // n, share), "ctx", 0, 0)
 
-    clock = [grad_down]
-    summed_down = lax.psum(grad_down, "dp")
-    d_in_1 += pieces_of(back_piece, r1, blocks_1[1:], *clock)
+    clock = []
+    grad_down = weight_grad(
+        [after(r0["active"][0], s0.sums)] + r0["active"][1:] + r1["active"],
+        r0["d_lowered"] + blocks_1,
+    )
+    down_line = begin(grad_down)
+    d_in_1 += pieces_of(back_piece, r1, blocks_1[1:], d_in_1[0], grad_down)
     s1 = Scatter(d_in_1, n)
     s0.far(d_in_1[-1])
     grad_gate = over_rows("inner", "d_gate", *s0.sent)
     gate_pieces = exchange(grad_gate)
     s1.mid(grad_gate)
     attend_back(0, r0, s0.finish(s1.sums))
-    s1.far(r0["d_kv"][0])
+    clock[:] = [r0["d_kv"][0]]
+    step(down_line)
+    s1.far(*clock)
     grad_up = over_rows("inner", "d_up", *s1.sent)
     up_pieces = exchange(grad_up)
     gate_halves = halves(gate_pieces)
     gl0 = begin(gate_halves[0], grad_up)
-    attend_back(1, r1, s1.finish(summed_down, *clock))
-    gl1 = begin(gate_halves[1], r1["d_kv"][0])
+    attend_back(1, r1, s1.finish(*clock))
+    clock[:] = [r1["d_kv"][0]]
+    step(down_line)
+    gl1 = begin(gate_halves[1], *clock)
     step(gl0)
     kv_scatter = Scatter(
         [jnp.stack([a, b], axis=1) for a, b in zip(r0["d_kv"], r1["d_kv"])], n
@@ -1166,6 +1170,7 @@
     )
     clock[:] = [d_kvs[0]]
     step(gl0)
+    land(down_line)
     step(u0)
     step(gl1)
     u1 = begin(up_halves[1], *clock)
@@ -1206,7 +1211,7 @@
     land(gl0)
     step(u1)
     step(u0)
-    summed_down = after(summed_down, *clock).astype(WIDE)
+    summed_down = last(down_line)
     result = after(jnp.stack([r["result"] for r in rows]), *clock)
     clock[:] = [summed_down, result]
     part_qkv = total_of(qkv_scatter.finish(*clock))

time: 611 us -> 606 us (level)
  local copies, waits for them, and re-layouts: 78.1 us -> 53.1 us
  starting transfers between devices: 126 us -> 145 us
  other arithmetic: 43.2 us -> 51.8 us
  waiting for transfers between devices: 191 us -> 183 us
    unnamed x313 -> x303, local copies, waits for them, and re-layouts: 61.9 us -> 37.2 us
    ppermute x21 -> x24, starting transfers between devices: 47.7 us -> 71.1 us  [send(): self.moved = lax.ppermute(self.total, 'dp', self.steps[self.at][1])]
    ppermute x21 -> x24, waiting for transfers between devices: 36 us -> 48.8 us  [send(): self.moved = lax.ppermute(self.total, 'dp', self.steps[self.at][1])]
    all_to_all x2, waiting for transfers between devices: 11.6 us -> 0.01 us  [exchange(): return lax.all_to_all(grad.reshape(n, width // n, share), 'ctx', 0, 0)]
    ppermute x66, waiting for transfers between devices: 128 us -> 119 us  [xor_permute(): return lax.ppermute(x, 'ctx', [(i, i ^ code) for i in range(axis_size)])]
    convert_element_type x12 -> x14, other arithmetic: 14 us -> 20.6 us  [step(): self.total = total.astype(self.total.dtype)]
  transfers between devices with their start and end apart: 95 -> 97, of which waited for: 48 -> 48; matrix products, arithmetic and copies ran while one was open for 10% -> 12% of each run, Pallas kernels for 17% -> 17%
where the time goes in v4:
time: 606 us; the launch traced here: 600 us
  waiting for transfers between devices  183 us (30%)
  Pallas kernels  148 us (24%)
  starting transfers between devices  145 us (24%)
  local copies, waits for them, and re-layouts  53.1 us (9%)
  other arithmetic  51.8 us (9%)
  between operations  16.4 us (3%)
    ppermute x66, waiting for transfers between devices, xor_permute(): return lax.ppermute(x, 'ctx', [(i, i ^ code) for i in range(axis_size)])  119 us
    ppermute x24, starting transfers between devices, send(): self.moved = lax.ppermute(self.total, 'dp', self.steps[self.at][1])  71.1 us
    ppermute x66, starting transfers between devices, xor_permute(): return lax.ppermute(x, 'ctx', [(i, i ^ code) for i in range(axis_size)])  58.3 us
    ppermute x24, waiting for transfers between devices, send(): self.moved = lax.ppermute(self.total, 'dp', self.steps[self.at][1])  48.8 us
    unnamed x303, local copies, waits for them, and re-layouts  37.2 us
    pallas_call x4, Pallas kernels, feed_backward(): vmem_call(kernel, (hidden, hidden, jax.ShapeDtypeStruct((tokens, width),...  30 us
    pallas_call x4, Pallas kernels, feed_forward(): vmem_call(kernel, (hidden, hidden, hidden, jax.ShapeDtypeStruct((tokens,...  28 us
    pallas_call x3, Pallas kernels, weight_grad(): vmem_call(kernel, jax.ShapeDtypeStruct((rows, columns), BF16), limit=24,...  23.9 us
  transfers between devices with their start and end apart: 97, of which 48 were waited for; matrix products, arithmetic and copies ran while one was open for 12% of the time, Pallas kernels for 17%

profile of v4, /device:TPU:0, one launch (start us, length us, event | category | flops | bytes accessed | tf_op | source)
XLA Modules:
  0.0 600.1 jit_solution(14764911037410501419)
XLA Ops:
  9.8 2.9 collective-permute-start
  18.4 3.0 collective-permute-done.3
  22.0 3.1 collective-permute-done.4
  36.5 4.6 all-to-all-start
  46.0 36.3 %collective-permute-done.8.a_ref = bf16[2,192,512]{2,1,0:T(8,128)(2,1)S(1)} collective-permute-done((bf16[2,192,512]{2,1,0:T(8,128)(2,1)}, bf16[2,192,512]{2,1,0:T(8,128)(2,1)S(1)}, u32[]{:S(2)}, u32[]{:S(2)}) %collective-permute-start.8) | collective-permute-done | bytes 393248 | tf_op jit(solution)/shard_map/ppermute | solution.py:63
  97.5 7.2 %shard_map.276 = (bf16[192,1024]{1,0:T(8,128)(2,1)S(1)}, f32[192,4]{1,0:T(8,128)S(1)}, f32[192,1152]{1,0:T(8,128)S(1)}, f32[192,1152]{1,0:T(8,128)S(1)}, bf16[192,1152]{1,0:T(8,128)(2,1)}) custom-call(bf16[384,1024]{1,0:T(8,128)(2,1)S(1)} %get-tuple-element.223.refs_0_.refs_9_, s32[192,1]{1,0:T(8,128)S(1)} %copy.57.refs_1_.refs_10_, ...), custom_call_target="tpu_custom_call" | custom-call | tf_op jit(solution)/shard_map/pallas_call | solution.py:376
  110.4 6.5 %shard_map.277 = (bf16[192,1024]{1,0:T(8,128)(2,1)S(1)}, f32[192,4]{1,0:T(8,128)S(1)}, f32[192,1152]{1,0:T(8,128)S(1)}, f32[192,1152]{1,0:T(8,128)S(1)}, bf16[192,1152]{1,0:T(8,128)(2,1)S(1)}) custom-call(bf16[384,1024]{1,0:T(8,128)(2,1)S(1)} %get-tuple-element.223.refs_0_.refs_9_, s32[192,1]{1,0:T(8,128)S(1)} %copy.59.refs_1_.refs_10_, ...), custom_call_target="tpu_custom_call" | custom-call | tf_op jit(solution)/shard_map/pallas_call | solution.py:376
  117.5 2.9 collective-permute-done.13.a_ref
  126.9 14.7 %collective-permute-done.17.second_ref = bf16[8,144,864]{2,1,0:T(8,128)(2,1)} collective-permute-done((bf16[8,144,864]{2,1,0:T(8,128)(2,1)}, bf16[8,144,864]{2,1,0:T(8,128)(2,1)}, u32[]{:S(2)}, u32[]{:S(2)}) %collective-permute-start.17) | collective-permute-done | bytes 1990688 | tf_op jit(solution)/shard_map/ppermute | solution.py:967
  141.6 4.9 shard_map.278
  148.6 7.0 %shard_map.280 = (bf16[768,864]{1,0:T(8,128)(2,1)S(1)}, bf16[768,864]{1,0:T(8,128)(2,1)S(1)}, bf16[768,864]{1,0:T(8,128)(2,1)S(1)}, bf16[768,1152]{1,0:T(8,128)(2,1)S(1)}) custom-call(bf16[768,1152]{1,0:T(8,128)(2,1)S(1)} %bitcast.189, bf16[1152,864]{1,0:T(8,128)(2,1)S(1)} %bitcast.173, bf16[1152,864]{1,0:T(8,128)(2,1)S(1)} %bitcast.181, ...), custom_call_target="tpu_custom_call" | custom-call | tf_op jit(solution)/shard_map/pallas_call | solution.py:712
  157.8 6.9 %shard_map.281 = (bf16[768,864]{1,0:T(8,128)(2,1)S(1)}, bf16[768,864]{1,0:T(8,128)(2,1)S(1)}, bf16[768,864]{1,0:T(8,128)(2,1)S(1)}, bf16[768,1152]{1,0:T(8,128)(2,1)S(1)}) custom-call(bf16[768,1152]{1,0:T(8,128)(2,1)S(1)} %bitcast.195, bf16[1152,864]{1,0:T(8,128)(2,1)S(1)} %bitcast.174, bf16[1152,864]{1,0:T(8,128)(2,1)S(1)} %bitcast.182, ...), custom_call_target="tpu_custom_call" | custom-call | tf_op jit(solution)/shard_map/pallas_call | solution.py:712
  168.4 5.2 collective-permute-done.22.d1_ref
  174.3 6.8 %shard_map.283 = (bf16[768,864]{1,0:T(8,128)(2,1)S(1)}, bf16[768,864]{1,0:T(8,128)(2,1)S(1)}, bf16[768,864]{1,0:T(8,128)(2,1)S(1)}, bf16[768,1152]{1,0:T(8,128)(2,1)S(1)}) custom-call(bf16[768,1152]{1,0:T(8,128)(2,1)S(1)} %bitcast.192, bf16[1152,864]{1,0:T(8,128)(2,1)S(1)} %bitcast.175, bf16[1152,864]{1,0:T(8,128)(2,1)S(1)} %bitcast.183, ...), custom_call_target="tpu_custom_call" | custom-call | tf_op jit(solution)/shard_map/pallas_call | solution.py:712
  184.4 7.3 %shard_map.284 = (bf16[768,864]{1,0:T(8,128)(2,1)S(1)}, bf16[768,864]{1,0:T(8,128)(2,1)S(1)}, bf16[768,864]{1,0:T(8,128)(2,1)S(1)}, bf16[768,1152]{1,0:T(8,128)(2,1)S(1)}) custom-call(bf16[768,1152]{1,0:T(8,128)(2,1)S(1)} %bitcast.198, bf16[1152,864]{1,0:T(8,128)(2,1)S(1)} %bitcast.176, bf16[1152,864]{1,0:T(8,128)(2,1)S(1)} %bitcast.184, ...), custom_call_target="tpu_custom_call" | custom-call | tf_op jit(solution)/shard_map/pallas_call | solution.py:712
  194.4 5.3 collective-permute-done.24
  206.2 8.3 %collective-permute-done.27.b_ref = bf16[192,1152]{1,0:T(8,128)(2,1)S(1)} collective-permute-done((bf16[192,1152]{1,0:T(8,128)(2,1)S(1)}, bf16[192,1152]{1,0:T(8,128)(2,1)S(1)}, u32[]{:S(2)}, u32[]{:S(2)}) %collective-permute-start.27) | collective-permute-done | bytes 442400 | tf_op jit(solution)/shard_map/ppermute | solution.py:63
  222.1 6.8 %collective-permute-done.34.a_ref = bf16[192,1152]{1,0:T(8,128)(2,1)S(1)} collective-permute-done((bf16[192,1152]{1,0:T(8,128)(2,1)S(1)}, bf16[192,1152]{1,0:T(8,128)(2,1)S(1)}, u32[]{:S(2)}, u32[]{:S(2)}) %collective-permute-start.34) | collective-permute-done | bytes 442400 | tf_op jit(solution)/shard_map/ppermute | solution.py:63
  232.5 5.9 collective-permute-done.32.b_ref
  243.3 7.0 %shard_map.288 = (bf16[768,864]{1,0:T(8,128)(2,1)S(1)}, bf16[768,864]{1,0:T(8,128)(2,1)S(1)}, bf16[768,1152]{1,0:T(8,128)(2,1)S(1)}) custom-call(bf16[768,1152]{1,0:T(8,128)(2,1)S(1)} %bitcast.201, bf16[768,864]{1,0:T(8,128)(2,1)S(1)} %copy-done.47, bf16[768,864]{1,0:T(8,128)(2,1)S(1)} %copy-done.49, bf16[1152,864]{1,0:T(8,128)(2,1)S(1)} %bitcast.177, ...), custom_call_target="tpu_custom_call" | custom-call | tf_op jit(solution)/shard_map/pallas_call | solution.py:739
  251.5 2.6 collective-permute-done.39.a_ref
  255.2 7.9 %shard_map.289 = (bf16[768,864]{1,0:T(8,128)(2,1)S(1)}, bf16[768,864]{1,0:T(8,128)(2,1)S(1)}, bf16[768,1152]{1,0:T(8,128)(2,1)}) custom-call(bf16[768,1152]{1,0:T(8,128)(2,1)S(1)} %bitcast.209, bf16[768,864]{1,0:T(8,128)(2,1)S(1)} %get-tuple-element.268.slope_ref, bf16[768,864]{1,0:T(8,128)(2,1)S(1)} %copy-done.43, bf16[1152,864]{1,0:T(8,128)(2,1)S(1)} %bitcast.178, ...), custom_call_target="tpu_custom_call" | custom-call | tf_op jit(solution)/shard_map/pallas_call | solution.py:739
  265.1 6.0 collective-permute-done.42.d1_ref
  273.5 7.2 %shard_map.291 = (bf16[768,864]{1,0:T(8,128)(2,1)S(1)}, bf16[768,864]{1,0:T(8,128)(2,1)S(1)}, bf16[768,1152]{1,0:T(8,128)(2,1)S(1)}) custom-call(bf16[768,1152]{1,0:T(8,128)(2,1)S(1)} %bitcast.203, bf16[768,864]{1,0:T(8,128)(2,1)S(1)} %copy-done.39, bf16[768,864]{1,0:T(8,128)(2,1)S(1)} %copy-done.41, bf16[1152,864]{1,0:T(8,128)(2,1)S(1)} %bitcast.179, ...), custom_call_target="tpu_custom_call" | custom-call | tf_op jit(solution)/shard_map/pallas_call | solution.py:739
  280.8 3.1 add_convert_fusion.4.refs_0_
  284.6 8.9 %shard_map.292 = bf16[864,1152]{1,0:T(8,128)(2,1)} custom-call(bf16[768,864]{1,0:T(8,128)(2,1)S(1)} %copy-done.61, bf16[768,864]{1,0:T(8,128)(2,1)S(1)} %copy-done.63, bf16[768,864]{1,0:T(8,128)(2,1)S(1)} %copy-done.65, bf16[768,864]{1,0:T(8,128)(2,1)S(1)} %copy-done.67, bf16[768,1152]{1,0:T(8,128)(2,1)S(1)} %bitcast.202, bf16[768,1152]{1,0:T(8,128)(2,1)S(1)} %bitcast.210, ...), custom_call_target="tpu_custom_call" | custom-call | tf_op jit(solution)/shard_map/pallas_call | solution.py:767
  293.5 7.8 %shard_map.293 = (bf16[768,864]{1,0:T(8,128)(2,1)S(1)}, bf16[768,864]{1,0:T(8,128)(2,1)S(1)}, bf16[768,1152]{1,0:T(8,128)(2,1)}) custom-call(bf16[768,1152]{1,0:T(8,128)(2,1)S(1)} %bitcast.212, bf16[768,864]{1,0:T(8,128)(2,1)S(1)} %get-tuple-element.284.slope_ref, bf16[768,864]{1,0:T(8,128)(2,1)S(1)} %get-tuple-element.285.value_ref, ...), custom_call_target="tpu_custom_call" | custom-call | tf_op jit(solution)/shard_map/pallas_call | solution.py:739
  304.2 4.9 collective-permute-start.45
  315.5 7.5 %shard_map.294 = bf16[1152,864]{1,0:T(8,128)(2,1)S(1)} custom-call(bf16[768,1152]{1,0:T(8,128)(2,1)S(1)} %bitcast.190, bf16[768,1152]{1,0:T(8,128)(2,1)S(1)} %bitcast.196, bf16[768,1152]{1,0:T(8,128)(2,1)S(1)} %bitcast.193, bf16[768,1152]{1,0:T(8,128)(2,1)S(1)} %bitcast.199, bf16[768,864]{1,0:T(8,128)(2,1)S(1)} %copy-done.57, ...), custom_call_target="tpu_custom_call" | custom-call | tf_op jit(solution)/shard_map/pallas_call | solution.py:767
  324.4 4.6 all-to-all-start.1
  329.0 2.4 add_convert_fusion.3.refs_0_
  335.2 11.0 %shard_map.295 = (f32[192,1152]{1,0:T(8,128)S(1)}, bf16[192,1152]{1,0:T(8,128)(2,1)S(1)}, f32[1,1152]{1,0:T(1,128)S(1)}, f32[1,1152]{1,0:T(1,128)S(1)}, bf16[192...) custom-call(bf16[4,192,1152]{2,1,0:T(8,128)(2,1)} %copy-done.137, ...), custom_call_target="tpu_custom_call" | custom-call | tf_op jit(solution)/shard_map/pallas_call | solution.py:549
  346.3 4.0 collective-permute-done.45
  350.3 3.9 add_convert_fusion.1
  362.8 3.2 fusion.35
  371.4 7.5 %shard_map.296 = bf16[1152,864]{1,0:T(8,128)(2,1)S(1)} custom-call(bf16[768,1152]{1,0:T(8,128)(2,1)S(1)} %bitcast.191, bf16[768,1152]{1,0:T(8,128)(2,1)S(1)} %bitcast.197, bf16[768,1152]{1,0:T(8,128)(2,1)S(1)} %bitcast.194, bf16[768,1152]{1,0:T(8,128)(2,1)S(1)} %bitcast.200, bf16[768,864]{1,0:T(8,128)(2,1)S(1)} %copy-done.45, ...), custom_call_target="tpu_custom_call" | custom-call | tf_op jit(solution)/shard_map/pallas_call | solution.py:767
  378.9 4.6 collective-permute-start.57
  383.5 4.5 all-to-all-start.2
  388.3 11.1 %shard_map.297 = (f32[192,1152]{1,0:T(8,128)S(1)}, bf16[192,1152]{1,0:T(8,128)(2,1)S(1)}, f32[1,1152]{1,0:T(1,128)S(1)}, f32[1,1152]{1,0:T(1,128)S(1)}, bf16[192...) custom-call(bf16[4,192,1152]{2,1,0:T(8,128)(2,1)} %copy-done.136, ...), custom_call_target="tpu_custom_call" | custom-call | tf_op jit(solution)/shard_map/pallas_call | solution.py:549
  401.7 3.9 add_convert_fusion
  407.0 6.9 %collective-permute-start.64 = (bf16[4,144,864]{2,1,0:T(8,128)(2,1)}, bf16[4,144,864]{2,1,0:T(8,128)(2,1)}, u32[]{:S(2)}, u32[]{:S(2)}) collective-permute-start(bf16[4,144,864]{2,1,0:T(8,128)(2,1)} %get-tuple-element.316), channel_id=1, source_target_pairs={{0,8},{24,16},{1,9},{25,17},{2,10},{26,18},{3,11},{27,19},{4,12},{... | collective-permute-start | bytes 2985992 | tf_op jit(solution)/shard_map/ppermute | solution.py:162
  413.9 2.7 add_convert_fusion.15
  424.8 2.7 fusion.34
  428.2 3.2 collective-permute-start.65
  433.2 3.2 collective-permute-done.64
  446.4 7.1 %collective-permute-done.56 = bf16[864,1152]{1,0:T(8,128)(2,1)} collective-permute-done((bf16[864,1152]{1,0:T(8,128)(2,1)}, bf16[864,1152]{1,0:T(8,128)(2,1)}, u32[]{:S(2)}, u32[]{:S(2)}) %collective-permute-start.56) | collective-permute-done | bytes 1990688 | tf_op jit(solution)/shard_map/ppermute | solution.py:162
  453.5 4.0 collective-permute-done.65
  459.8 5.6 shard_map.299
  470.8 19.5 %collective-permute-start.68 = (bf16[4,144,864]{2,1,0:T(8,128)(2,1)}, bf16[4,144,864]{2,1,0:T(8,128)(2,1)S(1)}, u32[]{:S(2)}, u32[]{:S(2)}) collective-permute-start(bf16[4,144,864]{2,1,0:T(8,128)(2,1)} %get-tuple-element.338), channel_id=1, source_target_pairs={{0,8},{24,16},{1,9},{25,17},{2,10},{26,18},{3,11},{27,19},{4,12},{... | collective-permute-start | bytes 2985992 | tf_op jit(solution)/shard_map/ppermute | solution.py:162
  490.3 2.8 add_convert_fusion.2
  494.8 3.6 shard_map.300
  502.7 5.5 collective-permute-done.69.refs_2_
  508.8 4.1 collective-permute-done.68
  517.5 3.8 select_convert_fusion
  521.5 6.9 %collective-permute-start.75 = (bf16[144,1536]{1,0:T(8,128)(2,1)S(1)}, bf16[144,1536]{1,0:T(8,128)(2,1)}, u32[]{:S(2)}, u32[]{:S(2)}) collective-permute-start(bf16[144,1536]{1,0:T(8,128)(2,1)S(1)} %fusion.5), channel_id=1, source_target_pairs={{0,8},{24,16},{1,9},{25,17},{2,10},{26,18},{3,11},{27,19},{4,12},{... | collective-permute-start | bytes 1327112 | tf_op jit(solution)/shard_map/ppermute | solution.py:162
  530.2 3.2 collective-permute-done.79
  534.0 3.2 collective-permute-done.80
  542.1 2.8 add_convert_fusion.8.refs_1_
  546.2 6.4 %collective-permute-done.82.refs_2_ = bf16[4,144,864]{2,1,0:T(8,128)(2,1)} collective-permute-done((bf16[4,144,864]{2,1,0:T(8,128)(2,1)S(1)}, bf16[4,144,864]{2,1,0:T(8,128)(2,1)}, u32[]{:S(2)}, u32[]{:S(2)}) %collective-permute-start.82) | collective-permute-done | bytes 995360 | tf_op jit(solution)/shard_map/ppermute | solution.py:162
  553.4 4.3 collective-permute-start.86
  568.8 2.4 shard_map.301
  571.3 4.3 collective-permute-done.89.refs_3_
  575.6 4.3 shard_map.302
  583.7 6.8 %collective-permute-done.84 = bf16[144,1536]{1,0:T(8,128)(2,1)S(1)} collective-permute-done((bf16[144,1536]{1,0:T(8,128)(2,1)S(1)}, bf16[144,1536]{1,0:T(8,128)(2,1)S(1)}, u32[]{:S(2)}, u32[]{:S(2)}) %collective-permute-start.84) | collective-permute-done | bytes 442400 | tf_op jit(solution)/shard_map/ppermute | solution.py:162
  (592 shorter events, 195.1 us)
Async XLA Ops:
  7.2 78.5 %all-gather.3.cloned.1.call-start = ((), (), s32[]{:S(2)}) async-start(), calls=%async_computation.4 | async-start | bytes 2654208 | tf_op jit(solution)/shard_map/all_gather | solution.py:916
  7.9 88.1 %all-gather.5.cloned.1.call-start = ((), (), s32[]{:S(2)}) async-start(), calls=%async_computation.5 | async-start | bytes 2654208 | tf_op jit(solution)/shard_map/all_gather | solution.py:962
  9.8 15.5 %collective-permute-start = (bf16[144,512]{1,0:T(8,128)(2,1)S(1)}, bf16[144,512]{1,0:T(8,128)(2,1)S(1)}, u32[]{:S(2)}, u32[]{:S(2)}) collective-permute-start(bf16[144,512]{1,0:T(8,128)(2,1)S(1)} %constant_dynamic-update-slice_fusion.x_ref), channel_id=1, source_target_pairs={{0,2},{1,3},{2,0},{3,1},{4,6},{5,7},{6,4},{7,5},{8,10},{9,11},{10,... | collective-permute-start | bytes 442376 | tf_op jit(solution)/shard_map/ppermute | solution.py:63
  12.7 12.6 %collective-permute-start.1 = (bf16[144,512]{1,0:T(8,128)(2,1)S(1)}, bf16[144,512]{1,0:T(8,128)(2,1)S(1)}, u32[]{:S(2)}, u32[]{:S(2)}) collective-permute-start(bf16[144,512]{1,0:T(8,128)(2,1)S(1)} %constant_dynamic-update-slice_fusion.x_ref), channel_id=1, source_target_pairs={{0,4},{1,5},{2,6},{3,7},{4,0},{5,1},{6,2},{7,3},{8,12},{9,13},{10,... | collective-permute-start | bytes 442376 | tf_op jit(solution)/shard_map/ppermute | solution.py:63
  36.5 45.9 %all-to-all-start = ((bf16[8,144,864]{2,1,0:T(8,128)(2,1)}), bf16[8,144,864]{2,1,0:T(8,128)(2,1)}, u32[]{:S(2)}, u32[]{:S(2)}) async-start(bf16[8,144,864]{2,1,0:T(8,128)(2,1)} %copy-done.16), calls=%async_computation | async-start | bytes 4128768 | tf_op jit(solution)/shard_map/all_to_all | solution.py:931
  41.1 41.2 %collective-permute-start.8 = (bf16[2,192,512]{2,1,0:T(8,128)(2,1)}, bf16[2,192,512]{2,1,0:T(8,128)(2,1)S(1)}, u32[]{:S(2)}, u32[]{:S(2)}) collective-permute-start(bf16[2,192,512]{2,1,0:T(8,128)(2,1)} %get-tuple-element.209.x_ref), channel_id=1, source_target_pairs={{0,2},{1,3},{2,0},{3,1},{4,6},{5,7},{6,4},{7,5},{8,10},{9,11},{10,... | collective-permute-start | bytes 1179656 | tf_op jit(solution)/shard_map/ppermute | solution.py:63
  43.1 39.2 %collective-permute-start.9 = (bf16[2,192,512]{2,1,0:T(8,128)(2,1)}, bf16[2,192,512]{2,1,0:T(8,128)(2,1)S(1)}, u32[]{:S(2)}, u32[]{:S(2)}) collective-permute-start(bf16[2,192,512]{2,1,0:T(8,128)(2,1)} %get-tuple-element.209.x_ref), channel_id=1, source_target_pairs={{0,4},{1,5},{2,6},{3,7},{4,0},{5,1},{6,2},{7,3},{8,12},{9,13},{10,... | collective-permute-start | bytes 1179656 | tf_op jit(solution)/shard_map/ppermute | solution.py:63
  94.0 47.7 %collective-permute-start.17 = (bf16[8,144,864]{2,1,0:T(8,128)(2,1)}, bf16[8,144,864]{2,1,0:T(8,128)(2,1)}, u32[]{:S(2)}, u32[]{:S(2)}) collective-permute-start(bf16[8,144,864]{2,1,0:T(8,128)(2,1)} %all-to-all-done.first_ref), channel_id=1, source_target_pairs={{0,8},{8,0},{16,24},{24,16},{1,9},{9,1},{17,25},{25,17},{2,10},{10... | collective-permute-start | bytes 5971976 | tf_op jit(solution)/shard_map/ppermute | solution.py:967
  107.9 12.5 %collective-permute-start.13 = (bf16[192,1152]{1,0:T(8,128)(2,1)}, bf16[192,1152]{1,0:T(8,128)(2,1)}, u32[]{:S(2)}, u32[]{:S(2)}) collective-permute-start(bf16[192,1152]{1,0:T(8,128)(2,1)} %get-tuple-element.222.x_ref), channel_id=1, source_target_pairs={{0,2},{1,3},{2,0},{3,1},{4,6},{5,7},{6,4},{7,5},{8,10},{9,11},{10,... | collective-permute-start | bytes 1327112 | tf_op jit(solution)/shard_map/ppermute | solution.py:63
  108.5 12.3 %collective-permute-start.14 = (bf16[192,1152]{1,0:T(8,128)(2,1)}, bf16[192,1152]{1,0:T(8,128)(2,1)}, u32[]{:S(2)}, u32[]{:S(2)}) collective-permute-start(bf16[192,1152]{1,0:T(8,128)(2,1)} %get-tuple-element.222.x_ref), channel_id=1, source_target_pairs={{0,4},{1,5},{2,6},{3,7},{4,0},{5,1},{6,2},{7,3},{8,12},{9,13},{10,... | collective-permute-start | bytes 1327112 | tf_op jit(solution)/shard_map/ppermute | solution.py:63
  120.8 25.8 %collective-permute-start.18 = (bf16[192,1152]{1,0:T(8,128)(2,1)S(1)}, bf16[192,1152]{1,0:T(8,128)(2,1)S(1)}, u32[]{:S(2)}, u32[]{:S(2)}) collective-permute-start(bf16[192,1152]{1,0:T(8,128)(2,1)S(1)} %get-tuple-element.229.x_ref), channel_id=1, source_target_pairs={{0,2},{1,3},{2,0},{3,1},{4,6},{5,7},{6,4},{7,5},{8,10},{9,11},{10,... | collective-permute-start | bytes 1327112 | tf_op jit(solution)/shard_map/ppermute | solution.py:63
  122.2 24.4 %collective-permute-start.19 = (bf16[192,1152]{1,0:T(8,128)(2,1)S(1)}, bf16[192,1152]{1,0:T(8,128)(2,1)S(1)}, u32[]{:S(2)}, u32[]{:S(2)}) collective-permute-start(bf16[192,1152]{1,0:T(8,128)(2,1)S(1)} %get-tuple-element.229.x_ref), channel_id=1, source_target_pairs={{0,4},{1,5},{2,6},{3,7},{4,0},{5,1},{6,2},{7,3},{8,12},{9,13},{10,... | collective-permute-start | bytes 1327112 | tf_op jit(solution)/shard_map/ppermute | solution.py:63
  123.7 22.9 %collective-permute-start.15 = (bf16[96,1152]{1,0:T(8,128)(2,1)S(1)}, bf16[96,1152]{1,0:T(8,128)(2,1)S(1)}, u32[]{:S(2)}, u32[]{:S(2)}) collective-permute-start(bf16[96,1152]{1,0:T(8,128)(2,1)S(1)} %slice.404), channel_id=1, source_target_pairs={{0,4},{1,5},{2,6},{3,7},{4,0},{5,1},{6,2},{7,3},{8,12},{9,13},{10,... | collective-permute-start | bytes 663560 | tf_op jit(solution)/shard_map/ppermute | solution.py:63
  126.2 20.4 %collective-permute-start.16 = (bf16[96,1152]{1,0:T(8,128)(2,1)S(1)}, bf16[96,1152]{1,0:T(8,128)(2,1)S(1)}, u32[]{:S(2)}, u32[]{:S(2)}) collective-permute-start(bf16[96,1152]{1,0:T(8,128)(2,1)S(1)} %slice.405), channel_id=1, source_target_pairs={{0,2},{1,3},{2,0},{3,1},{4,6},{5,7},{6,4},{7,5},{8,10},{9,11},{10,... | collective-permute-start | bytes 663560 | tf_op jit(solution)/shard_map/ppermute | solution.py:63
  165.7 17.6 %collective-permute-start.21 = (bf16[4,192,1152]{2,1,0:T(8,128)(2,1)S(1)}, bf16[4,192,1152]{2,1,0:T(8,128)(2,1)S(1)}, u32[]{:S(2)}, u32[]{:S(2)}) collective-permute-start(bf16[4,192,1152]{2,1,0:T(8,128)(2,1)S(1)} %bitcast.224), channel_id=1, source_target_pairs={{0,1},{1,0},{2,3},{3,2},{4,5},{5,4},{6,7},{7,6},{8,9},{9,8},{10,11... | collective-permute-start | bytes 5308424 | tf_op jit(solution)/shard_map/ppermute | solution.py:63
  191.7 11.6 %collective-permute-start.29 = (bf16[4,192,1152]{2,1,0:T(8,128)(2,1)S(1)}, bf16[4,192,1152]{2,1,0:T(8,128)(2,1)S(1)}, u32[]{:S(2)}, u32[]{:S(2)}) collective-permute-start(bf16[4,192,1152]{2,1,0:T(8,128)(2,1)S(1)} %bitcast.223), channel_id=1, source_target_pairs={{0,1},{1,0},{2,3},{3,2},{4,5},{5,4},{6,7},{7,6},{8,9},{9,8},{10,11... | collective-permute-start | bytes 5308424 | tf_op jit(solution)/shard_map/ppermute | solution.py:63
  201.4 13.2 %collective-permute-start.27 = (bf16[192,1152]{1,0:T(8,128)(2,1)S(1)}, bf16[192,1152]{1,0:T(8,128)(2,1)S(1)}, u32[]{:S(2)}, u32[]{:S(2)}) collective-permute-start(bf16[192,1152]{1,0:T(8,128)(2,1)S(1)} %pad_maximum_fusion.2), channel_id=1, source_target_pairs={{0,2},{1,3},{2,0},{3,1},{4,6},{5,7},{6,4},{7,5},{8,10},{9,11},{10,... | collective-permute-start | bytes 1327112 | tf_op jit(solution)/shard_map/ppermute | solution.py:63
  201.8 13.2 %collective-permute-start.28 = (bf16[192,1152]{1,0:T(8,128)(2,1)S(1)}, bf16[192,1152]{1,0:T(8,128)(2,1)S(1)}, u32[]{:S(2)}, u32[]{:S(2)}) collective-permute-start(bf16[192,1152]{1,0:T(8,128)(2,1)S(1)} %pad_maximum_fusion.3), channel_id=1, source_target_pairs={{0,4},{1,5},{2,6},{3,7},{4,0},{5,1},{6,2},{7,3},{8,12},{9,13},{10,... | collective-permute-start | bytes 1327112 | tf_op jit(solution)/shard_map/ppermute | solution.py:63
  203.9 15.4 %collective-permute-start.30 = (bf16[96,1152]{1,0:T(8,128)(2,1)S(1)}, bf16[96,1152]{1,0:T(8,128)(2,1)S(1)}, u32[]{:S(2)}, u32[]{:S(2)}) collective-permute-start(bf16[96,1152]{1,0:T(8,128)(2,1)S(1)} %get-tuple-element.427), channel_id=1, source_target_pairs={{0,2},{1,3},{2,0},{3,1},{4,6},{5,7},{6,4},{7,5},{8,10},{9,11},{10,... | collective-permute-start | bytes 663560 | tf_op jit(solution)/shard_map/ppermute | solution.py:63
  204.6 15.2 %collective-permute-start.31 = (bf16[96,1152]{1,0:T(8,128)(2,1)S(1)}, bf16[96,1152]{1,0:T(8,128)(2,1)S(1)}, u32[]{:S(2)}, u32[]{:S(2)}) collective-permute-start(bf16[96,1152]{1,0:T(8,128)(2,1)S(1)} %get-tuple-element.426), channel_id=1, source_target_pairs={{0,4},{1,5},{2,6},{3,7},{4,0},{5,1},{6,2},{7,3},{8,12},{9,13},{10,... | collective-permute-start | bytes 663560 | tf_op jit(solution)/shard_map/ppermute | solution.py:63
  215.7 13.2 %collective-permute-start.34 = (bf16[192,1152]{1,0:T(8,128)(2,1)S(1)}, bf16[192,1152]{1,0:T(8,128)(2,1)S(1)}, u32[]{:S(2)}, u32[]{:S(2)}) collective-permute-start(bf16[192,1152]{1,0:T(8,128)(2,1)S(1)} %get-tuple-element.251.x_ref), channel_id=1, source_target_pairs={{0,2},{1,3},{2,0},{3,1},{4,6},{5,7},{6,4},{7,5},{8,10},{9,11},{10,... | collective-permute-start | bytes 1327112 | tf_op jit(solution)/shard_map/ppermute | solution.py:63
  217.5 13.1 %collective-permute-start.35 = (bf16[192,1152]{1,0:T(8,128)(2,1)S(1)}, bf16[192,1152]{1,0:T(8,128)(2,1)S(1)}, u32[]{:S(2)}, u32[]{:S(2)}) collective-permute-start(bf16[192,1152]{1,0:T(8,128)(2,1)S(1)} %get-tuple-element.251.x_ref), channel_id=1, source_target_pairs={{0,4},{1,5},{2,6},{3,7},{4,0},{5,1},{6,2},{7,3},{8,12},{9,13},{10,... | collective-permute-start | bytes 1327112 | tf_op jit(solution)/shard_map/ppermute | solution.py:63
  219.9 18.5 %collective-permute-start.32 = (bf16[192,1152]{1,0:T(8,128)(2,1)S(1)}, bf16[192,1152]{1,0:T(8,128)(2,1)S(1)}, u32[]{:S(2)}, u32[]{:S(2)}) collective-permute-start(bf16[192,1152]{1,0:T(8,128)(2,1)S(1)} %pad_maximum_fusion.4), channel_id=1, source_target_pairs={{0,2},{1,3},{2,0},{3,1},{4,6},{5,7},{6,4},{7,5},{8,10},{9,11},{10,... | collective-permute-start | bytes 1327112 | tf_op jit(solution)/shard_map/ppermute | solution.py:63
  221.7 17.2 %collective-permute-start.33 = (bf16[192,1152]{1,0:T(8,128)(2,1)S(1)}, bf16[192,1152]{1,0:T(8,128)(2,1)S(1)}, u32[]{:S(2)}, u32[]{:S(2)}) collective-permute-start(bf16[192,1152]{1,0:T(8,128)(2,1)S(1)} %pad_maximum_fusion.5), channel_id=1, source_target_pairs={{0,4},{1,5},{2,6},{3,7},{4,0},{5,1},{6,2},{7,3},{8,12},{9,13},{10,... | collective-permute-start | bytes 1327112 | tf_op jit(solution)/shard_map/ppermute | solution.py:63
  230.6 10.6 %collective-permute-start.36 = (bf16[96,1152]{1,0:T(8,128)(2,1)S(1)}, bf16[96,1152]{1,0:T(8,128)(2,1)S(1)}, u32[]{:S(2)}, u32[]{:S(2)}) collective-permute-start(bf16[96,1152]{1,0:T(8,128)(2,1)S(1)} %slice.432), channel_id=1, source_target_pairs={{0,4},{1,5},{2,6},{3,7},{4,0},{5,1},{6,2},{7,3},{8,12},{9,13},{10,... | collective-permute-start | bytes 663560 | tf_op jit(solution)/shard_map/ppermute | solution.py:63
  241.4 13.8 %collective-permute-start.38 = (bf16[4,192,1152]{2,1,0:T(8,128)(2,1)S(1)}, bf16[4,192,1152]{2,1,0:T(8,128)(2,1)S(1)}, u32[]{:S(2)}, u32[]{:S(2)}) collective-permute-start(bf16[4,192,1152]{2,1,0:T(8,128)(2,1)S(1)} %shard_map.287), channel_id=1, source_target_pairs={{0,1},{1,0},{2,3},{3,2},{4,5},{5,4},{6,7},{7,6},{8,9},{9,8},{10,11... | collective-permute-start | bytes 5308424 | tf_op jit(solution)/shard_map/ppermute | solution.py:63
  241.5 12.6 %collective-permute-start.39 = (bf16[192,1152]{1,0:T(8,128)(2,1)S(1)}, bf16[192,1152]{1,0:T(8,128)(2,1)S(1)}, u32[]{:S(2)}, u32[]{:S(2)}) collective-permute-start(bf16[192,1152]{1,0:T(8,128)(2,1)S(1)} %get-tuple-element.261.x_ref), channel_id=1, source_target_pairs={{0,2},{1,3},{2,0},{3,1},{4,6},{5,7},{6,4},{7,5},{8,10},{9,11},{10,... | collective-permute-start | bytes 1327112 | tf_op jit(solution)/shard_map/ppermute | solution.py:63
  243.0 12.2 %collective-permute-start.40 = (bf16[192,1152]{1,0:T(8,128)(2,1)S(1)}, bf16[192,1152]{1,0:T(8,128)(2,1)S(1)}, u32[]{:S(2)}, u32[]{:S(2)}) collective-permute-start(bf16[192,1152]{1,0:T(8,128)(2,1)S(1)} %get-tuple-element.261.x_ref), channel_id=1, source_target_pairs={{0,4},{1,5},{2,6},{3,7},{4,0},{5,1},{6,2},{7,3},{8,12},{9,13},{10,... | collective-permute-start | bytes 1327112 | tf_op jit(solution)/shard_map/ppermute | solution.py:63
  263.1 17.6 %collective-permute-start.41 = (bf16[4,192,1152]{2,1,0:T(8,128)(2,1)}, bf16[4,192,1152]{2,1,0:T(8,128)(2,1)}, u32[]{:S(2)}, u32[]{:S(2)}) collective-permute-start(bf16[4,192,1152]{2,1,0:T(8,128)(2,1)} %bitcast.37), channel_id=1, source_target_pairs={{0,1},{1,0},{2,3},{3,2},{4,5},{5,4},{6,7},{7,6},{8,9},{9,8},{10,11... | collective-permute-start | bytes 5308424 | tf_op jit(solution)/shard_map/ppermute | solution.py:63
  301.4 27.6 %collective-permute-start.50 = (bf16[4,192,1152]{2,1,0:T(8,128)(2,1)}, bf16[4,192,1152]{2,1,0:T(8,128)(2,1)}, u32[]{:S(2)}, u32[]{:S(2)}) collective-permute-start(bf16[4,192,1152]{2,1,0:T(8,128)(2,1)} %bitcast.45), channel_id=1, source_target_pairs={{0,1},{1,0},{2,3},{3,2},{4,5},{5,4},{6,7},{7,6},{8,9},{9,8},{10,11... | collective-permute-start | bytes 5308424 | tf_op jit(solution)/shard_map/ppermute | solution.py:63
  304.2 46.1 %collective-permute-start.45 = (bf16[864,1152]{1,0:T(8,128)(2,1)}, bf16[864,1152]{1,0:T(8,128)(2,1)}, u32[]{:S(2)}, u32[]{:S(2)}) collective-permute-start(bf16[864,1152]{1,0:T(8,128)(2,1)} %shard_map.292), channel_id=1, source_target_pairs={{0,8},{24,16},{1,9},{25,17},{2,10},{26,18},{3,11},{27,19},{4,12},{... | collective-permute-start | bytes 5971976 | tf_op jit(solution)/shard_map/ppermute | solution.py:162
  312.4 19.1 %collective-permute-start.48 = (bf16[192,1152]{1,0:T(8,128)(2,1)}, bf16[192,1152]{1,0:T(8,128)(2,1)}, u32[]{:S(2)}, u32[]{:S(2)}) collective-permute-start(bf16[192,1152]{1,0:T(8,128)(2,1)} %pad_maximum_fusion.6), channel_id=1, source_target_pairs={{0,2},{1,3},{2,0},{3,1},{4,6},{5,7},{6,4},{7,5},{8,10},{9,11},{10,... | collective-permute-start | bytes 1327112 | tf_op jit(solution)/shard_map/ppermute | solution.py:63
  313.9 17.7 %collective-permute-start.49 = (bf16[192,1152]{1,0:T(8,128)(2,1)}, bf16[192,1152]{1,0:T(8,128)(2,1)}, u32[]{:S(2)}, u32[]{:S(2)}) collective-permute-start(bf16[192,1152]{1,0:T(8,128)(2,1)} %pad_maximum_fusion.7), channel_id=1, source_target_pairs={{0,4},{1,5},{2,6},{3,7},{4,0},{5,1},{6,2},{7,3},{8,12},{9,13},{10,... | collective-permute-start | bytes 1327112 | tf_op jit(solution)/shard_map/ppermute | solution.py:63
  324.4 38.4 %all-to-all-start.1 = ((bf16[8,144,864]{2,1,0:T(8,128)(2,1)}), bf16[8,144,864]{2,1,0:T(8,128)(2,1)}, u32[]{:S(2)}, u32[]{:S(2)}) async-start(bf16[8,144,864]{2,1,0:T(8,128)(2,1)} %bitcast.208), calls=%async_computation.1 | async-start | bytes 4128768 | tf_op jit(solution)/shard_map/all_to_all | solution.py:1102
  331.6 27.4 %collective-permute-start.52 = (bf16[96,1152]{1,0:T(8,128)(2,1)S(1)}, bf16[96,1152]{1,0:T(8,128)(2,1)S(1)}, u32[]{:S(2)}, u32[]{:S(2)}) collective-permute-start(bf16[96,1152]{1,0:T(8,128)(2,1)S(1)} %get-tuple-element.415), channel_id=1, source_target_pairs={{0,2},{1,3},{2,0},{3,1},{4,6},{5,7},{6,4},{7,5},{8,10},{9,11},{10,... | collective-permute-start | bytes 663560 | tf_op jit(solution)/shard_map/ppermute | solution.py:63
  333.6 25.4 %collective-permute-start.53 = (bf16[96,1152]{1,0:T(8,128)(2,1)S(1)}, bf16[96,1152]{1,0:T(8,128)(2,1)S(1)}, u32[]{:S(2)}, u32[]{:S(2)}) collective-permute-start(bf16[96,1152]{1,0:T(8,128)(2,1)S(1)} %get-tuple-element.414), channel_id=1, source_target_pairs={{0,4},{1,5},{2,6},{3,7},{4,0},{5,1},{6,2},{7,3},{8,12},{9,13},{10,... | collective-permute-start | bytes 663560 | tf_op jit(solution)/shard_map/ppermute | solution.py:63
  354.3 47.3 %collective-permute-start.51 = (bf16[864,1152]{1,0:T(8,128)(2,1)}, bf16[864,1152]{1,0:T(8,128)(2,1)}, u32[]{:S(2)}, u32[]{:S(2)}) collective-permute-start(bf16[864,1152]{1,0:T(8,128)(2,1)} %add_convert_fusion.1), channel_id=1, source_target_pairs={{8,16},{16,8},{9,17},{17,9},{10,18},{18,10},{11,19},{19,11},{12,20... | collective-permute-start | bytes 5971976 | tf_op jit(solution)/shard_map/ppermute | solution.py:162
  360.0 28.3 %collective-permute-start.54 = (bf16[192,1152]{1,0:T(8,128)(2,1)}, bf16[192,1152]{1,0:T(8,128)(2,1)}, u32[]{:S(2)}, u32[]{:S(2)}) collective-permute-start(bf16[192,1152]{1,0:T(8,128)(2,1)} %pad_maximum_fusion.8), channel_id=1, source_target_pairs={{0,2},{1,3},{2,0},{3,1},{4,6},{5,7},{6,4},{7,5},{8,10},{9,11},{10,... | collective-permute-start | bytes 1327112 | tf_op jit(solution)/shard_map/ppermute | solution.py:63
  362.2 26.1 %collective-permute-start.55 = (bf16[192,1152]{1,0:T(8,128)(2,1)}, bf16[192,1152]{1,0:T(8,128)(2,1)}, u32[]{:S(2)}, u32[]{:S(2)}) collective-permute-start(bf16[192,1152]{1,0:T(8,128)(2,1)} %pad_maximum_fusion.9), channel_id=1, source_target_pairs={{0,4},{1,5},{2,6},{3,7},{4,0},{5,1},{6,2},{7,3},{8,12},{9,13},{10,... | collective-permute-start | bytes 1327112 | tf_op jit(solution)/shard_map/ppermute | solution.py:63
  378.9 35.0 %collective-permute-start.57 = (bf16[4,144,864]{2,1,0:T(8,128)(2,1)}, bf16[4,144,864]{2,1,0:T(8,128)(2,1)}, u32[]{:S(2)}, u32[]{:S(2)}) collective-permute-start(bf16[4,144,864]{2,1,0:T(8,128)(2,1)} %get-tuple-element.309), channel_id=1, source_target_pairs={{0,8},{24,16},{1,9},{25,17},{2,10},{26,18},{3,11},{27,19},{4,12},{... | collective-permute-start | bytes 2985992 | tf_op jit(solution)/shard_map/ppermute | solution.py:162
  383.5 41.3 %all-to-all-start.2 = ((bf16[8,144,864]{2,1,0:T(8,128)(2,1)}), bf16[8,144,864]{2,1,0:T(8,128)(2,1)}, u32[]{:S(2)}, u32[]{:S(2)}) async-start(bf16[8,144,864]{2,1,0:T(8,128)(2,1)} %bitcast.207), calls=%async_computation.2 | async-start | bytes 4128768 | tf_op jit(solution)/shard_map/all_to_all | solution.py:1102
  388.0 150.8 %reduce-scatter.2.cloned.1.call-start = ((), (), s32[]{:S(2)}) async-start(), calls=%async_computation.6 | async-start | bytes 2654208 | tf_op jit(solution)/shard_map/reduce_scatter | solution.py:1137
  399.6 19.3 %collective-permute-start.59 = (bf16[4,2,192,512]{3,2,1,0:T(8,128)(2,1)S(1)}, bf16[4,2,192,512]{3,2,1,0:T(8,128)(2,1)}, u32[]{:S(2)}, u32[]{:S(2)}) collective-permute-start(bf16[4,2,192,512]{3,2,1,0:T(8,128)(2,1)S(1)} %pad_maximum_fusion), channel_id=1, source_target_pairs={{0,1},{1,0},{2,3},{3,2},{4,5},{5,4},{6,7},{7,6},{8,9},{9,8},{10,11... | collective-permute-start | bytes 4718600 | tf_op jit(solution)/shard_map/ppermute | solution.py:63
  405.6 47.9 %collective-permute-start.56 = (bf16[864,1152]{1,0:T(8,128)(2,1)}, bf16[864,1152]{1,0:T(8,128)(2,1)}, u32[]{:S(2)}, u32[]{:S(2)}) collective-permute-start(bf16[864,1152]{1,0:T(8,128)(2,1)} %add_convert_fusion), channel_id=1, source_target_pairs={{8,0},{16,24},{9,1},{17,25},{10,2},{18,26},{11,3},{19,27},{12,4},{... | collective-permute-start | bytes 5971976 | tf_op jit(solution)/shard_map/ppermute | solution.py:162
  407.0 29.4 %collective-permute-start.64 = (bf16[4,144,864]{2,1,0:T(8,128)(2,1)}, bf16[4,144,864]{2,1,0:T(8,128)(2,1)}, u32[]{:S(2)}, u32[]{:S(2)}) collective-permute-start(bf16[4,144,864]{2,1,0:T(8,128)(2,1)} %get-tuple-element.316), channel_id=1, source_target_pairs={{0,8},{24,16},{1,9},{25,17},{2,10},{26,18},{3,11},{27,19},{4,12},{... | collective-permute-start | bytes 2985992 | tf_op jit(solution)/shard_map/ppermute | solution.py:162
  427.5 18.6 %collective-permute-start.58 = (bf16[4,144,864]{2,1,0:T(8,128)(2,1)}, bf16[4,144,864]{2,1,0:T(8,128)(2,1)S(1)}, u32[]{:S(2)}, u32[]{:S(2)}) collective-permute-start(bf16[4,144,864]{2,1,0:T(8,128)(2,1)} %add_convert_fusion.15), channel_id=1, source_target_pairs={{8,16},{16,8},{9,17},{17,9},{10,18},{18,10},{11,19},{19,11},{12,20... | collective-permute-start | bytes 2985992 | tf_op jit(solution)/shard_map/ppermute | solution.py:162
  428.2 29.3 %collective-permute-start.65 = (bf16[4,144,864]{2,1,0:T(8,128)(2,1)S(1)}, bf16[4,144,864]{2,1,0:T(8,128)(2,1)S(1)}, u32[]{:S(2)}, u32[]{:S(2)}) collective-permute-start(bf16[4,144,864]{2,1,0:T(8,128)(2,1)S(1)} %get-tuple-element.326), channel_id=1, source_target_pairs={{0,8},{24,16},{1,9},{25,17},{2,10},{26,18},{3,11},{27,19},{4,12},{... | collective-permute-start | bytes 2985992 | tf_op jit(solution)/shard_map/ppermute | solution.py:162
  442.4 16.4 %collective-permute-start.67 = (bf16[4,144,864]{2,1,0:T(8,128)(2,1)S(1)}, bf16[4,144,864]{2,1,0:T(8,128)(2,1)S(1)}, u32[]{:S(2)}, u32[]{:S(2)}) collective-permute-start(bf16[4,144,864]{2,1,0:T(8,128)(2,1)S(1)} %add_convert_fusion.14), channel_id=1, source_target_pairs={{8,16},{16,8},{9,17},{17,9},{10,18},{18,10},{11,19},{19,11},{12,20... | collective-permute-start | bytes 2985992 | tf_op jit(solution)/shard_map/ppermute | solution.py:162
  466.5 23.7 %collective-permute-start.70 = (bf16[4,144,1536]{2,1,0:T(8,128)(2,1)}, bf16[4,144,1536]{2,1,0:T(8,128)(2,1)}, u32[]{:S(2)}, u32[]{:S(2)}) collective-permute-start(bf16[4,144,1536]{2,1,0:T(8,128)(2,1)} %get-tuple-element.345), channel_id=1, source_target_pairs={{0,1},{1,0},{2,3},{3,2},{4,5},{5,4},{6,7},{7,6},{8,9},{9,8},{10,11... | collective-permute-start | bytes 5308424 | tf_op jit(solution)/shard_map/ppermute | solution.py:63
  468.7 39.5 %collective-permute-start.69 = (bf16[4,144,864]{2,1,0:T(8,128)(2,1)S(1)}, bf16[4,144,864]{2,1,0:T(8,128)(2,1)S(1)}, u32[]{:S(2)}, u32[]{:S(2)}) collective-permute-start(bf16[4,144,864]{2,1,0:T(8,128)(2,1)S(1)} %add_convert_fusion.13.refs_0_), channel_id=1, source_target_pairs={{8,0},{16,24},{9,1},{17,25},{10,2},{18,26},{11,3},{19,27},{12,4},{... | collective-permute-start | bytes 2985992 | tf_op jit(solution)/shard_map/ppermute | solution.py:162
  470.0 44.2 %collective-permute-start.66 = (bf16[4,144,864]{2,1,0:T(8,128)(2,1)}, bf16[4,144,864]{2,1,0:T(8,128)(2,1)S(1)}, u32[]{:S(2)}, u32[]{:S(2)}) collective-permute-start(bf16[4,144,864]{2,1,0:T(8,128)(2,1)} %add_convert_fusion.12), channel_id=1, source_target_pairs={{8,16},{16,8},{9,17},{17,9},{10,18},{18,10},{11,19},{19,11},{12,20... | collective-permute-start | bytes 2985992 | tf_op jit(solution)/shard_map/ppermute | solution.py:162
  470.8 42.2 %collective-permute-start.68 = (bf16[4,144,864]{2,1,0:T(8,128)(2,1)}, bf16[4,144,864]{2,1,0:T(8,128)(2,1)S(1)}, u32[]{:S(2)}, u32[]{:S(2)}) collective-permute-start(bf16[4,144,864]{2,1,0:T(8,128)(2,1)} %get-tuple-element.338), channel_id=1, source_target_pairs={{0,8},{24,16},{1,9},{25,17},{2,10},{26,18},{3,11},{27,19},{4,12},{... | collective-permute-start | bytes 2985992 | tf_op jit(solution)/shard_map/ppermute | solution.py:162
  500.6 37.3 %collective-permute-start.76 = (bf16[4,144,864]{2,1,0:T(8,128)(2,1)S(1)}, bf16[4,144,864]{2,1,0:T(8,128)(2,1)S(1)}, u32[]{:S(2)}, u32[]{:S(2)}) collective-permute-start(bf16[4,144,864]{2,1,0:T(8,128)(2,1)S(1)} %add_convert_fusion.11.refs_1_), channel_id=1, source_target_pairs={{8,0},{16,24},{9,1},{17,25},{10,2},{18,26},{11,3},{19,27},{12,4},{... | collective-permute-start | bytes 2985992 | tf_op jit(solution)/shard_map/ppermute | solution.py:162
  502.0 19.2 %collective-permute-start.73 = (bf16[144,1536]{1,0:T(8,128)(2,1)S(1)}, bf16[144,1536]{1,0:T(8,128)(2,1)S(1)}, u32[]{:S(2)}, u32[]{:S(2)}) collective-permute-start(bf16[144,1536]{1,0:T(8,128)(2,1)S(1)} %pad_maximum_fusion.10), channel_id=1, source_target_pairs={{0,2},{1,3},{2,0},{3,1},{4,6},{5,7},{6,4},{7,5},{8,10},{9,11},{10,... | collective-permute-start | bytes 1327112 | tf_op jit(solution)/shard_map/ppermute | solution.py:63
  508.3 13.0 %collective-permute-start.74 = (bf16[144,1536]{1,0:T(8,128)(2,1)S(1)}, bf16[144,1536]{1,0:T(8,128)(2,1)S(1)}, u32[]{:S(2)}, u32[]{:S(2)}) collective-permute-start(bf16[144,1536]{1,0:T(8,128)(2,1)S(1)} %pad_maximum_fusion.11), channel_id=1, source_target_pairs={{0,4},{1,5},{2,6},{3,7},{4,0},{5,1},{6,2},{7,3},{8,12},{9,13},{10,... | collective-permute-start | bytes 1327112 | tf_op jit(solution)/shard_map/ppermute | solution.py:63
  514.5 38.1 %collective-permute-start.82 = (bf16[4,144,864]{2,1,0:T(8,128)(2,1)S(1)}, bf16[4,144,864]{2,1,0:T(8,128)(2,1)}, u32[]{:S(2)}, u32[]{:S(2)}) collective-permute-start(bf16[4,144,864]{2,1,0:T(8,128)(2,1)S(1)} %add_convert_fusion.9.refs_0_), channel_id=1, source_target_pairs={{8,0},{16,24},{9,1},{17,25},{10,2},{18,26},{11,3},{19,27},{12,4},{... | collective-permute-start | bytes 2985992 | tf_op jit(solution)/shard_map/ppermute | solution.py:162
  515.8 26.3 %collective-permute-start.83 = (bf16[4,144,864]{2,1,0:T(8,128)(2,1)}, bf16[4,144,864]{2,1,0:T(8,128)(2,1)}, u32[]{:S(2)}, u32[]{:S(2)}) collective-permute-start(bf16[4,144,864]{2,1,0:T(8,128)(2,1)} %add_convert_fusion.10), channel_id=1, source_target_pairs={{8,16},{16,8},{9,17},{17,9},{10,18},{18,10},{11,19},{19,11},{12,20... | collective-permute-start | bytes 2985992 | tf_op jit(solution)/shard_map/ppermute | solution.py:162
  521.5 18.7 %collective-permute-start.75 = (bf16[144,1536]{1,0:T(8,128)(2,1)S(1)}, bf16[144,1536]{1,0:T(8,128)(2,1)}, u32[]{:S(2)}, u32[]{:S(2)}) collective-permute-start(bf16[144,1536]{1,0:T(8,128)(2,1)S(1)} %fusion.5), channel_id=1, source_target_pairs={{0,8},{24,16},{1,9},{25,17},{2,10},{26,18},{3,11},{27,19},{4,12},{... | collective-permute-start | bytes 1327112 | tf_op jit(solution)/shard_map/ppermute | solution.py:162
  538.8 13.8 %collective-permute-start.81 = (bf16[128,1152]{1,0:T(8,128)(2,1)}, bf16[128,1152]{1,0:T(8,128)(2,1)S(1)}, u32[]{:S(2)}, u32[]{:S(2)}) collective-permute-start(bf16[128,1152]{1,0:T(8,128)(2,1)} %reduce-scatter.2.cloned.1.call-done), channel_id=1, source_target_pairs={{0,8},{24,16},{1,9},{25,17},{2,10},{26,18},{3,11},{27,19},{4,12},{... | collective-permute-start | bytes 884744 | tf_op jit(solution)/shard_map/ppermute | solution.py:162
  541.3 16.4 %collective-permute-start.77 = (bf16[144,1536]{1,0:T(8,128)(2,1)S(1)}, bf16[144,1536]{1,0:T(8,128)(2,1)S(1)}, u32[]{:S(2)}, u32[]{:S(2)}) collective-permute-start(bf16[144,1536]{1,0:T(8,128)(2,1)S(1)} %add_convert_fusion.17), channel_id=1, source_target_pairs={{8,16},{16,8},{9,17},{17,9},{10,18},{18,10},{11,19},{19,11},{12,20... | collective-permute-start | bytes 1327112 | tf_op jit(solution)/shard_map/ppermute | solution.py:162
  544.9 30.6 %collective-permute-start.89 = (bf16[4,144,864]{2,1,0:T(8,128)(2,1)}, bf16[4,144,864]{2,1,0:T(8,128)(2,1)}, u32[]{:S(2)}, u32[]{:S(2)}) collective-permute-start(bf16[4,144,864]{2,1,0:T(8,128)(2,1)} %add_convert_fusion.8.refs_1_), channel_id=1, source_target_pairs={{8,0},{16,24},{9,1},{17,25},{10,2},{18,26},{11,3},{19,27},{12,4},{... | collective-permute-start | bytes 2985992 | tf_op jit(solution)/shard_map/ppermute | solution.py:162
  560.5 21.4 %collective-permute-start.87 = (bf16[128,1152]{1,0:T(8,128)(2,1)}, bf16[128,1152]{1,0:T(8,128)(2,1)}, u32[]{:S(2)}, u32[]{:S(2)}) collective-permute-start(bf16[128,1152]{1,0:T(8,128)(2,1)} %add_convert_fusion.18), channel_id=1, source_target_pairs={{8,0},{16,24},{9,1},{17,25},{10,2},{18,26},{11,3},{19,27},{12,4},{... | collective-permute-start | bytes 884744 | tf_op jit(solution)/shard_map/ppermute | solution.py:162
  563.1 27.4 %collective-permute-start.84 = (bf16[144,1536]{1,0:T(8,128)(2,1)S(1)}, bf16[144,1536]{1,0:T(8,128)(2,1)S(1)}, u32[]{:S(2)}, u32[]{:S(2)}) collective-permute-start(bf16[144,1536]{1,0:T(8,128)(2,1)S(1)} %add_convert_fusion.16), channel_id=1, source_target_pairs={{8,0},{16,24},{9,1},{17,25},{10,2},{18,26},{11,3},{19,27},{12,4},{... | collective-permute-start | bytes 1327112 | tf_op jit(solution)/shard_map/ppermute | solution.py:162
  565.1 27.0 %collective-permute-start.90 = (f32[40,128]{1,0:T(8,128)S(1)}, f32[40,128]{1,0:T(8,128)S(1)}, u32[]{:S(2)}, u32[]{:S(2)}) collective-permute-start(f32[40,128]{1,0:T(8,128)S(1)} %add.384), channel_id=1, source_target_pairs={{8,0},{16,24},{9,1},{17,25},{10,2},{18,26},{11,3},{19,27},{12,4},{... | collective-permute-start | bytes 61448 | tf_op jit(solution)/shard_map/ppermute | solution.py:162
  (183 other events, 1831.6 us)
Sparse Core Ops, SparseCore 0:
  9.9 32.0 all-gather.2
  43.9 41.8 all-gather.4
  468.8 59.5 reduce-scatter.1

commit v5 on v4

--- a/solution.py
+++ b/solution.py
@@ -1173,6 +1173,7 @@
     land(down_line)
     step(u0)
     step(gl1)
+    out_line = begin(part_out, *clock)
     u1 = begin(up_halves[1], *clock)
     grad_qkv = blocks_grad(
         order,
@@ -1218,7 +1219,7 @@
     clock[:] = [part_qkv]
     qkv_line = begin(part_qkv, *clock)
     land(gl1)
-    out_line = begin(part_out, *clock)
+    step(out_line)
     code = 1
     while code < n:
         gains = gains + xor_permute(gains, n, code)

time: 606 us -> 615 us (1.015)
  waiting for transfers between devices: 183 us -> 190 us
    ppermute x24, waiting for transfers between devices: 48.8 us -> 55.7 us  [send(): self.moved = lax.ppermute(self.total, 'dp', self.steps[self.at][1])]
    unnamed x303 -> x331, local copies, waits for them, and re-layouts: 37.2 us -> 39 us
  transfers between devices with their start and end apart: 97 -> 97, of which waited for: 48 -> 49; matrix products, arithmetic and copies ran while one was open for 12% -> 11% of each run, Pallas kernels for 17% -> 17%
where the time goes in v5:
time: 615 us; the launch traced here: 609 us
  waiting for transfers between devices  190 us (31%)
  starting transfers between devices  150 us (24%)
  Pallas kernels  147 us (24%)
  local copies, waits for them, and re-layouts  54.8 us (9%)
  other arithmetic  47.2 us (8%)
  between operations  16.6 us (3%)
    ppermute x66, waiting for transfers between devices, xor_permute(): return lax.ppermute(x, 'ctx', [(i, i ^ code) for i in range(axis_size)])  118 us
    ppermute x24, starting transfers between devices, send(): self.moved = lax.ppermute(self.total, 'dp', self.steps[self.at][1])  76.6 us
    ppermute x66, starting transfers between devices, xor_permute(): return lax.ppermute(x, 'ctx', [(i, i ^ code) for i in range(axis_size)])  58.2 us
    ppermute x24, waiting for transfers between devices, send(): self.moved = lax.ppermute(self.total, 'dp', self.steps[self.at][1])  55.7 us
    unnamed x331, local copies, waits for them, and re-layouts  39 us
    pallas_call x4, Pallas kernels, feed_backward(): vmem_call(kernel, (hidden, hidden, jax.ShapeDtypeStruct((tokens, width),...  30 us
    pallas_call x4, Pallas kernels, feed_forward(): vmem_call(kernel, (hidden, hidden, hidden, jax.ShapeDtypeStruct((tokens,...  28 us
    pallas_call x3, Pallas kernels, weight_grad(): vmem_call(kernel, jax.ShapeDtypeStruct((rows, columns), BF16), limit=24,...  23.9 us
  transfers between devices with their start and end apart: 97, of which 49 were waited for; matrix products, arithmetic and copies ran while one was open for 11% of the time, Pallas kernels for 17%

profile of v5, /device:TPU:0, one launch (start us, length us, event | category | flops | bytes accessed | tf_op | source)
XLA Modules:
  0.0 609.0 jit_solution(7269281674441266524)
XLA Ops:
  9.8 2.9 collective-permute-start
  18.4 3.0 collective-permute-done.3
  22.0 3.1 collective-permute-done.4
  36.4 4.5 all-to-all-start
  46.0 36.3 %collective-permute-done.8.a_ref = bf16[2,192,512]{2,1,0:T(8,128)(2,1)S(1)} collective-permute-done((bf16[2,192,512]{2,1,0:T(8,128)(2,1)}, bf16[2,192,512]{2,1,0:T(8,128)(2,1)S(1)}, u32[]{:S(2)}, u32[]{:S(2)}) %collective-permute-start.8) | collective-permute-done | bytes 393248 | tf_op jit(solution)/shard_map/ppermute | solution.py:63
  97.5 7.2 %shard_map.276 = (bf16[192,1024]{1,0:T(8,128)(2,1)S(1)}, f32[192,4]{1,0:T(8,128)S(1)}, f32[192,1152]{1,0:T(8,128)S(1)}, f32[192,1152]{1,0:T(8,128)S(1)}, bf16[192,1152]{1,0:T(8,128)(2,1)}) custom-call(bf16[384,1024]{1,0:T(8,128)(2,1)S(1)} %get-tuple-element.223.refs_0_.refs_9_, s32[192,1]{1,0:T(8,128)S(1)} %copy.57.refs_1_.refs_10_, ...), custom_call_target="tpu_custom_call" | custom-call | tf_op jit(solution)/shard_map/pallas_call | solution.py:376
  110.3 6.5 %shard_map.277 = (bf16[192,1024]{1,0:T(8,128)(2,1)S(1)}, f32[192,4]{1,0:T(8,128)S(1)}, f32[192,1152]{1,0:T(8,128)S(1)}, f32[192,1152]{1,0:T(8,128)S(1)}, bf16[192,1152]{1,0:T(8,128)(2,1)S(1)}) custom-call(bf16[384,1024]{1,0:T(8,128)(2,1)S(1)} %get-tuple-element.223.refs_0_.refs_9_, s32[192,1]{1,0:T(8,128)S(1)} %copy.59.refs_1_.refs_10_, ...), custom_call_target="tpu_custom_call" | custom-call | tf_op jit(solution)/shard_map/pallas_call | solution.py:376
  117.5 2.9 collective-permute-done.13.a_ref
  126.9 14.7 %collective-permute-done.17.second_ref = bf16[8,144,864]{2,1,0:T(8,128)(2,1)} collective-permute-done((bf16[8,144,864]{2,1,0:T(8,128)(2,1)}, bf16[8,144,864]{2,1,0:T(8,128)(2,1)}, u32[]{:S(2)}, u32[]{:S(2)}) %collective-permute-start.17) | collective-permute-done | bytes 1990688 | tf_op jit(solution)/shard_map/ppermute | solution.py:967
  141.6 4.9 shard_map.278
  148.5 7.0 %shard_map.280 = (bf16[768,864]{1,0:T(8,128)(2,1)S(1)}, bf16[768,864]{1,0:T(8,128)(2,1)S(1)}, bf16[768,864]{1,0:T(8,128)(2,1)S(1)}, bf16[768,1152]{1,0:T(8,128)(2,1)S(1)}) custom-call(bf16[768,1152]{1,0:T(8,128)(2,1)S(1)} %bitcast.189, bf16[1152,864]{1,0:T(8,128)(2,1)S(1)} %bitcast.173, bf16[1152,864]{1,0:T(8,128)(2,1)S(1)} %bitcast.181, ...), custom_call_target="tpu_custom_call" | custom-call | tf_op jit(solution)/shard_map/pallas_call | solution.py:712
  157.7 6.9 %shard_map.281 = (bf16[768,864]{1,0:T(8,128)(2,1)S(1)}, bf16[768,864]{1,0:T(8,128)(2,1)S(1)}, bf16[768,864]{1,0:T(8,128)(2,1)S(1)}, bf16[768,1152]{1,0:T(8,128)(2,1)S(1)}) custom-call(bf16[768,1152]{1,0:T(8,128)(2,1)S(1)} %bitcast.195, bf16[1152,864]{1,0:T(8,128)(2,1)S(1)} %bitcast.174, bf16[1152,864]{1,0:T(8,128)(2,1)S(1)} %bitcast.182, ...), custom_call_target="tpu_custom_call" | custom-call | tf_op jit(solution)/shard_map/pallas_call | solution.py:712
  168.4 5.3 collective-permute-done.22.d1_ref
  174.2 6.8 %shard_map.283 = (bf16[768,864]{1,0:T(8,128)(2,1)S(1)}, bf16[768,864]{1,0:T(8,128)(2,1)S(1)}, bf16[768,864]{1,0:T(8,128)(2,1)S(1)}, bf16[768,1152]{1,0:T(8,128)(2,1)S(1)}) custom-call(bf16[768,1152]{1,0:T(8,128)(2,1)S(1)} %bitcast.192, bf16[1152,864]{1,0:T(8,128)(2,1)S(1)} %bitcast.175, bf16[1152,864]{1,0:T(8,128)(2,1)S(1)} %bitcast.183, ...), custom_call_target="tpu_custom_call" | custom-call | tf_op jit(solution)/shard_map/pallas_call | solution.py:712
  184.4 7.3 %shard_map.284 = (bf16[768,864]{1,0:T(8,128)(2,1)S(1)}, bf16[768,864]{1,0:T(8,128)(2,1)S(1)}, bf16[768,864]{1,0:T(8,128)(2,1)S(1)}, bf16[768,1152]{1,0:T(8,128)(2,1)S(1)}) custom-call(bf16[768,1152]{1,0:T(8,128)(2,1)S(1)} %bitcast.198, bf16[1152,864]{1,0:T(8,128)(2,1)S(1)} %bitcast.176, bf16[1152,864]{1,0:T(8,128)(2,1)S(1)} %bitcast.184, ...), custom_call_target="tpu_custom_call" | custom-call | tf_op jit(solution)/shard_map/pallas_call | solution.py:712
  194.4 5.3 collective-permute-done.24
  206.2 8.3 %collective-permute-done.27.b_ref = bf16[192,1152]{1,0:T(8,128)(2,1)S(1)} collective-permute-done((bf16[192,1152]{1,0:T(8,128)(2,1)S(1)}, bf16[192,1152]{1,0:T(8,128)(2,1)S(1)}, u32[]{:S(2)}, u32[]{:S(2)}) %collective-permute-start.27) | collective-permute-done | bytes 442400 | tf_op jit(solution)/shard_map/ppermute | solution.py:63
  222.1 6.8 %collective-permute-done.34.a_ref = bf16[192,1152]{1,0:T(8,128)(2,1)S(1)} collective-permute-done((bf16[192,1152]{1,0:T(8,128)(2,1)S(1)}, bf16[192,1152]{1,0:T(8,128)(2,1)S(1)}, u32[]{:S(2)}, u32[]{:S(2)}) %collective-permute-start.34) | collective-permute-done | bytes 442400 | tf_op jit(solution)/shard_map/ppermute | solution.py:63
  232.5 5.9 collective-permute-done.32.b_ref
  243.3 7.0 %shard_map.288 = (bf16[768,864]{1,0:T(8,128)(2,1)S(1)}, bf16[768,864]{1,0:T(8,128)(2,1)S(1)}, bf16[768,1152]{1,0:T(8,128)(2,1)S(1)}) custom-call(bf16[768,1152]{1,0:T(8,128)(2,1)S(1)} %bitcast.201, bf16[768,864]{1,0:T(8,128)(2,1)S(1)} %copy-done.51, bf16[768,864]{1,0:T(8,128)(2,1)S(1)} %copy-done.53, bf16[1152,864]{1,0:T(8,128)(2,1)S(1)} %bitcast.177, ...), custom_call_target="tpu_custom_call" | custom-call | tf_op jit(solution)/shard_map/pallas_call | solution.py:739
  251.4 2.6 collective-permute-done.39.a_ref
  255.2 7.9 %shard_map.289 = (bf16[768,864]{1,0:T(8,128)(2,1)S(1)}, bf16[768,864]{1,0:T(8,128)(2,1)S(1)}, bf16[768,1152]{1,0:T(8,128)(2,1)}) custom-call(bf16[768,1152]{1,0:T(8,128)(2,1)S(1)} %bitcast.209, bf16[768,864]{1,0:T(8,128)(2,1)S(1)} %get-tuple-element.268.slope_ref, bf16[768,864]{1,0:T(8,128)(2,1)S(1)} %copy-done.47, bf16[1152,864]{1,0:T(8,128)(2,1)S(1)} %bitcast.178, ...), custom_call_target="tpu_custom_call" | custom-call | tf_op jit(solution)/shard_map/pallas_call | solution.py:739
  265.0 6.0 collective-permute-done.42.d1_ref
  273.5 7.2 %shard_map.291 = (bf16[768,864]{1,0:T(8,128)(2,1)S(1)}, bf16[768,864]{1,0:T(8,128)(2,1)S(1)}, bf16[768,1152]{1,0:T(8,128)(2,1)S(1)}) custom-call(bf16[768,1152]{1,0:T(8,128)(2,1)S(1)} %bitcast.203, bf16[768,864]{1,0:T(8,128)(2,1)S(1)} %copy-done.43, bf16[768,864]{1,0:T(8,128)(2,1)S(1)} %copy-done.45, bf16[1152,864]{1,0:T(8,128)(2,1)S(1)} %bitcast.179, ...), custom_call_target="tpu_custom_call" | custom-call | tf_op jit(solution)/shard_map/pallas_call | solution.py:739
  280.7 3.1 add_convert_fusion.4.refs_0_
  284.5 8.9 %shard_map.292 = bf16[864,1152]{1,0:T(8,128)(2,1)} custom-call(bf16[768,864]{1,0:T(8,128)(2,1)S(1)} %copy-done.65, bf16[768,864]{1,0:T(8,128)(2,1)S(1)} %copy-done.67, bf16[768,864]{1,0:T(8,128)(2,1)S(1)} %copy-done.69, bf16[768,864]{1,0:T(8,128)(2,1)S(1)} %copy-done.71, bf16[768,1152]{1,0:T(8,128)(2,1)S(1)} %bitcast.202, bf16[768,1152]{1,0:T(8,128)(2,1)S(1)} %bitcast.210, ...), custom_call_target="tpu_custom_call" | custom-call | tf_op jit(solution)/shard_map/pallas_call | solution.py:767
  293.4 7.8 %shard_map.293 = (bf16[768,864]{1,0:T(8,128)(2,1)S(1)}, bf16[768,864]{1,0:T(8,128)(2,1)S(1)}, bf16[768,1152]{1,0:T(8,128)(2,1)}) custom-call(bf16[768,1152]{1,0:T(8,128)(2,1)S(1)} %bitcast.212, bf16[768,864]{1,0:T(8,128)(2,1)S(1)} %get-tuple-element.284.slope_ref, bf16[768,864]{1,0:T(8,128)(2,1)S(1)} %get-tuple-element.285.value_ref, ...), custom_call_target="tpu_custom_call" | custom-call | tf_op jit(solution)/shard_map/pallas_call | solution.py:739
  304.2 4.9 collective-permute-start.45
  315.5 7.5 %shard_map.294 = bf16[1152,864]{1,0:T(8,128)(2,1)S(1)} custom-call(bf16[768,1152]{1,0:T(8,128)(2,1)S(1)} %bitcast.190, bf16[768,1152]{1,0:T(8,128)(2,1)S(1)} %bitcast.196, bf16[768,1152]{1,0:T(8,128)(2,1)S(1)} %bitcast.193, bf16[768,1152]{1,0:T(8,128)(2,1)S(1)} %bitcast.199, bf16[768,864]{1,0:T(8,128)(2,1)S(1)} %copy-done.61, ...), custom_call_target="tpu_custom_call" | custom-call | tf_op jit(solution)/shard_map/pallas_call | solution.py:767
  324.3 4.6 all-to-all-start.1
  328.9 2.4 add_convert_fusion.3.refs_0_
  335.1 11.0 %shard_map.295 = (f32[192,1152]{1,0:T(8,128)S(1)}, bf16[192,1152]{1,0:T(8,128)(2,1)S(1)}, f32[1,1152]{1,0:T(1,128)S(1)}, f32[1,1152]{1,0:T(1,128)S(1)}, bf16[192...) custom-call(bf16[4,192,1152]{2,1,0:T(8,128)(2,1)} %copy-done.152, ...), custom_call_target="tpu_custom_call" | custom-call | tf_op jit(solution)/shard_map/pallas_call | solution.py:549
  346.3 4.0 collective-permute-done.45
  350.3 3.9 add_convert_fusion.1
  354.3 2.4 collective-permute-start.51
  362.8 3.1 fusion.35
  371.3 7.5 %shard_map.296 = bf16[1152,864]{1,0:T(8,128)(2,1)S(1)} custom-call(bf16[768,1152]{1,0:T(8,128)(2,1)S(1)} %bitcast.191, bf16[768,1152]{1,0:T(8,128)(2,1)S(1)} %bitcast.197, bf16[768,1152]{1,0:T(8,128)(2,1)S(1)} %bitcast.194, bf16[768,1152]{1,0:T(8,128)(2,1)S(1)} %bitcast.200, bf16[768,864]{1,0:T(8,128)(2,1)S(1)} %copy-done.49, ...), custom_call_target="tpu_custom_call" | custom-call | tf_op jit(solution)/shard_map/pallas_call | solution.py:767
  378.8 4.5 collective-permute-start.57
  383.4 4.5 all-to-all-start.2
  388.2 11.1 %shard_map.297 = (f32[192,1152]{1,0:T(8,128)S(1)}, bf16[192,1152]{1,0:T(8,128)(2,1)S(1)}, f32[1,1152]{1,0:T(1,128)S(1)}, f32[1,1152]{1,0:T(1,128)S(1)}, bf16[192...) custom-call(bf16[4,192,1152]{2,1,0:T(8,128)(2,1)} %copy-done.151, ...), custom_call_target="tpu_custom_call" | custom-call | tf_op jit(solution)/shard_map/pallas_call | solution.py:549
  401.6 3.9 add_convert_fusion
  405.5 2.8 add_convert_fusion.15
  412.1 6.9 %collective-permute-start.64 = (bf16[4,144,864]{2,1,0:T(8,128)(2,1)}, bf16[4,144,864]{2,1,0:T(8,128)(2,1)}, u32[]{:S(2)}, u32[]{:S(2)}) collective-permute-start(bf16[4,144,864]{2,1,0:T(8,128)(2,1)} %get-tuple-element.316), channel_id=1, source_target_pairs={{0,8},{24,16},{1,9},{25,17},{2,10},{26,18},{3,11},{27,19},{4,12},{... | collective-permute-start | bytes 2985992 | tf_op jit(solution)/shard_map/ppermute | solution.py:162
  424.5 2.7 fusion.34
  427.9 3.3 collective-permute-start.65
  432.1 9.4 %collective-permute-done.64 = bf16[4,144,864]{2,1,0:T(8,128)(2,1)} collective-permute-done((bf16[4,144,864]{2,1,0:T(8,128)(2,1)}, bf16[4,144,864]{2,1,0:T(8,128)(2,1)}, u32[]{:S(2)}, u32[]{:S(2)}) %collective-permute-start.64) | collective-permute-done | bytes 995360 | tf_op jit(solution)/shard_map/ppermute | solution.py:162
  445.2 2.5 collective-permute-done.62.b_ref
  452.9 5.7 collective-permute-done.56
  458.6 4.0 collective-permute-done.65
  466.8 5.5 shard_map.299
  477.8 14.4 %collective-permute-start.68 = (bf16[4,144,864]{2,1,0:T(8,128)(2,1)}, bf16[4,144,864]{2,1,0:T(8,128)(2,1)S(1)}, u32[]{:S(2)}, u32[]{:S(2)}) collective-permute-start(bf16[4,144,864]{2,1,0:T(8,128)(2,1)} %get-tuple-element.339), channel_id=1, source_target_pairs={{0,8},{24,16},{1,9},{25,17},{2,10},{26,18},{3,11},{27,19},{4,12},{... | collective-permute-start | bytes 2985992 | tf_op jit(solution)/shard_map/ppermute | solution.py:162
  496.0 3.6 shard_map.300
  503.2 4.6 collective-permute-start.76
  510.7 4.9 collective-permute-done.68
  517.6 4.8 collective-permute-done.80
  523.0 3.8 select_convert_fusion
  531.3 6.1 collective-permute-start.75
  538.2 7.9 %collective-permute-done.75 = bf16[144,1536]{1,0:T(8,128)(2,1)S(1)} collective-permute-done((bf16[144,1536]{1,0:T(8,128)(2,1)S(1)}, bf16[144,1536]{1,0:T(8,128)(2,1)S(1)}, u32[]{:S(2)}, u32[]{:S(2)}) %collective-permute-start.75) | collective-permute-done | bytes 442400 | tf_op jit(solution)/shard_map/ppermute | solution.py:162
  549.5 5.9 collective-permute-done.83.refs_2_
  558.4 13.3 %collective-permute-start.87 = (f32[40,128]{1,0:T(8,128)S(1)}, f32[40,128]{1,0:T(8,128)S(1)}, u32[]{:S(2)}, u32[]{:S(2)}) collective-permute-start(f32[40,128]{1,0:T(8,128)S(1)} %add.379), channel_id=1, source_target_pairs={{0,8},{24,16},{1,9},{25,17},{2,10},{26,18},{3,11},{27,19},{4,12},{... | collective-permute-start | bytes 61448 | tf_op jit(solution)/shard_map/ppermute | solution.py:162
  580.8 2.4 shard_map.301
  583.2 4.0 collective-permute-done.89.refs_3_
  587.2 4.0 shard_map.302
  595.4 4.0 collective-permute-done.85
  (620 shorter events, 194.3 us)
Async XLA Ops:
  7.2 78.5 %all-gather.3.cloned.1.call-start = ((), (), s32[]{:S(2)}) async-start(), calls=%async_computation.4 | async-start | bytes 2654208 | tf_op jit(solution)/shard_map/all_gather | solution.py:916
  7.9 88.0 %all-gather.5.cloned.1.call-start = ((), (), s32[]{:S(2)}) async-start(), calls=%async_computation.5 | async-start | bytes 2654208 | tf_op jit(solution)/shard_map/all_gather | solution.py:962
  9.8 15.5 %collective-permute-start = (bf16[144,512]{1,0:T(8,128)(2,1)S(1)}, bf16[144,512]{1,0:T(8,128)(2,1)S(1)}, u32[]{:S(2)}, u32[]{:S(2)}) collective-permute-start(bf16[144,512]{1,0:T(8,128)(2,1)S(1)} %constant_dynamic-update-slice_fusion.x_ref), channel_id=1, source_target_pairs={{0,2},{1,3},{2,0},{3,1},{4,6},{5,7},{6,4},{7,5},{8,10},{9,11},{10,... | collective-permute-start | bytes 442376 | tf_op jit(solution)/shard_map/ppermute | solution.py:63
  12.7 12.6 %collective-permute-start.1 = (bf16[144,512]{1,0:T(8,128)(2,1)S(1)}, bf16[144,512]{1,0:T(8,128)(2,1)S(1)}, u32[]{:S(2)}, u32[]{:S(2)}) collective-permute-start(bf16[144,512]{1,0:T(8,128)(2,1)S(1)} %constant_dynamic-update-slice_fusion.x_ref), channel_id=1, source_target_pairs={{0,4},{1,5},{2,6},{3,7},{4,0},{5,1},{6,2},{7,3},{8,12},{9,13},{10,... | collective-permute-start | bytes 442376 | tf_op jit(solution)/shard_map/ppermute | solution.py:63
  36.4 45.9 %all-to-all-start = ((bf16[8,144,864]{2,1,0:T(8,128)(2,1)}), bf16[8,144,864]{2,1,0:T(8,128)(2,1)}, u32[]{:S(2)}, u32[]{:S(2)}) async-start(bf16[8,144,864]{2,1,0:T(8,128)(2,1)} %copy-done.16), calls=%async_computation | async-start | bytes 4128768 | tf_op jit(solution)/shard_map/all_to_all | solution.py:931
  41.1 41.2 %collective-permute-start.8 = (bf16[2,192,512]{2,1,0:T(8,128)(2,1)}, bf16[2,192,512]{2,1,0:T(8,128)(2,1)S(1)}, u32[]{:S(2)}, u32[]{:S(2)}) collective-permute-start(bf16[2,192,512]{2,1,0:T(8,128)(2,1)} %get-tuple-element.209.x_ref), channel_id=1, source_target_pairs={{0,2},{1,3},{2,0},{3,1},{4,6},{5,7},{6,4},{7,5},{8,10},{9,11},{10,... | collective-permute-start | bytes 1179656 | tf_op jit(solution)/shard_map/ppermute | solution.py:63
  43.1 39.2 %collective-permute-start.9 = (bf16[2,192,512]{2,1,0:T(8,128)(2,1)}, bf16[2,192,512]{2,1,0:T(8,128)(2,1)S(1)}, u32[]{:S(2)}, u32[]{:S(2)}) collective-permute-start(bf16[2,192,512]{2,1,0:T(8,128)(2,1)} %get-tuple-element.209.x_ref), channel_id=1, source_target_pairs={{0,4},{1,5},{2,6},{3,7},{4,0},{5,1},{6,2},{7,3},{8,12},{9,13},{10,... | collective-permute-start | bytes 1179656 | tf_op jit(solution)/shard_map/ppermute | solution.py:63
  93.9 47.7 %collective-permute-start.17 = (bf16[8,144,864]{2,1,0:T(8,128)(2,1)}, bf16[8,144,864]{2,1,0:T(8,128)(2,1)}, u32[]{:S(2)}, u32[]{:S(2)}) collective-permute-start(bf16[8,144,864]{2,1,0:T(8,128)(2,1)} %all-to-all-done.first_ref), channel_id=1, source_target_pairs={{0,8},{8,0},{16,24},{24,16},{1,9},{9,1},{17,25},{25,17},{2,10},{10... | collective-permute-start | bytes 5971976 | tf_op jit(solution)/shard_map/ppermute | solution.py:967
  107.9 12.5 %collective-permute-start.13 = (bf16[192,1152]{1,0:T(8,128)(2,1)}, bf16[192,1152]{1,0:T(8,128)(2,1)}, u32[]{:S(2)}, u32[]{:S(2)}) collective-permute-start(bf16[192,1152]{1,0:T(8,128)(2,1)} %get-tuple-element.222.x_ref), channel_id=1, source_target_pairs={{0,2},{1,3},{2,0},{3,1},{4,6},{5,7},{6,4},{7,5},{8,10},{9,11},{10,... | collective-permute-start | bytes 1327112 | tf_op jit(solution)/shard_map/ppermute | solution.py:63
  108.5 12.2 %collective-permute-start.14 = (bf16[192,1152]{1,0:T(8,128)(2,1)}, bf16[192,1152]{1,0:T(8,128)(2,1)}, u32[]{:S(2)}, u32[]{:S(2)}) collective-permute-start(bf16[192,1152]{1,0:T(8,128)(2,1)} %get-tuple-element.222.x_ref), channel_id=1, source_target_pairs={{0,4},{1,5},{2,6},{3,7},{4,0},{5,1},{6,2},{7,3},{8,12},{9,13},{10,... | collective-permute-start | bytes 1327112 | tf_op jit(solution)/shard_map/ppermute | solution.py:63
  120.8 25.8 %collective-permute-start.18 = (bf16[192,1152]{1,0:T(8,128)(2,1)S(1)}, bf16[192,1152]{1,0:T(8,128)(2,1)S(1)}, u32[]{:S(2)}, u32[]{:S(2)}) collective-permute-start(bf16[192,1152]{1,0:T(8,128)(2,1)S(1)} %get-tuple-element.229.x_ref), channel_id=1, source_target_pairs={{0,2},{1,3},{2,0},{3,1},{4,6},{5,7},{6,4},{7,5},{8,10},{9,11},{10,... | collective-permute-start | bytes 1327112 | tf_op jit(solution)/shard_map/ppermute | solution.py:63
  122.1 24.4 %collective-permute-start.19 = (bf16[192,1152]{1,0:T(8,128)(2,1)S(1)}, bf16[192,1152]{1,0:T(8,128)(2,1)S(1)}, u32[]{:S(2)}, u32[]{:S(2)}) collective-permute-start(bf16[192,1152]{1,0:T(8,128)(2,1)S(1)} %get-tuple-element.229.x_ref), channel_id=1, source_target_pairs={{0,4},{1,5},{2,6},{3,7},{4,0},{5,1},{6,2},{7,3},{8,12},{9,13},{10,... | collective-permute-start | bytes 1327112 | tf_op jit(solution)/shard_map/ppermute | solution.py:63
  123.7 22.9 %collective-permute-start.15 = (bf16[96,1152]{1,0:T(8,128)(2,1)S(1)}, bf16[96,1152]{1,0:T(8,128)(2,1)S(1)}, u32[]{:S(2)}, u32[]{:S(2)}) collective-permute-start(bf16[96,1152]{1,0:T(8,128)(2,1)S(1)} %slice.404), channel_id=1, source_target_pairs={{0,4},{1,5},{2,6},{3,7},{4,0},{5,1},{6,2},{7,3},{8,12},{9,13},{10,... | collective-permute-start | bytes 663560 | tf_op jit(solution)/shard_map/ppermute | solution.py:63
  126.1 20.4 %collective-permute-start.16 = (bf16[96,1152]{1,0:T(8,128)(2,1)S(1)}, bf16[96,1152]{1,0:T(8,128)(2,1)S(1)}, u32[]{:S(2)}, u32[]{:S(2)}) collective-permute-start(bf16[96,1152]{1,0:T(8,128)(2,1)S(1)} %slice.405), channel_id=1, source_target_pairs={{0,2},{1,3},{2,0},{3,1},{4,6},{5,7},{6,4},{7,5},{8,10},{9,11},{10,... | collective-permute-start | bytes 663560 | tf_op jit(solution)/shard_map/ppermute | solution.py:63
  165.7 17.6 %collective-permute-start.21 = (bf16[4,192,1152]{2,1,0:T(8,128)(2,1)S(1)}, bf16[4,192,1152]{2,1,0:T(8,128)(2,1)S(1)}, u32[]{:S(2)}, u32[]{:S(2)}) collective-permute-start(bf16[4,192,1152]{2,1,0:T(8,128)(2,1)S(1)} %bitcast.224), channel_id=1, source_target_pairs={{0,1},{1,0},{2,3},{3,2},{4,5},{5,4},{6,7},{7,6},{8,9},{9,8},{10,11... | collective-permute-start | bytes 5308424 | tf_op jit(solution)/shard_map/ppermute | solution.py:63
  201.3 13.2 %collective-permute-start.27 = (bf16[192,1152]{1,0:T(8,128)(2,1)S(1)}, bf16[192,1152]{1,0:T(8,128)(2,1)S(1)}, u32[]{:S(2)}, u32[]{:S(2)}) collective-permute-start(bf16[192,1152]{1,0:T(8,128)(2,1)S(1)} %pad_maximum_fusion.2), channel_id=1, source_target_pairs={{0,2},{1,3},{2,0},{3,1},{4,6},{5,7},{6,4},{7,5},{8,10},{9,11},{10,... | collective-permute-start | bytes 1327112 | tf_op jit(solution)/shard_map/ppermute | solution.py:63
  201.8 13.2 %collective-permute-start.28 = (bf16[192,1152]{1,0:T(8,128)(2,1)S(1)}, bf16[192,1152]{1,0:T(8,128)(2,1)S(1)}, u32[]{:S(2)}, u32[]{:S(2)}) collective-permute-start(bf16[192,1152]{1,0:T(8,128)(2,1)S(1)} %pad_maximum_fusion.3), channel_id=1, source_target_pairs={{0,4},{1,5},{2,6},{3,7},{4,0},{5,1},{6,2},{7,3},{8,12},{9,13},{10,... | collective-permute-start | bytes 1327112 | tf_op jit(solution)/shard_map/ppermute | solution.py:63
  203.8 15.4 %collective-permute-start.30 = (bf16[96,1152]{1,0:T(8,128)(2,1)S(1)}, bf16[96,1152]{1,0:T(8,128)(2,1)S(1)}, u32[]{:S(2)}, u32[]{:S(2)}) collective-permute-start(bf16[96,1152]{1,0:T(8,128)(2,1)S(1)} %get-tuple-element.427), channel_id=1, source_target_pairs={{0,2},{1,3},{2,0},{3,1},{4,6},{5,7},{6,4},{7,5},{8,10},{9,11},{10,... | collective-permute-start | bytes 663560 | tf_op jit(solution)/shard_map/ppermute | solution.py:63
  204.5 15.2 %collective-permute-start.31 = (bf16[96,1152]{1,0:T(8,128)(2,1)S(1)}, bf16[96,1152]{1,0:T(8,128)(2,1)S(1)}, u32[]{:S(2)}, u32[]{:S(2)}) collective-permute-start(bf16[96,1152]{1,0:T(8,128)(2,1)S(1)} %get-tuple-element.426), channel_id=1, source_target_pairs={{0,4},{1,5},{2,6},{3,7},{4,0},{5,1},{6,2},{7,3},{8,12},{9,13},{10,... | collective-permute-start | bytes 663560 | tf_op jit(solution)/shard_map/ppermute | solution.py:63
  215.7 13.2 %collective-permute-start.34 = (bf16[192,1152]{1,0:T(8,128)(2,1)S(1)}, bf16[192,1152]{1,0:T(8,128)(2,1)S(1)}, u32[]{:S(2)}, u32[]{:S(2)}) collective-permute-start(bf16[192,1152]{1,0:T(8,128)(2,1)S(1)} %get-tuple-element.251.x_ref), channel_id=1, source_target_pairs={{0,2},{1,3},{2,0},{3,1},{4,6},{5,7},{6,4},{7,5},{8,10},{9,11},{10,... | collective-permute-start | bytes 1327112 | tf_op jit(solution)/shard_map/ppermute | solution.py:63
  217.5 13.1 %collective-permute-start.35 = (bf16[192,1152]{1,0:T(8,128)(2,1)S(1)}, bf16[192,1152]{1,0:T(8,128)(2,1)S(1)}, u32[]{:S(2)}, u32[]{:S(2)}) collective-permute-start(bf16[192,1152]{1,0:T(8,128)(2,1)S(1)} %get-tuple-element.251.x_ref), channel_id=1, source_target_pairs={{0,4},{1,5},{2,6},{3,7},{4,0},{5,1},{6,2},{7,3},{8,12},{9,13},{10,... | collective-permute-start | bytes 1327112 | tf_op jit(solution)/shard_map/ppermute | solution.py:63
  219.9 18.5 %collective-permute-start.32 = (bf16[192,1152]{1,0:T(8,128)(2,1)S(1)}, bf16[192,1152]{1,0:T(8,128)(2,1)S(1)}, u32[]{:S(2)}, u32[]{:S(2)}) collective-permute-start(bf16[192,1152]{1,0:T(8,128)(2,1)S(1)} %pad_maximum_fusion.4), channel_id=1, source_target_pairs={{0,2},{1,3},{2,0},{3,1},{4,6},{5,7},{6,4},{7,5},{8,10},{9,11},{10,... | collective-permute-start | bytes 1327112 | tf_op jit(solution)/shard_map/ppermute | solution.py:63
  221.7 17.2 %collective-permute-start.33 = (bf16[192,1152]{1,0:T(8,128)(2,1)S(1)}, bf16[192,1152]{1,0:T(8,128)(2,1)S(1)}, u32[]{:S(2)}, u32[]{:S(2)}) collective-permute-start(bf16[192,1152]{1,0:T(8,128)(2,1)S(1)} %pad_maximum_fusion.5), channel_id=1, source_target_pairs={{0,4},{1,5},{2,6},{3,7},{4,0},{5,1},{6,2},{7,3},{8,12},{9,13},{10,... | collective-permute-start | bytes 1327112 | tf_op jit(solution)/shard_map/ppermute | solution.py:63
  241.4 13.8 %collective-permute-start.38 = (bf16[4,192,1152]{2,1,0:T(8,128)(2,1)S(1)}, bf16[4,192,1152]{2,1,0:T(8,128)(2,1)S(1)}, u32[]{:S(2)}, u32[]{:S(2)}) collective-permute-start(bf16[4,192,1152]{2,1,0:T(8,128)(2,1)S(1)} %shard_map.287), channel_id=1, source_target_pairs={{0,1},{1,0},{2,3},{3,2},{4,5},{5,4},{6,7},{7,6},{8,9},{9,8},{10,11... | collective-permute-start | bytes 5308424 | tf_op jit(solution)/shard_map/ppermute | solution.py:63
  241.4 12.6 %collective-permute-start.39 = (bf16[192,1152]{1,0:T(8,128)(2,1)S(1)}, bf16[192,1152]{1,0:T(8,128)(2,1)S(1)}, u32[]{:S(2)}, u32[]{:S(2)}) collective-permute-start(bf16[192,1152]{1,0:T(8,128)(2,1)S(1)} %get-tuple-element.261.x_ref), channel_id=1, source_target_pairs={{0,2},{1,3},{2,0},{3,1},{4,6},{5,7},{6,4},{7,5},{8,10},{9,11},{10,... | collective-permute-start | bytes 1327112 | tf_op jit(solution)/shard_map/ppermute | solution.py:63
  263.1 17.6 %collective-permute-start.41 = (bf16[4,192,1152]{2,1,0:T(8,128)(2,1)}, bf16[4,192,1152]{2,1,0:T(8,128)(2,1)}, u32[]{:S(2)}, u32[]{:S(2)}) collective-permute-start(bf16[4,192,1152]{2,1,0:T(8,128)(2,1)} %bitcast.37), channel_id=1, source_target_pairs={{0,1},{1,0},{2,3},{3,2},{4,5},{5,4},{6,7},{7,6},{8,9},{9,8},{10,11... | collective-permute-start | bytes 5308424 | tf_op jit(solution)/shard_map/ppermute | solution.py:63
  301.3 27.6 %collective-permute-start.50 = (bf16[4,192,1152]{2,1,0:T(8,128)(2,1)}, bf16[4,192,1152]{2,1,0:T(8,128)(2,1)}, u32[]{:S(2)}, u32[]{:S(2)}) collective-permute-start(bf16[4,192,1152]{2,1,0:T(8,128)(2,1)} %bitcast.45), channel_id=1, source_target_pairs={{0,1},{1,0},{2,3},{3,2},{4,5},{5,4},{6,7},{7,6},{8,9},{9,8},{10,11... | collective-permute-start | bytes 5308424 | tf_op jit(solution)/shard_map/ppermute | solution.py:63
  304.2 46.1 %collective-permute-start.45 = (bf16[864,1152]{1,0:T(8,128)(2,1)}, bf16[864,1152]{1,0:T(8,128)(2,1)}, u32[]{:S(2)}, u32[]{:S(2)}) collective-permute-start(bf16[864,1152]{1,0:T(8,128)(2,1)} %shard_map.292), channel_id=1, source_target_pairs={{0,8},{24,16},{1,9},{25,17},{2,10},{26,18},{3,11},{27,19},{4,12},{... | collective-permute-start | bytes 5971976 | tf_op jit(solution)/shard_map/ppermute | solution.py:162
  312.3 19.1 %collective-permute-start.48 = (bf16[192,1152]{1,0:T(8,128)(2,1)}, bf16[192,1152]{1,0:T(8,128)(2,1)}, u32[]{:S(2)}, u32[]{:S(2)}) collective-permute-start(bf16[192,1152]{1,0:T(8,128)(2,1)} %pad_maximum_fusion.6), channel_id=1, source_target_pairs={{0,2},{1,3},{2,0},{3,1},{4,6},{5,7},{6,4},{7,5},{8,10},{9,11},{10,... | collective-permute-start | bytes 1327112 | tf_op jit(solution)/shard_map/ppermute | solution.py:63
  313.8 17.7 %collective-permute-start.49 = (bf16[192,1152]{1,0:T(8,128)(2,1)}, bf16[192,1152]{1,0:T(8,128)(2,1)}, u32[]{:S(2)}, u32[]{:S(2)}) collective-permute-start(bf16[192,1152]{1,0:T(8,128)(2,1)} %pad_maximum_fusion.7), channel_id=1, source_target_pairs={{0,4},{1,5},{2,6},{3,7},{4,0},{5,1},{6,2},{7,3},{8,12},{9,13},{10,... | collective-permute-start | bytes 1327112 | tf_op jit(solution)/shard_map/ppermute | solution.py:63
  324.3 38.4 %all-to-all-start.1 = ((bf16[8,144,864]{2,1,0:T(8,128)(2,1)}), bf16[8,144,864]{2,1,0:T(8,128)(2,1)}, u32[]{:S(2)}, u32[]{:S(2)}) async-start(bf16[8,144,864]{2,1,0:T(8,128)(2,1)} %bitcast.208), calls=%async_computation.1 | async-start | bytes 4128768 | tf_op jit(solution)/shard_map/all_to_all | solution.py:1102
  331.6 27.4 %collective-permute-start.52 = (bf16[96,1152]{1,0:T(8,128)(2,1)S(1)}, bf16[96,1152]{1,0:T(8,128)(2,1)S(1)}, u32[]{:S(2)}, u32[]{:S(2)}) collective-permute-start(bf16[96,1152]{1,0:T(8,128)(2,1)S(1)} %get-tuple-element.415), channel_id=1, source_target_pairs={{0,2},{1,3},{2,0},{3,1},{4,6},{5,7},{6,4},{7,5},{8,10},{9,11},{10,... | collective-permute-start | bytes 663560 | tf_op jit(solution)/shard_map/ppermute | solution.py:63
  333.6 25.4 %collective-permute-start.53 = (bf16[96,1152]{1,0:T(8,128)(2,1)S(1)}, bf16[96,1152]{1,0:T(8,128)(2,1)S(1)}, u32[]{:S(2)}, u32[]{:S(2)}) collective-permute-start(bf16[96,1152]{1,0:T(8,128)(2,1)S(1)} %get-tuple-element.414), channel_id=1, source_target_pairs={{0,4},{1,5},{2,6},{3,7},{4,0},{5,1},{6,2},{7,3},{8,12},{9,13},{10,... | collective-permute-start | bytes 663560 | tf_op jit(solution)/shard_map/ppermute | solution.py:63
  354.3 47.4 %collective-permute-start.51 = (bf16[864,1152]{1,0:T(8,128)(2,1)}, bf16[864,1152]{1,0:T(8,128)(2,1)}, u32[]{:S(2)}, u32[]{:S(2)}) collective-permute-start(bf16[864,1152]{1,0:T(8,128)(2,1)} %add_convert_fusion.1), channel_id=1, source_target_pairs={{8,16},{16,8},{9,17},{17,9},{10,18},{18,10},{11,19},{19,11},{12,20... | collective-permute-start | bytes 5971976 | tf_op jit(solution)/shard_map/ppermute | solution.py:162
  359.9 28.2 %collective-permute-start.54 = (bf16[192,1152]{1,0:T(8,128)(2,1)}, bf16[192,1152]{1,0:T(8,128)(2,1)}, u32[]{:S(2)}, u32[]{:S(2)}) collective-permute-start(bf16[192,1152]{1,0:T(8,128)(2,1)} %pad_maximum_fusion.8), channel_id=1, source_target_pairs={{0,2},{1,3},{2,0},{3,1},{4,6},{5,7},{6,4},{7,5},{8,10},{9,11},{10,... | collective-permute-start | bytes 1327112 | tf_op jit(solution)/shard_map/ppermute | solution.py:63
  362.1 26.0 %collective-permute-start.55 = (bf16[192,1152]{1,0:T(8,128)(2,1)}, bf16[192,1152]{1,0:T(8,128)(2,1)}, u32[]{:S(2)}, u32[]{:S(2)}) collective-permute-start(bf16[192,1152]{1,0:T(8,128)(2,1)} %pad_maximum_fusion.9), channel_id=1, source_target_pairs={{0,4},{1,5},{2,6},{3,7},{4,0},{5,1},{6,2},{7,3},{8,12},{9,13},{10,... | collective-permute-start | bytes 1327112 | tf_op jit(solution)/shard_map/ppermute | solution.py:63
  378.8 26.8 %collective-permute-start.57 = (bf16[4,144,864]{2,1,0:T(8,128)(2,1)}, bf16[4,144,864]{2,1,0:T(8,128)(2,1)}, u32[]{:S(2)}, u32[]{:S(2)}) collective-permute-start(bf16[4,144,864]{2,1,0:T(8,128)(2,1)} %get-tuple-element.309), channel_id=1, source_target_pairs={{0,8},{24,16},{1,9},{25,17},{2,10},{26,18},{3,11},{27,19},{4,12},{... | collective-permute-start | bytes 2985992 | tf_op jit(solution)/shard_map/ppermute | solution.py:162
  383.4 41.1 %all-to-all-start.2 = ((bf16[8,144,864]{2,1,0:T(8,128)(2,1)}), bf16[8,144,864]{2,1,0:T(8,128)(2,1)}, u32[]{:S(2)}, u32[]{:S(2)}) async-start(bf16[8,144,864]{2,1,0:T(8,128)(2,1)} %bitcast.207), calls=%async_computation.2 | async-start | bytes 4128768 | tf_op jit(solution)/shard_map/all_to_all | solution.py:1102
  387.9 76.2 %reduce-scatter.2.cloned.1.call-start = ((), (), s32[]{:S(2)}) async-start(), calls=%async_computation.6 | async-start | bytes 2654208 | tf_op jit(solution)/shard_map/reduce_scatter | solution.py:1137
  399.5 19.5 %collective-permute-start.59 = (bf16[4,2,192,512]{3,2,1,0:T(8,128)(2,1)S(1)}, bf16[4,2,192,512]{3,2,1,0:T(8,128)(2,1)}, u32[]{:S(2)}, u32[]{:S(2)}) collective-permute-start(bf16[4,2,192,512]{3,2,1,0:T(8,128)(2,1)S(1)} %pad_maximum_fusion), channel_id=1, source_target_pairs={{0,1},{1,0},{2,3},{3,2},{4,5},{5,4},{6,7},{7,6},{8,9},{9,8},{10,11... | collective-permute-start | bytes 4718600 | tf_op jit(solution)/shard_map/ppermute | solution.py:63
  410.7 47.9 %collective-permute-start.56 = (bf16[864,1152]{1,0:T(8,128)(2,1)}, bf16[864,1152]{1,0:T(8,128)(2,1)}, u32[]{:S(2)}, u32[]{:S(2)}) collective-permute-start(bf16[864,1152]{1,0:T(8,128)(2,1)} %add_convert_fusion), channel_id=1, source_target_pairs={{8,0},{16,24},{9,1},{17,25},{10,2},{18,26},{11,3},{19,27},{12,4},{... | collective-permute-start | bytes 5971976 | tf_op jit(solution)/shard_map/ppermute | solution.py:162
  412.1 29.4 %collective-permute-start.64 = (bf16[4,144,864]{2,1,0:T(8,128)(2,1)}, bf16[4,144,864]{2,1,0:T(8,128)(2,1)}, u32[]{:S(2)}, u32[]{:S(2)}) collective-permute-start(bf16[4,144,864]{2,1,0:T(8,128)(2,1)} %get-tuple-element.316), channel_id=1, source_target_pairs={{0,8},{24,16},{1,9},{25,17},{2,10},{26,18},{3,11},{27,19},{4,12},{... | collective-permute-start | bytes 2985992 | tf_op jit(solution)/shard_map/ppermute | solution.py:162
  427.2 24.1 %collective-permute-start.58 = (bf16[4,144,864]{2,1,0:T(8,128)(2,1)}, bf16[4,144,864]{2,1,0:T(8,128)(2,1)S(1)}, u32[]{:S(2)}, u32[]{:S(2)}) collective-permute-start(bf16[4,144,864]{2,1,0:T(8,128)(2,1)} %add_convert_fusion.15), channel_id=1, source_target_pairs={{8,16},{16,8},{9,17},{17,9},{10,18},{18,10},{11,19},{19,11},{12,20... | collective-permute-start | bytes 2985992 | tf_op jit(solution)/shard_map/ppermute | solution.py:162
  427.9 34.7 %collective-permute-start.65 = (bf16[4,144,864]{2,1,0:T(8,128)(2,1)S(1)}, bf16[4,144,864]{2,1,0:T(8,128)(2,1)S(1)}, u32[]{:S(2)}, u32[]{:S(2)}) collective-permute-start(bf16[4,144,864]{2,1,0:T(8,128)(2,1)S(1)} %get-tuple-element.326), channel_id=1, source_target_pairs={{0,8},{24,16},{1,9},{25,17},{2,10},{26,18},{3,11},{27,19},{4,12},{... | collective-permute-start | bytes 2985992 | tf_op jit(solution)/shard_map/ppermute | solution.py:162
  431.4 16.3 %collective-permute-start.62 = (bf16[2,192,512]{2,1,0:T(8,128)(2,1)S(1)}, bf16[2,192,512]{2,1,0:T(8,128)(2,1)S(1)}, u32[]{:S(2)}, u32[]{:S(2)}) collective-permute-start(bf16[2,192,512]{2,1,0:T(8,128)(2,1)S(1)} %pad_maximum_fusion.12), channel_id=1, source_target_pairs={{0,2},{1,3},{2,0},{3,1},{4,6},{5,7},{6,4},{7,5},{8,10},{9,11},{10,... | collective-permute-start | bytes 1179656 | tf_op jit(solution)/shard_map/ppermute | solution.py:63
  447.7 16.2 %collective-permute-start.67 = (bf16[4,144,864]{2,1,0:T(8,128)(2,1)S(1)}, bf16[4,144,864]{2,1,0:T(8,128)(2,1)S(1)}, u32[]{:S(2)}, u32[]{:S(2)}) collective-permute-start(bf16[4,144,864]{2,1,0:T(8,128)(2,1)S(1)} %add_convert_fusion.14), channel_id=1, source_target_pairs={{8,16},{16,8},{9,17},{17,9},{10,18},{18,10},{11,19},{19,11},{12,20... | collective-permute-start | bytes 2985992 | tf_op jit(solution)/shard_map/ppermute | solution.py:162
  473.5 18.7 %collective-permute-start.70 = (bf16[4,144,1536]{2,1,0:T(8,128)(2,1)}, bf16[4,144,1536]{2,1,0:T(8,128)(2,1)}, u32[]{:S(2)}, u32[]{:S(2)}) collective-permute-start(bf16[4,144,1536]{2,1,0:T(8,128)(2,1)} %get-tuple-element.346), channel_id=1, source_target_pairs={{0,1},{1,0},{2,3},{3,2},{4,5},{5,4},{6,7},{7,6},{8,9},{9,8},{10,11... | collective-permute-start | bytes 5308424 | tf_op jit(solution)/shard_map/ppermute | solution.py:63
  475.8 34.3 %collective-permute-start.69 = (bf16[4,144,864]{2,1,0:T(8,128)(2,1)S(1)}, bf16[4,144,864]{2,1,0:T(8,128)(2,1)S(1)}, u32[]{:S(2)}, u32[]{:S(2)}) collective-permute-start(bf16[4,144,864]{2,1,0:T(8,128)(2,1)S(1)} %add_convert_fusion.13.refs_0_), channel_id=1, source_target_pairs={{8,0},{16,24},{9,1},{17,25},{10,2},{18,26},{11,3},{19,27},{12,4},{... | collective-permute-start | bytes 2985992 | tf_op jit(solution)/shard_map/ppermute | solution.py:162
  477.1 38.8 %collective-permute-start.66 = (bf16[4,144,864]{2,1,0:T(8,128)(2,1)}, bf16[4,144,864]{2,1,0:T(8,128)(2,1)S(1)}, u32[]{:S(2)}, u32[]{:S(2)}) collective-permute-start(bf16[4,144,864]{2,1,0:T(8,128)(2,1)} %add_convert_fusion.12), channel_id=1, source_target_pairs={{8,16},{16,8},{9,17},{17,9},{10,18},{18,10},{11,19},{19,11},{12,20... | collective-permute-start | bytes 2985992 | tf_op jit(solution)/shard_map/ppermute | solution.py:162
  477.8 37.8 %collective-permute-start.68 = (bf16[4,144,864]{2,1,0:T(8,128)(2,1)}, bf16[4,144,864]{2,1,0:T(8,128)(2,1)S(1)}, u32[]{:S(2)}, u32[]{:S(2)}) collective-permute-start(bf16[4,144,864]{2,1,0:T(8,128)(2,1)} %get-tuple-element.339), channel_id=1, source_target_pairs={{0,8},{24,16},{1,9},{25,17},{2,10},{26,18},{3,11},{27,19},{4,12},{... | collective-permute-start | bytes 2985992 | tf_op jit(solution)/shard_map/ppermute | solution.py:162
  501.8 35.5 %collective-permute-start.77 = (bf16[4,144,864]{2,1,0:T(8,128)(2,1)S(1)}, bf16[4,144,864]{2,1,0:T(8,128)(2,1)S(1)}, u32[]{:S(2)}, u32[]{:S(2)}) collective-permute-start(bf16[4,144,864]{2,1,0:T(8,128)(2,1)S(1)} %add_convert_fusion.11.refs_1_), channel_id=1, source_target_pairs={{8,0},{16,24},{9,1},{17,25},{10,2},{18,26},{11,3},{19,27},{12,4},{... | collective-permute-start | bytes 2985992 | tf_op jit(solution)/shard_map/ppermute | solution.py:162
  503.2 34.2 %collective-permute-start.76 = (bf16[128,1152]{1,0:T(8,128)(2,1)S(1)}, bf16[128,1152]{1,0:T(8,128)(2,1)S(1)}, u32[]{:S(2)}, u32[]{:S(2)}) collective-permute-start(bf16[128,1152]{1,0:T(8,128)(2,1)S(1)} %copy-done.156), channel_id=1, source_target_pairs={{0,8},{24,16},{1,9},{25,17},{2,10},{26,18},{3,11},{27,19},{4,12},{... | collective-permute-start | bytes 884744 | tf_op jit(solution)/shard_map/ppermute | solution.py:162
  510.2 20.2 %collective-permute-start.73 = (bf16[144,1536]{1,0:T(8,128)(2,1)S(1)}, bf16[144,1536]{1,0:T(8,128)(2,1)S(1)}, u32[]{:S(2)}, u32[]{:S(2)}) collective-permute-start(bf16[144,1536]{1,0:T(8,128)(2,1)S(1)} %pad_maximum_fusion.10), channel_id=1, source_target_pairs={{0,2},{1,3},{2,0},{3,1},{4,6},{5,7},{6,4},{7,5},{8,10},{9,11},{10,... | collective-permute-start | bytes 1327112 | tf_op jit(solution)/shard_map/ppermute | solution.py:63
  515.9 15.1 %collective-permute-start.74 = (bf16[144,1536]{1,0:T(8,128)(2,1)S(1)}, bf16[144,1536]{1,0:T(8,128)(2,1)S(1)}, u32[]{:S(2)}, u32[]{:S(2)}) collective-permute-start(bf16[144,1536]{1,0:T(8,128)(2,1)S(1)} %pad_maximum_fusion.11), channel_id=1, source_target_pairs={{0,4},{1,5},{2,6},{3,7},{4,0},{5,1},{6,2},{7,3},{8,12},{9,13},{10,... | collective-permute-start | bytes 1327112 | tf_op jit(solution)/shard_map/ppermute | solution.py:63
  529.0 26.3 %collective-permute-start.83 = (bf16[4,144,864]{2,1,0:T(8,128)(2,1)S(1)}, bf16[4,144,864]{2,1,0:T(8,128)(2,1)S(1)}, u32[]{:S(2)}, u32[]{:S(2)}) collective-permute-start(bf16[4,144,864]{2,1,0:T(8,128)(2,1)S(1)} %add_convert_fusion.9.refs_0_), channel_id=1, source_target_pairs={{8,0},{16,24},{9,1},{17,25},{10,2},{18,26},{11,3},{19,27},{12,4},{... | collective-permute-start | bytes 2985992 | tf_op jit(solution)/shard_map/ppermute | solution.py:162
  530.3 16.6 %collective-permute-start.84 = (bf16[4,144,864]{2,1,0:T(8,128)(2,1)S(1)}, bf16[4,144,864]{2,1,0:T(8,128)(2,1)S(1)}, u32[]{:S(2)}, u32[]{:S(2)}) collective-permute-start(bf16[4,144,864]{2,1,0:T(8,128)(2,1)S(1)} %add_convert_fusion.10), channel_id=1, source_target_pairs={{8,16},{16,8},{9,17},{17,9},{10,18},{18,10},{11,19},{19,11},{12,20... | collective-permute-start | bytes 2985992 | tf_op jit(solution)/shard_map/ppermute | solution.py:162
  531.3 14.8 %collective-permute-start.75 = (bf16[144,1536]{1,0:T(8,128)(2,1)S(1)}, bf16[144,1536]{1,0:T(8,128)(2,1)S(1)}, u32[]{:S(2)}, u32[]{:S(2)}) collective-permute-start(bf16[144,1536]{1,0:T(8,128)(2,1)S(1)} %fusion.5), channel_id=1, source_target_pairs={{0,8},{24,16},{1,9},{25,17},{2,10},{26,18},{3,11},{27,19},{4,12},{... | collective-permute-start | bytes 1327112 | tf_op jit(solution)/shard_map/ppermute | solution.py:162
  537.5 18.8 %collective-permute-start.82 = (bf16[128,1152]{1,0:T(8,128)(2,1)S(1)}, bf16[128,1152]{1,0:T(8,128)(2,1)S(1)}, u32[]{:S(2)}, u32[]{:S(2)}) collective-permute-start(bf16[128,1152]{1,0:T(8,128)(2,1)S(1)} %add_convert_fusion.19), channel_id=1, source_target_pairs={{8,16},{16,8},{9,17},{17,9},{10,18},{18,10},{11,19},{19,11},{12,20... | collective-permute-start | bytes 884744 | tf_op jit(solution)/shard_map/ppermute | solution.py:162
  546.2 25.5 %collective-permute-start.78 = (bf16[144,1536]{1,0:T(8,128)(2,1)S(1)}, bf16[144,1536]{1,0:T(8,128)(2,1)S(1)}, u32[]{:S(2)}, u32[]{:S(2)}) collective-permute-start(bf16[144,1536]{1,0:T(8,128)(2,1)S(1)} %add_convert_fusion.17), channel_id=1, source_target_pairs={{8,16},{16,8},{9,17},{17,9},{10,18},{18,10},{11,19},{19,11},{12,20... | collective-permute-start | bytes 1327112 | tf_op jit(solution)/shard_map/ppermute | solution.py:162
  548.2 39.0 %collective-permute-start.89 = (bf16[4,144,864]{2,1,0:T(8,128)(2,1)}, bf16[4,144,864]{2,1,0:T(8,128)(2,1)}, u32[]{:S(2)}, u32[]{:S(2)}) collective-permute-start(bf16[4,144,864]{2,1,0:T(8,128)(2,1)} %add_convert_fusion.8.refs_1_), channel_id=1, source_target_pairs={{8,0},{16,24},{9,1},{17,25},{10,2},{18,26},{11,3},{19,27},{12,4},{... | collective-permute-start | bytes 2985992 | tf_op jit(solution)/shard_map/ppermute | solution.py:162
  557.1 36.5 %collective-permute-start.86 = (bf16[128,1152]{1,0:T(8,128)(2,1)}, bf16[128,1152]{1,0:T(8,128)(2,1)}, u32[]{:S(2)}, u32[]{:S(2)}) collective-permute-start(bf16[128,1152]{1,0:T(8,128)(2,1)} %add_convert_fusion.18), channel_id=1, source_target_pairs={{8,0},{16,24},{9,1},{17,25},{10,2},{18,26},{11,3},{19,27},{12,4},{... | collective-permute-start | bytes 884744 | tf_op jit(solution)/shard_map/ppermute | solution.py:162
  558.4 14.8 %collective-permute-start.87 = (f32[40,128]{1,0:T(8,128)S(1)}, f32[40,128]{1,0:T(8,128)S(1)}, u32[]{:S(2)}, u32[]{:S(2)}) collective-permute-start(f32[40,128]{1,0:T(8,128)S(1)} %add.379), channel_id=1, source_target_pairs={{0,8},{24,16},{1,9},{25,17},{2,10},{26,18},{3,11},{27,19},{4,12},{... | collective-permute-start | bytes 61448 | tf_op jit(solution)/shard_map/ppermute | solution.py:162
  575.0 24.4 %collective-permute-start.85 = (bf16[144,1536]{1,0:T(8,128)(2,1)S(1)}, bf16[144,1536]{1,0:T(8,128)(2,1)S(1)}, u32[]{:S(2)}, u32[]{:S(2)}) collective-permute-start(bf16[144,1536]{1,0:T(8,128)(2,1)S(1)} %add_convert_fusion.16), channel_id=1, source_target_pairs={{8,0},{16,24},{9,1},{17,25},{10,2},{18,26},{11,3},{19,27},{12,4},{... | collective-permute-start | bytes 1327112 | tf_op jit(solution)/shard_map/ppermute | solution.py:162
  577.0 24.0 %collective-permute-start.90 = (f32[40,128]{1,0:T(8,128)S(1)}, f32[40,128]{1,0:T(8,128)S(1)}, u32[]{:S(2)}, u32[]{:S(2)}) collective-permute-start(f32[40,128]{1,0:T(8,128)S(1)} %add.384), channel_id=1, source_target_pairs={{8,0},{16,24},{9,1},{17,25},{10,2},{18,26},{11,3},{19,27},{12,4},{... | collective-permute-start | bytes 61448 | tf_op jit(solution)/shard_map/ppermute | solution.py:162
  (197 other events, 1911.3 us)
Sparse Core Ops, SparseCore 0:
  9.9 32.0 all-gather.2
  43.9 41.8 all-gather.4
  410.8 47.5 reduce-scatter.1
